TPU v7x, 256 devices: a whole 4x4x8 slice. The times are simulated.
256 devices in a mesh: seq: 8 (over y, z_lo), head: 32 (over x, z_hi, core).
Axes of the slice: x: 4, y: 4, z: 8 (z_hi: 4, z_lo: 2; z = z_hi * 2 + z_lo), core: 2. Of those that a mesh axis runs over, the one named last changes fastest.
Arguments:
- queries: bfloat16 [2048, 128, 576], P('seq', 'head'), may hold values from -200 to 200
- latent_cache: bfloat16 [2048, 576], P('seq'), may hold values from -6 to 6
- grad_output: bfloat16 [2048, 128, 512], P('seq', 'head'), may hold values from -6 to 6
- query_blocks: int32 [8], replicated, may hold values from 0 to 127, as said below
- key_blocks: int32 [8], replicated, may hold values from 0 to 127, as said below
Outputs:
- grad_queries: bfloat16 [2048, 128, 576], P('seq', 'head')
- grad_cache: float32 [2048, 576], P(('seq', 'head'))
Inputs may be any that keep to these rules, and one draw needn't show every extreme that they name: `query_blocks`: the groups hold distinct block positions, one of them 16 * 8 - 1. `key_blocks`: the groups hold distinct block positions, one of them 0 and one 16 * 8 - 1.
All inputs are finite; a program needn't handle non-finite values.
Results may differ from a plain program's by a relative error of at most 0.013.
Values may be sent and summed in bfloat16 or wider, within the bound.
No kernel may reach another device: no remote copies, remote signals or barrier semaphores. Data moves between devices by JAX's collectives and lax.ppermute only.
A program may use at most 64 MiB of HBM per device.

v0:
```python
import jax
import jax.numpy as jnp
from jax import lax
from jax.sharding import PartitionSpec as P

DL = 512
DR = 64


softmax_scale = 0.07216878364870322


def shards(queries, latent_cache, grad_output, query_blocks, key_blocks):
    gathered = lax.all_gather(latent_cache, "seq", axis=0, tiled=True)
    tile_rows = queries.shape[0]
    group_index = lax.axis_index("seq")
    offsets = jnp.arange(tile_rows, dtype=jnp.int32)
    query_pos = query_blocks[group_index] * tile_rows + offsets
    key_pos = (key_blocks[:, None] * tile_rows + offsets[None, :]).reshape(-1)
    values = gathered[:, :DL]
    scores = softmax_scale * jnp.einsum(
        "qhd,kd->qhk", queries, gathered, preferred_element_type=jnp.float32
    )
    visible = key_pos[None, None, :] <= query_pos[:, None, None]
    masked = jnp.where(visible, scores, -jnp.inf)
    row_max = jnp.max(masked, axis=-1, keepdims=True)
    weights = jnp.exp(masked - row_max)
    probability = weights / jnp.sum(weights, axis=-1, keepdims=True)
    prob_bf16 = probability.astype(jnp.bfloat16)
    grad_probs = jnp.einsum("qhe,ke->qhk", grad_output, values, preferred_element_type=jnp.float32)
    output = jnp.einsum("qhk,ke->qhe", prob_bf16, values, preferred_element_type=jnp.float32)
    correction = jnp.sum(grad_output.astype(jnp.float32) * output, axis=-1, keepdims=True)
    grad_scores = (softmax_scale * probability * (grad_probs - correction)).astype(jnp.bfloat16)
    grad_queries = jnp.einsum(
        "qhk,kd->qhd", grad_scores, gathered, preferred_element_type=jnp.float32
    ).astype(jnp.bfloat16)
    grad_keys = jnp.einsum("qhk,qhd->kd", grad_scores, queries, preferred_element_type=jnp.float32)
    grad_values = jnp.einsum(
        "qhk,qhe->ke", prob_bf16, grad_output, preferred_element_type=jnp.float32
    )
    zeros_rope = jnp.zeros((grad_values.shape[0], DR), jnp.float32)
    partial_value = grad_keys + jnp.concatenate([grad_values, zeros_rope], axis=1)
    grad_cache = lax.psum_scatter(partial_value, ("seq", "head"), scatter_dimension=0, tiled=True)
    return (grad_queries, grad_cache)


def solution(mesh):
    placed = (P("seq", "head", None), P("seq", None), P("seq", "head", None), P(), P())
    return jax.shard_map(
        shards,
        mesh=mesh,
        in_specs=placed,
        out_specs=(P("seq", "head", None), P(("seq", "head"), None)),
        check_vma=False,
    )
```

profile of v0, /device:TPU:32, one launch (start us, length us, event | category | flops | bytes accessed | tf_op | source)
XLA Modules:
  0.0 382.5 jit_solution(10992031810698439277)
XLA Ops:
  7.2 0.0 copy-start
  7.2 0.0 all-gather.2.cloned.1.call-start
  7.2 0.7 all-gather.2.cloned.1.call-update
  7.9 0.0 all-reduce.4.cloned.1.call-start
  8.0 0.7 broadcast_multiply_fusion
  8.6 0.1 add_bitcast_fusion
  8.7 1.2 dynamic_slice.3
  10.6 0.4 broadcast_compare_fusion
  11.0 59.3 %all-gather.2.cloned.1.call-done = bf16[2048,576]{0,1:T(8,128)(2,1)} async-done(((bf16[256,576]{0,1:T(8,128)(2,1)}), bf16[2048,576]{0,1:T(8,128)(2,1)}) %all-gather.2.cloned.1.call-update) | async-done | bytes 2359312 | tf_op jit(solution)/shard_map/all_gather | solution.py:14
  70.2 0.0 copy-done
  70.2 7.3 %fusion.8 = f32[256,4,2048]{2,0,1:T(8,128)} fusion(bf16[256,4,576]{0,2,1:T(8,128)(2,1)S(1)} %copy-done, bf16[2048,576]{0,1:T(8,128)(2,1)} %all-gather.2.cloned.1.call-done), kind=kOutput, calls=%fused_computation.14 | convolution fusion | flops 2415919104 | bytes 11927552 | tf_op jit(solution)/shard_map/qhd,kd->qhk/dot_general | solution.py:21
  77.5 9.4 %fusion.17 = (f32[256,4]{0,1:T(4,128)S(1)}, f32[256,4,2048]{2,0,1:T(8,128)S(1)}) fusion(f32[256,4,2048]{2,0,1:T(8,128)} %fusion.8, pred[256,2048]{1,0:T(8,128)(4,1)S(1)} %broadcast_compare_fusion), kind=kOutput, calls=%fused_computation.28 | output fusion | flops 12584959 | bytes 17305600 | tf_op jit(solution)/shard_map/sub | solution.py:27
  87.0 0.0 copy-start.2
  87.0 1.4 fusion.5
  88.4 0.0 copy-done.2
  88.4 0.0 copy-start.1
  88.4 2.5 convolution_bitcast_fusion
  90.9 0.0 copy-done.1
  90.9 2.5 multiply_reduce_fusion
  93.4 3.3 multiply_convert_fusion
  96.7 0.0 copy-start.3
  96.7 2.1 copy-done.3
  98.7 5.3 %bitcast_add_fusion = f32[2048,576]{1,0:T(8,128)} fusion(f32[2048,512]{1,0:T(8,128)S(1)} %convolution_bitcast_fusion, bf16[256,4,2048]{2,0,1:T(8,128)(2,1)S(1)} %multiply_convert_fusion, bf16[256,4,576]{0,2,1:T(8,128)(2,1)S(1)} %copy-done), kind=kOutput, calls=%fused_computation.5 | convolution fusion | flops 2417098752 | bytes 14286848 | tf_op jit(solution)/shard_map/qhk,qhd->kd/dot_general | solution.py:37
  104.1 0.0 all-reduce.4.cloned.1.call-update
  104.1 5.8 %fusion.10 = bf16[256,4,576]{0,2,1:T(8,128)(2,1)} fusion(bf16[256,4,2048]{2,0,1:T(8,128)(2,1)} %copy-done.3, bf16[2048,576]{0,1:T(8,128)(2,1)S(1)} %copy-done.1), kind=kOutput, calls=%fused_computation.18 | convolution fusion | flops 2416508928 | bytes 7733248 | tf_op jit(solution)/shard_map/qhk,kd->qhd/dot_general | solution.py:34
  109.9 264.4 %all-reduce.4.cloned.1.call-done = f32[2048,576]{1,0:T(8,128)} async-done(((f32[2048,576]{1,0:T(8,128)}), f32[2048,576]{1,0:T(8,128)}) %all-reduce.4.cloned.1.call-update) | async-done | bytes 4718608
  374.3 1.3 constant_dynamic-slice_fusion
  (2 shorter events, 0.0 us)
Async XLA Ops:
  7.2 63.1 %copy-start = (bf16[256,4,576]{0,2,1:T(8,128)(2,1)S(1)}, bf16[256,4,576]{0,2,1:T(8,128)(2,1)}, u32[]{:S(2)}) copy-start(bf16[256,4,576]{0,2,1:T(8,128)(2,1)} %param.5) | copy-start | bytes 3538948
  7.2 63.1 %all-gather.2.cloned.1.call-start = ((), (), s32[]{:S(2)}) async-start(), calls=%async_computation | async-start | bytes 2654208 | tf_op jit(solution)/shard_map/all_gather | solution.py:14
  7.9 366.4 %all-reduce.4.cloned.1.call-start = ((), (), s32[]{:S(2)}) async-start(), calls=%async_computation.1 | async-start | bytes 10485760
  87.0 1.4 copy-start.2
  88.4 2.5 copy-start.1
  96.7 2.1 copy-start.3
Sparse Core Ops, SparseCore 0:
  9.7 60.4 all-gather.1
  104.2 270.0 all-reduce.3
where the time goes:
time: 385 us; the launch traced here: 382 us
  waiting for transfers between devices  324 us (84%)
  matrix products  26.7 us (7%)
  between operations  14.8 us (4%)
  other arithmetic  11.9 us (3%)
  local copies, waits for them, and re-layouts  4.67 us (1%)
    unnamed x3, waiting for transfers between devices  265 us
    all_gather x1, waiting for transfers between devices, shards(): gathered = lax.all_gather(latent_cache, 'seq', axis=0, tiled=True)  59.3 us
    sub x1, other arithmetic, shards(): weights = jnp.exp(masked - row_max)  9.45 us
  transfers between devices with their start and end apart: 2, of which 2 were waited for; matrix products, arithmetic and copies ran while one was open for 2% of the time, Pallas kernels for 0%

commit v1 on v0

v1 whole, which is shorter than its diff:
```python
import functools

import jax
import jax.numpy as jnp
import numpy as np
from jax import lax
from jax.experimental import pallas as pl
from jax.experimental.pallas import tpu as pltpu
from jax.sharding import Mesh
from jax.sharding import PartitionSpec as P

H_LOC = 4
DL = 512
DR = 64
DK = 576
TILE = 256
HALF = 128
NG = 8
KEYS = NG * TILE
LOG2E = 1.4426950408889634

softmax_scale = 0.07216878364870322

BF = jnp.bfloat16
F32 = jnp.float32


def dot(a, b):
    return lax.dot_general(a, b, (((1,), (0,)), ((), ())), preferred_element_type=F32)


def dot_nt(a, b):
    return lax.dot_general(a, b, (((1,), (1,)), ((), ())), preferred_element_type=F32)


def attn_kernel(
    limit_ref, qt_ref, go_ref, k0_ref, k1_ref,
    dqt_ref, own_ref, other_ref,
    kt_s, k_s, s_s, gp_s, w_s, gl_s, gr_s, delta_s,
):
    head = pl.program_id(0)
    chunks = KEYS // TILE

    @pl.when(head == 0)
    def _():
        for half, ref in enumerate((k0_ref, k1_ref)):
            for group in range(NG):
                at = half * NG * HALF + group * HALF
                block = ref[group]
                kt_s[:, at : at + HALF] = block
                k_s[at : at + HALF, :] = block.T
        t = lax.broadcasted_iota(jnp.int32, (HALF, TILE), 0)
        i = lax.broadcasted_iota(jnp.int32, (HALF, TILE), 1)
        delta_s[...] = (t // 8) * 16 + t % 8 - i

    qt = qt_ref[0]
    go = go_ref[0]
    gl_s[pl.ds(head * 2 * TILE, TILE), :] = go
    q = qt.T
    gl_s[pl.ds(head * 2 * TILE + TILE, TILE), :] = q[:, :DL]
    gr_s[pl.ds(head * TILE, TILE), :] = q[:, DL:]
    got = go.T

    delta = delta_s[...]
    peak = jnp.full((1, TILE), -jnp.inf, F32)
    for c in range(chunks):
        rows = slice(c * TILE, (c + 1) * TILE)
        scores = dot(k_s[rows, :], qt) * (softmax_scale * LOG2E)
        parts = []
        for b in range(2):
            part = scores[b * HALF : (b + 1) * HALF]
            part = jnp.where(delta <= limit_ref[2 * c + b], part, -jnp.inf)
            s_s[c * TILE + b * HALF : c * TILE + (b + 1) * HALF, :] = part
            peak = jnp.maximum(peak, jnp.max(part, axis=0, keepdims=True))
        gp_s[rows, :] = dot(k_s[rows, :DL], got)
    total = jnp.zeros((1, TILE), F32)
    for c in range(chunks):
        rows = slice(c * TILE, (c + 1) * TILE)
        e = jnp.exp2(s_s[rows, :] - peak)
        s_s[rows, :] = e
        total = total + jnp.sum(e, axis=0, keepdims=True)
    inv = 1.0 / total
    corr = jnp.zeros((1, TILE), F32)
    for c in range(chunks):
        rows = slice(c * TILE, (c + 1) * TILE)
        pb = (s_s[rows, :] * inv).astype(BF)
        w_s[rows, pl.ds(head * 2 * TILE, TILE)] = pb
        corr = corr + jnp.sum(pb.astype(F32) * gp_s[rows, :], axis=0, keepdims=True)
    inv_scale = inv * softmax_scale
    dqt = jnp.zeros((DK, TILE), F32)
    for c in range(chunks):
        rows = slice(c * TILE, (c + 1) * TILE)
        ds = (s_s[rows, :] * inv_scale * (gp_s[rows, :] - corr)).astype(BF)
        w_s[rows, pl.ds(head * 2 * TILE + TILE, TILE)] = ds
        dqt = dqt + dot(kt_s[:, rows], ds)
    dqt_ref[0] = dqt.astype(BF)

    @pl.when(head == H_LOC - 1)
    def _():
        for c in range(chunks):
            rows = slice(c * TILE, (c + 1) * TILE)
            w = w_s[rows, :]
            lat = dot(w, gl_s[...])
            wr = jnp.concatenate(
                [w[:, (2 * h + 1) * TILE : (2 * h + 2) * TILE] for h in range(H_LOC)], axis=1
            )
            rope = dot(wr, gr_s[...])
            if c < chunks // 2:
                own_ref[rows, :DL] = lat
                own_ref[rows, DL:] = rope
            else:
                to = slice((c - chunks // 2) * TILE, (c + 1 - chunks // 2) * TILE)
                other_ref[to, :DL] = lat.astype(BF)
                other_ref[to, DL:] = rope.astype(BF)


def attention(limits, qt, go, k_own, k_other):
    whole = lambda *shape: pl.BlockSpec(shape, lambda h: (0,) * len(shape))
    return pl.pallas_call(
        attn_kernel,
        grid=(H_LOC,),
        in_specs=[
            pl.BlockSpec(memory_space=pltpu.SMEM),
            pl.BlockSpec((1, DK, TILE), lambda h: (h, 0, 0)),
            pl.BlockSpec((1, TILE, DL), lambda h: (h, 0, 0)),
            whole(NG, DK, HALF),
            whole(NG, DK, HALF),
        ],
        out_specs=[
            pl.BlockSpec((1, DK, TILE), lambda h: (h, 0, 0)),
            whole(KEYS // 2, DK),
            whole(KEYS // 2, DK),
        ],
        out_shape=[
            jax.ShapeDtypeStruct((H_LOC, DK, TILE), BF),
            jax.ShapeDtypeStruct((KEYS // 2, DK), F32),
            jax.ShapeDtypeStruct((KEYS // 2, DK), BF),
        ],
        scratch_shapes=[
            pltpu.VMEM((DK, KEYS), BF),
            pltpu.VMEM((KEYS, DK), BF),
            pltpu.VMEM((KEYS, TILE), F32),
            pltpu.VMEM((KEYS, TILE), F32),
            pltpu.VMEM((KEYS, H_LOC * 2 * TILE), BF),
            pltpu.VMEM((H_LOC * 2 * TILE, DL), BF),
            pltpu.VMEM((H_LOC * TILE, DR), BF),
            pltpu.VMEM((HALF, TILE), jnp.int32),
        ],
        compiler_params=pltpu.CompilerParams(vmem_limit_bytes=48 * 1024 * 1024),
    )(limits, qt, go, k_own, k_other)


def swap_cores(x):
    return lax.ppermute(x, "c", [(0, 1), (1, 0)])


def shards(queries, latent_cache, grad_output, query_blocks, key_blocks):
    core = lax.axis_index("c")
    group = lax.axis_index("y") * 2 + lax.axis_index("zl")
    row = lax.broadcasted_iota(jnp.int32, (TILE, HALF), 0)
    t = lax.broadcasted_iota(jnp.int32, (TILE, HALF), 1)
    pick = (row == (t // 8) * 16 + core * 8 + t % 8).astype(BF)
    mine = lax.dot_general(
        latent_cache, pick, (((0,), (0,)), ((), ())), preferred_element_type=F32
    ).astype(BF)
    sent = jnp.broadcast_to(mine[None], (NG, DK, HALF))
    k_own = lax.all_to_all(sent, ("y", "zl"), 0, 0, tiled=True)
    k_other = swap_cores(k_own)

    qt = queries.transpose(1, 2, 0)
    go = grad_output.transpose(1, 0, 2)
    lag = (query_blocks[group] - key_blocks) * TILE
    limits = jnp.concatenate([lag - core * 8, lag - (1 - core) * 8])
    dqt, own, other = attention(limits, qt, go, k_own, k_other)

    chip = (own + swap_cores(other).astype(F32)).astype(BF)
    got = lax.all_to_all(chip.reshape(32, 32, DK), ("y", "zl", "x"), 0, 0, tiled=True)
    part = jnp.sum(got.astype(F32), axis=0).astype(BF)
    got = lax.all_to_all(part.reshape(4, 8, DK), "zh", 0, 0, tiled=True)
    return dqt.transpose(2, 0, 1), jnp.sum(got.astype(F32), axis=0)


def solution(mesh):
    fine = Mesh(mesh.devices.reshape(4, 2, 4, 4, 2), ("y", "zl", "x", "zh", "c"))
    seq, head = ("y", "zl"), ("x", "zh", "c")
    placed = (P(seq, head, None), P(seq, None), P(seq, head, None), P(), P())
    return jax.shard_map(
        shards,
        mesh=fine,
        in_specs=placed,
        out_specs=(P(seq, head, None), P(seq + head, None)),
        check_vma=False,
    )
```

time: 385 us -> 103 us (0.27)
  waiting for transfers between devices: 324 us -> 2.75 us
  blocking collectives: 0 us -> 63.2 us
  matrix products: 26.7 us -> 0.25 us
  Pallas kernels: 0 us -> 23.5 us
  between operations: 14.8 us -> 0.73 us
  other arithmetic: 11.9 us -> 3.55 us
    unnamed x3 -> x0, waiting for transfers between devices: 265 us -> none
    all_to_all x0 -> x3, blocking collectives: none -> 63.2 us  [the longest x1 26.2 us: shards(): lax.all_to_all(chip.reshape(32, 32, DK), ('y', 'zl', 'x'), 0, 0, tiled=True)]
    all_gather x1 -> x0, waiting for transfers between devices: 59.3 us -> none  [shards(): gathered = lax.all_gather(latent_cache, 'seq', axis=0, tiled=True)]
    dot_general x6 -> x1, matrix products: 26.7 us -> 0.25 us  [shards(): lax.dot_general(latent_cache, pick, (((0,), (0,)), ((), ())), preferred_e...]
    pallas_call x0 -> x1, Pallas kernels: none -> 23.5 us  [attention(): pl.pallas_call(attn_kernel, grid=(H_LOC,), in_specs=[pl.BlockSpec(memory_...]
    sub x1, other arithmetic: 9.45 us -> 0.65 us  [shards(): limits = jnp.concatenate([lag - core * 8, lag - (1 - core) * 8])]
  transfers between devices with their start and end apart: 2 -> 2, of which waited for: 2 -> 2; matrix products, arithmetic and copies ran while one was open for 2% -> 3% of each run, Pallas kernels for 0% -> 0%
where the time goes in v1:
time: 103 us; the launch traced here: 102 us
  blocking collectives  63.2 us (61%)
  Pallas kernels  23.5 us (23%)
  local copies, waits for them, and re-layouts  7.71 us (7%)
  other arithmetic  3.55 us (3%)
  waiting for transfers between devices  2.75 us (3%)
    all_to_all x1, blocking collectives, shards(): lax.all_to_all(chip.reshape(32, 32, DK), ('y', 'zl', 'x'), 0, 0, tiled=True)  26.2 us
    pallas_call x1, Pallas kernels, attention(): pl.pallas_call(attn_kernel, grid=(H_LOC,), in_specs=[pl.BlockSpec(memory_...  23.5 us
    all_to_all x1, blocking collectives, shards(): k_own = lax.all_to_all(sent, ('y', 'zl'), 0, 0, tiled=True)  21.7 us
    all_to_all x1, blocking collectives, shards(): got = lax.all_to_all(part.reshape(4, 8, DK), 'zh', 0, 0, tiled=True)  15.4 us
    unnamed x11, local copies, waits for them, and re-layouts  4.69 us
    ppermute x2, waiting for transfers between devices, swap_cores(): return lax.ppermute(x, 'c', [(0, 1), (1, 0)])  2.75 us
  transfers between devices with their start and end apart: 2, of which 2 were waited for; matrix products, arithmetic and copies ran while one was open for 3% of the time, Pallas kernels for 0%

profile of v1, /device:TPU:32, one launch (start us, length us, event | category | flops | bytes accessed | tf_op | source)
XLA Modules:
  0.0 102.1 jit_solution(12522300316833668093)
XLA Ops:
  0.6 0.0 copy-start
  0.7 0.9 copy-done
  1.6 0.2 fusion
  1.8 0.2 broadcast_in_dim.2
  2.0 21.7 %all_to_all.15.k0_ref = bf16[8,576,128]{2,1,0:T(8,128)(2,1)S(1)} all-to-all(bf16[8,576,128]{2,1,0:T(8,128)(2,1)S(1)} %broadcast_in_dim.2), channel_id=1, replica_groups=mesh['y'=4,'zl'=2,'x'=4,'zh'=4,'c'=2] {'y','zl'}, dimensions={0} | all-to-all | bytes 2359296 | tf_op jit(solution)/shard_map/all_to_all | solution.py:167
  23.7 0.0 copy-start.4
  23.7 0.0 copy-start.3
  23.7 0.0 collective-permute-start
  23.7 1.4 %copy.15 = bf16[256,4,512]{2,0,1:T(8,128)(2,1)S(1)} copy(bf16[256,4,512]{2,1,0:T(4,128)(2,1)} %param.7) | data formatting | bytes 2097152 | tf_op args[2]
  25.1 0.0 copy-done.4
  25.1 0.6 dynamic_slice.3
  25.7 0.0 copy-done.3
  25.7 0.6 broadcast_subtract_fusion.1
  26.4 0.1 pad_add_fusion.limit_ref
  26.5 0.2 collective-permute-done.k1_ref
  26.7 0.0 copy-start.2
  26.7 1.3 %copy-done.2 = bf16[256,4,576]{0,2,1:T(8,128)(2,1)S(1)} copy-done((bf16[256,4,576]{0,2,1:T(8,128)(2,1)S(1)}, bf16[256,4,576]{0,2,1:T(8,128)(2,1)}, u32[]{:S(2)}) %copy-start.2) | copy-done | bytes 1179672
  27.9 23.5 %shard_map.68 = (bf16[4,576,256]{2,1,0:T(8,128)(2,1)}, f32[1024,576]{1,0:T(8,128)}, bf16[1024,576]{1,0:T(8,128)(2,1)S(1)}) custom-call(s32[16]{0:T(128)S(1)} %pad_add_fusion.limit_ref, bf16[4,576,256]{2,1,0:T(8,128)(2,1)S(1)} %bitcast.12, bf16[4,256,512]{2,1,0:T(8,128)(2,1)S(1)} %bitcast.11, bf16[8,576,128]{2,1,0:T(8,128)(2,1)S(1)} %all_to_all.15.k0_ref, ...), custom_call_target="tpu_custom_call" | custom-call | tf_op jit(solution)/shard_map/pallas_call | solution.py:119
  51.5 0.0 copy-start.1
  51.5 1.1 %copy-done.1 = bf16[1024,576]{1,0:T(8,128)(2,1)} copy-done((bf16[1024,576]{1,0:T(8,128)(2,1)}, bf16[1024,576]{1,0:T(8,128)(2,1)S(1)}, u32[]{:S(2)}) %copy-start.1) | copy-done | bytes 1179672
  52.5 1.6 %copy.12 = bf16[1024,576]{0,1:T(8,128)(2,1)S(1)} copy(bf16[1024,576]{1,0:T(8,128)(2,1)} %copy-done.1) | data formatting | bytes 2359296 | tf_op jit(solution)/shard_map/pallas_call | solution.py:119
  54.1 0.4 collective-permute-start.1
  54.5 2.6 %collective-permute-done.1 = bf16[1024,576]{0,1:T(8,128)(2,1)S(1)} collective-permute-done((bf16[1024,576]{0,1:T(8,128)(2,1)S(1)}, bf16[1024,576]{0,1:T(8,128)(2,1)S(1)}, u32[]{:S(2)}, u32[]{:S(2)}) %collective-permute-start.1) | collective-permute-done | bytes 1179680 | tf_op jit(solution)/shard_map/ppermute | solution.py:154
  57.0 0.7 copy.13
  57.8 2.0 %add_convert_fusion = bf16[1024,576]{1,0:T(8,128)(2,1)S(1)} fusion(f32[1024,576]{1,0:T(8,128)} %get-tuple-element.6, bf16[1024,576]{1,0:T(8,128)(2,1)S(1)} %copy.13), kind=kLoop, calls=%fused_computation | loop fusion | flops 1769472 | bytes 4718592 | tf_op jit(solution)/shard_map/convert_element_type | solution.py:176
  59.7 26.2 %all_to_all.16 = bf16[32,32,576]{2,1,0:T(8,128)(2,1)S(1)} all-to-all(bf16[32,32,576]{2,1,0:T(8,128)(2,1)S(1)} %bitcast.13), channel_id=1, replica_groups=mesh['y'=4,'zl'=2,'x'=4,'zh'=4,'c'=2] {'y','zl','x'}, dimensions={0} | all-to-all | bytes 2359296 | tf_op jit(solution)/shard_map/all_to_all | solution.py:177
  85.9 0.2 reduce_sum.21
  86.1 15.4 %all_to_all.17 = bf16[4,8,576]{2,1,0:T(8,128)(2,1)S(1)} all-to-all(bf16[4,8,576]{2,1,0:T(8,128)(2,1)S(1)} %bitcast.14), channel_id=1, replica_groups=mesh['y'=4,'zl'=2,'x'=4,'zh'=4,'c'=2] {'zh'}, dimensions={0} | all-to-all | bytes 73728 | tf_op jit(solution)/shard_map/all_to_all | solution.py:179
  101.5 0.6 convert_reduce_fusion
  (3 shorter events, 0.0 us)
Async XLA Ops:
  0.6 1.0 copy-start
  23.7 1.5 %copy-start.4 = (s32[8]{0:T(128)S(1)}, s32[8]{0:T(128)}, u32[]{:S(2)}) copy-start(s32[8]{0:T(128)} %param.8) | copy-start | bytes 100
  23.7 2.1 %copy-start.3 = (s32[8]{0:T(128)S(1)}, s32[8]{0:T(128)}, u32[]{:S(2)}) copy-start(s32[8]{0:T(128)} %param.9) | copy-start | bytes 100
  23.7 3.0 %collective-permute-start = (bf16[8,576,128]{2,1,0:T(8,128)(2,1)S(1)}, bf16[8,576,128]{2,1,0:T(8,128)(2,1)}, u32[]{:S(2)}, u32[]{:S(2)}) collective-permute-start(bf16[8,576,128]{2,1,0:T(8,128)(2,1)S(1)} %all_to_all.15.k0_ref), channel_id=1, source_target_pairs={{0,1},{1,0},{2,3},{3,2},{4,5},{5,4},{6,7},{7,6},{8,9},{9,8},{10,11... | collective-permute-start | bytes 3538952 | tf_op jit(solution)/shard_map/ppermute | solution.py:154
  26.7 1.3 %copy-start.2 = (bf16[256,4,576]{0,2,1:T(8,128)(2,1)S(1)}, bf16[256,4,576]{0,2,1:T(8,128)(2,1)}, u32[]{:S(2)}) copy-start(bf16[256,4,576]{0,2,1:T(8,128)(2,1)} %param.5) | copy-start | bytes 3538948
  51.5 1.1 %copy-start.1 = (bf16[1024,576]{1,0:T(8,128)(2,1)}, bf16[1024,576]{1,0:T(8,128)(2,1)S(1)}, u32[]{:S(2)}) copy-start(bf16[1024,576]{1,0:T(8,128)(2,1)S(1)} %get-tuple-element.7) | copy-start | bytes 3538948
  54.1 2.9 %collective-permute-start.1 = (bf16[1024,576]{0,1:T(8,128)(2,1)S(1)}, bf16[1024,576]{0,1:T(8,128)(2,1)S(1)}, u32[]{:S(2)}, u32[]{:S(2)}) collective-permute-start(bf16[1024,576]{0,1:T(8,128)(2,1)S(1)} %copy.12), channel_id=1, source_target_pairs={{0,1},{1,0},{2,3},{3,2},{4,5},{5,4},{6,7},{7,6},{8,9},{9,8},{10,11... | collective-permute-start | bytes 3538952 | tf_op jit(solution)/shard_map/ppermute | solution.py:154

commit v2 on v0

v2 whole, which is shorter than its diff:
```python
import functools

import jax
import jax.numpy as jnp
import numpy as np
from jax import lax
from jax.experimental import pallas as pl
from jax.experimental.pallas import tpu as pltpu
from jax.sharding import Mesh
from jax.sharding import PartitionSpec as P

H_LOC = 4
DL = 512
DR = 64
DK = 576
TILE = 256
HALF = 128
NG = 8
KEYS = NG * TILE
LOG2E = 1.4426950408889634
LOW = -jnp.inf
FLOOR = -1e30
SLOTS = ((0, 0), (2, 1), (2, 0), (1, 1), (3, 1), (1, 0), (3, 0), (0, 1))
LANES = 128
OWNED = 32
PACKED = OWNED * DK // LANES
OWN_TYPE = jnp.float32
VMEM_LIMIT = 44 * 1024 * 1024

softmax_scale = 0.07216878364870322

BF = jnp.bfloat16
F32 = jnp.float32


def dot(a, b):
    return lax.dot_general(a, b, (((1,), (0,)), ((), ())), preferred_element_type=F32)


def dot_nt(a, b):
    return lax.dot_general(a, b, (((1,), (1,)), ((), ())), preferred_element_type=F32)


def attn_kernel(
    place_ref, query_blocks_ref, key_blocks_ref, qt_ref, go_ref, *refs
):
    k_refs = refs[: 2 * NG]
    dqt_ref, own_ref, other_ref, kt_s, k_s, e_s, gp_s, w_s, gl_s, gr_s, got_s = refs[2 * NG :]
    chunks = KEYS // TILE
    core, y, zl = (place_ref[n] for n in range(3))
    groups = [((y - dy) & 3) * 2 + (zl ^ dz) for dy, dz in SLOTS]
    lags = [(query_blocks_ref[groups[0]] - key_blocks_ref[g]) * TILE for g in groups]
    limits = [lag - (core ^ half) * 8 for half in range(2) for lag in lags]
    for n, ref in enumerate(k_refs):
        block = ref[...]
        kt_s[:, n * HALF : (n + 1) * HALF] = block
        k_s[n * HALF : (n + 1) * HALF, :] = block.T
    t = lax.broadcasted_iota(jnp.int32, (HALF, TILE), 0)
    i = lax.broadcasted_iota(jnp.int32, (HALF, TILE), 1)
    delta = (t >> 3) * 16 + (t & 7) - i

    peaks = [[None] * chunks for _ in range(H_LOC)]
    sums = [[None] * chunks for _ in range(H_LOC)]
    factors = [None] * H_LOC
    corrs = [None] * H_LOC

    def span(c):
        return slice(c * TILE, (c + 1) * TILE)

    def load(h):
        go = go_ref[h]
        gl_s[h * 2 * TILE : h * 2 * TILE + TILE, :] = go
        got_s[h] = go.T
        q = qt_ref[h].T
        gl_s[h * 2 * TILE + TILE : (h + 1) * 2 * TILE, :] = q[:, :DL]
        gr_s[h * TILE : (h + 1) * TILE, :] = q[:, DL:]

    def weigh(h, c):
        scores = dot(k_s[span(c), :], qt_ref[h]) * (softmax_scale * LOG2E)
        parts = [
            jnp.where(delta <= limits[2 * c + b], scores[b * HALF : (b + 1) * HALF], LOW)
            for b in range(2)
        ]
        peak = jnp.maximum(*[jnp.max(p, axis=0, keepdims=True) for p in parts])
        total = jnp.zeros((1, TILE), F32)
        for b in range(2):
            e = jnp.exp2(parts[b] - jnp.maximum(peak, FLOOR))
            e_s[h, c * TILE + b * HALF : c * TILE + (b + 1) * HALF, :] = e
            total = total + jnp.sum(e, axis=0, keepdims=True)
        peaks[h][c] = peak
        sums[h][c] = total
        gp_s[h, span(c), :] = dot(k_s[span(c), :DL], got_s[h])

    def settle(h):
        peak = functools.reduce(jnp.maximum, peaks[h])
        shares = [jnp.exp2(p - peak) for p in peaks[h]]
        inv = 1.0 / sum(f * s for f, s in zip(shares, sums[h]))
        factors[h] = [f * inv for f in shares]
        corrs[h] = jnp.zeros((1, TILE), F32)

    def correct(h, c):
        pb = (e_s[h, span(c), :] * factors[h][c]).astype(BF)
        w_s[span(c), h * 2 * TILE : h * 2 * TILE + TILE] = pb
        corrs[h] = corrs[h] + jnp.sum(pb.astype(F32) * gp_s[h, span(c), :], axis=0, keepdims=True)

    def differ(h, c):
        p = e_s[h, span(c), :] * (factors[h][c] * softmax_scale)
        ds = (p * (gp_s[h, span(c), :] - corrs[h])).astype(BF)
        w_s[span(c), h * 2 * TILE + TILE : (h + 1) * 2 * TILE] = ds

    def to_queries(h):
        for r in range(2):
            rows = slice(r * DK // 2, (r + 1) * DK // 2)
            out = dot(kt_s[rows, :], w_s[:, h * 2 * TILE + TILE : (h + 1) * 2 * TILE])
            dqt_ref[h, rows, :] = out.astype(BF)

    def to_keys(c):
        w = w_s[span(c), :]
        lat = dot(w, gl_s[...])
        wr = jnp.concatenate(
            [w[:, (2 * h + 1) * TILE : (2 * h + 2) * TILE] for h in range(H_LOC)], axis=1
        )
        rope = dot(wr, gr_s[...])
        ref = own_ref if c < chunks // 2 else other_ref
        for b in range(2):
            group = groups[(2 * c + b) % NG]
            for x in range(4):
                at = b * HALF + x * OWNED
                to = group * 4 + x
                for n in range(DL // LANES):
                    ref[to, n * OWNED : (n + 1) * OWNED, :] = lat[
                        at : at + OWNED, n * LANES : (n + 1) * LANES
                    ].astype(ref.dtype)
                both = jnp.concatenate(
                    [rope[at : at + OWNED // 2], rope[at + OWNED // 2 : at + OWNED]], axis=1
                )
                ref[to, DL // LANES * OWNED :, :] = both.astype(ref.dtype)

    for step in range(H_LOC + 2):
        if step < H_LOC:
            load(step)
        if 1 <= step <= H_LOC:
            settle(step - 1)
        for c in range(chunks):
            if step < H_LOC:
                weigh(step, c)
            if 1 <= step <= H_LOC:
                correct(step - 1, c)
            if step >= 2:
                differ(step - 2, c)
        if step >= 2:
            to_queries(step - 2)
    for c in range(chunks):
        to_keys(c)


def attention(place, query_blocks, key_blocks, qt, go, k_blocks):
    vmem = pl.BlockSpec(memory_space=pltpu.VMEM)
    smem = pl.BlockSpec(memory_space=pltpu.SMEM)
    return pl.pallas_call(
        attn_kernel,
        in_specs=[smem] * 3 + [vmem] * (2 + len(k_blocks)),
        out_specs=[vmem] * 3,
        out_shape=[
            jax.ShapeDtypeStruct((H_LOC, DK, TILE), BF),
            jax.ShapeDtypeStruct((NG * 4, PACKED, LANES), OWN_TYPE),
            jax.ShapeDtypeStruct((NG * 4, PACKED, LANES), BF),
        ],
        scratch_shapes=[
            pltpu.VMEM((DK, KEYS), BF),
            pltpu.VMEM((KEYS, DK), BF),
            pltpu.VMEM((H_LOC, KEYS, TILE), F32),
            pltpu.VMEM((H_LOC, KEYS, TILE), F32),
            pltpu.VMEM((KEYS, H_LOC * 2 * TILE), BF),
            pltpu.VMEM((H_LOC * 2 * TILE, DL), BF),
            pltpu.VMEM((H_LOC * TILE, DR), BF),
            pltpu.VMEM((H_LOC, DL, TILE), BF),
        ],
        compiler_params=pltpu.CompilerParams(vmem_limit_bytes=VMEM_LIMIT),
    )(place, query_blocks, key_blocks, qt, go, *k_blocks)


def swap_cores(x):
    return lax.ppermute(x, "c", [(0, 1), (1, 0)])


def from_group(x, dy, dz):
    pairs = [(y * 2 + z, (y + dy) % 4 * 2 + (z ^ dz)) for y in range(4) for z in range(2)]
    return lax.ppermute(x, ("y", "zl"), pairs)


def unpack(x):
    lat = x[: DL // LANES * OWNED].reshape(DL // LANES, 4, 8, LANES)
    lat = lat.transpose(1, 2, 0, 3).reshape(4, 8, DL)
    rope = x[DL // LANES * OWNED :].reshape(2, 8, 2, DR).transpose(2, 0, 1, 3).reshape(4, 8, DR)
    return jnp.concatenate([lat, rope], axis=2)


def shards(queries, latent_cache, grad_output, query_blocks, key_blocks):
    core, y, zl = (lax.axis_index(a) for a in ("c", "y", "zl"))
    row = lax.broadcasted_iota(jnp.int32, (TILE, TILE), 0)
    t = lax.broadcasted_iota(jnp.int32, (TILE, TILE), 1)
    half, t = t >> 7, t & 127
    pick = (row == (t >> 3) * 16 + (core ^ half) * 8 + (t & 7)).astype(BF)
    here = lax.dot_general(
        latent_cache, pick, (((0,), (0,)), ((), ())), preferred_element_type=F32
    ).astype(BF)
    mine = here[:, :HALF]
    k_own = [from_group(mine, dy, dz) for dy, dz in SLOTS[1:]]
    k_other = [swap_cores(k) for k in k_own]
    qt = queries.transpose(1, 2, 0)
    go = grad_output.transpose(1, 0, 2)
    blocks = [mine] + k_own + [here[:, HALF:]] + k_other
    dqt, own, other = attention(
        jnp.stack([core, y, zl]), query_blocks, key_blocks, qt, go, blocks
    )

    chip = (own + swap_cores(other).astype(F32)).astype(BF)
    got = lax.all_to_all(chip, ("y", "zl", "x"), 0, 0, tiled=True)
    part = unpack(jnp.sum(got.astype(F32), axis=0)).astype(BF)
    got = lax.all_to_all(part, "zh", 0, 0, tiled=True)
    return dqt.transpose(2, 0, 1), jnp.sum(got.astype(F32), axis=0)


def solution(mesh):
    fine = Mesh(mesh.devices.reshape(4, 2, 4, 4, 2), ("y", "zl", "x", "zh", "c"))
    seq, head = ("y", "zl"), ("x", "zh", "c")
    placed = (P(seq, head, None), P(seq, None), P(seq, head, None), P(), P())
    return jax.shard_map(
        shards,
        mesh=fine,
        in_specs=placed,
        out_specs=(P(seq, head, None), P(seq + head, None)),
        check_vma=False,
    )
```

time: 385 us -> 89.2 us (0.23)
  waiting for transfers between devices: 324 us -> 9.05 us
  blocking collectives: 0 us -> 40.5 us
  matrix products: 26.7 us -> 0.25 us
  Pallas kernels: 0 us -> 19.1 us
  starting transfers between devices: 0.08 us -> 15.3 us
  between operations: 14.8 us -> 0.78 us
  other arithmetic: 11.9 us -> 1.14 us
    unnamed x3 -> x0, waiting for transfers between devices: 265 us -> none
    all_gather x1 -> x0, waiting for transfers between devices: 59.3 us -> none  [shards(): gathered = lax.all_gather(latent_cache, 'seq', axis=0, tiled=True)]
    all_to_all x0 -> x2, blocking collectives: none -> 40.5 us  [the longest x1 24.8 us: shards(): got = lax.all_to_all(chip, ('y', 'zl', 'x'), 0, 0, tiled=True)]
    dot_general x6 -> x1, matrix products: 26.7 us -> 0.25 us  [shards(): lax.dot_general(latent_cache, pick, (((0,), (0,)), ((), ())), preferred_e...]
    pallas_call x0 -> x1, Pallas kernels: none -> 19.1 us  [attention(): pl.pallas_call(attn_kernel, in_specs=[smem] * 3 + [vmem] * (2 + len(k_blo...]
    ppermute x0 -> x15, starting transfers between devices: none -> 15.3 us  [the longest x7 13.4 us: from_group(): return lax.ppermute(x, ('y', 'zl'), pairs)]
    sub x1 -> x0, other arithmetic: 9.45 us -> none  [shards(): weights = jnp.exp(masked - row_max)]
    ppermute x0 -> x15, waiting for transfers between devices: none -> 9.05 us  [the longest x7 6.46 us: from_group(): return lax.ppermute(x, ('y', 'zl'), pairs)]
  transfers between devices with their start and end apart: 2 -> 15, of which waited for: 2 -> 3; matrix products, arithmetic and copies ran while one was open for 2% -> 2% of each run, Pallas kernels for 0% -> 0%
where the time goes in v2:
time: 89.2 us; the launch traced here: 88.5 us
  blocking collectives  40.5 us (45%)
  Pallas kernels  19.1 us (21%)
  starting transfers between devices  15.3 us (17%)
  waiting for transfers between devices  9.05 us (10%)
  local copies, waits for them, and re-layouts  2.51 us (3%)
  other arithmetic  1.14 us (1%)
    all_to_all x1, blocking collectives, shards(): got = lax.all_to_all(chip, ('y', 'zl', 'x'), 0, 0, tiled=True)  24.8 us
    pallas_call x1, Pallas kernels, attention(): pl.pallas_call(attn_kernel, in_specs=[smem] * 3 + [vmem] * (2 + len(k_blo...  19.1 us
    all_to_all x1, blocking collectives, shards(): got = lax.all_to_all(part, 'zh', 0, 0, tiled=True)  15.7 us
    ppermute x7, starting transfers between devices, from_group(): return lax.ppermute(x, ('y', 'zl'), pairs)  13.4 us
    ppermute x7, waiting for transfers between devices, from_group(): return lax.ppermute(x, ('y', 'zl'), pairs)  6.46 us
    ppermute x8, waiting for transfers between devices, swap_cores(): return lax.ppermute(x, 'c', [(0, 1), (1, 0)])  2.58 us
    unnamed x9, local copies, waits for them, and re-layouts  2.38 us
    ppermute x8, starting transfers between devices, swap_cores(): return lax.ppermute(x, 'c', [(0, 1), (1, 0)])  1.82 us
  transfers between devices with their start and end apart: 15, of which 3 were waited for; matrix products, arithmetic and copies ran while one was open for 2% of the time, Pallas kernels for 0%

profile of v2, /device:TPU:32, one launch (start us, length us, event | category | flops | bytes accessed | tf_op | source)
XLA Modules:
  0.0 88.5 jit_solution(9787596350053162581)
XLA Ops:
  0.6 0.0 copy-start
  0.7 0.9 %copy-done = bf16[256,576]{0,1:T(8,128)(2,1)S(1)} copy-done((bf16[256,576]{0,1:T(8,128)(2,1)S(1)}, bf16[256,576]{0,1:T(8,128)(2,1)}, u32[]{:S(2)}) %copy-start) | copy-done | bytes 294936
  1.6 0.2 fusion
  1.9 0.0 copy-start.1
  1.9 0.0 copy-start.2
  1.9 0.0 copy-start.3
  1.9 1.9 %collective-permute-start.6 = (bf16[576,128]{1,0:T(8,128)(2,1)S(1)}, bf16[576,128]{1,0:T(8,128)(2,1)S(1)}, u32[]{:S(2)}, u32[]{:S(2)}) collective-permute-start(bf16[576,128]{1,0:T(8,128)(2,1)S(1)} %get-tuple-element.9.refs_0_), channel_id=1, source_target_pairs={{0,32},{32,0},{64,96},{96,64},{128,160},{160,128},{192,224},{224,1... | collective-permute-start | bytes 442376 | tf_op jit(solution)/shard_map/ppermute | solution.py:189
  3.9 1.3 %collective-permute-start.5 = (bf16[576,128]{1,0:T(8,128)(2,1)S(1)}, bf16[576,128]{1,0:T(8,128)(2,1)S(1)}, u32[]{:S(2)}, u32[]{:S(2)}) collective-permute-start(bf16[576,128]{1,0:T(8,128)(2,1)S(1)} %get-tuple-element.9.refs_0_), channel_id=1, source_target_pairs={{0,192},{32,224},{64,0},{96,32},{128,64},{160,96},{192,128},{224,1... | collective-permute-start | bytes 442376 | tf_op jit(solution)/shard_map/ppermute | solution.py:189
  5.1 0.7 collective-permute-start.4
  5.9 3.8 %collective-permute-start.3 = (bf16[576,128]{1,0:T(8,128)(2,1)S(1)}, bf16[576,128]{1,0:T(8,128)(2,1)S(1)}, u32[]{:S(2)}, u32[]{:S(2)}) collective-permute-start(bf16[576,128]{1,0:T(8,128)(2,1)S(1)} %get-tuple-element.9.refs_0_), channel_id=1, source_target_pairs={{0,224},{32,192},{64,32},{96,0},{128,96},{160,64},{192,160},{224,1... | collective-permute-start | bytes 442376 | tf_op jit(solution)/shard_map/ppermute | solution.py:189
  9.7 0.0 collective-permute-start.2
  9.7 0.0 collective-permute-done.6.refs_7_
  9.7 2.2 %collective-permute-start.1 = (bf16[576,128]{1,0:T(8,128)(2,1)S(1)}, bf16[576,128]{1,0:T(8,128)(2,1)S(1)}, u32[]{:S(2)}, u32[]{:S(2)}) collective-permute-start(bf16[576,128]{1,0:T(8,128)(2,1)S(1)} %get-tuple-element.9.refs_0_), channel_id=1, source_target_pairs={{0,128},{32,160},{64,192},{96,224},{128,0},{160,32},{192,64},{224,... | collective-permute-start | bytes 442376 | tf_op jit(solution)/shard_map/ppermute | solution.py:189
  11.9 0.0 collective-permute-done.5.refs_6_
  11.9 3.4 %collective-permute-start = (bf16[576,128]{1,0:T(8,128)(2,1)S(1)}, bf16[576,128]{1,0:T(8,128)(2,1)S(1)}, u32[]{:S(2)}, u32[]{:S(2)}) collective-permute-start(bf16[576,128]{1,0:T(8,128)(2,1)S(1)} %get-tuple-element.9.refs_0_), channel_id=1, source_target_pairs={{0,160},{32,128},{64,224},{96,192},{128,32},{160,0},{192,96},{224,... | collective-permute-start | bytes 442376 | tf_op jit(solution)/shard_map/ppermute | solution.py:189
  15.4 0.0 collective-permute-done.4.refs_5_
  15.4 0.0 collective-permute-start.13
  15.4 0.0 collective-permute-done.3.refs_4_
  15.4 0.5 collective-permute-start.12
  15.9 2.7 %collective-permute-done.2.refs_3_ = bf16[576,128]{1,0:T(8,128)(2,1)S(1)} collective-permute-done((bf16[576,128]{1,0:T(8,128)(2,1)S(1)}, bf16[576,128]{1,0:T(8,128)(2,1)S(1)}, u32[]{:S(2)}, u32[]{:S(2)}) %collective-permute-start.2) | collective-permute-done | bytes 147488 | tf_op jit(solution)/shard_map/ppermute | solution.py:189
  18.6 0.0 collective-permute-start.11
  18.6 3.7 %collective-permute-done.1.refs_2_ = bf16[576,128]{1,0:T(8,128)(2,1)S(1)} collective-permute-done((bf16[576,128]{1,0:T(8,128)(2,1)S(1)}, bf16[576,128]{1,0:T(8,128)(2,1)S(1)}, u32[]{:S(2)}, u32[]{:S(2)}) %collective-permute-start.1) | collective-permute-done | bytes 147488 | tf_op jit(solution)/shard_map/ppermute | solution.py:189
  22.4 0.0 collective-permute-start.10
  22.4 0.0 collective-permute-done.refs_1_
  22.4 0.5 collective-permute-start.9
  22.9 0.0 collective-permute-done.13.refs_15_
  22.9 0.1 collective-permute-start.8
  23.0 0.0 collective-permute-done.12.refs_14_
  23.0 0.4 collective-permute-start.7
  23.4 1.4 %copy.14 = bf16[256,4,512]{2,0,1:T(8,128)(2,1)S(1)} copy(bf16[256,4,512]{2,1,0:T(4,128)(2,1)} %param.7) | data formatting | bytes 2097152 | tf_op args[2]
  24.8 0.1 pad_add_fusion.place_ref
  24.9 0.0 collective-permute-done.11.refs_13_
  24.9 0.0 collective-permute-done.10.refs_12_
  24.9 0.0 collective-permute-done.9.refs_11_
  24.9 0.0 collective-permute-done.8.refs_10_
  24.9 0.0 collective-permute-done.7.refs_9_
  24.9 0.0 copy-done.1
  24.9 0.0 copy-done.2
  24.9 0.0 copy-done.3
  25.0 19.1 %shard_map.68 = (bf16[4,576,256]{2,1,0:T(8,128)(2,1)}, f32[32,144,128]{2,1,0:T(8,128)S(1)}, bf16[32,144,128]{2,1,0:T(8,128)(2,1)S(1)}) custom-call(s32[3]{0:T(128)S(1)} %pad_add_fusion.place_ref, s32[8]{0:T(128)S(1)} %copy-done.2, s32[8]{0:T(128)S(1)} %copy-done.3, bf16[4,576,256]{2,1,0:T(8,128)(2,1)S(1)} %bitcast.20, bf16[4,256,512]{2,1,0:T(8,128)(2,1)S(1)} %bitcast.19, ...), custom_call_target="tpu_custom_call" | custom-call | tf_op jit(solution)/shard_map/pallas_call | solution.py:160
  44.0 0.3 collective-permute-start.14
  44.3 2.6 %collective-permute-done.14 = bf16[32,144,128]{2,1,0:T(8,128)(2,1)S(1)} collective-permute-done((bf16[32,144,128]{2,1,0:T(8,128)(2,1)S(1)}, bf16[32,144,128]{2,1,0:T(8,128)(2,1)S(1)}, u32[]{:S(2)}, u32[]{:S(2)}) %collective-permute-start.14) | collective-permute-done | bytes 1179680 | tf_op jit(solution)/shard_map/ppermute | solution.py:184
  46.9 0.3 add_convert_fusion
  47.1 24.8 %all_to_all.10 = bf16[32,144,128]{2,1,0:T(8,128)(2,1)S(1)} all-to-all(bf16[32,144,128]{2,1,0:T(8,128)(2,1)S(1)} %add_convert_fusion), channel_id=1, replica_groups=mesh['y'=4,'zl'=2,'x'=4,'zh'=4,'c'=2] {'y','zl','x'}, dimensions={0} | all-to-all | bytes 2359296 | tf_op jit(solution)/shard_map/all_to_all | solution.py:219
  71.9 0.2 reduce
  72.1 0.1 reshape.22
  72.2 15.7 %all_to_all.11 = bf16[4,8,576]{2,1,0:T(8,128)(2,1)S(1)} all-to-all(bf16[4,8,576]{2,1,0:T(8,128)(2,1)S(1)} %pad_maximum_fusion), channel_id=1, replica_groups=mesh['y'=4,'zl'=2,'x'=4,'zh'=4,'c'=2] {'zh'}, dimensions={0} | all-to-all | bytes 73728 | tf_op jit(solution)/shard_map/all_to_all | solution.py:221
  87.9 0.6 convert_reduce_fusion
  (7 shorter events, 0.1 us)
Async XLA Ops:
  0.6 1.0 %copy-start = (bf16[256,576]{0,1:T(8,128)(2,1)S(1)}, bf16[256,576]{0,1:T(8,128)(2,1)}, u32[]{:S(2)}) copy-start(bf16[256,576]{0,1:T(8,128)(2,1)} %param.6) | copy-start | bytes 884740
  1.9 23.0 %copy-start.1 = (bf16[256,4,576]{0,2,1:T(8,128)(2,1)S(1)}, bf16[256,4,576]{0,2,1:T(8,128)(2,1)}, u32[]{:S(2)}) copy-start(bf16[256,4,576]{0,2,1:T(8,128)(2,1)} %param.5) | copy-start | bytes 3538948
  1.9 23.0 %copy-start.2 = (s32[8]{0:T(128)S(1)}, s32[8]{0:T(128)}, u32[]{:S(2)}) copy-start(s32[8]{0:T(128)} %query_blocks_ref.1) | copy-start | bytes 100
  1.9 23.0 %copy-start.3 = (s32[8]{0:T(128)S(1)}, s32[8]{0:T(128)}, u32[]{:S(2)}) copy-start(s32[8]{0:T(128)} %key_blocks_ref.1) | copy-start | bytes 100
  1.9 7.8 %collective-permute-start.6 = (bf16[576,128]{1,0:T(8,128)(2,1)S(1)}, bf16[576,128]{1,0:T(8,128)(2,1)S(1)}, u32[]{:S(2)}, u32[]{:S(2)}) collective-permute-start(bf16[576,128]{1,0:T(8,128)(2,1)S(1)} %get-tuple-element.9.refs_0_), channel_id=1, source_target_pairs={{0,32},{32,0},{64,96},{96,64},{128,160},{160,128},{192,224},{224,1... | collective-permute-start | bytes 442376 | tf_op jit(solution)/shard_map/ppermute | solution.py:189
  3.9 8.1 %collective-permute-start.5 = (bf16[576,128]{1,0:T(8,128)(2,1)S(1)}, bf16[576,128]{1,0:T(8,128)(2,1)S(1)}, u32[]{:S(2)}, u32[]{:S(2)}) collective-permute-start(bf16[576,128]{1,0:T(8,128)(2,1)S(1)} %get-tuple-element.9.refs_0_), channel_id=1, source_target_pairs={{0,192},{32,224},{64,0},{96,32},{128,64},{160,96},{192,128},{224,1... | collective-permute-start | bytes 442376 | tf_op jit(solution)/shard_map/ppermute | solution.py:189
  5.1 10.3 %collective-permute-start.4 = (bf16[576,128]{1,0:T(8,128)(2,1)S(1)}, bf16[576,128]{1,0:T(8,128)(2,1)S(1)}, u32[]{:S(2)}, u32[]{:S(2)}) collective-permute-start(bf16[576,128]{1,0:T(8,128)(2,1)S(1)} %get-tuple-element.9.refs_0_), channel_id=1, source_target_pairs={{0,64},{32,96},{64,128},{96,160},{128,192},{160,224},{192,0},{224,... | collective-permute-start | bytes 442376 | tf_op jit(solution)/shard_map/ppermute | solution.py:189
  5.9 9.5 %collective-permute-start.3 = (bf16[576,128]{1,0:T(8,128)(2,1)S(1)}, bf16[576,128]{1,0:T(8,128)(2,1)S(1)}, u32[]{:S(2)}, u32[]{:S(2)}) collective-permute-start(bf16[576,128]{1,0:T(8,128)(2,1)S(1)} %get-tuple-element.9.refs_0_), channel_id=1, source_target_pairs={{0,224},{32,192},{64,32},{96,0},{128,96},{160,64},{192,160},{224,1... | collective-permute-start | bytes 442376 | tf_op jit(solution)/shard_map/ppermute | solution.py:189
  9.7 8.9 %collective-permute-start.2 = (bf16[576,128]{1,0:T(8,128)(2,1)S(1)}, bf16[576,128]{1,0:T(8,128)(2,1)S(1)}, u32[]{:S(2)}, u32[]{:S(2)}) collective-permute-start(bf16[576,128]{1,0:T(8,128)(2,1)S(1)} %get-tuple-element.9.refs_0_), channel_id=1, source_target_pairs={{0,96},{32,64},{64,160},{96,128},{128,224},{160,192},{192,32},{224... | collective-permute-start | bytes 442376 | tf_op jit(solution)/shard_map/ppermute | solution.py:189
  9.7 12.6 %collective-permute-start.1 = (bf16[576,128]{1,0:T(8,128)(2,1)S(1)}, bf16[576,128]{1,0:T(8,128)(2,1)S(1)}, u32[]{:S(2)}, u32[]{:S(2)}) collective-permute-start(bf16[576,128]{1,0:T(8,128)(2,1)S(1)} %get-tuple-element.9.refs_0_), channel_id=1, source_target_pairs={{0,128},{32,160},{64,192},{96,224},{128,0},{160,32},{192,64},{224,... | collective-permute-start | bytes 442376 | tf_op jit(solution)/shard_map/ppermute | solution.py:189
  11.9 10.4 %collective-permute-start = (bf16[576,128]{1,0:T(8,128)(2,1)S(1)}, bf16[576,128]{1,0:T(8,128)(2,1)S(1)}, u32[]{:S(2)}, u32[]{:S(2)}) collective-permute-start(bf16[576,128]{1,0:T(8,128)(2,1)S(1)} %get-tuple-element.9.refs_0_), channel_id=1, source_target_pairs={{0,160},{32,128},{64,224},{96,192},{128,32},{160,0},{192,96},{224,... | collective-permute-start | bytes 442376 | tf_op jit(solution)/shard_map/ppermute | solution.py:189
  15.4 7.5 %collective-permute-start.13 = (bf16[576,128]{1,0:T(8,128)(2,1)S(1)}, bf16[576,128]{1,0:T(8,128)(2,1)S(1)}, u32[]{:S(2)}, u32[]{:S(2)}) collective-permute-start(bf16[576,128]{1,0:T(8,128)(2,1)S(1)} %collective-permute-done.6.refs_7_), channel_id=1, source_target_pairs={{0,1},{1,0},{2,3},{3,2},{4,5},{5,4},{6,7},{7,6},{8,9},{9,8},{10,11... | collective-permute-start | bytes 442376 | tf_op jit(solution)/shard_map/ppermute | solution.py:184
  15.4 7.6 %collective-permute-start.12 = (bf16[576,128]{1,0:T(8,128)(2,1)S(1)}, bf16[576,128]{1,0:T(8,128)(2,1)S(1)}, u32[]{:S(2)}, u32[]{:S(2)}) collective-permute-start(bf16[576,128]{1,0:T(8,128)(2,1)S(1)} %collective-permute-done.5.refs_6_), channel_id=1, source_target_pairs={{0,1},{1,0},{2,3},{3,2},{4,5},{5,4},{6,7},{7,6},{8,9},{9,8},{10,11... | collective-permute-start | bytes 442376 | tf_op jit(solution)/shard_map/ppermute | solution.py:184
  18.6 6.3 %collective-permute-start.11 = (bf16[576,128]{1,0:T(8,128)(2,1)S(1)}, bf16[576,128]{1,0:T(8,128)(2,1)S(1)}, u32[]{:S(2)}, u32[]{:S(2)}) collective-permute-start(bf16[576,128]{1,0:T(8,128)(2,1)S(1)} %collective-permute-done.4.refs_5_), channel_id=1, source_target_pairs={{0,1},{1,0},{2,3},{3,2},{4,5},{5,4},{6,7},{7,6},{8,9},{9,8},{10,11... | collective-permute-start | bytes 442376 | tf_op jit(solution)/shard_map/ppermute | solution.py:184
  22.4 2.5 %collective-permute-start.10 = (bf16[576,128]{1,0:T(8,128)(2,1)S(1)}, bf16[576,128]{1,0:T(8,128)(2,1)S(1)}, u32[]{:S(2)}, u32[]{:S(2)}) collective-permute-start(bf16[576,128]{1,0:T(8,128)(2,1)S(1)} %collective-permute-done.3.refs_4_), channel_id=1, source_target_pairs={{0,1},{1,0},{2,3},{3,2},{4,5},{5,4},{6,7},{7,6},{8,9},{9,8},{10,11... | collective-permute-start | bytes 442376 | tf_op jit(solution)/shard_map/ppermute | solution.py:184
  22.4 2.5 %collective-permute-start.9 = (bf16[576,128]{1,0:T(8,128)(2,1)S(1)}, bf16[576,128]{1,0:T(8,128)(2,1)S(1)}, u32[]{:S(2)}, u32[]{:S(2)}) collective-permute-start(bf16[576,128]{1,0:T(8,128)(2,1)S(1)} %collective-permute-done.2.refs_3_), channel_id=1, source_target_pairs={{0,1},{1,0},{2,3},{3,2},{4,5},{5,4},{6,7},{7,6},{8,9},{9,8},{10,11... | collective-permute-start | bytes 442376 | tf_op jit(solution)/shard_map/ppermute | solution.py:184
  22.9 2.0 %collective-permute-start.8 = (bf16[576,128]{1,0:T(8,128)(2,1)S(1)}, bf16[576,128]{1,0:T(8,128)(2,1)}, u32[]{:S(2)}, u32[]{:S(2)}) collective-permute-start(bf16[576,128]{1,0:T(8,128)(2,1)S(1)} %collective-permute-done.1.refs_2_), channel_id=1, source_target_pairs={{0,1},{1,0},{2,3},{3,2},{4,5},{5,4},{6,7},{7,6},{8,9},{9,8},{10,11... | collective-permute-start | bytes 442376 | tf_op jit(solution)/shard_map/ppermute | solution.py:184
  23.0 2.0 %collective-permute-start.7 = (bf16[576,128]{1,0:T(8,128)(2,1)S(1)}, bf16[576,128]{1,0:T(8,128)(2,1)}, u32[]{:S(2)}, u32[]{:S(2)}) collective-permute-start(bf16[576,128]{1,0:T(8,128)(2,1)S(1)} %collective-permute-done.refs_1_), channel_id=1, source_target_pairs={{0,1},{1,0},{2,3},{3,2},{4,5},{5,4},{6,7},{7,6},{8,9},{9,8},{10,11... | collective-permute-start | bytes 442376 | tf_op jit(solution)/shard_map/ppermute | solution.py:184
  44.0 2.8 %collective-permute-start.14 = (bf16[32,144,128]{2,1,0:T(8,128)(2,1)S(1)}, bf16[32,144,128]{2,1,0:T(8,128)(2,1)S(1)}, u32[]{:S(2)}, u32[]{:S(2)}) collective-permute-start(bf16[32,144,128]{2,1,0:T(8,128)(2,1)S(1)} %get-tuple-element.7), channel_id=1, source_target_pairs={{0,1},{1,0},{2,3},{3,2},{4,5},{5,4},{6,7},{7,6},{8,9},{9,8},{10,11... | collective-permute-start | bytes 3538952 | tf_op jit(solution)/shard_map/ppermute | solution.py:184

commit v3 on v2

--- a/solution.py
+++ b/solution.py
@@ -20,7 +20,7 @@
 LOG2E = 1.4426950408889634
 LOW = -jnp.inf
 FLOOR = -1e30
-SLOTS = ((0, 0), (2, 1), (2, 0), (1, 1), (3, 1), (1, 0), (3, 0), (0, 1))
+K_ROWS = ((0, 1), (0, 1), (1, 0), (0, 1), (1, 0), (0, None), (0, None), (0, None)) + ((None, 0),) * 3
 LANES = 128
 OWNED = 32
 PACKED = OWNED * DK // LANES
@@ -44,17 +44,26 @@
 def attn_kernel(
     place_ref, query_blocks_ref, key_blocks_ref, qt_ref, go_ref, *refs
 ):
-    k_refs = refs[: 2 * NG]
-    dqt_ref, own_ref, other_ref, kt_s, k_s, e_s, gp_s, w_s, gl_s, gr_s, got_s = refs[2 * NG :]
+    k_refs = refs[: len(K_ROWS)]
+    dqt_ref, own_ref, other_ref, kt_s, k_s, e_s, gp_s, w_s, gl_s, gr_s, got_s = refs[len(K_ROWS) :]
     chunks = KEYS // TILE
-    core, y, zl = (place_ref[n] for n in range(3))
-    groups = [((y - dy) & 3) * 2 + (zl ^ dz) for dy, dz in SLOTS]
+    core, y, zl, x = (place_ref[n] for n in range(4))
+    behind = (0, 1 + 2 * core, 3 - 2 * core, 1 + 2 * core, 3 - 2 * core, 0, 2, 2)
+    across = (0, 0, 0, 1, 1, 1, 0, 1)
+    ahead = [(0 - dy) & 3 for dy in behind]
+    floors = [zl ^ dz for dz in across]
+    groups = [((y + up) & 3) * 2 + z for up, z in zip(ahead, floors)]
     lags = [(query_blocks_ref[groups[0]] - key_blocks_ref[g]) * TILE for g in groups]
     limits = [lag - (core ^ half) * 8 for half in range(2) for lag in lags]
-    for n, ref in enumerate(k_refs):
-        block = ref[...]
-        kt_s[:, n * HALF : (n + 1) * HALF] = block
-        k_s[n * HALF : (n + 1) * HALF, :] = block.T
+    n = 0
+    for half in range(2):
+        for ref, rows in zip(k_refs, K_ROWS):
+            if rows[half] is None:
+                continue
+            block = ref[rows[half] * DK : (rows[half] + 1) * DK, :]
+            kt_s[:, n * HALF : (n + 1) * HALF] = block
+            k_s[n * HALF : (n + 1) * HALF, :] = block.T
+            n += 1
     t = lax.broadcasted_iota(jnp.int32, (HALF, TILE), 0)
     i = lax.broadcasted_iota(jnp.int32, (HALF, TILE), 1)
     delta = (t >> 3) * 16 + (t & 7) - i
@@ -123,18 +132,20 @@
         rope = dot(wr, gr_s[...])
         ref = own_ref if c < chunks // 2 else other_ref
         for b in range(2):
-            group = groups[(2 * c + b) % NG]
-            for x in range(4):
-                at = b * HALF + x * OWNED
-                to = group * 4 + x
+            up, floor = ahead[(2 * c + b) % NG], floors[(2 * c + b) % NG]
+            for to in range(4):
+                at = b * HALF + to * OWNED
+                right = (to - x) & 3
+                i = jnp.where(floor == 0, right, up)
+                j = jnp.where(floor == 0, up, right)
                 for n in range(DL // LANES):
-                    ref[to, n * OWNED : (n + 1) * OWNED, :] = lat[
+                    ref[floor, i, j, n * OWNED : (n + 1) * OWNED, :] = lat[
                         at : at + OWNED, n * LANES : (n + 1) * LANES
                     ].astype(ref.dtype)
                 both = jnp.concatenate(
                     [rope[at : at + OWNED // 2], rope[at + OWNED // 2 : at + OWNED]], axis=1
                 )
-                ref[to, DL // LANES * OWNED :, :] = both.astype(ref.dtype)
+                ref[floor, i, j, DL // LANES * OWNED :, :] = both.astype(ref.dtype)
 
     for step in range(H_LOC + 2):
         if step < H_LOC:
@@ -163,8 +174,8 @@
         out_specs=[vmem] * 3,
         out_shape=[
             jax.ShapeDtypeStruct((H_LOC, DK, TILE), BF),
-            jax.ShapeDtypeStruct((NG * 4, PACKED, LANES), OWN_TYPE),
-            jax.ShapeDtypeStruct((NG * 4, PACKED, LANES), BF),
+            jax.ShapeDtypeStruct((2, 4, 4, PACKED, LANES), OWN_TYPE),
+            jax.ShapeDtypeStruct((2, 4, 4, PACKED, LANES), BF),
         ],
         scratch_shapes=[
             pltpu.VMEM((DK, KEYS), BF),
@@ -184,9 +195,18 @@
     return lax.ppermute(x, "c", [(0, 1), (1, 0)])
 
 
-def from_group(x, dy, dz):
-    pairs = [(y * 2 + z, (y + dy) % 4 * 2 + (z ^ dz)) for y in range(4) for z in range(2)]
-    return lax.ppermute(x, ("y", "zl"), pairs)
+def onward(x, dz):
+    pairs = [
+        ((y * 2 + z) * 2 + c, ((y + 1 - 2 * c) % 4 * 2 + (z ^ dz)) * 2 + c)
+        for y in range(4)
+        for z in range(2)
+        for c in range(2)
+    ]
+    return lax.ppermute(x, ("y", "zl", "c"), pairs)
+
+
+def shift(x, axis, step):
+    return lax.ppermute(x, axis, [(n, (n + step) % 4) for n in range(4)])
 
 
 def unpack(x):
@@ -197,7 +217,7 @@
 
 
 def shards(queries, latent_cache, grad_output, query_blocks, key_blocks):
-    core, y, zl = (lax.axis_index(a) for a in ("c", "y", "zl"))
+    core, y, zl, x = (lax.axis_index(a) for a in ("c", "y", "zl", "x"))
     row = lax.broadcasted_iota(jnp.int32, (TILE, TILE), 0)
     t = lax.broadcasted_iota(jnp.int32, (TILE, TILE), 1)
     half, t = t >> 7, t & 127
@@ -205,20 +225,32 @@
     here = lax.dot_general(
         latent_cache, pick, (((0,), (0,)), ((), ())), preferred_element_type=F32
     ).astype(BF)
-    mine = here[:, :HALF]
-    k_own = [from_group(mine, dy, dz) for dy, dz in SLOTS[1:]]
-    k_other = [swap_cores(k) for k in k_own]
+    here = jnp.concatenate([here[:, :HALF], here[:, HALF:]], axis=0)
+
+    near = onward(here, 0)
+    slant = onward(here, 1)
+    beside = lax.ppermute(here[:DK], "zl", [(0, 1), (1, 0)])
+    far = onward(near[:DK], 0)
+    far_slant = onward(slant[:DK], 0)
+    singles = [beside, far, far_slant]
+    blocks = [here, near, swap_cores(near), slant, swap_cores(slant)]
+    blocks += singles + [swap_cores(k) for k in singles]
+
     qt = queries.transpose(1, 2, 0)
     go = grad_output.transpose(1, 0, 2)
-    blocks = [mine] + k_own + [here[:, HALF:]] + k_other
-    dqt, own, other = attention(
-        jnp.stack([core, y, zl]), query_blocks, key_blocks, qt, go, blocks
-    )
-
-    chip = (own + swap_cores(other).astype(F32)).astype(BF)
-    got = lax.all_to_all(chip, ("y", "zl", "x"), 0, 0, tiled=True)
-    part = unpack(jnp.sum(got.astype(F32), axis=0)).astype(BF)
-    got = lax.all_to_all(part, "zh", 0, 0, tiled=True)
+    place = jnp.stack([core, y, zl, x])
+    dqt, own, other = attention(place, query_blocks, key_blocks, qt, go, blocks)
+
+    other = swap_cores(other)
+    sums = [[own[h, d] + other[h, d].astype(F32) for d in range(4)] for h in range(2)]
+    for axes in (("x", "y"), ("y", "x")):
+        got = [
+            [shift(sums[h][d].astype(BF), axes[h], d).astype(F32) for h in range(2)]
+            for d in (2, 1, 3)
+        ]
+        sums = [sums[h][0] + sum(g[h] for g in got) for h in range(2)]
+    part = jnp.concatenate([unpack(s).astype(BF) for s in sums], axis=0)
+    got = lax.all_to_all(part, ("zl", "zh"), 0, 0, tiled=True)
     return dqt.transpose(2, 0, 1), jnp.sum(got.astype(F32), axis=0)
 
 

time: 89.2 us -> 89.1 us (level)
  blocking collectives: 40.5 us -> 15.5 us
  waiting for transfers between devices: 9.05 us -> 24.8 us
  starting transfers between devices: 15.3 us -> 24.2 us
    all_to_all x2 -> x1, blocking collectives: 40.5 us -> 15.5 us  [shards(): got = lax.all_to_all(part, ('zl', 'zh'), 0, 0, tiled=True)]
    ppermute x7 -> x17, waiting for transfers between devices: 6.46 us -> 22.3 us  [the longest x4 11.7 us: onward(): return lax.ppermute(x, ('y', 'zl', 'c'), pairs)]
    ppermute x7 -> x17, starting transfers between devices: 13.4 us -> 20.4 us  [the longest x12 15.4 us: shift(): return lax.ppermute(x, axis, [(n, (n + step) % 4) for n in range(4)])]
    ppermute x8 -> x6, starting transfers between devices: 1.82 us -> 3.85 us  [swap_cores(): return lax.ppermute(x, 'c', [(0, 1), (1, 0)])]
    ppermute x8 -> x6, waiting for transfers between devices: 2.58 us -> 2.49 us  [swap_cores(): return lax.ppermute(x, 'c', [(0, 1), (1, 0)])]
  transfers between devices with their start and end apart: 15 -> 23, of which waited for: 3 -> 11; matrix products, arithmetic and copies ran while one was open for 2% -> 2% of each run, Pallas kernels for 0% -> 0%
where the time goes in v3:
time: 89.1 us; the launch traced here: 88.1 us
  waiting for transfers between devices  24.8 us (28%)
  starting transfers between devices  24.2 us (27%)
  Pallas kernels  18.7 us (21%)
  blocking collectives  15.5 us (17%)
  local copies, waits for them, and re-layouts  2.64 us (3%)
  other arithmetic  1.21 us (1%)
    pallas_call x1, Pallas kernels, attention(): pl.pallas_call(attn_kernel, in_specs=[smem] * 3 + [vmem] * (2 + len(k_blo...  18.7 us
    all_to_all x1, blocking collectives, shards(): got = lax.all_to_all(part, ('zl', 'zh'), 0, 0, tiled=True)  15.5 us
    ppermute x12, starting transfers between devices, shift(): return lax.ppermute(x, axis, [(n, (n + step) % 4) for n in range(4)])  15.4 us
    ppermute x4, waiting for transfers between devices, onward(): return lax.ppermute(x, ('y', 'zl', 'c'), pairs)  11.7 us
    ppermute x12, waiting for transfers between devices, shift(): return lax.ppermute(x, axis, [(n, (n + step) % 4) for n in range(4)])  10.6 us
    ppermute x6, starting transfers between devices, swap_cores(): return lax.ppermute(x, 'c', [(0, 1), (1, 0)])  3.85 us
    ppermute x4, starting transfers between devices, onward(): return lax.ppermute(x, ('y', 'zl', 'c'), pairs)  3.05 us
    ppermute x6, waiting for transfers between devices, swap_cores(): return lax.ppermute(x, 'c', [(0, 1), (1, 0)])  2.49 us
  transfers between devices with their start and end apart: 23, of which 11 were waited for; matrix products, arithmetic and copies ran while one was open for 2% of the time, Pallas kernels for 0%

profile of v3, /device:TPU:32, one launch (start us, length us, event | category | flops | bytes accessed | tf_op | source)
XLA Modules:
  0.0 88.1 jit_solution(4552624689096024905)
XLA Ops:
  0.6 0.0 copy-start
  0.7 0.9 %copy-done = bf16[256,576]{0,1:T(8,128)(2,1)S(1)} copy-done((bf16[256,576]{0,1:T(8,128)(2,1)S(1)}, bf16[256,576]{0,1:T(8,128)(2,1)}, u32[]{:S(2)}) %copy-start) | copy-done | bytes 294936
  1.6 0.2 fusion
  1.9 1.2 %collective-permute-start.2 = (bf16[1152,128]{1,0:T(8,128)(2,1)S(1)}, bf16[1152,128]{1,0:T(8,128)(2,1)S(1)}, u32[]{:S(2)}, u32[]{:S(2)}) collective-permute-start(bf16[1152,128]{1,0:T(8,128)(2,1)S(1)} %pad_maximum_fusion.refs_0_), channel_id=1, source_target_pairs={{0,96},{1,225},{32,64},{33,193},{64,160},{65,33},{96,128},{97,1},{... | collective-permute-start | bytes 884744 | tf_op jit(solution)/shard_map/ppermute | solution.py:205
  3.1 1.6 %collective-permute-start = (bf16[1152,128]{1,0:T(8,128)(2,1)S(1)}, bf16[1152,128]{1,0:T(8,128)(2,1)S(1)}, u32[]{:S(2)}, u32[]{:S(2)}) collective-permute-start(bf16[1152,128]{1,0:T(8,128)(2,1)S(1)} %pad_maximum_fusion.refs_0_), channel_id=1, source_target_pairs={{0,64},{1,193},{32,96},{33,225},{64,128},{65,1},{96,160},{97,33},{... | collective-permute-start | bytes 884744 | tf_op jit(solution)/shard_map/ppermute | solution.py:205
  4.7 1.9 %collective-permute-start.4 = (bf16[576,128]{1,0:T(8,128)(2,1)S(1)}, bf16[576,128]{1,0:T(8,128)(2,1)S(1)}, u32[]{:S(2)}, u32[]{:S(2)}) collective-permute-start(bf16[576,128]{1,0:T(8,128)(2,1)S(1)} %get-tuple-element.20), channel_id=1, source_target_pairs={{0,32},{32,0},{1,33},{33,1},{2,34},{34,2},{3,35},{35,3},{4,36},{36... | collective-permute-start | bytes 442376 | tf_op jit(solution)/shard_map/ppermute | solution.py:232
  6.6 7.3 %collective-permute-done.2.refs_3_ = bf16[1152,128]{1,0:T(8,128)(2,1)S(1)} collective-permute-done((bf16[1152,128]{1,0:T(8,128)(2,1)S(1)}, bf16[1152,128]{1,0:T(8,128)(2,1)S(1)}, u32[]{:S(2)}, u32[]{:S(2)}) %collective-permute-start.2) | collective-permute-done | bytes 294944 | tf_op jit(solution)/shard_map/ppermute | solution.py:205
  13.9 0.0 copy-start.1
  14.0 0.0 copy-start.2
  14.0 0.0 copy-start.3
  14.0 0.2 collective-permute-start.6
  14.2 1.4 %collective-permute-start.3 = (bf16[1152,128]{1,0:T(8,128)(2,1)S(1)}, bf16[1152,128]{1,0:T(8,128)(2,1)S(1)}, u32[]{:S(2)}, u32[]{:S(2)}) collective-permute-start(bf16[1152,128]{1,0:T(8,128)(2,1)S(1)} %collective-permute-done.2.refs_3_), channel_id=1, source_target_pairs={{0,1},{1,0},{2,3},{3,2},{4,5},{5,4},{6,7},{7,6},{8,9},{9,8},{10,11... | collective-permute-start | bytes 884744 | tf_op jit(solution)/shard_map/ppermute | solution.py:195
  15.5 0.0 collective-permute-done.refs_1_
  15.6 0.1 collective-permute-start.5
  15.6 2.0 %collective-permute-start.1 = (bf16[1152,128]{1,0:T(8,128)(2,1)S(1)}, bf16[1152,128]{1,0:T(8,128)(2,1)S(1)}, u32[]{:S(2)}, u32[]{:S(2)}) collective-permute-start(bf16[1152,128]{1,0:T(8,128)(2,1)S(1)} %collective-permute-done.refs_1_), channel_id=1, source_target_pairs={{0,1},{1,0},{2,3},{3,2},{4,5},{5,4},{6,7},{7,6},{8,9},{9,8},{10,11... | collective-permute-start | bytes 884744 | tf_op jit(solution)/shard_map/ppermute | solution.py:195
  17.6 0.0 collective-permute-done.4.refs_5_
  17.6 0.0 collective-permute-start.7
  17.6 2.8 %collective-permute-done.6.refs_7_ = bf16[576,128]{1,0:T(8,128)(2,1)S(1)} collective-permute-done((bf16[576,128]{1,0:T(8,128)(2,1)S(1)}, bf16[576,128]{1,0:T(8,128)(2,1)S(1)}, u32[]{:S(2)}, u32[]{:S(2)}) %collective-permute-start.6) | collective-permute-done | bytes 147488 | tf_op jit(solution)/shard_map/ppermute | solution.py:205
  20.4 0.0 collective-permute-start.9
  20.4 1.6 %collective-permute-done.5.refs_6_ = bf16[576,128]{1,0:T(8,128)(2,1)S(1)} collective-permute-done((bf16[576,128]{1,0:T(8,128)(2,1)S(1)}, bf16[576,128]{1,0:T(8,128)(2,1)S(1)}, u32[]{:S(2)}, u32[]{:S(2)}) %collective-permute-start.5) | collective-permute-done | bytes 147488 | tf_op jit(solution)/shard_map/ppermute | solution.py:205
  22.0 0.0 collective-permute-start.8
  22.0 1.4 %copy.16 = bf16[256,4,512]{2,0,1:T(8,128)(2,1)S(1)} copy(bf16[256,4,512]{2,1,0:T(4,128)(2,1)} %param.7) | data formatting | bytes 2097152 | tf_op args[2]
  23.4 0.1 pad_add_fusion.place_ref
  23.5 0.0 collective-permute-done.7.refs_8_
  23.5 0.0 collective-permute-done.9.refs_10_
  23.5 0.0 collective-permute-done.3.refs_4_
  23.5 0.0 collective-permute-done.8.refs_9_
  23.5 0.0 collective-permute-done.1.refs_2_
  23.5 0.0 copy-done.1
  23.5 0.0 copy-done.2
  23.6 0.0 copy-done.3
  23.6 18.7 %shard_map.68 = (bf16[4,576,256]{2,1,0:T(8,128)(2,1)}, f32[2,4,4,144,128]{4,3,2,1,0:T(8,128)S(1)}, bf16[2,4,4,144,128]{4,3,2,1,0:T(8,128)(2,1)S(1)}) custom-call(s32[4]{0:T(128)S(1)} %pad_add_fusion.place_ref, s32[8]{0:T(128)S(1)} %copy-done.2, s32[8]{0:T(128)S(1)} %copy-done.3, bf16[4,576,256]{2,1,0:T(8,128)(2,1)S(1)} %bitcast.71, ...), custom_call_target="tpu_custom_call" | custom-call | tf_op jit(solution)/shard_map/pallas_call | solution.py:171
  42.3 0.5 collective-permute-start.10
  42.8 2.5 %collective-permute-done.10 = bf16[2,4,4,144,128]{4,3,2,1,0:T(8,128)(2,1)S(1)} collective-permute-done((bf16[2,4,4,144,128]{4,3,2,1,0:T(8,128)(2,1)S(1)}, bf16[2,4,4,144,128]{4,3,2,1,0:T(8,128)(2,1)S(1)}, u32[]{:S(2)}, u32[]{:S(2)}) %collective-permute-start.10) | collective-permute-done | bytes 1179680 | tf_op jit(solution)/shard_map/ppermute | solution.py:195
  45.2 0.2 fusion.1
  45.5 3.1 %collective-permute-start.11 = (bf16[4,144,128]{2,1,0:T(8,128)(2,1)S(1)}, bf16[4,144,128]{2,1,0:T(8,128)(2,1)S(1)}, u32[]{:S(2)}, u32[]{:S(2)}) collective-permute-start(bf16[4,144,128]{2,1,0:T(8,128)(2,1)S(1)} %get-tuple-element.14), channel_id=1, source_target_pairs={{0,16},{8,24},{16,0},{24,8},{1,17},{9,25},{17,1},{25,9},{2,18},{10... | collective-permute-start | bytes 442376 | tf_op jit(solution)/shard_map/ppermute | solution.py:209
  48.6 1.0 %collective-permute-start.19 = (bf16[4,144,128]{2,1,0:T(8,128)(2,1)S(1)}, bf16[4,144,128]{2,1,0:T(8,128)(2,1)S(1)}, u32[]{:S(2)}, u32[]{:S(2)}) collective-permute-start(bf16[4,144,128]{2,1,0:T(8,128)(2,1)S(1)} %get-tuple-element.15), channel_id=1, source_target_pairs={{0,192},{64,0},{128,64},{192,128},{1,193},{65,1},{129,65},{193,129... | collective-permute-start | bytes 442376 | tf_op jit(solution)/shard_map/ppermute | solution.py:209
  49.5 1.1 %collective-permute-start.18 = (bf16[4,144,128]{2,1,0:T(8,128)(2,1)S(1)}, bf16[4,144,128]{2,1,0:T(8,128)(2,1)S(1)}, u32[]{:S(2)}, u32[]{:S(2)}) collective-permute-start(bf16[4,144,128]{2,1,0:T(8,128)(2,1)S(1)} %get-tuple-element.16), channel_id=1, source_target_pairs={{0,64},{64,128},{128,192},{192,0},{1,65},{65,129},{129,193},{193,1... | collective-permute-start | bytes 442376 | tf_op jit(solution)/shard_map/ppermute | solution.py:209
  50.6 0.4 collective-permute-start.17
  51.0 1.1 %collective-permute-start.13 = (bf16[4,144,128]{2,1,0:T(8,128)(2,1)S(1)}, bf16[4,144,128]{2,1,0:T(8,128)(2,1)S(1)}, u32[]{:S(2)}, u32[]{:S(2)}) collective-permute-start(bf16[4,144,128]{2,1,0:T(8,128)(2,1)S(1)} %get-tuple-element.18), channel_id=1, source_target_pairs={{0,24},{8,0},{16,8},{24,16},{1,25},{9,1},{17,9},{25,17},{2,26},{10... | collective-permute-start | bytes 442376 | tf_op jit(solution)/shard_map/ppermute | solution.py:209
  52.2 1.0 %collective-permute-done.11 = bf16[4,144,128]{2,1,0:T(8,128)(2,1)S(1)} collective-permute-done((bf16[4,144,128]{2,1,0:T(8,128)(2,1)S(1)}, bf16[4,144,128]{2,1,0:T(8,128)(2,1)S(1)}, u32[]{:S(2)}, u32[]{:S(2)}) %collective-permute-start.11) | collective-permute-done | bytes 147488 | tf_op jit(solution)/shard_map/ppermute | solution.py:209
  53.2 2.0 %collective-permute-start.12 = (bf16[4,144,128]{2,1,0:T(8,128)(2,1)S(1)}, bf16[4,144,128]{2,1,0:T(8,128)(2,1)S(1)}, u32[]{:S(2)}, u32[]{:S(2)}) collective-permute-start(bf16[4,144,128]{2,1,0:T(8,128)(2,1)S(1)} %get-tuple-element.19), channel_id=1, source_target_pairs={{0,8},{8,16},{16,24},{24,0},{1,9},{9,17},{17,25},{25,1},{2,10},{10... | collective-permute-start | bytes 442376 | tf_op jit(solution)/shard_map/ppermute | solution.py:209
  55.2 0.1 collective-permute-done.19
  55.3 4.0 %collective-permute-done.18 = bf16[4,144,128]{2,1,0:T(8,128)(2,1)S(1)} collective-permute-done((bf16[4,144,128]{2,1,0:T(8,128)(2,1)S(1)}, bf16[4,144,128]{2,1,0:T(8,128)(2,1)S(1)}, u32[]{:S(2)}, u32[]{:S(2)}) %collective-permute-start.18) | collective-permute-done | bytes 147488 | tf_op jit(solution)/shard_map/ppermute | solution.py:209
  59.2 0.0 collective-permute-done.17
  59.3 0.0 collective-permute-done.13
  59.3 0.4 collective-permute-done.12
  59.7 0.2 fusion.12
  59.9 2.0 %collective-permute-start.14 = (bf16[144,128]{1,0:T(8,128)(2,1)S(1)}, bf16[144,128]{1,0:T(8,128)(2,1)S(1)}, u32[]{:S(2)}, u32[]{:S(2)}) collective-permute-start(bf16[144,128]{1,0:T(8,128)(2,1)S(1)} %get-tuple-element.22), channel_id=1, source_target_pairs={{0,128},{64,192},{128,0},{192,64},{1,129},{65,193},{129,1},{193,65... | collective-permute-start | bytes 110600 | tf_op jit(solution)/shard_map/ppermute | solution.py:209
  62.0 2.2 %collective-permute-start.16 = (bf16[144,128]{1,0:T(8,128)(2,1)S(1)}, bf16[144,128]{1,0:T(8,128)(2,1)S(1)}, u32[]{:S(2)}, u32[]{:S(2)}) collective-permute-start(bf16[144,128]{1,0:T(8,128)(2,1)S(1)} %get-tuple-element.23), channel_id=1, source_target_pairs={{0,192},{64,0},{128,64},{192,128},{1,193},{65,1},{129,65},{193,129... | collective-permute-start | bytes 110600 | tf_op jit(solution)/shard_map/ppermute | solution.py:209
  64.1 0.0 collective-permute-start.15
  64.1 0.4 collective-permute-start.20
  64.5 2.0 %collective-permute-start.22 = (bf16[144,128]{1,0:T(8,128)(2,1)S(1)}, bf16[144,128]{1,0:T(8,128)(2,1)S(1)}, u32[]{:S(2)}, u32[]{:S(2)}) collective-permute-start(bf16[144,128]{1,0:T(8,128)(2,1)S(1)} %get-tuple-element.26), channel_id=1, source_target_pairs={{0,24},{8,0},{16,8},{24,16},{1,25},{9,1},{17,9},{25,17},{2,26},{10... | collective-permute-start | bytes 110600 | tf_op jit(solution)/shard_map/ppermute | solution.py:209
  66.6 0.0 collective-permute-done.14
  66.6 0.0 collective-permute-start.21
  66.6 0.0 collective-permute-done.16
  66.6 2.7 %collective-permute-done.15 = bf16[144,128]{1,0:T(8,128)(2,1)S(1)} collective-permute-done((bf16[144,128]{1,0:T(8,128)(2,1)S(1)}, bf16[144,128]{1,0:T(8,128)(2,1)S(1)}, u32[]{:S(2)}, u32[]{:S(2)}) %collective-permute-start.15) | collective-permute-done | bytes 36896 | tf_op jit(solution)/shard_map/ppermute | solution.py:209
  69.4 0.3 collective-permute-done.20
  69.7 0.0 collective-permute-done.22
  69.7 2.1 %collective-permute-done.21 = bf16[144,128]{1,0:T(8,128)(2,1)S(1)} collective-permute-done((bf16[144,128]{1,0:T(8,128)(2,1)S(1)}, bf16[144,128]{1,0:T(8,128)(2,1)S(1)}, u32[]{:S(2)}, u32[]{:S(2)}) %collective-permute-start.21) | collective-permute-done | bytes 36896 | tf_op jit(solution)/shard_map/ppermute | solution.py:209
  71.8 0.1 reshape.66
  71.9 0.1 reshape.70
  72.0 15.5 %all_to_all.5 = bf16[8,8,576]{2,1,0:T(8,128)(2,1)S(1)} all-to-all(bf16[8,8,576]{2,1,0:T(8,128)(2,1)S(1)} %maximum_maximum_fusion), channel_id=1, replica_groups=mesh['y'=4,'zl'=2,'x'=4,'zh'=4,'c'=2] {'zl','zh'}, dimensions={0} | all-to-all | bytes 147456 | tf_op jit(solution)/shard_map/all_to_all | solution.py:253
  87.5 0.6 convert_reduce_fusion
  (17 shorter events, 0.2 us)
Async XLA Ops:
  0.6 1.0 %copy-start = (bf16[256,576]{0,1:T(8,128)(2,1)S(1)}, bf16[256,576]{0,1:T(8,128)(2,1)}, u32[]{:S(2)}) copy-start(bf16[256,576]{0,1:T(8,128)(2,1)} %param.6) | copy-start | bytes 884740
  1.9 12.0 %collective-permute-start.2 = (bf16[1152,128]{1,0:T(8,128)(2,1)S(1)}, bf16[1152,128]{1,0:T(8,128)(2,1)S(1)}, u32[]{:S(2)}, u32[]{:S(2)}) collective-permute-start(bf16[1152,128]{1,0:T(8,128)(2,1)S(1)} %pad_maximum_fusion.refs_0_), channel_id=1, source_target_pairs={{0,96},{1,225},{32,64},{33,193},{64,160},{65,33},{96,128},{97,1},{... | collective-permute-start | bytes 884744 | tf_op jit(solution)/shard_map/ppermute | solution.py:205
  3.1 12.4 %collective-permute-start = (bf16[1152,128]{1,0:T(8,128)(2,1)S(1)}, bf16[1152,128]{1,0:T(8,128)(2,1)S(1)}, u32[]{:S(2)}, u32[]{:S(2)}) collective-permute-start(bf16[1152,128]{1,0:T(8,128)(2,1)S(1)} %pad_maximum_fusion.refs_0_), channel_id=1, source_target_pairs={{0,64},{1,193},{32,96},{33,225},{64,128},{65,1},{96,160},{97,33},{... | collective-permute-start | bytes 884744 | tf_op jit(solution)/shard_map/ppermute | solution.py:205
  4.7 12.9 %collective-permute-start.4 = (bf16[576,128]{1,0:T(8,128)(2,1)S(1)}, bf16[576,128]{1,0:T(8,128)(2,1)S(1)}, u32[]{:S(2)}, u32[]{:S(2)}) collective-permute-start(bf16[576,128]{1,0:T(8,128)(2,1)S(1)} %get-tuple-element.20), channel_id=1, source_target_pairs={{0,32},{32,0},{1,33},{33,1},{2,34},{34,2},{3,35},{35,3},{4,36},{36... | collective-permute-start | bytes 442376 | tf_op jit(solution)/shard_map/ppermute | solution.py:232
  13.9 9.6 %copy-start.1 = (bf16[256,4,576]{0,2,1:T(8,128)(2,1)S(1)}, bf16[256,4,576]{0,2,1:T(8,128)(2,1)}, u32[]{:S(2)}) copy-start(bf16[256,4,576]{0,2,1:T(8,128)(2,1)} %param.5) | copy-start | bytes 3538948
  14.0 9.6 %copy-start.2 = (s32[8]{0:T(128)S(1)}, s32[8]{0:T(128)}, u32[]{:S(2)}) copy-start(s32[8]{0:T(128)} %query_blocks_ref.1) | copy-start | bytes 100
  14.0 9.6 %copy-start.3 = (s32[8]{0:T(128)S(1)}, s32[8]{0:T(128)}, u32[]{:S(2)}) copy-start(s32[8]{0:T(128)} %key_blocks_ref.1) | copy-start | bytes 100
  14.0 6.4 %collective-permute-start.6 = (bf16[576,128]{1,0:T(8,128)(2,1)S(1)}, bf16[576,128]{1,0:T(8,128)(2,1)S(1)}, u32[]{:S(2)}, u32[]{:S(2)}) collective-permute-start(bf16[576,128]{1,0:T(8,128)(2,1)S(1)} %slice.141), channel_id=1, source_target_pairs={{0,64},{1,193},{32,96},{33,225},{64,128},{65,1},{96,160},{97,33},{... | collective-permute-start | bytes 442376 | tf_op jit(solution)/shard_map/ppermute | solution.py:205
  14.2 9.3 %collective-permute-start.3 = (bf16[1152,128]{1,0:T(8,128)(2,1)S(1)}, bf16[1152,128]{1,0:T(8,128)(2,1)S(1)}, u32[]{:S(2)}, u32[]{:S(2)}) collective-permute-start(bf16[1152,128]{1,0:T(8,128)(2,1)S(1)} %collective-permute-done.2.refs_3_), channel_id=1, source_target_pairs={{0,1},{1,0},{2,3},{3,2},{4,5},{5,4},{6,7},{7,6},{8,9},{9,8},{10,11... | collective-permute-start | bytes 884744 | tf_op jit(solution)/shard_map/ppermute | solution.py:195
  15.6 6.4 %collective-permute-start.5 = (bf16[576,128]{1,0:T(8,128)(2,1)S(1)}, bf16[576,128]{1,0:T(8,128)(2,1)S(1)}, u32[]{:S(2)}, u32[]{:S(2)}) collective-permute-start(bf16[576,128]{1,0:T(8,128)(2,1)S(1)} %slice.140), channel_id=1, source_target_pairs={{0,64},{1,193},{32,96},{33,225},{64,128},{65,1},{96,160},{97,33},{... | collective-permute-start | bytes 442376 | tf_op jit(solution)/shard_map/ppermute | solution.py:205
  15.6 7.9 %collective-permute-start.1 = (bf16[1152,128]{1,0:T(8,128)(2,1)S(1)}, bf16[1152,128]{1,0:T(8,128)(2,1)S(1)}, u32[]{:S(2)}, u32[]{:S(2)}) collective-permute-start(bf16[1152,128]{1,0:T(8,128)(2,1)S(1)} %collective-permute-done.refs_1_), channel_id=1, source_target_pairs={{0,1},{1,0},{2,3},{3,2},{4,5},{5,4},{6,7},{7,6},{8,9},{9,8},{10,11... | collective-permute-start | bytes 884744 | tf_op jit(solution)/shard_map/ppermute | solution.py:195
  17.6 5.9 %collective-permute-start.7 = (bf16[576,128]{1,0:T(8,128)(2,1)S(1)}, bf16[576,128]{1,0:T(8,128)(2,1)S(1)}, u32[]{:S(2)}, u32[]{:S(2)}) collective-permute-start(bf16[576,128]{1,0:T(8,128)(2,1)S(1)} %collective-permute-done.4.refs_5_), channel_id=1, source_target_pairs={{0,1},{1,0},{2,3},{3,2},{4,5},{5,4},{6,7},{7,6},{8,9},{9,8},{10,11... | collective-permute-start | bytes 442376 | tf_op jit(solution)/shard_map/ppermute | solution.py:195
  20.4 3.1 %collective-permute-start.9 = (bf16[576,128]{1,0:T(8,128)(2,1)S(1)}, bf16[576,128]{1,0:T(8,128)(2,1)}, u32[]{:S(2)}, u32[]{:S(2)}) collective-permute-start(bf16[576,128]{1,0:T(8,128)(2,1)S(1)} %collective-permute-done.6.refs_7_), channel_id=1, source_target_pairs={{0,1},{1,0},{2,3},{3,2},{4,5},{5,4},{6,7},{7,6},{8,9},{9,8},{10,11... | collective-permute-start | bytes 442376 | tf_op jit(solution)/shard_map/ppermute | solution.py:195
  22.0 1.5 %collective-permute-start.8 = (bf16[576,128]{1,0:T(8,128)(2,1)S(1)}, bf16[576,128]{1,0:T(8,128)(2,1)}, u32[]{:S(2)}, u32[]{:S(2)}) collective-permute-start(bf16[576,128]{1,0:T(8,128)(2,1)S(1)} %collective-permute-done.5.refs_6_), channel_id=1, source_target_pairs={{0,1},{1,0},{2,3},{3,2},{4,5},{5,4},{6,7},{7,6},{8,9},{9,8},{10,11... | collective-permute-start | bytes 442376 | tf_op jit(solution)/shard_map/ppermute | solution.py:195
  42.3 3.0 %collective-permute-start.10 = (bf16[2,4,4,144,128]{4,3,2,1,0:T(8,128)(2,1)S(1)}, bf16[2,4,4,144,128]{4,3,2,1,0:T(8,128)(2,1)S(1)}, u32[]{:S(2)}, u32[]{:S(2)}) collective-permute-start(bf16[2,4,4,144,128]{4,3,2,1,0:T(8,128)(2,1)S(1)} %get-tuple-element.7), channel_id=1, source_target_pairs={{0,1},{1,0},{2,3},{3,2},{4,5},{5,4},{6,7},{7,6},{8,9},{9,8},{10,11... | collective-permute-start | bytes 3538952 | tf_op jit(solution)/shard_map/ppermute | solution.py:195
  45.5 7.7 %collective-permute-start.11 = (bf16[4,144,128]{2,1,0:T(8,128)(2,1)S(1)}, bf16[4,144,128]{2,1,0:T(8,128)(2,1)S(1)}, u32[]{:S(2)}, u32[]{:S(2)}) collective-permute-start(bf16[4,144,128]{2,1,0:T(8,128)(2,1)S(1)} %get-tuple-element.14), channel_id=1, source_target_pairs={{0,16},{8,24},{16,0},{24,8},{1,17},{9,25},{17,1},{25,9},{2,18},{10... | collective-permute-start | bytes 442376 | tf_op jit(solution)/shard_map/ppermute | solution.py:209
  48.6 6.7 %collective-permute-start.19 = (bf16[4,144,128]{2,1,0:T(8,128)(2,1)S(1)}, bf16[4,144,128]{2,1,0:T(8,128)(2,1)S(1)}, u32[]{:S(2)}, u32[]{:S(2)}) collective-permute-start(bf16[4,144,128]{2,1,0:T(8,128)(2,1)S(1)} %get-tuple-element.15), channel_id=1, source_target_pairs={{0,192},{64,0},{128,64},{192,128},{1,193},{65,1},{129,65},{193,129... | collective-permute-start | bytes 442376 | tf_op jit(solution)/shard_map/ppermute | solution.py:209
  49.5 9.7 %collective-permute-start.18 = (bf16[4,144,128]{2,1,0:T(8,128)(2,1)S(1)}, bf16[4,144,128]{2,1,0:T(8,128)(2,1)S(1)}, u32[]{:S(2)}, u32[]{:S(2)}) collective-permute-start(bf16[4,144,128]{2,1,0:T(8,128)(2,1)S(1)} %get-tuple-element.16), channel_id=1, source_target_pairs={{0,64},{64,128},{128,192},{192,0},{1,65},{65,129},{129,193},{193,1... | collective-permute-start | bytes 442376 | tf_op jit(solution)/shard_map/ppermute | solution.py:209
  50.6 8.6 %collective-permute-start.17 = (bf16[4,144,128]{2,1,0:T(8,128)(2,1)S(1)}, bf16[4,144,128]{2,1,0:T(8,128)(2,1)S(1)}, u32[]{:S(2)}, u32[]{:S(2)}) collective-permute-start(bf16[4,144,128]{2,1,0:T(8,128)(2,1)S(1)} %get-tuple-element.17), channel_id=1, source_target_pairs={{0,128},{64,192},{128,0},{192,64},{1,129},{65,193},{129,1},{193,65... | collective-permute-start | bytes 442376 | tf_op jit(solution)/shard_map/ppermute | solution.py:209
  51.0 8.2 %collective-permute-start.13 = (bf16[4,144,128]{2,1,0:T(8,128)(2,1)S(1)}, bf16[4,144,128]{2,1,0:T(8,128)(2,1)S(1)}, u32[]{:S(2)}, u32[]{:S(2)}) collective-permute-start(bf16[4,144,128]{2,1,0:T(8,128)(2,1)S(1)} %get-tuple-element.18), channel_id=1, source_target_pairs={{0,24},{8,0},{16,8},{24,16},{1,25},{9,1},{17,9},{25,17},{2,26},{10... | collective-permute-start | bytes 442376 | tf_op jit(solution)/shard_map/ppermute | solution.py:209
  53.2 6.5 %collective-permute-start.12 = (bf16[4,144,128]{2,1,0:T(8,128)(2,1)S(1)}, bf16[4,144,128]{2,1,0:T(8,128)(2,1)S(1)}, u32[]{:S(2)}, u32[]{:S(2)}) collective-permute-start(bf16[4,144,128]{2,1,0:T(8,128)(2,1)S(1)} %get-tuple-element.19), channel_id=1, source_target_pairs={{0,8},{8,16},{16,24},{24,0},{1,9},{9,17},{17,25},{25,1},{2,10},{10... | collective-permute-start | bytes 442376 | tf_op jit(solution)/shard_map/ppermute | solution.py:209
  59.9 6.7 %collective-permute-start.14 = (bf16[144,128]{1,0:T(8,128)(2,1)S(1)}, bf16[144,128]{1,0:T(8,128)(2,1)S(1)}, u32[]{:S(2)}, u32[]{:S(2)}) collective-permute-start(bf16[144,128]{1,0:T(8,128)(2,1)S(1)} %get-tuple-element.22), channel_id=1, source_target_pairs={{0,128},{64,192},{128,0},{192,64},{1,129},{65,193},{129,1},{193,65... | collective-permute-start | bytes 110600 | tf_op jit(solution)/shard_map/ppermute | solution.py:209
  62.0 4.6 %collective-permute-start.16 = (bf16[144,128]{1,0:T(8,128)(2,1)S(1)}, bf16[144,128]{1,0:T(8,128)(2,1)S(1)}, u32[]{:S(2)}, u32[]{:S(2)}) collective-permute-start(bf16[144,128]{1,0:T(8,128)(2,1)S(1)} %get-tuple-element.23), channel_id=1, source_target_pairs={{0,192},{64,0},{128,64},{192,128},{1,193},{65,1},{129,65},{193,129... | collective-permute-start | bytes 110600 | tf_op jit(solution)/shard_map/ppermute | solution.py:209
  64.1 5.2 %collective-permute-start.15 = (bf16[144,128]{1,0:T(8,128)(2,1)S(1)}, bf16[144,128]{1,0:T(8,128)(2,1)S(1)}, u32[]{:S(2)}, u32[]{:S(2)}) collective-permute-start(bf16[144,128]{1,0:T(8,128)(2,1)S(1)} %get-tuple-element.24), channel_id=1, source_target_pairs={{0,64},{64,128},{128,192},{192,0},{1,65},{65,129},{129,193},{193,1... | collective-permute-start | bytes 110600 | tf_op jit(solution)/shard_map/ppermute | solution.py:209
  64.1 5.5 %collective-permute-start.20 = (bf16[144,128]{1,0:T(8,128)(2,1)S(1)}, bf16[144,128]{1,0:T(8,128)(2,1)S(1)}, u32[]{:S(2)}, u32[]{:S(2)}) collective-permute-start(bf16[144,128]{1,0:T(8,128)(2,1)S(1)} %get-tuple-element.25), channel_id=1, source_target_pairs={{0,16},{8,24},{16,0},{24,8},{1,17},{9,25},{17,1},{25,9},{2,18},{10... | collective-permute-start | bytes 110600 | tf_op jit(solution)/shard_map/ppermute | solution.py:209
  64.5 5.2 %collective-permute-start.22 = (bf16[144,128]{1,0:T(8,128)(2,1)S(1)}, bf16[144,128]{1,0:T(8,128)(2,1)S(1)}, u32[]{:S(2)}, u32[]{:S(2)}) collective-permute-start(bf16[144,128]{1,0:T(8,128)(2,1)S(1)} %get-tuple-element.26), channel_id=1, source_target_pairs={{0,24},{8,0},{16,8},{24,16},{1,25},{9,1},{17,9},{25,17},{2,26},{10... | collective-permute-start | bytes 110600 | tf_op jit(solution)/shard_map/ppermute | solution.py:209
  66.6 5.2 %collective-permute-start.21 = (bf16[144,128]{1,0:T(8,128)(2,1)S(1)}, bf16[144,128]{1,0:T(8,128)(2,1)S(1)}, u32[]{:S(2)}, u32[]{:S(2)}) collective-permute-start(bf16[144,128]{1,0:T(8,128)(2,1)S(1)} %get-tuple-element.27), channel_id=1, source_target_pairs={{0,8},{8,16},{16,24},{24,0},{1,9},{9,17},{17,25},{25,1},{2,10},{10... | collective-permute-start | bytes 110600 | tf_op jit(solution)/shard_map/ppermute | solution.py:209

commit v4 on v3

v4 whole, which is shorter than its diff:
```python
import functools

import jax
import jax.numpy as jnp
import numpy as np
from jax import lax
from jax.experimental import pallas as pl
from jax.experimental.pallas import tpu as pltpu
from jax.sharding import Mesh
from jax.sharding import PartitionSpec as P

H_LOC = 4
DL = 512
DR = 64
DK = 576
TILE = 256
HALF = 128
NG = 8
KEYS = NG * TILE
LOG2E = 1.4426950408889634
FLOOR = -1e30
LANES = 128
OWNED = 32
PACKED = OWNED * DK // LANES
MAIN_VMEM = 28 * 1024 * 1024
FIRST = 5
SWAPPED = (2, 4)

softmax_scale = 0.07216878364870322

BF = jnp.bfloat16
F32 = jnp.float32


def dot(a, b):
    return lax.dot_general(a, b, (((1,), (0,)), ((), ())), preferred_element_type=F32)


def dot_nt(a, b):
    return lax.dot_general(a, b, (((1,), (1,)), ((), ())), preferred_element_type=F32)


def positions(place_ref, query_blocks_ref, key_blocks_ref):
    core, y, zl = (place_ref[n] for n in range(3))
    turn = 2 * core
    ahead = [(0 - dy) & 3 for dy in (0, 1 + turn, 3 - turn, 1 + turn, 3 - turn, 0, 2, 2)]
    floors = [zl ^ dz for dz in (0, 0, 0, 1, 1, 1, 0, 1)]
    mine = query_blocks_ref[y * 2 + zl]
    limits = []
    for up, floor in zip(ahead, floors):
        lag = (mine - key_blocks_ref[((y + up) & 3) * 2 + floor]) * TILE
        limits.append((lag - core * 8, lag - (core ^ 1) * 8))
    return ahead, floors, limits


def halves(refs):
    out = []
    for slot in range(FIRST):
        flip = slot in SWAPPED
        blocks = [refs[slot][n * DK : (n + 1) * DK, :] for n in range(2)]
        out.append(blocks[::-1] if flip else blocks)
    rest = refs[FIRST:]
    for slot in range(len(rest) // 2):
        out.append([rest[slot][...], rest[slot + len(rest) // 2][...]])
    return out


def offsets():
    t = lax.broadcasted_iota(jnp.int32, (HALF, TILE), 0)
    i = lax.broadcasted_iota(jnp.int32, (HALF, TILE), 1)
    return (t >> 3) * 16 + (t & 7) - i


def span(c):
    return slice(c * TILE, (c + 1) * TILE)


def weigh(keys, qt, got, delta, limits):
    scores = dot(keys, qt) * (softmax_scale * LOG2E)
    parts = [
        jnp.where(delta <= limits[b], scores[b * HALF : (b + 1) * HALF], -jnp.inf)
        for b in range(2)
    ]
    peak = jnp.maximum(*[jnp.max(p, axis=0, keepdims=True) for p in parts])
    floor = jnp.maximum(peak, FLOOR)
    e = [jnp.exp2(p - floor) for p in parts]
    total = sum(jnp.sum(p, axis=0, keepdims=True) for p in e)
    return e, dot(keys[:, :DL], got), peak, total


def first_kernel(place_ref, query_blocks_ref, key_blocks_ref, qt_ref, go_ref, *refs):
    e_ref, gp_ref, stat_ref, gl_ref, gr_ref, got_ref, k_s = refs[FIRST:]
    limits = positions(place_ref, query_blocks_ref, key_blocks_ref)[2]
    for slot, pair in enumerate(halves(refs[:FIRST])):
        for b in range(2):
            at = slot * TILE + b * HALF
            k_s[at : at + HALF, :] = pair[b].T
    delta = offsets()
    for h in range(H_LOC):
        go = go_ref[h]
        gl_ref[h * 2 * TILE : h * 2 * TILE + TILE, :] = go
        got_ref[h] = go.T
        q = qt_ref[h].T
        gl_ref[h * 2 * TILE + TILE : (h + 1) * 2 * TILE, :] = q[:, :DL]
        gr_ref[h * TILE : (h + 1) * TILE, :] = q[:, DL:]
        for c in range(FIRST):
            e, gp, peak, total = weigh(k_s[span(c), :], qt_ref[h], got_ref[h], delta, limits[c])
            for b in range(2):
                at = c * TILE + b * HALF
                e_ref[h, at : at + HALF, :] = e[b]
            gp_ref[h, span(c), :] = gp
            stat_ref[0, h, c : c + 1, :] = peak
            stat_ref[1, h, c : c + 1, :] = total


def main_kernel(place_ref, query_blocks_ref, key_blocks_ref, qt_ref, *refs):
    k_refs, refs = refs[: 2 * NG - FIRST], refs[2 * NG - FIRST :]
    e1_ref, gp1_ref, stat_ref, gl_ref, gr_ref, got_ref = refs[:6]
    dqt_ref, own_ref, other_ref, kt_s, k_s, e_s, gp_s, w_s = refs[6:]
    ahead, floors, limits = positions(place_ref, query_blocks_ref, key_blocks_ref)
    core, x = place_ref[0], place_ref[3]
    for slot, pair in enumerate(halves(k_refs)):
        for b in range(2):
            at = slot * TILE + b * HALF
            kt_s[:, at : at + HALF] = pair[b]
            if slot >= FIRST:
                at -= FIRST * TILE
                k_s[at : at + HALF, :] = pair[b].T
    delta = offsets()
    peaks = [[stat_ref[0, h, c : c + 1, :] for c in range(FIRST)] for h in range(H_LOC)]
    sums = [[stat_ref[1, h, c : c + 1, :] for c in range(FIRST)] for h in range(H_LOC)]
    factors = [None] * H_LOC
    corrs = [None] * H_LOC

    def load(h, c):
        if c < FIRST:
            return e1_ref[h, span(c), :], gp1_ref[h, span(c), :]
        return e_s[h, span(c - FIRST), :], gp_s[h, span(c - FIRST), :]

    def settle(h):
        peak = functools.reduce(jnp.maximum, peaks[h])
        shares = [jnp.exp2(p - peak) for p in peaks[h]]
        inv = 1.0 / sum(f * s for f, s in zip(shares, sums[h]))
        factors[h] = [f * inv for f in shares]
        corrs[h] = jnp.zeros((1, TILE), F32)

    def correct(h, c):
        e, gp = load(h, c)
        pb = (e * factors[h][c]).astype(BF)
        w_s[span(c), h * 2 * TILE : h * 2 * TILE + TILE] = pb
        corrs[h] = corrs[h] + jnp.sum(pb.astype(F32) * gp, axis=0, keepdims=True)

    def differ(h, c):
        e, gp = load(h, c)
        ds = (e * (factors[h][c] * softmax_scale) * (gp - corrs[h])).astype(BF)
        w_s[span(c), h * 2 * TILE + TILE : (h + 1) * 2 * TILE] = ds

    def to_queries(h):
        for r in range(2):
            rows = slice(r * DK // 2, (r + 1) * DK // 2)
            out = dot(kt_s[rows, :], w_s[:, h * 2 * TILE + TILE : (h + 1) * 2 * TILE])
            dqt_ref[h, rows, :] = out.astype(BF)

    def to_keys(c):
        w = w_s[span(c), :]
        lat = dot(w, gl_ref[...])
        wr = jnp.concatenate(
            [w[:, (2 * h + 1) * TILE : (2 * h + 2) * TILE] for h in range(H_LOC)], axis=1
        )
        rope = dot(wr, gr_ref[...])
        for b, ref in enumerate((own_ref, other_ref)):
            down = core ^ b
            up = jnp.where(down == 0, ahead[c], 0 - ahead[c]) & 3
            for to in range(4):
                at = b * HALF + to * OWNED
                right = jnp.where(down == 0, to - x, x - to) & 3
                for n in range(DL // LANES):
                    ref[right, up, floors[c], n * OWNED : (n + 1) * OWNED, :] = lat[
                        at : at + OWNED, n * LANES : (n + 1) * LANES
                    ].astype(ref.dtype)
                both = jnp.concatenate(
                    [rope[at : at + OWNED // 2], rope[at + OWNED // 2 : at + OWNED]], axis=1
                )
                ref[right, up, floors[c], DL // LANES * OWNED :, :] = both.astype(ref.dtype)

    for step in range(H_LOC + 2):
        if 1 <= step <= H_LOC:
            settle(step - 1)
        for c in range(NG):
            if step < H_LOC and c >= FIRST:
                e, gp, peak, total = weigh(
                    k_s[span(c - FIRST), :], qt_ref[step], got_ref[step], delta, limits[c]
                )
                for b in range(2):
                    at = (c - FIRST) * TILE + b * HALF
                    e_s[step, at : at + HALF, :] = e[b]
                gp_s[step, span(c - FIRST), :] = gp
                peaks[step].append(peak)
                sums[step].append(total)
            if 1 <= step <= H_LOC:
                correct(step - 1, c)
            if step >= 2:
                differ(step - 2, c)
        if step >= 2:
            to_queries(step - 2)
    for c in range(NG):
        to_keys(c)


VMEM = pl.BlockSpec(memory_space=pltpu.VMEM)
SMEM = pl.BlockSpec(memory_space=pltpu.SMEM)


def first_part(place, query_blocks, key_blocks, qt, go, k_blocks):
    shapes = [
        ((H_LOC, FIRST * TILE, TILE), F32),
        ((H_LOC, FIRST * TILE, TILE), F32),
        ((2, H_LOC, 8, TILE), F32),
        ((H_LOC * 2 * TILE, DL), BF),
        ((H_LOC * TILE, DR), BF),
        ((H_LOC, DL, TILE), BF),
    ]
    return pl.pallas_call(
        first_kernel,
        in_specs=[SMEM] * 3 + [VMEM] * (2 + FIRST),
        out_specs=[VMEM] * len(shapes),
        out_shape=[jax.ShapeDtypeStruct(*s) for s in shapes],
        scratch_shapes=[pltpu.VMEM((FIRST * TILE, DK), BF)],
        cost_estimate=pl.CostEstimate(
            flops=2 * 1024 * FIRST * TILE * (DK + DL), bytes_accessed=20_000_000, transcendentals=0
        ),
        compiler_params=pltpu.CompilerParams(vmem_limit_bytes=24 * 1024 * 1024),
    )(place, query_blocks, key_blocks, qt, go, *k_blocks)


def main_part(place, query_blocks, key_blocks, qt, k_blocks, early):
    rest = (NG - FIRST) * TILE
    return pl.pallas_call(
        main_kernel,
        in_specs=[SMEM] * 3 + [VMEM] * (1 + len(k_blocks) + len(early)),
        out_specs=[VMEM] * 3,
        out_shape=[
            jax.ShapeDtypeStruct((H_LOC, DK, TILE), BF),
            jax.ShapeDtypeStruct((4, 4, 2, PACKED, LANES), F32),
            jax.ShapeDtypeStruct((4, 4, 2, PACKED, LANES), BF),
        ],
        scratch_shapes=[
            pltpu.VMEM((DK, KEYS), BF),
            pltpu.VMEM((rest, DK), BF),
            pltpu.VMEM((H_LOC, rest, TILE), F32),
            pltpu.VMEM((H_LOC, rest, TILE), F32),
            pltpu.VMEM((KEYS, H_LOC * 2 * TILE), BF),
        ],
        compiler_params=pltpu.CompilerParams(vmem_limit_bytes=MAIN_VMEM),
    )(place, query_blocks, key_blocks, qt, *k_blocks, *early)


def swap_cores(x):
    return lax.ppermute(x, "c", [(0, 1), (1, 0)])


def onward(x, dz):
    pairs = [
        ((y * 2 + z) * 2 + c, ((y + 1 - 2 * c) % 4 * 2 + (z ^ dz)) * 2 + c)
        for y in range(4)
        for z in range(2)
        for c in range(2)
    ]
    return lax.ppermute(x, ("y", "zl", "c"), pairs)


def mirrored(x, axis, step):
    pairs = [
        (n * 2 + c, (n + (step if c == 0 else -step)) % 4 * 2 + c)
        for n in range(4)
        for c in range(2)
    ]
    return lax.ppermute(x, (axis, "c"), pairs)


def opposite(x, dz):
    pairs = [(y * 2 + z, (y + 2) % 4 * 2 + (z ^ dz)) for y in range(4) for z in range(2)]
    return lax.ppermute(x, ("y", "zl"), pairs)


def unpack(x):
    lat = x[: DL // LANES * OWNED].reshape(DL // LANES, 4, 8, LANES)
    lat = lat.transpose(1, 2, 0, 3).reshape(4, 8, DL)
    rope = x[DL // LANES * OWNED :].reshape(2, 8, 2, DR).transpose(2, 0, 1, 3).reshape(4, 8, DR)
    return jnp.concatenate([lat, rope], axis=2)


def shards(queries, latent_cache, grad_output, query_blocks, key_blocks):
    core, y, zl, x = (lax.axis_index(a) for a in ("c", "y", "zl", "x"))
    row = lax.broadcasted_iota(jnp.int32, (TILE, TILE), 0)
    t = lax.broadcasted_iota(jnp.int32, (TILE, TILE), 1)
    half, t = t >> 7, t & 127
    pick = (row == (t >> 3) * 16 + (core ^ half) * 8 + (t & 7)).astype(BF)
    here = lax.dot_general(
        latent_cache, pick, (((0,), (0,)), ((), ())), preferred_element_type=F32
    ).astype(BF)
    here = jnp.concatenate([here[:, :HALF], here[:, HALF:]], axis=0)

    near = onward(here, 0)
    slant = onward(here, 1)
    singles = [
        lax.ppermute(here[:DK], "zl", [(0, 1), (1, 0)]),
        opposite(here[:DK], 0),
        opposite(here[:DK], 1),
    ]
    blocks = [here, near, swap_cores(near), slant, swap_cores(slant)]

    qt = queries.transpose(1, 2, 0)
    go = grad_output.transpose(1, 0, 2)
    place = jnp.stack([core, y, zl, x])
    early = first_part(place, query_blocks, key_blocks, qt, go, blocks)
    blocks += singles + [swap_cores(k) for k in singles]
    dqt, own, other = main_part(place, query_blocks, key_blocks, qt, blocks, early)

    other = swap_cores(other)
    sums = [own[d] + other[d].astype(F32) for d in range(4)]
    for axis in ("x", "y"):
        got = [mirrored(sums[d].astype(BF), axis, d) for d in (1, 3, 2)]
        sums = sums[0] + sum(g.astype(F32) for g in got)
    part = jnp.concatenate([unpack(sums[z]).astype(BF) for z in range(2)], axis=0)
    got = lax.all_to_all(part, ("zl", "zh"), 0, 0, tiled=True)
    return dqt.transpose(2, 0, 1), jnp.sum(got.astype(F32), axis=0)


def solution(mesh):
    fine = Mesh(mesh.devices.reshape(4, 2, 4, 4, 2), ("y", "zl", "x", "zh", "c"))
    seq, head = ("y", "zl"), ("x", "zh", "c")
    placed = (P(seq, head, None), P(seq, None), P(seq, head, None), P(), P())
    return jax.shard_map(
        shards,
        mesh=fine,
        in_specs=placed,
        out_specs=(P(seq, head, None), P(seq + head, None)),
        check_vma=False,
    )
```

time: 89.1 us -> 92.3 us (1.036)
  waiting for transfers between devices: 24.8 us -> 32.2 us
  starting transfers between devices: 24.2 us -> 18.5 us
  Pallas kernels: 18.7 us -> 19.7 us
    ppermute x13 -> x9, waiting for transfers between devices: 10.6 us -> 19.9 us  [the longest x6 14.6 us: mirrored(): return lax.ppermute(x, (axis, 'c'), pairs)]
    ppermute x6, starting transfers between devices: 3.85 us -> 0.57 us  [swap_cores(): return lax.ppermute(x, 'c', [(0, 1), (1, 0)])]
    ppermute x4 -> x2, waiting for transfers between devices: 11.7 us -> 9.46 us  [onward(): return lax.ppermute(x, ('y', 'zl', 'c'), pairs)]
    ppermute x13 -> x9, starting transfers between devices: 17.3 us -> 15.2 us  [the longest x6 10.2 us: mirrored(): return lax.ppermute(x, (axis, 'c'), pairs)]
    pallas_call x1 -> x2, Pallas kernels: 18.7 us -> 19.7 us  [the longest x1 15 us: main_part(): pl.pallas_call(main_kernel, in_specs=[SMEM] * 3 + [VMEM] * (1 + len(k_blo...]
    ppermute x4 -> x2, starting transfers between devices: 3.05 us -> 2.78 us  [onward(): return lax.ppermute(x, ('y', 'zl', 'c'), pairs)]
  transfers between devices with their start and end apart: 23 -> 17, of which waited for: 11 -> 8; matrix products, arithmetic and copies ran while one was open for 2% -> 2% of each run, Pallas kernels for 0% -> 5%
where the time goes in v4:
time: 92.3 us; the launch traced here: 91.7 us
  waiting for transfers between devices  32.2 us (35%)
  Pallas kernels  19.7 us (21%)
  starting transfers between devices  18.5 us (20%)
  blocking collectives  16.4 us (18%)
  local copies, waits for them, and re-layouts  2.57 us (3%)
  other arithmetic  1.18 us (1%)
    all_to_all x1, blocking collectives, shards(): got = lax.all_to_all(part, ('zl', 'zh'), 0, 0, tiled=True)  16.4 us
    pallas_call x1, Pallas kernels, main_part(): pl.pallas_call(main_kernel, in_specs=[SMEM] * 3 + [VMEM] * (1 + len(k_blo...  15 us
    ppermute x6, waiting for transfers between devices, mirrored(): return lax.ppermute(x, (axis, 'c'), pairs)  14.6 us
    ppermute x6, starting transfers between devices, mirrored(): return lax.ppermute(x, (axis, 'c'), pairs)  10.2 us
    ppermute x2, waiting for transfers between devices, onward(): return lax.ppermute(x, ('y', 'zl', 'c'), pairs)  9.46 us
    ppermute x2, waiting for transfers between devices, opposite(): return lax.ppermute(x, ('y', 'zl'), pairs)  5.32 us
    ppermute x2, starting transfers between devices, opposite(): return lax.ppermute(x, ('y', 'zl'), pairs)  4.83 us
    pallas_call x1, Pallas kernels, first_part(): pl.pallas_call(first_kernel, in_specs=[SMEM] * 3 + [VMEM] * (2 + FIRST),...  4.75 us
  transfers between devices with their start and end apart: 17, of which 8 were waited for; matrix products, arithmetic and copies ran while one was open for 2% of the time, Pallas kernels for 5%

profile of v4, /device:TPU:32, one launch (start us, length us, event | category | flops | bytes accessed | tf_op | source)
XLA Modules:
  0.0 91.7 jit_solution(16063312248234852924)
XLA Ops:
  0.6 0.0 copy-start
  0.6 0.0 copy-start.3
  0.7 0.0 copy-start.2
  0.7 0.0 copy-start.1
  0.7 0.9 copy-done
  1.6 0.2 fusion
  1.9 1.2 %collective-permute-start.2 = (bf16[1152,128]{1,0:T(8,128)(2,1)S(1)}, bf16[1152,128]{1,0:T(8,128)(2,1)S(1)}, u32[]{:S(2)}, u32[]{:S(2)}) collective-permute-start(bf16[1152,128]{1,0:T(8,128)(2,1)S(1)} %pad_maximum_fusion.refs_0_), channel_id=1, source_target_pairs={{0,96},{1,225},{32,64},{33,193},{64,160},{65,33},{96,128},{97,1},{... | collective-permute-start | bytes 884744 | tf_op jit(solution)/shard_map/ppermute | solution.py:269
  3.1 1.6 %collective-permute-start = (bf16[1152,128]{1,0:T(8,128)(2,1)S(1)}, bf16[1152,128]{1,0:T(8,128)(2,1)S(1)}, u32[]{:S(2)}, u32[]{:S(2)}) collective-permute-start(bf16[1152,128]{1,0:T(8,128)(2,1)S(1)} %pad_maximum_fusion.refs_0_), channel_id=1, source_target_pairs={{0,64},{1,193},{32,96},{33,225},{64,128},{65,1},{96,160},{97,33},{... | collective-permute-start | bytes 884744 | tf_op jit(solution)/shard_map/ppermute | solution.py:269
  4.7 8.8 %collective-permute-done.2.refs_3_ = bf16[1152,128]{1,0:T(8,128)(2,1)S(1)} collective-permute-done((bf16[1152,128]{1,0:T(8,128)(2,1)S(1)}, bf16[1152,128]{1,0:T(8,128)(2,1)S(1)}, u32[]{:S(2)}, u32[]{:S(2)}) %collective-permute-start.2) | collective-permute-done | bytes 294944 | tf_op jit(solution)/shard_map/ppermute | solution.py:269
  13.5 0.0 collective-permute-start.3
  13.5 0.7 collective-permute-done.refs_1_
  14.2 0.0 collective-permute-start.1
  14.2 2.3 %collective-permute-start.6 = (bf16[576,128]{1,0:T(8,128)(2,1)S(1)}, bf16[576,128]{1,0:T(8,128)(2,1)S(1)}, u32[]{:S(2)}, u32[]{:S(2)}) collective-permute-start(bf16[576,128]{1,0:T(8,128)(2,1)S(1)} %get-tuple-element.28), channel_id=1, source_target_pairs={{0,160},{32,128},{64,224},{96,192},{128,32},{160,0},{192,96},{224,... | collective-permute-start | bytes 442376 | tf_op jit(solution)/shard_map/ppermute | solution.py:283
  16.4 2.6 %collective-permute-start.5 = (bf16[576,128]{1,0:T(8,128)(2,1)S(1)}, bf16[576,128]{1,0:T(8,128)(2,1)S(1)}, u32[]{:S(2)}, u32[]{:S(2)}) collective-permute-start(bf16[576,128]{1,0:T(8,128)(2,1)S(1)} %get-tuple-element.28), channel_id=1, source_target_pairs={{0,128},{32,160},{64,192},{96,224},{128,0},{160,32},{192,64},{224,... | collective-permute-start | bytes 442376 | tf_op jit(solution)/shard_map/ppermute | solution.py:283
  19.0 0.2 collective-permute-start.4
  19.1 1.4 %copy.16 = bf16[256,4,512]{2,0,1:T(8,128)(2,1)S(1)} copy(bf16[256,4,512]{2,1,0:T(4,128)(2,1)} %param.7) | data formatting | bytes 2097152 | tf_op args[2]
  20.6 0.1 pad_add_fusion.place_ref
  20.7 2.6 %collective-permute-done.6.refs_7_ = bf16[576,128]{1,0:T(8,128)(2,1)S(1)} collective-permute-done((bf16[576,128]{1,0:T(8,128)(2,1)S(1)}, bf16[576,128]{1,0:T(8,128)(2,1)S(1)}, u32[]{:S(2)}, u32[]{:S(2)}) %collective-permute-start.6) | collective-permute-done | bytes 147488 | tf_op jit(solution)/shard_map/ppermute | solution.py:283
  23.2 0.0 collective-permute-start.9
  23.2 2.8 %collective-permute-done.5.refs_6_ = bf16[576,128]{1,0:T(8,128)(2,1)S(1)} collective-permute-done((bf16[576,128]{1,0:T(8,128)(2,1)S(1)}, bf16[576,128]{1,0:T(8,128)(2,1)S(1)}, u32[]{:S(2)}, u32[]{:S(2)}) %collective-permute-start.5) | collective-permute-done | bytes 147488 | tf_op jit(solution)/shard_map/ppermute | solution.py:283
  26.0 0.0 collective-permute-start.8
  26.0 0.0 collective-permute-done.4.refs_5_
  26.0 0.5 collective-permute-start.7
  26.5 0.0 collective-permute-done.3.refs_4_
  26.5 0.0 collective-permute-done.1.refs_2_
  26.5 0.0 copy-done.3
  26.5 0.0 copy-done.2
  26.5 0.0 copy-done.1
  26.5 4.8 %shard_map.68 = (f32[4,1280,256]{2,1,0:T(8,128)S(1)}, f32[4,1280,256]{2,1,0:T(8,128)S(1)}, f32[2,4,8,256]{3,2,1,0:T(8,128)S(1)}, bf16[2048,512]{1,0:T(8,128)(2,1...) custom-call(s32[4]{0:T(128)S(1)} %pad_add_fusion.place_ref, s32[8]{0:T(128)S(1)} %copy-done.2, ...), custom_call_target="tpu_custom_call" | custom-call | flops 2852126720 | bytes 20000000 | tf_op jit(solution)/shard_map/pallas_call | solution.py:223
  31.3 0.0 collective-permute-done.9.refs_10_
  31.3 0.0 collective-permute-done.8.refs_9_
  31.3 0.0 collective-permute-done.7.refs_8_
  31.3 15.0 %shard_map.69 = (bf16[4,576,256]{2,1,0:T(8,128)(2,1)}, f32[4,4,2,144,128]{4,3,2,1,0:T(8,128)S(1)}, bf16[4,4,2,144,128]{4,3,2,1,0:T(8,128)(2,1)S(1)}) custom-call(s32[4]{0:T(128)S(1)} %pad_add_fusion.place_ref, s32[8]{0:T(128)S(1)} %copy-done.2, s32[8]{0:T(128)S(1)} %copy-done.3, bf16[4,576,256]{2,1,0:T(8,128)(2,1)S(1)} %bitcast.50, ...), custom_call_target="tpu_custom_call" | custom-call | tf_op jit(solution)/shard_map/pallas_call | solution.py:238
  46.3 0.1 collective-permute-start.10
  46.4 2.8 %collective-permute-done.10 = bf16[4,4,2,144,128]{4,3,2,1,0:T(8,128)(2,1)S(1)} collective-permute-done((bf16[4,4,2,144,128]{4,3,2,1,0:T(8,128)(2,1)S(1)}, bf16[4,4,2,144,128]{4,3,2,1,0:T(8,128)(2,1)S(1)}, u32[]{:S(2)}, u32[]{:S(2)}) %collective-permute-start.10) | collective-permute-done | bytes 1179680 | tf_op jit(solution)/shard_map/ppermute | solution.py:259
  49.2 0.2 fusion.1
  49.4 1.5 %collective-permute-start.11 = (bf16[4,2,144,128]{3,2,1,0:T(8,128)(2,1)S(1)}, bf16[4,2,144,128]{3,2,1,0:T(8,128)(2,1)S(1)}, u32[]{:S(2)}, u32[]{:S(2)}) collective-permute-start(bf16[4,2,144,128]{3,2,1,0:T(8,128)(2,1)S(1)} %get-tuple-element.22), channel_id=1, source_target_pairs={{0,8},{1,25},{8,16},{9,1},{16,24},{17,9},{24,0},{25,17},{2,10},{3,... | collective-permute-start | bytes 884744 | tf_op jit(solution)/shard_map/ppermute | solution.py:278
  50.9 2.7 %collective-permute-start.13 = (bf16[4,2,144,128]{3,2,1,0:T(8,128)(2,1)S(1)}, bf16[4,2,144,128]{3,2,1,0:T(8,128)(2,1)S(1)}, u32[]{:S(2)}, u32[]{:S(2)}) collective-permute-start(bf16[4,2,144,128]{3,2,1,0:T(8,128)(2,1)S(1)} %get-tuple-element.23), channel_id=1, source_target_pairs={{0,16},{1,17},{8,24},{9,25},{16,0},{17,1},{24,8},{25,9},{2,18},{3,... | collective-permute-start | bytes 884744 | tf_op jit(solution)/shard_map/ppermute | solution.py:278
  53.6 1.4 %collective-permute-start.12 = (bf16[4,2,144,128]{3,2,1,0:T(8,128)(2,1)S(1)}, bf16[4,2,144,128]{3,2,1,0:T(8,128)(2,1)S(1)}, u32[]{:S(2)}, u32[]{:S(2)}) collective-permute-start(bf16[4,2,144,128]{3,2,1,0:T(8,128)(2,1)S(1)} %get-tuple-element.24), channel_id=1, source_target_pairs={{0,24},{1,9},{8,0},{9,17},{16,8},{17,25},{24,16},{25,1},{2,26},{3,... | collective-permute-start | bytes 884744 | tf_op jit(solution)/shard_map/ppermute | solution.py:278
  55.0 7.8 %collective-permute-done.11 = bf16[4,2,144,128]{3,2,1,0:T(8,128)(2,1)S(1)} collective-permute-done((bf16[4,2,144,128]{3,2,1,0:T(8,128)(2,1)S(1)}, bf16[4,2,144,128]{3,2,1,0:T(8,128)(2,1)S(1)}, u32[]{:S(2)}, u32[]{:S(2)}) %collective-permute-start.11) | collective-permute-done | bytes 294944 | tf_op jit(solution)/shard_map/ppermute | solution.py:278
  62.8 4.0 %collective-permute-done.13 = bf16[4,2,144,128]{3,2,1,0:T(8,128)(2,1)S(1)} collective-permute-done((bf16[4,2,144,128]{3,2,1,0:T(8,128)(2,1)S(1)}, bf16[4,2,144,128]{3,2,1,0:T(8,128)(2,1)S(1)}, u32[]{:S(2)}, u32[]{:S(2)}) %collective-permute-start.13) | collective-permute-done | bytes 294944 | tf_op jit(solution)/shard_map/ppermute | solution.py:278
  66.8 0.0 collective-permute-done.12
  66.8 0.2 fusion.7
  67.0 0.4 collective-permute-start.14
  67.4 2.5 %collective-permute-start.16 = (bf16[2,144,128]{2,1,0:T(8,128)(2,1)S(1)}, bf16[2,144,128]{2,1,0:T(8,128)(2,1)S(1)}, u32[]{:S(2)}, u32[]{:S(2)}) collective-permute-start(bf16[2,144,128]{2,1,0:T(8,128)(2,1)S(1)} %get-tuple-element.26), channel_id=1, source_target_pairs={{0,128},{1,129},{64,192},{65,193},{128,0},{129,1},{192,64},{193,65... | collective-permute-start | bytes 221192 | tf_op jit(solution)/shard_map/ppermute | solution.py:278
  69.9 1.7 %collective-permute-start.15 = (bf16[2,144,128]{2,1,0:T(8,128)(2,1)S(1)}, bf16[2,144,128]{2,1,0:T(8,128)(2,1)S(1)}, u32[]{:S(2)}, u32[]{:S(2)}) collective-permute-start(bf16[2,144,128]{2,1,0:T(8,128)(2,1)S(1)} %get-tuple-element.27), channel_id=1, source_target_pairs={{0,192},{1,65},{64,0},{65,129},{128,64},{129,193},{192,128},{193,1... | collective-permute-start | bytes 221192 | tf_op jit(solution)/shard_map/ppermute | solution.py:278
  71.6 2.8 %collective-permute-done.14 = bf16[2,144,128]{2,1,0:T(8,128)(2,1)S(1)} collective-permute-done((bf16[2,144,128]{2,1,0:T(8,128)(2,1)S(1)}, bf16[2,144,128]{2,1,0:T(8,128)(2,1)S(1)}, u32[]{:S(2)}, u32[]{:S(2)}) %collective-permute-start.14) | collective-permute-done | bytes 73760 | tf_op jit(solution)/shard_map/ppermute | solution.py:278
  74.4 0.0 collective-permute-done.16
  74.4 0.0 collective-permute-done.15
  74.5 0.1 reshape.60
  74.6 0.1 reshape.64
  74.7 16.4 %all_to_all.5 = bf16[8,8,576]{2,1,0:T(8,128)(2,1)S(1)} all-to-all(bf16[8,8,576]{2,1,0:T(8,128)(2,1)S(1)} %maximum_maximum_fusion), channel_id=1, replica_groups=mesh['y'=4,'zl'=2,'x'=4,'zh'=4,'c'=2] {'zl','zh'}, dimensions={0} | all-to-all | bytes 147456 | tf_op jit(solution)/shard_map/all_to_all | solution.py:326
  91.0 0.6 convert_reduce_fusion
  (11 shorter events, 0.1 us)
Async XLA Ops:
  0.6 1.0 %copy-start = (bf16[256,576]{0,1:T(8,128)(2,1)S(1)}, bf16[256,576]{0,1:T(8,128)(2,1)}, u32[]{:S(2)}) copy-start(bf16[256,576]{0,1:T(8,128)(2,1)} %param.6) | copy-start | bytes 884740
  0.6 25.9 %copy-start.3 = (s32[8]{0:T(128)S(1)}, s32[8]{0:T(128)}, u32[]{:S(2)}) copy-start(s32[8]{0:T(128)} %key_blocks_ref.3) | copy-start | bytes 100
  0.7 25.9 %copy-start.2 = (s32[8]{0:T(128)S(1)}, s32[8]{0:T(128)}, u32[]{:S(2)}) copy-start(s32[8]{0:T(128)} %query_blocks_ref.3) | copy-start | bytes 100
  0.7 25.9 %copy-start.1 = (bf16[256,4,576]{0,2,1:T(8,128)(2,1)S(1)}, bf16[256,4,576]{0,2,1:T(8,128)(2,1)}, u32[]{:S(2)}) copy-start(bf16[256,4,576]{0,2,1:T(8,128)(2,1)} %param.5) | copy-start | bytes 3538948
  1.9 11.6 %collective-permute-start.2 = (bf16[1152,128]{1,0:T(8,128)(2,1)S(1)}, bf16[1152,128]{1,0:T(8,128)(2,1)S(1)}, u32[]{:S(2)}, u32[]{:S(2)}) collective-permute-start(bf16[1152,128]{1,0:T(8,128)(2,1)S(1)} %pad_maximum_fusion.refs_0_), channel_id=1, source_target_pairs={{0,96},{1,225},{32,64},{33,193},{64,160},{65,33},{96,128},{97,1},{... | collective-permute-start | bytes 884744 | tf_op jit(solution)/shard_map/ppermute | solution.py:269
  3.1 11.0 %collective-permute-start = (bf16[1152,128]{1,0:T(8,128)(2,1)S(1)}, bf16[1152,128]{1,0:T(8,128)(2,1)S(1)}, u32[]{:S(2)}, u32[]{:S(2)}) collective-permute-start(bf16[1152,128]{1,0:T(8,128)(2,1)S(1)} %pad_maximum_fusion.refs_0_), channel_id=1, source_target_pairs={{0,64},{1,193},{32,96},{33,225},{64,128},{65,1},{96,160},{97,33},{... | collective-permute-start | bytes 884744 | tf_op jit(solution)/shard_map/ppermute | solution.py:269
  13.5 13.0 %collective-permute-start.3 = (bf16[1152,128]{1,0:T(8,128)(2,1)S(1)}, bf16[1152,128]{1,0:T(8,128)(2,1)S(1)}, u32[]{:S(2)}, u32[]{:S(2)}) collective-permute-start(bf16[1152,128]{1,0:T(8,128)(2,1)S(1)} %collective-permute-done.2.refs_3_), channel_id=1, source_target_pairs={{0,1},{1,0},{2,3},{3,2},{4,5},{5,4},{6,7},{7,6},{8,9},{9,8},{10,11... | collective-permute-start | bytes 884744 | tf_op jit(solution)/shard_map/ppermute | solution.py:259
  14.2 12.3 %collective-permute-start.1 = (bf16[1152,128]{1,0:T(8,128)(2,1)S(1)}, bf16[1152,128]{1,0:T(8,128)(2,1)S(1)}, u32[]{:S(2)}, u32[]{:S(2)}) collective-permute-start(bf16[1152,128]{1,0:T(8,128)(2,1)S(1)} %collective-permute-done.refs_1_), channel_id=1, source_target_pairs={{0,1},{1,0},{2,3},{3,2},{4,5},{5,4},{6,7},{7,6},{8,9},{9,8},{10,11... | collective-permute-start | bytes 884744 | tf_op jit(solution)/shard_map/ppermute | solution.py:259
  14.2 9.1 %collective-permute-start.6 = (bf16[576,128]{1,0:T(8,128)(2,1)S(1)}, bf16[576,128]{1,0:T(8,128)(2,1)S(1)}, u32[]{:S(2)}, u32[]{:S(2)}) collective-permute-start(bf16[576,128]{1,0:T(8,128)(2,1)S(1)} %get-tuple-element.28), channel_id=1, source_target_pairs={{0,160},{32,128},{64,224},{96,192},{128,32},{160,0},{192,96},{224,... | collective-permute-start | bytes 442376 | tf_op jit(solution)/shard_map/ppermute | solution.py:283
  16.4 9.6 %collective-permute-start.5 = (bf16[576,128]{1,0:T(8,128)(2,1)S(1)}, bf16[576,128]{1,0:T(8,128)(2,1)S(1)}, u32[]{:S(2)}, u32[]{:S(2)}) collective-permute-start(bf16[576,128]{1,0:T(8,128)(2,1)S(1)} %get-tuple-element.28), channel_id=1, source_target_pairs={{0,128},{32,160},{64,192},{96,224},{128,0},{160,32},{192,64},{224,... | collective-permute-start | bytes 442376 | tf_op jit(solution)/shard_map/ppermute | solution.py:283
  19.0 7.0 %collective-permute-start.4 = (bf16[576,128]{1,0:T(8,128)(2,1)S(1)}, bf16[576,128]{1,0:T(8,128)(2,1)S(1)}, u32[]{:S(2)}, u32[]{:S(2)}) collective-permute-start(bf16[576,128]{1,0:T(8,128)(2,1)S(1)} %get-tuple-element.28), channel_id=1, source_target_pairs={{0,32},{32,0},{1,33},{33,1},{2,34},{34,2},{3,35},{35,3},{4,36},{36... | collective-permute-start | bytes 442376 | tf_op jit(solution)/shard_map/ppermute | solution.py:307
  23.2 8.1 %collective-permute-start.9 = (bf16[576,128]{1,0:T(8,128)(2,1)S(1)}, bf16[576,128]{1,0:T(8,128)(2,1)S(1)}, u32[]{:S(2)}, u32[]{:S(2)}) collective-permute-start(bf16[576,128]{1,0:T(8,128)(2,1)S(1)} %collective-permute-done.6.refs_7_), channel_id=1, source_target_pairs={{0,1},{1,0},{2,3},{3,2},{4,5},{5,4},{6,7},{7,6},{8,9},{9,8},{10,11... | collective-permute-start | bytes 442376 | tf_op jit(solution)/shard_map/ppermute | solution.py:259
  26.0 5.3 %collective-permute-start.8 = (bf16[576,128]{1,0:T(8,128)(2,1)S(1)}, bf16[576,128]{1,0:T(8,128)(2,1)S(1)}, u32[]{:S(2)}, u32[]{:S(2)}) collective-permute-start(bf16[576,128]{1,0:T(8,128)(2,1)S(1)} %collective-permute-done.5.refs_6_), channel_id=1, source_target_pairs={{0,1},{1,0},{2,3},{3,2},{4,5},{5,4},{6,7},{7,6},{8,9},{9,8},{10,11... | collective-permute-start | bytes 442376 | tf_op jit(solution)/shard_map/ppermute | solution.py:259
  26.0 5.3 %collective-permute-start.7 = (bf16[576,128]{1,0:T(8,128)(2,1)S(1)}, bf16[576,128]{1,0:T(8,128)(2,1)S(1)}, u32[]{:S(2)}, u32[]{:S(2)}) collective-permute-start(bf16[576,128]{1,0:T(8,128)(2,1)S(1)} %collective-permute-done.4.refs_5_), channel_id=1, source_target_pairs={{0,1},{1,0},{2,3},{3,2},{4,5},{5,4},{6,7},{7,6},{8,9},{9,8},{10,11... | collective-permute-start | bytes 442376 | tf_op jit(solution)/shard_map/ppermute | solution.py:259
  46.3 2.8 %collective-permute-start.10 = (bf16[4,4,2,144,128]{4,3,2,1,0:T(8,128)(2,1)S(1)}, bf16[4,4,2,144,128]{4,3,2,1,0:T(8,128)(2,1)S(1)}, u32[]{:S(2)}, u32[]{:S(2)}) collective-permute-start(bf16[4,4,2,144,128]{4,3,2,1,0:T(8,128)(2,1)S(1)} %get-tuple-element.19), channel_id=1, source_target_pairs={{0,1},{1,0},{2,3},{3,2},{4,5},{5,4},{6,7},{7,6},{8,9},{9,8},{10,11... | collective-permute-start | bytes 3538952 | tf_op jit(solution)/shard_map/ppermute | solution.py:259
  49.4 13.5 %collective-permute-start.11 = (bf16[4,2,144,128]{3,2,1,0:T(8,128)(2,1)S(1)}, bf16[4,2,144,128]{3,2,1,0:T(8,128)(2,1)S(1)}, u32[]{:S(2)}, u32[]{:S(2)}) collective-permute-start(bf16[4,2,144,128]{3,2,1,0:T(8,128)(2,1)S(1)} %get-tuple-element.22), channel_id=1, source_target_pairs={{0,8},{1,25},{8,16},{9,1},{16,24},{17,9},{24,0},{25,17},{2,10},{3,... | collective-permute-start | bytes 884744 | tf_op jit(solution)/shard_map/ppermute | solution.py:278
  50.9 16.0 %collective-permute-start.13 = (bf16[4,2,144,128]{3,2,1,0:T(8,128)(2,1)S(1)}, bf16[4,2,144,128]{3,2,1,0:T(8,128)(2,1)S(1)}, u32[]{:S(2)}, u32[]{:S(2)}) collective-permute-start(bf16[4,2,144,128]{3,2,1,0:T(8,128)(2,1)S(1)} %get-tuple-element.23), channel_id=1, source_target_pairs={{0,16},{1,17},{8,24},{9,25},{16,0},{17,1},{24,8},{25,9},{2,18},{3,... | collective-permute-start | bytes 884744 | tf_op jit(solution)/shard_map/ppermute | solution.py:278
  53.6 13.2 %collective-permute-start.12 = (bf16[4,2,144,128]{3,2,1,0:T(8,128)(2,1)S(1)}, bf16[4,2,144,128]{3,2,1,0:T(8,128)(2,1)S(1)}, u32[]{:S(2)}, u32[]{:S(2)}) collective-permute-start(bf16[4,2,144,128]{3,2,1,0:T(8,128)(2,1)S(1)} %get-tuple-element.24), channel_id=1, source_target_pairs={{0,24},{1,9},{8,0},{9,17},{16,8},{17,25},{24,16},{25,1},{2,26},{3,... | collective-permute-start | bytes 884744 | tf_op jit(solution)/shard_map/ppermute | solution.py:278
  67.0 7.4 %collective-permute-start.14 = (bf16[2,144,128]{2,1,0:T(8,128)(2,1)S(1)}, bf16[2,144,128]{2,1,0:T(8,128)(2,1)S(1)}, u32[]{:S(2)}, u32[]{:S(2)}) collective-permute-start(bf16[2,144,128]{2,1,0:T(8,128)(2,1)S(1)} %get-tuple-element.25), channel_id=1, source_target_pairs={{0,64},{1,193},{64,128},{65,1},{128,192},{129,65},{192,0},{193,129... | collective-permute-start | bytes 221192 | tf_op jit(solution)/shard_map/ppermute | solution.py:278
  67.4 7.0 %collective-permute-start.16 = (bf16[2,144,128]{2,1,0:T(8,128)(2,1)S(1)}, bf16[2,144,128]{2,1,0:T(8,128)(2,1)S(1)}, u32[]{:S(2)}, u32[]{:S(2)}) collective-permute-start(bf16[2,144,128]{2,1,0:T(8,128)(2,1)S(1)} %get-tuple-element.26), channel_id=1, source_target_pairs={{0,128},{1,129},{64,192},{65,193},{128,0},{129,1},{192,64},{193,65... | collective-permute-start | bytes 221192 | tf_op jit(solution)/shard_map/ppermute | solution.py:278
  69.9 4.5 %collective-permute-start.15 = (bf16[2,144,128]{2,1,0:T(8,128)(2,1)S(1)}, bf16[2,144,128]{2,1,0:T(8,128)(2,1)S(1)}, u32[]{:S(2)}, u32[]{:S(2)}) collective-permute-start(bf16[2,144,128]{2,1,0:T(8,128)(2,1)S(1)} %get-tuple-element.27), channel_id=1, source_target_pairs={{0,192},{1,65},{64,0},{65,129},{128,64},{129,193},{192,128},{193,1... | collective-permute-start | bytes 221192 | tf_op jit(solution)/shard_map/ppermute | solution.py:278

commit v5 on v4

--- a/solution.py
+++ b/solution.py
@@ -23,8 +23,9 @@
 OWNED = 32
 PACKED = OWNED * DK // LANES
 MAIN_VMEM = 28 * 1024 * 1024
-FIRST = 5
-SWAPPED = (2, 4)
+FIRST = 3
+WHOLE = 5
+SWAPPED = (3, 4)
 
 softmax_scale = 0.07216878364870322
 
@@ -43,8 +44,8 @@
 def positions(place_ref, query_blocks_ref, key_blocks_ref):
     core, y, zl = (place_ref[n] for n in range(3))
     turn = 2 * core
-    ahead = [(0 - dy) & 3 for dy in (0, 1 + turn, 3 - turn, 1 + turn, 3 - turn, 0, 2, 2)]
-    floors = [zl ^ dz for dz in (0, 0, 0, 1, 1, 1, 0, 1)]
+    ahead = [(0 - dy) & 3 for dy in (0, 1 + turn, 1 + turn, 3 - turn, 3 - turn, 0, 2, 2)]
+    floors = [zl ^ dz for dz in (0, 0, 1, 0, 1, 1, 0, 1)]
     mine = query_blocks_ref[y * 2 + zl]
     limits = []
     for up, floor in zip(ahead, floors):
@@ -55,11 +56,11 @@
 
 def halves(refs):
     out = []
-    for slot in range(FIRST):
+    for slot in range(min(WHOLE, len(refs))):
         flip = slot in SWAPPED
         blocks = [refs[slot][n * DK : (n + 1) * DK, :] for n in range(2)]
         out.append(blocks[::-1] if flip else blocks)
-    rest = refs[FIRST:]
+    rest = refs[WHOLE:]
     for slot in range(len(rest) // 2):
         out.append([rest[slot][...], rest[slot + len(rest) // 2][...]])
     return out
@@ -114,7 +115,7 @@
 
 
 def main_kernel(place_ref, query_blocks_ref, key_blocks_ref, qt_ref, *refs):
-    k_refs, refs = refs[: 2 * NG - FIRST], refs[2 * NG - FIRST :]
+    k_refs, refs = refs[: 2 * NG - WHOLE], refs[2 * NG - WHOLE :]
     e1_ref, gp1_ref, stat_ref, gl_ref, gr_ref, got_ref = refs[:6]
     dqt_ref, own_ref, other_ref, kt_s, k_s, e_s, gp_s, w_s = refs[6:]
     ahead, floors, limits = positions(place_ref, query_blocks_ref, key_blocks_ref)
@@ -169,19 +170,20 @@
         )
         rope = dot(wr, gr_ref[...])
         for b, ref in enumerate((own_ref, other_ref)):
-            down = core ^ b
-            up = jnp.where(down == 0, ahead[c], 0 - ahead[c]) & 3
+            later = core ^ b
             for to in range(4):
                 at = b * HALF + to * OWNED
-                right = jnp.where(down == 0, to - x, x - to) & 3
+                right = (to - x) & 3
+                i = jnp.where(later == 0, right, ahead[c])
+                j = jnp.where(later == 0, ahead[c], right)
                 for n in range(DL // LANES):
-                    ref[right, up, floors[c], n * OWNED : (n + 1) * OWNED, :] = lat[
+                    ref[i, j, floors[c], n * OWNED : (n + 1) * OWNED, :] = lat[
                         at : at + OWNED, n * LANES : (n + 1) * LANES
                     ].astype(ref.dtype)
                 both = jnp.concatenate(
                     [rope[at : at + OWNED // 2], rope[at + OWNED // 2 : at + OWNED]], axis=1
                 )
-                ref[right, up, floors[c], DL // LANES * OWNED :, :] = both.astype(ref.dtype)
+                ref[i, j, floors[c], DL // LANES * OWNED :, :] = both.astype(ref.dtype)
 
     for step in range(H_LOC + 2):
         if 1 <= step <= H_LOC:
@@ -269,13 +271,16 @@
     return lax.ppermute(x, ("y", "zl", "c"), pairs)
 
 
-def mirrored(x, axis, step):
-    pairs = [
-        (n * 2 + c, (n + (step if c == 0 else -step)) % 4 * 2 + c)
-        for n in range(4)
-        for c in range(2)
-    ]
-    return lax.ppermute(x, (axis, "c"), pairs)
+def crossed(x, first, step):
+    def target(n):
+        y, x, c = n // 8, n // 2 % 4, n % 2
+        if (c == 0) == first:
+            x = (x + step) % 4
+        else:
+            y = (y + step) % 4
+        return (y * 4 + x) * 2 + c
+
+    return lax.ppermute(x, ("y", "x", "c"), [(n, target(n)) for n in range(32)])
 
 
 def opposite(x, dz):
@@ -308,19 +313,20 @@
         opposite(here[:DK], 0),
         opposite(here[:DK], 1),
     ]
-    blocks = [here, near, swap_cores(near), slant, swap_cores(slant)]
 
     qt = queries.transpose(1, 2, 0)
     go = grad_output.transpose(1, 0, 2)
+    go, near, slant, *singles = lax.optimization_barrier((go, near, slant, *singles))
+    blocks = [here, near, slant]
     place = jnp.stack([core, y, zl, x])
     early = first_part(place, query_blocks, key_blocks, qt, go, blocks)
-    blocks += singles + [swap_cores(k) for k in singles]
+    blocks += [swap_cores(near), swap_cores(slant)] + singles + [swap_cores(k) for k in singles]
     dqt, own, other = main_part(place, query_blocks, key_blocks, qt, blocks, early)
 
     other = swap_cores(other)
     sums = [own[d] + other[d].astype(F32) for d in range(4)]
-    for axis in ("x", "y"):
-        got = [mirrored(sums[d].astype(BF), axis, d) for d in (1, 3, 2)]
+    for first in (True, False):
+        got = [crossed(sums[d].astype(BF), first, d) for d in (2, 1, 3)]
         sums = sums[0] + sum(g.astype(F32) for g in got)
     part = jnp.concatenate([unpack(sums[z]).astype(BF) for z in range(2)], axis=0)
     got = lax.all_to_all(part, ("zl", "zh"), 0, 0, tiled=True)

time: 92.3 us -> 84.1 us (0.911)
  waiting for transfers between devices: 32.2 us -> 24.5 us
  starting transfers between devices: 18.5 us -> 16.4 us
  local copies, waits for them, and re-layouts: 2.57 us -> 4.59 us
    ppermute x2, waiting for transfers between devices: 9.46 us -> 0.01 us  [onward(): return lax.ppermute(x, ('y', 'zl', 'c'), pairs)]
    ppermute x2, waiting for transfers between devices: 5.32 us -> 10.8 us  [opposite(): return lax.ppermute(x, ('y', 'zl'), pairs)]
    ppermute x6, waiting for transfers between devices: 14.6 us -> 11.2 us  [crossed(): return lax.ppermute(x, ('y', 'x', 'c'), [(n, target(n)) for n in range(32)])]
    ppermute x6, starting transfers between devices: 10.2 us -> 7.12 us  [crossed(): return lax.ppermute(x, ('y', 'x', 'c'), [(n, target(n)) for n in range(32)])]
    pallas_call x1, Pallas kernels: 15 us -> 17.2 us  [main_part(): pl.pallas_call(main_kernel, in_specs=[SMEM] * 3 + [VMEM] * (1 + len(k_blo...]
    unnamed x9 -> x17, local copies, waits for them, and re-layouts: 2.34 us -> 4.36 us
    pallas_call x1, Pallas kernels: 4.75 us -> 3.02 us  [first_part(): pl.pallas_call(first_kernel, in_specs=[SMEM] * 3 + [VMEM] * (2 + FIRST),...]
    ppermute x6, starting transfers between devices: 0.57 us -> 1.52 us  [swap_cores(): return lax.ppermute(x, 'c', [(0, 1), (1, 0)])]
  transfers between devices with their start and end apart: 17 -> 17, of which waited for: 8 -> 8; matrix products, arithmetic and copies ran while one was open for 2% -> 2% of each run, Pallas kernels for 5% -> 4%
where the time goes in v5:
time: 84.1 us; the launch traced here: 83.7 us
  waiting for transfers between devices  24.5 us (29%)
  Pallas kernels  20.2 us (24%)
  starting transfers between devices  16.4 us (20%)
  blocking collectives  15.8 us (19%)
  local copies, waits for them, and re-layouts  4.59 us (5%)
  other arithmetic  1.18 us (1%)
    pallas_call x1, Pallas kernels, main_part(): pl.pallas_call(main_kernel, in_specs=[SMEM] * 3 + [VMEM] * (1 + len(k_blo...  17.2 us
    all_to_all x1, blocking collectives, shards(): got = lax.all_to_all(part, ('zl', 'zh'), 0, 0, tiled=True)  15.8 us
    ppermute x6, waiting for transfers between devices, crossed(): return lax.ppermute(x, ('y', 'x', 'c'), [(n, target(n)) for n in range(32)])  11.2 us
    ppermute x2, waiting for transfers between devices, opposite(): return lax.ppermute(x, ('y', 'zl'), pairs)  10.8 us
    ppermute x6, starting transfers between devices, crossed(): return lax.ppermute(x, ('y', 'x', 'c'), [(n, target(n)) for n in range(32)])  7.12 us
    ppermute x2, starting transfers between devices, opposite(): return lax.ppermute(x, ('y', 'zl'), pairs)  4.89 us
    unnamed x17, local copies, waits for them, and re-layouts  4.36 us
    pallas_call x1, Pallas kernels, first_part(): pl.pallas_call(first_kernel, in_specs=[SMEM] * 3 + [VMEM] * (2 + FIRST),...  3.02 us
  transfers between devices with their start and end apart: 17, of which 8 were waited for; matrix products, arithmetic and copies ran while one was open for 2% of the time, Pallas kernels for 4%

profile of v5, /device:TPU:32, one launch (start us, length us, event | category | flops | bytes accessed | tf_op | source)
XLA Modules:
  0.0 83.7 jit_solution(13049591972128081352)
XLA Ops:
  0.6 0.0 copy-start
  0.6 0.0 copy-start.1
  0.7 0.9 %copy-done = bf16[256,576]{0,1:T(8,128)(2,1)S(1)} copy-done((bf16[256,576]{0,1:T(8,128)(2,1)S(1)}, bf16[256,576]{0,1:T(8,128)(2,1)}, u32[]{:S(2)}) %copy-start) | copy-done | bytes 294936
  1.6 0.2 fusion
  1.9 1.2 %collective-permute-start.1 = (bf16[1152,128]{1,0:T(8,128)(2,1)S(1)}, bf16[1152,128]{1,0:T(8,128)(2,1)S(1)}, u32[]{:S(2)}, u32[]{:S(2)}) collective-permute-start(bf16[1152,128]{1,0:T(8,128)(2,1)S(1)} %pad_maximum_fusion.refs_0_), channel_id=1, source_target_pairs={{0,96},{1,225},{32,64},{33,193},{64,160},{65,33},{96,128},{97,1},{... | collective-permute-start | bytes 884744 | tf_op jit(solution)/shard_map/ppermute | solution.py:271
  3.1 1.6 %collective-permute-start = (bf16[1152,128]{1,0:T(8,128)(2,1)S(1)}, bf16[1152,128]{1,0:T(8,128)(2,1)S(1)}, u32[]{:S(2)}, u32[]{:S(2)}) collective-permute-start(bf16[1152,128]{1,0:T(8,128)(2,1)S(1)} %pad_maximum_fusion.refs_0_), channel_id=1, source_target_pairs={{0,64},{1,193},{32,96},{33,225},{64,128},{65,1},{96,160},{97,33},{... | collective-permute-start | bytes 884744 | tf_op jit(solution)/shard_map/ppermute | solution.py:271
  4.7 2.9 %collective-permute-start.4 = (bf16[576,128]{1,0:T(8,128)(2,1)S(1)}, bf16[576,128]{1,0:T(8,128)(2,1)S(1)}, u32[]{:S(2)}, u32[]{:S(2)}) collective-permute-start(bf16[576,128]{1,0:T(8,128)(2,1)S(1)} %get-tuple-element.40), channel_id=1, source_target_pairs={{0,160},{32,128},{64,224},{96,192},{128,32},{160,0},{192,96},{224,... | collective-permute-start | bytes 442376 | tf_op jit(solution)/shard_map/ppermute | solution.py:288
  7.6 2.0 %collective-permute-start.3 = (bf16[576,128]{1,0:T(8,128)(2,1)S(1)}, bf16[576,128]{1,0:T(8,128)(2,1)S(1)}, u32[]{:S(2)}, u32[]{:S(2)}) collective-permute-start(bf16[576,128]{1,0:T(8,128)(2,1)S(1)} %get-tuple-element.40), channel_id=1, source_target_pairs={{0,128},{32,160},{64,192},{96,224},{128,0},{160,32},{192,64},{224,... | collective-permute-start | bytes 442376 | tf_op jit(solution)/shard_map/ppermute | solution.py:288
  9.6 0.1 collective-permute-start.2
  9.7 1.4 %copy.16 = bf16[256,4,512]{2,0,1:T(8,128)(2,1)S(1)} copy(bf16[256,4,512]{2,1,0:T(4,128)(2,1)} %param.7) | data formatting | bytes 2097152 | tf_op args[2]
  11.1 7.0 %collective-permute-done.4.refs_7_ = bf16[576,128]{1,0:T(8,128)(2,1)S(1)} collective-permute-done((bf16[576,128]{1,0:T(8,128)(2,1)S(1)}, bf16[576,128]{1,0:T(8,128)(2,1)S(1)}, u32[]{:S(2)}, u32[]{:S(2)}) %collective-permute-start.4) | collective-permute-done | bytes 147488 | tf_op jit(solution)/shard_map/ppermute | solution.py:288
  18.1 3.7 %collective-permute-done.3.refs_6_ = bf16[576,128]{1,0:T(8,128)(2,1)S(1)} collective-permute-done((bf16[576,128]{1,0:T(8,128)(2,1)S(1)}, bf16[576,128]{1,0:T(8,128)(2,1)S(1)}, u32[]{:S(2)}, u32[]{:S(2)}) %collective-permute-start.3) | collective-permute-done | bytes 147488 | tf_op jit(solution)/shard_map/ppermute | solution.py:288
  21.9 0.0 copy-start.2
  21.9 0.0 collective-permute-done.2.refs_5_
  21.9 0.0 copy-start.4
  21.9 0.0 collective-permute-done.1.refs_2_
  21.9 0.0 collective-permute-done.refs_1_
  21.9 0.6 copy-done.2
  22.5 0.0 collective-permute-start.5
  22.5 0.0 copy-done.4
  22.6 0.5 collective-permute-start.6
  23.1 0.1 pad_add_fusion.place_ref
  23.1 0.1 collective-permute-start.7
  23.2 0.5 collective-permute-start.8
  23.7 0.1 collective-permute-start.9
  23.8 0.0 copy-done.1
  23.8 0.0 copy-start.6
  23.8 0.7 copy-done.6
  24.4 0.0 copy-start.7
  24.4 0.7 copy-done.7
  25.1 0.0 copy-start.3
  25.1 0.0 copy-start.5
  25.1 3.0 %shard_map.68 = (f32[4,768,256]{2,1,0:T(8,128)S(1)}, f32[4,768,256]{2,1,0:T(8,128)S(1)}, f32[2,4,8,256]{3,2,1,0:T(8,128)S(1)}, bf16[2048,512]{1,0:T(8,128)(2,1)S...) custom-call(s32[4]{0:T(128)S(1)} %pad_add_fusion.place_ref, s32[8]{0:T(128)S(1)} %copy-done.6, ...), custom_call_target="tpu_custom_call" | custom-call | flops 1711276032 | bytes 20000000 | tf_op jit(solution)/shard_map/pallas_call | solution.py:225
  28.1 0.0 collective-permute-done.7.refs_8_
  28.1 0.0 collective-permute-done.8.refs_9_
  28.1 0.0 collective-permute-done.9.refs_10_
  28.2 0.0 collective-permute-done.5.refs_3_
  28.2 0.0 collective-permute-done.6.refs_4_
  28.2 0.0 copy-done.3
  28.2 0.0 copy-done.5
  28.2 17.2 %shard_map.69 = (bf16[4,576,256]{2,1,0:T(8,128)(2,1)}, f32[4,4,2,144,128]{4,3,2,1,0:T(8,128)S(1)}, bf16[4,4,2,144,128]{4,3,2,1,0:T(8,128)(2,1)S(1)}) custom-call(s32[4]{0:T(128)S(1)} %pad_add_fusion.place_ref, s32[8]{0:T(128)S(1)} %copy-done.6, s32[8]{0:T(128)S(1)} %copy-done.7, bf16[4,576,256]{2,1,0:T(8,128)(2,1)S(1)} %bitcast.50, ...), custom_call_target="tpu_custom_call" | custom-call | tf_op jit(solution)/shard_map/pallas_call | solution.py:240
  45.4 0.4 collective-permute-start.10
  45.8 2.5 %collective-permute-done.10 = bf16[4,4,2,144,128]{4,3,2,1,0:T(8,128)(2,1)S(1)} collective-permute-done((bf16[4,4,2,144,128]{4,3,2,1,0:T(8,128)(2,1)S(1)}, bf16[4,4,2,144,128]{4,3,2,1,0:T(8,128)(2,1)S(1)}, u32[]{:S(2)}, u32[]{:S(2)}) %collective-permute-start.10) | collective-permute-done | bytes 1179680 | tf_op jit(solution)/shard_map/ppermute | solution.py:261
  48.2 0.2 fusion.1
  48.5 2.0 %collective-permute-start.11 = (bf16[4,2,144,128]{3,2,1,0:T(8,128)(2,1)S(1)}, bf16[4,2,144,128]{3,2,1,0:T(8,128)(2,1)S(1)}, u32[]{:S(2)}, u32[]{:S(2)}) collective-permute-start(bf16[4,2,144,128]{3,2,1,0:T(8,128)(2,1)S(1)} %get-tuple-element.34), channel_id=1, source_target_pairs={{0,16},{1,129},{8,24},{9,137},{16,0},{17,145},{24,8},{25,153},{64,... | collective-permute-start | bytes 884744 | tf_op jit(solution)/shard_map/ppermute | solution.py:283
  50.4 1.2 %collective-permute-start.13 = (bf16[4,2,144,128]{3,2,1,0:T(8,128)(2,1)S(1)}, bf16[4,2,144,128]{3,2,1,0:T(8,128)(2,1)S(1)}, u32[]{:S(2)}, u32[]{:S(2)}) collective-permute-start(bf16[4,2,144,128]{3,2,1,0:T(8,128)(2,1)S(1)} %get-tuple-element.35), channel_id=1, source_target_pairs={{0,24},{1,193},{8,0},{9,201},{16,8},{17,209},{24,16},{25,217},{64,... | collective-permute-start | bytes 884744 | tf_op jit(solution)/shard_map/ppermute | solution.py:283
  51.6 0.9 %collective-permute-start.12 = (bf16[4,2,144,128]{3,2,1,0:T(8,128)(2,1)S(1)}, bf16[4,2,144,128]{3,2,1,0:T(8,128)(2,1)S(1)}, u32[]{:S(2)}, u32[]{:S(2)}) collective-permute-start(bf16[4,2,144,128]{3,2,1,0:T(8,128)(2,1)S(1)} %get-tuple-element.36), channel_id=1, source_target_pairs={{0,8},{1,65},{8,16},{9,73},{16,24},{17,81},{24,0},{25,89},{64,72},... | collective-permute-start | bytes 884744 | tf_op jit(solution)/shard_map/ppermute | solution.py:283
  52.4 4.4 %collective-permute-done.11 = bf16[4,2,144,128]{3,2,1,0:T(8,128)(2,1)S(1)} collective-permute-done((bf16[4,2,144,128]{3,2,1,0:T(8,128)(2,1)S(1)}, bf16[4,2,144,128]{3,2,1,0:T(8,128)(2,1)S(1)}, u32[]{:S(2)}, u32[]{:S(2)}) %collective-permute-start.11) | collective-permute-done | bytes 294944 | tf_op jit(solution)/shard_map/ppermute | solution.py:283
  56.8 2.1 %collective-permute-done.13 = bf16[4,2,144,128]{3,2,1,0:T(8,128)(2,1)S(1)} collective-permute-done((bf16[4,2,144,128]{3,2,1,0:T(8,128)(2,1)S(1)}, bf16[4,2,144,128]{3,2,1,0:T(8,128)(2,1)S(1)}, u32[]{:S(2)}, u32[]{:S(2)}) %collective-permute-start.13) | collective-permute-done | bytes 294944 | tf_op jit(solution)/shard_map/ppermute | solution.py:283
  58.9 1.0 %collective-permute-done.12 = bf16[4,2,144,128]{3,2,1,0:T(8,128)(2,1)S(1)} collective-permute-done((bf16[4,2,144,128]{3,2,1,0:T(8,128)(2,1)S(1)}, bf16[4,2,144,128]{3,2,1,0:T(8,128)(2,1)S(1)}, u32[]{:S(2)}, u32[]{:S(2)}) %collective-permute-start.12) | collective-permute-done | bytes 294944 | tf_op jit(solution)/shard_map/ppermute | solution.py:283
  59.9 0.2 fusion.7
  60.2 1.1 %collective-permute-start.14 = (bf16[2,144,128]{2,1,0:T(8,128)(2,1)S(1)}, bf16[2,144,128]{2,1,0:T(8,128)(2,1)S(1)}, u32[]{:S(2)}, u32[]{:S(2)}) collective-permute-start(bf16[2,144,128]{2,1,0:T(8,128)(2,1)S(1)} %get-tuple-element.37), channel_id=1, source_target_pairs={{0,128},{1,17},{8,136},{9,25},{16,144},{17,1},{24,152},{25,9},{64,... | collective-permute-start | bytes 221192 | tf_op jit(solution)/shard_map/ppermute | solution.py:283
  61.3 0.2 collective-permute-start.16
  61.5 1.8 %collective-permute-start.15 = (bf16[2,144,128]{2,1,0:T(8,128)(2,1)S(1)}, bf16[2,144,128]{2,1,0:T(8,128)(2,1)S(1)}, u32[]{:S(2)}, u32[]{:S(2)}) collective-permute-start(bf16[2,144,128]{2,1,0:T(8,128)(2,1)S(1)} %get-tuple-element.39), channel_id=1, source_target_pairs={{0,64},{1,9},{8,72},{9,17},{16,80},{17,25},{24,88},{25,1},{64,128}... | collective-permute-start | bytes 221192 | tf_op jit(solution)/shard_map/ppermute | solution.py:283
  63.3 2.8 %collective-permute-done.14 = bf16[2,144,128]{2,1,0:T(8,128)(2,1)S(1)} collective-permute-done((bf16[2,144,128]{2,1,0:T(8,128)(2,1)S(1)}, bf16[2,144,128]{2,1,0:T(8,128)(2,1)S(1)}, u32[]{:S(2)}, u32[]{:S(2)}) %collective-permute-start.14) | collective-permute-done | bytes 73760 | tf_op jit(solution)/shard_map/ppermute | solution.py:283
  66.1 0.0 collective-permute-done.16
  66.1 0.9 %collective-permute-done.15 = bf16[2,144,128]{2,1,0:T(8,128)(2,1)S(1)} collective-permute-done((bf16[2,144,128]{2,1,0:T(8,128)(2,1)S(1)}, bf16[2,144,128]{2,1,0:T(8,128)(2,1)S(1)}, u32[]{:S(2)}, u32[]{:S(2)}) %collective-permute-start.15) | collective-permute-done | bytes 73760 | tf_op jit(solution)/shard_map/ppermute | solution.py:283
  67.1 0.1 reshape.60
  67.2 0.1 reshape.64
  67.3 15.8 %all_to_all.5 = bf16[8,8,576]{2,1,0:T(8,128)(2,1)S(1)} all-to-all(bf16[8,8,576]{2,1,0:T(8,128)(2,1)S(1)} %maximum_maximum_fusion), channel_id=1, replica_groups=mesh['y'=4,'zl'=2,'x'=4,'zh'=4,'c'=2] {'zl','zh'}, dimensions={0} | all-to-all | bytes 147456 | tf_op jit(solution)/shard_map/all_to_all | solution.py:332
  83.1 0.6 convert_reduce_fusion
  (11 shorter events, 0.2 us)
Async XLA Ops:
  0.6 1.0 %copy-start = (bf16[256,576]{0,1:T(8,128)(2,1)S(1)}, bf16[256,576]{0,1:T(8,128)(2,1)}, u32[]{:S(2)}) copy-start(bf16[256,576]{0,1:T(8,128)(2,1)} %param.6) | copy-start | bytes 884740
  0.6 23.1 %copy-start.1 = (bf16[256,4,576]{0,2,1:T(8,128)(2,1)S(1)}, bf16[256,4,576]{0,2,1:T(8,128)(2,1)}, u32[]{:S(2)}) copy-start(bf16[256,4,576]{0,2,1:T(8,128)(2,1)} %param.5) | copy-start | bytes 3538948
  1.9 20.0 %collective-permute-start.1 = (bf16[1152,128]{1,0:T(8,128)(2,1)S(1)}, bf16[1152,128]{1,0:T(8,128)(2,1)S(1)}, u32[]{:S(2)}, u32[]{:S(2)}) collective-permute-start(bf16[1152,128]{1,0:T(8,128)(2,1)S(1)} %pad_maximum_fusion.refs_0_), channel_id=1, source_target_pairs={{0,96},{1,225},{32,64},{33,193},{64,160},{65,33},{96,128},{97,1},{... | collective-permute-start | bytes 884744 | tf_op jit(solution)/shard_map/ppermute | solution.py:271
  3.1 18.8 %collective-permute-start = (bf16[1152,128]{1,0:T(8,128)(2,1)S(1)}, bf16[1152,128]{1,0:T(8,128)(2,1)S(1)}, u32[]{:S(2)}, u32[]{:S(2)}) collective-permute-start(bf16[1152,128]{1,0:T(8,128)(2,1)S(1)} %pad_maximum_fusion.refs_0_), channel_id=1, source_target_pairs={{0,64},{1,193},{32,96},{33,225},{64,128},{65,1},{96,160},{97,33},{... | collective-permute-start | bytes 884744 | tf_op jit(solution)/shard_map/ppermute | solution.py:271
  4.7 13.4 %collective-permute-start.4 = (bf16[576,128]{1,0:T(8,128)(2,1)S(1)}, bf16[576,128]{1,0:T(8,128)(2,1)S(1)}, u32[]{:S(2)}, u32[]{:S(2)}) collective-permute-start(bf16[576,128]{1,0:T(8,128)(2,1)S(1)} %get-tuple-element.40), channel_id=1, source_target_pairs={{0,160},{32,128},{64,224},{96,192},{128,32},{160,0},{192,96},{224,... | collective-permute-start | bytes 442376 | tf_op jit(solution)/shard_map/ppermute | solution.py:288
  7.6 14.3 %collective-permute-start.3 = (bf16[576,128]{1,0:T(8,128)(2,1)S(1)}, bf16[576,128]{1,0:T(8,128)(2,1)S(1)}, u32[]{:S(2)}, u32[]{:S(2)}) collective-permute-start(bf16[576,128]{1,0:T(8,128)(2,1)S(1)} %get-tuple-element.40), channel_id=1, source_target_pairs={{0,128},{32,160},{64,192},{96,224},{128,0},{160,32},{192,64},{224,... | collective-permute-start | bytes 442376 | tf_op jit(solution)/shard_map/ppermute | solution.py:288
  9.6 12.3 %collective-permute-start.2 = (bf16[576,128]{1,0:T(8,128)(2,1)S(1)}, bf16[576,128]{1,0:T(8,128)(2,1)S(1)}, u32[]{:S(2)}, u32[]{:S(2)}) collective-permute-start(bf16[576,128]{1,0:T(8,128)(2,1)S(1)} %get-tuple-element.40), channel_id=1, source_target_pairs={{0,32},{32,0},{1,33},{33,1},{2,34},{34,2},{3,35},{35,3},{4,36},{36... | collective-permute-start | bytes 442376 | tf_op jit(solution)/shard_map/ppermute | solution.py:312
  21.9 0.7 copy-start.2
  21.9 0.7 copy-start.4
  22.5 5.6 %collective-permute-start.5 = (bf16[1152,128]{1,0:T(8,128)(2,1)S(1)}, bf16[1152,128]{1,0:T(8,128)(2,1)}, u32[]{:S(2)}, u32[]{:S(2)}) collective-permute-start(bf16[1152,128]{1,0:T(8,128)(2,1)S(1)} %collective-permute-done.refs_1_), channel_id=1, source_target_pairs={{0,1},{1,0},{2,3},{3,2},{4,5},{5,4},{6,7},{7,6},{8,9},{9,8},{10,11... | collective-permute-start | bytes 884744 | tf_op jit(solution)/shard_map/ppermute | solution.py:261
  22.6 5.6 %collective-permute-start.6 = (bf16[1152,128]{1,0:T(8,128)(2,1)S(1)}, bf16[1152,128]{1,0:T(8,128)(2,1)}, u32[]{:S(2)}, u32[]{:S(2)}) collective-permute-start(bf16[1152,128]{1,0:T(8,128)(2,1)S(1)} %collective-permute-done.1.refs_2_), channel_id=1, source_target_pairs={{0,1},{1,0},{2,3},{3,2},{4,5},{5,4},{6,7},{7,6},{8,9},{9,8},{10,11... | collective-permute-start | bytes 884744 | tf_op jit(solution)/shard_map/ppermute | solution.py:261
  23.1 5.0 %collective-permute-start.7 = (bf16[576,128]{1,0:T(8,128)(2,1)}, bf16[576,128]{1,0:T(8,128)(2,1)S(1)}, u32[]{:S(2)}, u32[]{:S(2)}) collective-permute-start(bf16[576,128]{1,0:T(8,128)(2,1)} %copy-done.4), channel_id=1, source_target_pairs={{0,1},{1,0},{2,3},{3,2},{4,5},{5,4},{6,7},{7,6},{8,9},{9,8},{10,11... | collective-permute-start | bytes 442376 | tf_op jit(solution)/shard_map/ppermute | solution.py:261
  23.2 4.9 %collective-permute-start.8 = (bf16[576,128]{1,0:T(8,128)(2,1)}, bf16[576,128]{1,0:T(8,128)(2,1)S(1)}, u32[]{:S(2)}, u32[]{:S(2)}) collective-permute-start(bf16[576,128]{1,0:T(8,128)(2,1)} %copy-done.2), channel_id=1, source_target_pairs={{0,1},{1,0},{2,3},{3,2},{4,5},{5,4},{6,7},{7,6},{8,9},{9,8},{10,11... | collective-permute-start | bytes 442376 | tf_op jit(solution)/shard_map/ppermute | solution.py:261
  23.7 4.5 %collective-permute-start.9 = (bf16[576,128]{1,0:T(8,128)(2,1)S(1)}, bf16[576,128]{1,0:T(8,128)(2,1)S(1)}, u32[]{:S(2)}, u32[]{:S(2)}) collective-permute-start(bf16[576,128]{1,0:T(8,128)(2,1)S(1)} %collective-permute-done.4.refs_7_), channel_id=1, source_target_pairs={{0,1},{1,0},{2,3},{3,2},{4,5},{5,4},{6,7},{7,6},{8,9},{9,8},{10,11... | collective-permute-start | bytes 442376 | tf_op jit(solution)/shard_map/ppermute | solution.py:261
  23.8 0.7 copy-start.6
  24.4 0.7 copy-start.7
  25.1 3.1 %copy-start.3 = (bf16[576,128]{1,0:T(8,128)(2,1)S(1)}, bf16[576,128]{1,0:T(8,128)(2,1)}, u32[]{:S(2)}) copy-start(bf16[576,128]{1,0:T(8,128)(2,1)} %copy-done.2) | copy-start | bytes 442372
  25.1 3.1 %copy-start.5 = (bf16[576,128]{1,0:T(8,128)(2,1)S(1)}, bf16[576,128]{1,0:T(8,128)(2,1)}, u32[]{:S(2)}) copy-start(bf16[576,128]{1,0:T(8,128)(2,1)} %copy-done.4) | copy-start | bytes 442372
  45.4 2.9 %collective-permute-start.10 = (bf16[4,4,2,144,128]{4,3,2,1,0:T(8,128)(2,1)S(1)}, bf16[4,4,2,144,128]{4,3,2,1,0:T(8,128)(2,1)S(1)}, u32[]{:S(2)}, u32[]{:S(2)}) collective-permute-start(bf16[4,4,2,144,128]{4,3,2,1,0:T(8,128)(2,1)S(1)} %get-tuple-element.31), channel_id=1, source_target_pairs={{0,1},{1,0},{2,3},{3,2},{4,5},{5,4},{6,7},{7,6},{8,9},{9,8},{10,11... | collective-permute-start | bytes 3538952 | tf_op jit(solution)/shard_map/ppermute | solution.py:261
  48.5 8.4 %collective-permute-start.11 = (bf16[4,2,144,128]{3,2,1,0:T(8,128)(2,1)S(1)}, bf16[4,2,144,128]{3,2,1,0:T(8,128)(2,1)S(1)}, u32[]{:S(2)}, u32[]{:S(2)}) collective-permute-start(bf16[4,2,144,128]{3,2,1,0:T(8,128)(2,1)S(1)} %get-tuple-element.34), channel_id=1, source_target_pairs={{0,16},{1,129},{8,24},{9,137},{16,0},{17,145},{24,8},{25,153},{64,... | collective-permute-start | bytes 884744 | tf_op jit(solution)/shard_map/ppermute | solution.py:283
  50.4 8.5 %collective-permute-start.13 = (bf16[4,2,144,128]{3,2,1,0:T(8,128)(2,1)S(1)}, bf16[4,2,144,128]{3,2,1,0:T(8,128)(2,1)S(1)}, u32[]{:S(2)}, u32[]{:S(2)}) collective-permute-start(bf16[4,2,144,128]{3,2,1,0:T(8,128)(2,1)S(1)} %get-tuple-element.35), channel_id=1, source_target_pairs={{0,24},{1,193},{8,0},{9,201},{16,8},{17,209},{24,16},{25,217},{64,... | collective-permute-start | bytes 884744 | tf_op jit(solution)/shard_map/ppermute | solution.py:283
  51.6 8.4 %collective-permute-start.12 = (bf16[4,2,144,128]{3,2,1,0:T(8,128)(2,1)S(1)}, bf16[4,2,144,128]{3,2,1,0:T(8,128)(2,1)S(1)}, u32[]{:S(2)}, u32[]{:S(2)}) collective-permute-start(bf16[4,2,144,128]{3,2,1,0:T(8,128)(2,1)S(1)} %get-tuple-element.36), channel_id=1, source_target_pairs={{0,8},{1,65},{8,16},{9,73},{16,24},{17,81},{24,0},{25,89},{64,72},... | collective-permute-start | bytes 884744 | tf_op jit(solution)/shard_map/ppermute | solution.py:283
  60.2 5.9 %collective-permute-start.14 = (bf16[2,144,128]{2,1,0:T(8,128)(2,1)S(1)}, bf16[2,144,128]{2,1,0:T(8,128)(2,1)S(1)}, u32[]{:S(2)}, u32[]{:S(2)}) collective-permute-start(bf16[2,144,128]{2,1,0:T(8,128)(2,1)S(1)} %get-tuple-element.37), channel_id=1, source_target_pairs={{0,128},{1,17},{8,136},{9,25},{16,144},{17,1},{24,152},{25,9},{64,... | collective-permute-start | bytes 221192 | tf_op jit(solution)/shard_map/ppermute | solution.py:283
  61.3 4.8 %collective-permute-start.16 = (bf16[2,144,128]{2,1,0:T(8,128)(2,1)S(1)}, bf16[2,144,128]{2,1,0:T(8,128)(2,1)S(1)}, u32[]{:S(2)}, u32[]{:S(2)}) collective-permute-start(bf16[2,144,128]{2,1,0:T(8,128)(2,1)S(1)} %get-tuple-element.38), channel_id=1, source_target_pairs={{0,192},{1,25},{8,200},{9,1},{16,208},{17,9},{24,216},{25,17},{64,... | collective-permute-start | bytes 221192 | tf_op jit(solution)/shard_map/ppermute | solution.py:283
  61.5 5.6 %collective-permute-start.15 = (bf16[2,144,128]{2,1,0:T(8,128)(2,1)S(1)}, bf16[2,144,128]{2,1,0:T(8,128)(2,1)S(1)}, u32[]{:S(2)}, u32[]{:S(2)}) collective-permute-start(bf16[2,144,128]{2,1,0:T(8,128)(2,1)S(1)} %get-tuple-element.39), channel_id=1, source_target_pairs={{0,64},{1,9},{8,72},{9,17},{16,80},{17,25},{24,88},{25,1},{64,128}... | collective-permute-start | bytes 221192 | tf_op jit(solution)/shard_map/ppermute | solution.py:283

commit v6 on v5

--- a/solution.py
+++ b/solution.py
@@ -41,15 +41,15 @@
     return lax.dot_general(a, b, (((1,), (1,)), ((), ())), preferred_element_type=F32)
 
 
-def positions(place_ref, query_blocks_ref, key_blocks_ref):
+def positions(place_ref):
     core, y, zl = (place_ref[n] for n in range(3))
     turn = 2 * core
     ahead = [(0 - dy) & 3 for dy in (0, 1 + turn, 1 + turn, 3 - turn, 3 - turn, 0, 2, 2)]
     floors = [zl ^ dz for dz in (0, 0, 1, 0, 1, 1, 0, 1)]
-    mine = query_blocks_ref[y * 2 + zl]
+    mine = place_ref[4 + y * 2 + zl]
     limits = []
     for up, floor in zip(ahead, floors):
-        lag = (mine - key_blocks_ref[((y + up) & 3) * 2 + floor]) * TILE
+        lag = (mine - place_ref[4 + NG + ((y + up) & 3) * 2 + floor]) * TILE
         limits.append((lag - core * 8, lag - (core ^ 1) * 8))
     return ahead, floors, limits
 
@@ -89,9 +89,9 @@
     return e, dot(keys[:, :DL], got), peak, total
 
 
-def first_kernel(place_ref, query_blocks_ref, key_blocks_ref, qt_ref, go_ref, *refs):
+def first_kernel(place_ref, qt_ref, go_ref, *refs):
     e_ref, gp_ref, stat_ref, gl_ref, gr_ref, got_ref, k_s = refs[FIRST:]
-    limits = positions(place_ref, query_blocks_ref, key_blocks_ref)[2]
+    limits = positions(place_ref)[2]
     for slot, pair in enumerate(halves(refs[:FIRST])):
         for b in range(2):
             at = slot * TILE + b * HALF
@@ -114,18 +114,46 @@
             stat_ref[1, h, c : c + 1, :] = total
 
 
-def main_kernel(place_ref, query_blocks_ref, key_blocks_ref, qt_ref, *refs):
+def to_keys(place_ref, half, w_ref, gl_ref, gr_ref, ref):
+    ahead, floors, _ = positions(place_ref)
+    core, x = place_ref[0], place_ref[3]
+    later = core ^ half
+    for c in range(NG // 2):
+        w = w_ref[span(c), :]
+        lat = dot(w, gl_ref[...])
+        wr = jnp.concatenate(
+            [w[:, (2 * h + 1) * TILE : (2 * h + 2) * TILE] for h in range(H_LOC)], axis=1
+        )
+        rope = dot(wr, gr_ref[...])
+        for b in range(2):
+            slot = 2 * c + b
+            for to in range(4):
+                at = b * HALF + to * OWNED
+                right = (to - x) & 3
+                i = jnp.where(later == 0, right, ahead[slot])
+                j = jnp.where(later == 0, ahead[slot], right)
+                for n in range(DL // LANES):
+                    ref[i, j, floors[slot], n * OWNED : (n + 1) * OWNED, :] = lat[
+                        at : at + OWNED, n * LANES : (n + 1) * LANES
+                    ].astype(ref.dtype)
+                both = jnp.concatenate(
+                    [rope[at : at + OWNED // 2], rope[at + OWNED // 2 : at + OWNED]], axis=1
+                )
+                ref[i, j, floors[slot], DL // LANES * OWNED :, :] = both.astype(ref.dtype)
+
+
+def main_kernel(place_ref, qt_ref, *refs):
     k_refs, refs = refs[: 2 * NG - WHOLE], refs[2 * NG - WHOLE :]
     e1_ref, gp1_ref, stat_ref, gl_ref, gr_ref, got_ref = refs[:6]
-    dqt_ref, own_ref, other_ref, kt_s, k_s, e_s, gp_s, w_s = refs[6:]
-    ahead, floors, limits = positions(place_ref, query_blocks_ref, key_blocks_ref)
-    core, x = place_ref[0], place_ref[3]
+    dqt_ref, own_w_ref, other_ref, kt_s, k_s, e_s, gp_s, other_w_s = refs[6:]
+    limits = positions(place_ref)[2]
+    w_refs = (own_w_ref, other_w_s)
     for slot, pair in enumerate(halves(k_refs)):
         for b in range(2):
-            at = slot * TILE + b * HALF
+            at = b * KEYS // 2 + slot * HALF
             kt_s[:, at : at + HALF] = pair[b]
             if slot >= FIRST:
-                at -= FIRST * TILE
+                at = (slot - FIRST) * TILE + b * HALF
                 k_s[at : at + HALF, :] = pair[b].T
     delta = offsets()
     peaks = [[stat_ref[0, h, c : c + 1, :] for c in range(FIRST)] for h in range(H_LOC)]
@@ -138,6 +166,11 @@
             return e1_ref[h, span(c), :], gp1_ref[h, span(c), :]
         return e_s[h, span(c - FIRST), :], gp_s[h, span(c - FIRST), :]
 
+    def keep(h, c, kind, value):
+        at = (2 * h + kind) * TILE
+        for b, ref in enumerate(w_refs):
+            ref[c * HALF : (c + 1) * HALF, at : at + TILE] = value[b * HALF : (b + 1) * HALF]
+
     def settle(h):
         peak = functools.reduce(jnp.maximum, peaks[h])
         shares = [jnp.exp2(p - peak) for p in peaks[h]]
@@ -148,42 +181,21 @@
     def correct(h, c):
         e, gp = load(h, c)
         pb = (e * factors[h][c]).astype(BF)
-        w_s[span(c), h * 2 * TILE : h * 2 * TILE + TILE] = pb
+        keep(h, c, 0, pb)
         corrs[h] = corrs[h] + jnp.sum(pb.astype(F32) * gp, axis=0, keepdims=True)
 
     def differ(h, c):
         e, gp = load(h, c)
         ds = (e * (factors[h][c] * softmax_scale) * (gp - corrs[h])).astype(BF)
-        w_s[span(c), h * 2 * TILE + TILE : (h + 1) * 2 * TILE] = ds
+        keep(h, c, 1, ds)
 
     def to_queries(h):
         for r in range(2):
             rows = slice(r * DK // 2, (r + 1) * DK // 2)
-            out = dot(kt_s[rows, :], w_s[:, h * 2 * TILE + TILE : (h + 1) * 2 * TILE])
+            at = (2 * h + 1) * TILE
+            out = dot(kt_s[rows, : KEYS // 2], own_w_ref[:, at : at + TILE])
+            out = out + dot(kt_s[rows, KEYS // 2 :], other_w_s[:, at : at + TILE])
             dqt_ref[h, rows, :] = out.astype(BF)
-
-    def to_keys(c):
-        w = w_s[span(c), :]
-        lat = dot(w, gl_ref[...])
-        wr = jnp.concatenate(
-            [w[:, (2 * h + 1) * TILE : (2 * h + 2) * TILE] for h in range(H_LOC)], axis=1
-        )
-        rope = dot(wr, gr_ref[...])
-        for b, ref in enumerate((own_ref, other_ref)):
-            later = core ^ b
-            for to in range(4):
-                at = b * HALF + to * OWNED
-                right = (to - x) & 3
-                i = jnp.where(later == 0, right, ahead[c])
-                j = jnp.where(later == 0, ahead[c], right)
-                for n in range(DL // LANES):
-                    ref[i, j, floors[c], n * OWNED : (n + 1) * OWNED, :] = lat[
-                        at : at + OWNED, n * LANES : (n + 1) * LANES
-                    ].astype(ref.dtype)
-                both = jnp.concatenate(
-                    [rope[at : at + OWNED // 2], rope[at + OWNED // 2 : at + OWNED]], axis=1
-                )
-                ref[i, j, floors[c], DL // LANES * OWNED :, :] = both.astype(ref.dtype)
 
     for step in range(H_LOC + 2):
         if 1 <= step <= H_LOC:
@@ -205,15 +217,18 @@
                 differ(step - 2, c)
         if step >= 2:
             to_queries(step - 2)
-    for c in range(NG):
-        to_keys(c)
+    to_keys(place_ref, 1, other_w_s, gl_ref, gr_ref, other_ref)
+
+
+def own_kernel(place_ref, w_ref, gl_ref, gr_ref, own_ref):
+    to_keys(place_ref, 0, w_ref, gl_ref, gr_ref, own_ref)
 
 
 VMEM = pl.BlockSpec(memory_space=pltpu.VMEM)
 SMEM = pl.BlockSpec(memory_space=pltpu.SMEM)
 
 
-def first_part(place, query_blocks, key_blocks, qt, go, k_blocks):
+def first_part(place, qt, go, k_blocks):
     shapes = [
         ((H_LOC, FIRST * TILE, TILE), F32),
         ((H_LOC, FIRST * TILE, TILE), F32),
@@ -224,7 +239,7 @@
     ]
     return pl.pallas_call(
         first_kernel,
-        in_specs=[SMEM] * 3 + [VMEM] * (2 + FIRST),
+        in_specs=[SMEM] + [VMEM] * (2 + FIRST),
         out_specs=[VMEM] * len(shapes),
         out_shape=[jax.ShapeDtypeStruct(*s) for s in shapes],
         scratch_shapes=[pltpu.VMEM((FIRST * TILE, DK), BF)],
@@ -232,18 +247,18 @@
             flops=2 * 1024 * FIRST * TILE * (DK + DL), bytes_accessed=20_000_000, transcendentals=0
         ),
         compiler_params=pltpu.CompilerParams(vmem_limit_bytes=24 * 1024 * 1024),
-    )(place, query_blocks, key_blocks, qt, go, *k_blocks)
-
-
-def main_part(place, query_blocks, key_blocks, qt, k_blocks, early):
+    )(place, qt, go, *k_blocks)
+
+
+def main_part(place, qt, k_blocks, early):
     rest = (NG - FIRST) * TILE
     return pl.pallas_call(
         main_kernel,
-        in_specs=[SMEM] * 3 + [VMEM] * (1 + len(k_blocks) + len(early)),
+        in_specs=[SMEM] + [VMEM] * (1 + len(k_blocks) + len(early)),
         out_specs=[VMEM] * 3,
         out_shape=[
             jax.ShapeDtypeStruct((H_LOC, DK, TILE), BF),
-            jax.ShapeDtypeStruct((4, 4, 2, PACKED, LANES), F32),
+            jax.ShapeDtypeStruct((KEYS // 2, H_LOC * 2 * TILE), BF),
             jax.ShapeDtypeStruct((4, 4, 2, PACKED, LANES), BF),
         ],
         scratch_shapes=[
@@ -251,10 +266,23 @@
             pltpu.VMEM((rest, DK), BF),
             pltpu.VMEM((H_LOC, rest, TILE), F32),
             pltpu.VMEM((H_LOC, rest, TILE), F32),
-            pltpu.VMEM((KEYS, H_LOC * 2 * TILE), BF),
+            pltpu.VMEM((KEYS // 2, H_LOC * 2 * TILE), BF),
         ],
         compiler_params=pltpu.CompilerParams(vmem_limit_bytes=MAIN_VMEM),
-    )(place, query_blocks, key_blocks, qt, *k_blocks, *early)
+    )(place, qt, *k_blocks, *early)
+
+
+def own_part(place, weights, gl, gr):
+    return pl.pallas_call(
+        own_kernel,
+        in_specs=[SMEM] + [VMEM] * 3,
+        out_specs=VMEM,
+        out_shape=jax.ShapeDtypeStruct((4, 4, 2, PACKED, LANES), F32),
+        cost_estimate=pl.CostEstimate(
+            flops=KEYS * H_LOC * 2 * TILE * DK, bytes_accessed=9_000_000, transcendentals=0
+        ),
+        compiler_params=pltpu.CompilerParams(vmem_limit_bytes=16 * 1024 * 1024),
+    )(place, weights, gl, gr)
 
 
 def swap_cores(x):
@@ -314,16 +342,19 @@
         opposite(here[:DK], 1),
     ]
 
+    place = jnp.concatenate([jnp.stack([core, y, zl, x]), query_blocks, key_blocks])
     qt = queries.transpose(1, 2, 0)
     go = grad_output.transpose(1, 0, 2)
-    go, near, slant, *singles = lax.optimization_barrier((go, near, slant, *singles))
+    go, place = lax.optimization_barrier((go, place))
     blocks = [here, near, slant]
-    place = jnp.stack([core, y, zl, x])
-    early = first_part(place, query_blocks, key_blocks, qt, go, blocks)
-    blocks += [swap_cores(near), swap_cores(slant)] + singles + [swap_cores(k) for k in singles]
-    dqt, own, other = main_part(place, query_blocks, key_blocks, qt, blocks, early)
-
+    early = list(first_part(place, qt, go, blocks))
+    blocks += [swap_cores(near), swap_cores(slant)]
+    early[2], *singles = lax.optimization_barrier((early[2], *singles))
+    blocks += singles + [swap_cores(k) for k in singles]
+    dqt, weights, other = main_part(place, qt, blocks, early)
     other = swap_cores(other)
+    own = own_part(place, weights, early[3], early[4])
+
     sums = [own[d] + other[d].astype(F32) for d in range(4)]
     for first in (True, False):
         got = [crossed(sums[d].astype(BF), first, d) for d in (2, 1, 3)]

time: 84.1 us -> 82.8 us (0.985)
  waiting for transfers between devices: 24.5 us -> 19.1 us
  starting transfers between devices: 16.4 us -> 18.4 us
  blocking collectives: 15.8 us -> 16.7 us
    ppermute x2, waiting for transfers between devices: 10.8 us -> 0.01 us  [opposite(): return lax.ppermute(x, ('y', 'zl'), pairs)]
    ppermute x2, waiting for transfers between devices: 0.01 us -> 6.24 us  [onward(): return lax.ppermute(x, ('y', 'zl', 'c'), pairs)]
    ppermute x6, starting transfers between devices: 7.12 us -> 8.89 us  [crossed(): return lax.ppermute(x, ('y', 'x', 'c'), [(n, target(n)) for n in range(32)])]
    ppermute x6, waiting for transfers between devices: 2.49 us -> 1.08 us  [swap_cores(): return lax.ppermute(x, 'c', [(0, 1), (1, 0)])]
    unnamed x17 -> x7, local copies, waits for them, and re-layouts: 4.36 us -> 3.02 us
    concatenate x0 -> x1, local copies, waits for them, and re-layouts: none -> 1.34 us  [shards(): jnp.concatenate([jnp.stack([core, y, zl, x]), query_blocks, key_blocks])]
    all_to_all x1, blocking collectives: 15.8 us -> 16.7 us  [shards(): got = lax.all_to_all(part, ('zl', 'zh'), 0, 0, tiled=True)]
    concatenate x1, other arithmetic: 0.02 us -> 0.93 us  [shards(): here = jnp.concatenate([here[:, :HALF], here[:, HALF:]], axis=0)]
  transfers between devices with their start and end apart: 17 -> 17, of which waited for: 8 -> 10; matrix products, arithmetic and copies ran while one was open for 2% -> 3% of each run, Pallas kernels for 4% -> 8%
where the time goes in v6:
time: 82.8 us; the launch traced here: 82.6 us
  Pallas kernels  20.2 us (24%)
  waiting for transfers between devices  19.1 us (23%)
  starting transfers between devices  18.4 us (22%)
  blocking collectives  16.7 us (20%)
  local copies, waits for them, and re-layouts  5.25 us (6%)
  other arithmetic  1.98 us (2%)
    all_to_all x1, blocking collectives, shards(): got = lax.all_to_all(part, ('zl', 'zh'), 0, 0, tiled=True)  16.7 us
    pallas_call x1, Pallas kernels, main_part(): pl.pallas_call(main_kernel, in_specs=[SMEM] + [VMEM] * (1 + len(k_blocks)...  13.6 us
    ppermute x6, waiting for transfers between devices, crossed(): return lax.ppermute(x, ('y', 'x', 'c'), [(n, target(n)) for n in range(32)])  11.7 us
    ppermute x6, starting transfers between devices, crossed(): return lax.ppermute(x, ('y', 'x', 'c'), [(n, target(n)) for n in range(32)])  8.89 us
    ppermute x2, waiting for transfers between devices, onward(): return lax.ppermute(x, ('y', 'zl', 'c'), pairs)  6.24 us
    ppermute x2, starting transfers between devices, opposite(): return lax.ppermute(x, ('y', 'zl'), pairs)  4.89 us
    pallas_call x1, Pallas kernels, own_part(): pl.pallas_call(own_kernel, in_specs=[SMEM] + [VMEM] * 3, out_specs=VMEM,...  3.58 us
    unnamed x7, local copies, waits for them, and re-layouts  3.02 us
  transfers between devices with their start and end apart: 17, of which 10 were waited for; matrix products, arithmetic and copies ran while one was open for 3% of the time, Pallas kernels for 8%

profile of v6, /device:TPU:32, one launch (start us, length us, event | category | flops | bytes accessed | tf_op | source)
XLA Modules:
  0.0 82.6 jit_solution(12700891429803729949)
XLA Ops:
  0.6 0.0 copy-start
  0.6 0.0 copy-start.1
  0.7 0.9 %copy-done = bf16[256,576]{0,1:T(8,128)(2,1)S(1)} copy-done((bf16[256,576]{0,1:T(8,128)(2,1)S(1)}, bf16[256,576]{0,1:T(8,128)(2,1)}, u32[]{:S(2)}) %copy-start) | copy-done | bytes 294936
  1.6 0.2 fusion
  1.9 0.7 fusion.14
  2.5 0.9 %pad_maximum_fusion.refs_0_ = bf16[1152,128]{1,0:T(8,128)(2,1)S(1)} fusion(bf16[576,128]{1,0:T(8,128)(2,1)S(1)} %get-tuple-element.41, bf16[576,128]{1,0:T(8,128)(2,1)} %get-tuple-element.40), kind=kLoop, calls=%fused_computation.15 | loop fusion | flops 589824 | bytes 589824 | tf_op jit(solution)/shard_map/concatenate | solution.py:335
  3.5 1.2 %collective-permute-start.1 = (bf16[1152,128]{1,0:T(8,128)(2,1)S(1)}, bf16[1152,128]{1,0:T(8,128)(2,1)S(1)}, u32[]{:S(2)}, u32[]{:S(2)}) collective-permute-start(bf16[1152,128]{1,0:T(8,128)(2,1)S(1)} %pad_maximum_fusion.refs_0_), channel_id=1, source_target_pairs={{0,96},{1,225},{32,64},{33,193},{64,160},{65,33},{96,128},{97,1},{... | collective-permute-start | bytes 884744 | tf_op jit(solution)/shard_map/ppermute | solution.py:299
  4.7 1.6 %collective-permute-start = (bf16[1152,128]{1,0:T(8,128)(2,1)S(1)}, bf16[1152,128]{1,0:T(8,128)(2,1)S(1)}, u32[]{:S(2)}, u32[]{:S(2)}) collective-permute-start(bf16[1152,128]{1,0:T(8,128)(2,1)S(1)} %pad_maximum_fusion.refs_0_), channel_id=1, source_target_pairs={{0,64},{1,193},{32,96},{33,225},{64,128},{65,1},{96,160},{97,33},{... | collective-permute-start | bytes 884744 | tf_op jit(solution)/shard_map/ppermute | solution.py:299
  6.2 2.9 %collective-permute-start.6 = (bf16[576,128]{1,0:T(8,128)(2,1)}, bf16[576,128]{1,0:T(8,128)(2,1)S(1)}, u32[]{:S(2)}, u32[]{:S(2)}) collective-permute-start(bf16[576,128]{1,0:T(8,128)(2,1)} %get-tuple-element.40), channel_id=1, source_target_pairs={{0,160},{32,128},{64,224},{96,192},{128,32},{160,0},{192,96},{224,... | collective-permute-start | bytes 442376 | tf_op jit(solution)/shard_map/ppermute | solution.py:316
  9.1 2.0 %collective-permute-start.5 = (bf16[576,128]{1,0:T(8,128)(2,1)}, bf16[576,128]{1,0:T(8,128)(2,1)}, u32[]{:S(2)}, u32[]{:S(2)}) collective-permute-start(bf16[576,128]{1,0:T(8,128)(2,1)} %get-tuple-element.40), channel_id=1, source_target_pairs={{0,128},{32,160},{64,192},{96,224},{128,0},{160,32},{192,64},{224,... | collective-permute-start | bytes 442376 | tf_op jit(solution)/shard_map/ppermute | solution.py:316
  11.1 0.1 collective-permute-start.4
  11.2 1.4 %copy.16 = bf16[256,4,512]{2,0,1:T(8,128)(2,1)S(1)} copy(bf16[256,4,512]{2,1,0:T(4,128)(2,1)} %param.7) | data formatting | bytes 2097152 | tf_op args[2]
  12.7 1.3 %concatenate.17.place_ref = s32[20]{0:T(128)} concatenate(s32[1]{0:T(128)} %bitcast.1, s32[1]{0:T(128)} %bitcast.2, s32[1]{0:T(128)} %bitcast.3, s32[1]{0:T(128)} %bitcast.4, s32[8]{0:T(128)} %param.8, s32[8]{0:T(128)} %param.9), dimensions={0} | concatenate | bytes 160 | tf_op jit(solution)/shard_map/concatenate | solution.py:345
  14.0 1.6 %collective-permute-done.1.refs_2_ = bf16[1152,128]{1,0:T(8,128)(2,1)S(1)} collective-permute-done((bf16[1152,128]{1,0:T(8,128)(2,1)S(1)}, bf16[1152,128]{1,0:T(8,128)(2,1)S(1)}, u32[]{:S(2)}, u32[]{:S(2)}) %collective-permute-start.1) | collective-permute-done | bytes 294944 | tf_op jit(solution)/shard_map/ppermute | solution.py:299
  15.6 0.0 collective-permute-start.3
  15.6 4.7 %collective-permute-done.refs_1_ = bf16[1152,128]{1,0:T(8,128)(2,1)S(1)} collective-permute-done((bf16[1152,128]{1,0:T(8,128)(2,1)S(1)}, bf16[1152,128]{1,0:T(8,128)(2,1)S(1)}, u32[]{:S(2)}, u32[]{:S(2)}) %collective-permute-start) | collective-permute-done | bytes 294944 | tf_op jit(solution)/shard_map/ppermute | solution.py:299
  20.2 0.0 collective-permute-start.2
  20.2 0.0 copy-done.1
  20.2 0.0 copy-start.2
  20.3 0.7 copy-done.2
  20.9 3.0 %shard_map.68 = (f32[4,768,256]{2,1,0:T(8,128)S(1)}, f32[4,768,256]{2,1,0:T(8,128)S(1)}, f32[2,4,8,256]{3,2,1,0:T(8,128)S(1)}, bf16[2048,512]{1,0:T(8,128)(2,1)S...) custom-call(s32[20]{0:T(128)S(1)} %copy-done.2, bf16[4,576,256]{2,1,0:T(8,128)(2,1)S(1)} %bitcast.51, ...), custom_call_target="tpu_custom_call" | custom-call | flops 1711276032 | bytes 20000000 | tf_op jit(solution)/shard_map/pallas_call | solution.py:240
  23.9 0.0 collective-permute-done.6.refs_7_
  24.0 0.0 collective-permute-done.5.refs_6_
  24.0 0.0 collective-permute-done.4.refs_5_
  24.0 0.6 collective-permute-start.7
  24.6 0.1 collective-permute-start.8
  24.7 0.4 collective-permute-start.9
  25.1 0.7 collective-permute-done.7.refs_8_
  25.8 0.4 collective-permute-done.8.refs_9_
  26.2 0.0 collective-permute-done.9.refs_10_
  26.2 0.0 collective-permute-done.3.refs_4_
  26.2 0.0 collective-permute-done.2.refs_3_
  26.2 13.6 %shard_map.69 = (bf16[4,576,256]{2,1,0:T(8,128)(2,1)}, bf16[1024,2048]{1,0:T(8,128)(2,1)S(1)}, bf16[4,4,2,144,128]{4,3,2,1,0:T(8,128)(2,1)S(1)}) custom-call(s32[20]{0:T(128)S(1)} %copy-done.2, bf16[4,576,256]{2,1,0:T(8,128)(2,1)S(1)} %bitcast.52, bf16[1152,128]{1,0:T(8,128)(2,1)S(1)} %pad_maximum_fusion.refs_0_, ...), custom_call_target="tpu_custom_call" | custom-call | tf_op jit(solution)/shard_map/pallas_call | solution.py:255
  39.8 0.6 collective-permute-start.10
  40.4 3.6 %shard_map.70 = f32[4,4,2,144,128]{4,3,2,1,0:T(8,128)S(1)} custom-call(s32[20]{0:T(128)S(1)} %copy-done.2, bf16[1024,2048]{1,0:T(8,128)(2,1)S(1)} %get-tuple-element.30.w_ref, bf16[2048,512]{1,0:T(8,128)(2,1)S(1)} %get-tuple-element.26.refs_14_.gl_ref, bf16[1024,64]{1,0:T(8,128)(2,1)S(1)} %get-tuple-element.27.refs_15_.gr_ref), custom_call_target="tpu_custom_call" | custom-call | flops 2415919104 | bytes 9000000 | tf_op jit(solution)/shard_map/pallas_call | solution.py:276
  43.9 0.0 collective-permute-done.10
  43.9 0.2 fusion.6
  44.1 2.9 %collective-permute-start.11 = (bf16[4,2,144,128]{3,2,1,0:T(8,128)(2,1)S(1)}, bf16[4,2,144,128]{3,2,1,0:T(8,128)(2,1)S(1)}, u32[]{:S(2)}, u32[]{:S(2)}) collective-permute-start(bf16[4,2,144,128]{3,2,1,0:T(8,128)(2,1)S(1)} %get-tuple-element.34), channel_id=1, source_target_pairs={{0,16},{1,129},{8,24},{9,137},{16,0},{17,145},{24,8},{25,153},{64,... | collective-permute-start | bytes 884744 | tf_op jit(solution)/shard_map/ppermute | solution.py:311
  47.0 1.1 %collective-permute-start.13 = (bf16[4,2,144,128]{3,2,1,0:T(8,128)(2,1)S(1)}, bf16[4,2,144,128]{3,2,1,0:T(8,128)(2,1)S(1)}, u32[]{:S(2)}, u32[]{:S(2)}) collective-permute-start(bf16[4,2,144,128]{3,2,1,0:T(8,128)(2,1)S(1)} %get-tuple-element.35), channel_id=1, source_target_pairs={{0,24},{1,193},{8,0},{9,201},{16,8},{17,209},{24,16},{25,217},{64,... | collective-permute-start | bytes 884744 | tf_op jit(solution)/shard_map/ppermute | solution.py:311
  48.1 0.9 %collective-permute-start.12 = (bf16[4,2,144,128]{3,2,1,0:T(8,128)(2,1)S(1)}, bf16[4,2,144,128]{3,2,1,0:T(8,128)(2,1)S(1)}, u32[]{:S(2)}, u32[]{:S(2)}) collective-permute-start(bf16[4,2,144,128]{3,2,1,0:T(8,128)(2,1)S(1)} %get-tuple-element.36), channel_id=1, source_target_pairs={{0,8},{1,65},{8,16},{9,73},{16,24},{17,81},{24,0},{25,89},{64,72},... | collective-permute-start | bytes 884744 | tf_op jit(solution)/shard_map/ppermute | solution.py:311
  49.0 3.4 %collective-permute-done.11 = bf16[4,2,144,128]{3,2,1,0:T(8,128)(2,1)S(1)} collective-permute-done((bf16[4,2,144,128]{3,2,1,0:T(8,128)(2,1)S(1)}, bf16[4,2,144,128]{3,2,1,0:T(8,128)(2,1)S(1)}, u32[]{:S(2)}, u32[]{:S(2)}) %collective-permute-start.11) | collective-permute-done | bytes 294944 | tf_op jit(solution)/shard_map/ppermute | solution.py:311
  52.4 3.0 %collective-permute-done.13 = bf16[4,2,144,128]{3,2,1,0:T(8,128)(2,1)S(1)} collective-permute-done((bf16[4,2,144,128]{3,2,1,0:T(8,128)(2,1)S(1)}, bf16[4,2,144,128]{3,2,1,0:T(8,128)(2,1)S(1)}, u32[]{:S(2)}, u32[]{:S(2)}) %collective-permute-start.13) | collective-permute-done | bytes 294944 | tf_op jit(solution)/shard_map/ppermute | solution.py:311
  55.5 0.6 collective-permute-done.12
  56.1 0.2 fusion.12
  56.3 2.0 %collective-permute-start.14 = (bf16[2,144,128]{2,1,0:T(8,128)(2,1)S(1)}, bf16[2,144,128]{2,1,0:T(8,128)(2,1)S(1)}, u32[]{:S(2)}, u32[]{:S(2)}) collective-permute-start(bf16[2,144,128]{2,1,0:T(8,128)(2,1)S(1)} %get-tuple-element.37), channel_id=1, source_target_pairs={{0,128},{1,17},{8,136},{9,25},{16,144},{17,1},{24,152},{25,9},{64,... | collective-permute-start | bytes 221192 | tf_op jit(solution)/shard_map/ppermute | solution.py:311
  58.3 1.2 %collective-permute-start.16 = (bf16[2,144,128]{2,1,0:T(8,128)(2,1)S(1)}, bf16[2,144,128]{2,1,0:T(8,128)(2,1)S(1)}, u32[]{:S(2)}, u32[]{:S(2)}) collective-permute-start(bf16[2,144,128]{2,1,0:T(8,128)(2,1)S(1)} %get-tuple-element.38), channel_id=1, source_target_pairs={{0,192},{1,25},{8,200},{9,1},{16,208},{17,9},{24,216},{25,17},{64,... | collective-permute-start | bytes 221192 | tf_op jit(solution)/shard_map/ppermute | solution.py:311
  59.4 0.9 %collective-permute-start.15 = (bf16[2,144,128]{2,1,0:T(8,128)(2,1)S(1)}, bf16[2,144,128]{2,1,0:T(8,128)(2,1)S(1)}, u32[]{:S(2)}, u32[]{:S(2)}) collective-permute-start(bf16[2,144,128]{2,1,0:T(8,128)(2,1)S(1)} %get-tuple-element.39), channel_id=1, source_target_pairs={{0,64},{1,9},{8,72},{9,17},{16,80},{17,25},{24,88},{25,1},{64,128}... | collective-permute-start | bytes 221192 | tf_op jit(solution)/shard_map/ppermute | solution.py:311
  60.3 1.9 %collective-permute-done.14 = bf16[2,144,128]{2,1,0:T(8,128)(2,1)S(1)} collective-permute-done((bf16[2,144,128]{2,1,0:T(8,128)(2,1)S(1)}, bf16[2,144,128]{2,1,0:T(8,128)(2,1)S(1)}, u32[]{:S(2)}, u32[]{:S(2)}) %collective-permute-start.14) | collective-permute-done | bytes 73760 | tf_op jit(solution)/shard_map/ppermute | solution.py:311
  62.2 0.6 collective-permute-done.16
  62.8 2.2 %collective-permute-done.15 = bf16[2,144,128]{2,1,0:T(8,128)(2,1)S(1)} collective-permute-done((bf16[2,144,128]{2,1,0:T(8,128)(2,1)S(1)}, bf16[2,144,128]{2,1,0:T(8,128)(2,1)S(1)}, u32[]{:S(2)}, u32[]{:S(2)}) %collective-permute-start.15) | collective-permute-done | bytes 73760 | tf_op jit(solution)/shard_map/ppermute | solution.py:311
  65.1 0.1 reshape.60
  65.1 0.1 reshape.64
  65.3 16.7 %all_to_all.5 = bf16[8,8,576]{2,1,0:T(8,128)(2,1)S(1)} all-to-all(bf16[8,8,576]{2,1,0:T(8,128)(2,1)S(1)} %maximum_maximum_fusion), channel_id=1, replica_groups=mesh['y'=4,'zl'=2,'x'=4,'zh'=4,'c'=2] {'zl','zh'}, dimensions={0} | all-to-all | bytes 147456 | tf_op jit(solution)/shard_map/all_to_all | solution.py:363
  82.0 0.6 convert_reduce_fusion
  (9 shorter events, 0.1 us)
Async XLA Ops:
  0.6 1.0 %copy-start = (bf16[256,576]{0,1:T(8,128)(2,1)S(1)}, bf16[256,576]{0,1:T(8,128)(2,1)}, u32[]{:S(2)}) copy-start(bf16[256,576]{0,1:T(8,128)(2,1)} %param.6) | copy-start | bytes 884740
  0.6 19.6 %copy-start.1 = (bf16[256,4,576]{0,2,1:T(8,128)(2,1)S(1)}, bf16[256,4,576]{0,2,1:T(8,128)(2,1)}, u32[]{:S(2)}) copy-start(bf16[256,4,576]{0,2,1:T(8,128)(2,1)} %param.5) | copy-start | bytes 3538948
  3.5 12.1 %collective-permute-start.1 = (bf16[1152,128]{1,0:T(8,128)(2,1)S(1)}, bf16[1152,128]{1,0:T(8,128)(2,1)S(1)}, u32[]{:S(2)}, u32[]{:S(2)}) collective-permute-start(bf16[1152,128]{1,0:T(8,128)(2,1)S(1)} %pad_maximum_fusion.refs_0_), channel_id=1, source_target_pairs={{0,96},{1,225},{32,64},{33,193},{64,160},{65,33},{96,128},{97,1},{... | collective-permute-start | bytes 884744 | tf_op jit(solution)/shard_map/ppermute | solution.py:299
  4.7 15.6 %collective-permute-start = (bf16[1152,128]{1,0:T(8,128)(2,1)S(1)}, bf16[1152,128]{1,0:T(8,128)(2,1)S(1)}, u32[]{:S(2)}, u32[]{:S(2)}) collective-permute-start(bf16[1152,128]{1,0:T(8,128)(2,1)S(1)} %pad_maximum_fusion.refs_0_), channel_id=1, source_target_pairs={{0,64},{1,193},{32,96},{33,225},{64,128},{65,1},{96,160},{97,33},{... | collective-permute-start | bytes 884744 | tf_op jit(solution)/shard_map/ppermute | solution.py:299
  6.2 17.7 %collective-permute-start.6 = (bf16[576,128]{1,0:T(8,128)(2,1)}, bf16[576,128]{1,0:T(8,128)(2,1)S(1)}, u32[]{:S(2)}, u32[]{:S(2)}) collective-permute-start(bf16[576,128]{1,0:T(8,128)(2,1)} %get-tuple-element.40), channel_id=1, source_target_pairs={{0,160},{32,128},{64,224},{96,192},{128,32},{160,0},{192,96},{224,... | collective-permute-start | bytes 442376 | tf_op jit(solution)/shard_map/ppermute | solution.py:316
  9.1 14.8 %collective-permute-start.5 = (bf16[576,128]{1,0:T(8,128)(2,1)}, bf16[576,128]{1,0:T(8,128)(2,1)}, u32[]{:S(2)}, u32[]{:S(2)}) collective-permute-start(bf16[576,128]{1,0:T(8,128)(2,1)} %get-tuple-element.40), channel_id=1, source_target_pairs={{0,128},{32,160},{64,192},{96,224},{128,0},{160,32},{192,64},{224,... | collective-permute-start | bytes 442376 | tf_op jit(solution)/shard_map/ppermute | solution.py:316
  11.1 12.8 %collective-permute-start.4 = (bf16[576,128]{1,0:T(8,128)(2,1)}, bf16[576,128]{1,0:T(8,128)(2,1)}, u32[]{:S(2)}, u32[]{:S(2)}) collective-permute-start(bf16[576,128]{1,0:T(8,128)(2,1)} %get-tuple-element.40), channel_id=1, source_target_pairs={{0,32},{32,0},{1,33},{33,1},{2,34},{34,2},{3,35},{35,3},{4,36},{36... | collective-permute-start | bytes 442376 | tf_op jit(solution)/shard_map/ppermute | solution.py:340
  15.6 10.6 %collective-permute-start.3 = (bf16[1152,128]{1,0:T(8,128)(2,1)S(1)}, bf16[1152,128]{1,0:T(8,128)(2,1)S(1)}, u32[]{:S(2)}, u32[]{:S(2)}) collective-permute-start(bf16[1152,128]{1,0:T(8,128)(2,1)S(1)} %collective-permute-done.1.refs_2_), channel_id=1, source_target_pairs={{0,1},{1,0},{2,3},{3,2},{4,5},{5,4},{6,7},{7,6},{8,9},{9,8},{10,11... | collective-permute-start | bytes 884744 | tf_op jit(solution)/shard_map/ppermute | solution.py:289
  20.2 5.9 %collective-permute-start.2 = (bf16[1152,128]{1,0:T(8,128)(2,1)S(1)}, bf16[1152,128]{1,0:T(8,128)(2,1)S(1)}, u32[]{:S(2)}, u32[]{:S(2)}) collective-permute-start(bf16[1152,128]{1,0:T(8,128)(2,1)S(1)} %collective-permute-done.refs_1_), channel_id=1, source_target_pairs={{0,1},{1,0},{2,3},{3,2},{4,5},{5,4},{6,7},{7,6},{8,9},{9,8},{10,11... | collective-permute-start | bytes 884744 | tf_op jit(solution)/shard_map/ppermute | solution.py:289
  20.2 0.7 copy-start.2
  24.0 1.8 %collective-permute-start.7 = (bf16[576,128]{1,0:T(8,128)(2,1)}, bf16[576,128]{1,0:T(8,128)(2,1)S(1)}, u32[]{:S(2)}, u32[]{:S(2)}) collective-permute-start(bf16[576,128]{1,0:T(8,128)(2,1)} %collective-permute-done.4.refs_5_), channel_id=1, source_target_pairs={{0,1},{1,0},{2,3},{3,2},{4,5},{5,4},{6,7},{7,6},{8,9},{9,8},{10,11... | collective-permute-start | bytes 442376 | tf_op jit(solution)/shard_map/ppermute | solution.py:289
  24.6 1.6 %collective-permute-start.8 = (bf16[576,128]{1,0:T(8,128)(2,1)}, bf16[576,128]{1,0:T(8,128)(2,1)S(1)}, u32[]{:S(2)}, u32[]{:S(2)}) collective-permute-start(bf16[576,128]{1,0:T(8,128)(2,1)} %collective-permute-done.5.refs_6_), channel_id=1, source_target_pairs={{0,1},{1,0},{2,3},{3,2},{4,5},{5,4},{6,7},{7,6},{8,9},{9,8},{10,11... | collective-permute-start | bytes 442376 | tf_op jit(solution)/shard_map/ppermute | solution.py:289
  24.7 1.5 %collective-permute-start.9 = (bf16[576,128]{1,0:T(8,128)(2,1)S(1)}, bf16[576,128]{1,0:T(8,128)(2,1)S(1)}, u32[]{:S(2)}, u32[]{:S(2)}) collective-permute-start(bf16[576,128]{1,0:T(8,128)(2,1)S(1)} %collective-permute-done.6.refs_7_), channel_id=1, source_target_pairs={{0,1},{1,0},{2,3},{3,2},{4,5},{5,4},{6,7},{7,6},{8,9},{9,8},{10,11... | collective-permute-start | bytes 442376 | tf_op jit(solution)/shard_map/ppermute | solution.py:289
  39.8 4.2 %collective-permute-start.10 = (bf16[4,4,2,144,128]{4,3,2,1,0:T(8,128)(2,1)S(1)}, bf16[4,4,2,144,128]{4,3,2,1,0:T(8,128)(2,1)S(1)}, u32[]{:S(2)}, u32[]{:S(2)}) collective-permute-start(bf16[4,4,2,144,128]{4,3,2,1,0:T(8,128)(2,1)S(1)} %get-tuple-element.31), channel_id=1, source_target_pairs={{0,1},{1,0},{2,3},{3,2},{4,5},{5,4},{6,7},{7,6},{8,9},{9,8},{10,11... | collective-permute-start | bytes 3538952 | tf_op jit(solution)/shard_map/ppermute | solution.py:289
  44.1 8.3 %collective-permute-start.11 = (bf16[4,2,144,128]{3,2,1,0:T(8,128)(2,1)S(1)}, bf16[4,2,144,128]{3,2,1,0:T(8,128)(2,1)S(1)}, u32[]{:S(2)}, u32[]{:S(2)}) collective-permute-start(bf16[4,2,144,128]{3,2,1,0:T(8,128)(2,1)S(1)} %get-tuple-element.34), channel_id=1, source_target_pairs={{0,16},{1,129},{8,24},{9,137},{16,0},{17,145},{24,8},{25,153},{64,... | collective-permute-start | bytes 884744 | tf_op jit(solution)/shard_map/ppermute | solution.py:311
  47.0 8.5 %collective-permute-start.13 = (bf16[4,2,144,128]{3,2,1,0:T(8,128)(2,1)S(1)}, bf16[4,2,144,128]{3,2,1,0:T(8,128)(2,1)S(1)}, u32[]{:S(2)}, u32[]{:S(2)}) collective-permute-start(bf16[4,2,144,128]{3,2,1,0:T(8,128)(2,1)S(1)} %get-tuple-element.35), channel_id=1, source_target_pairs={{0,24},{1,193},{8,0},{9,201},{16,8},{17,209},{24,16},{25,217},{64,... | collective-permute-start | bytes 884744 | tf_op jit(solution)/shard_map/ppermute | solution.py:311
  48.1 7.9 %collective-permute-start.12 = (bf16[4,2,144,128]{3,2,1,0:T(8,128)(2,1)S(1)}, bf16[4,2,144,128]{3,2,1,0:T(8,128)(2,1)S(1)}, u32[]{:S(2)}, u32[]{:S(2)}) collective-permute-start(bf16[4,2,144,128]{3,2,1,0:T(8,128)(2,1)S(1)} %get-tuple-element.36), channel_id=1, source_target_pairs={{0,8},{1,65},{8,16},{9,73},{16,24},{17,81},{24,0},{25,89},{64,72},... | collective-permute-start | bytes 884744 | tf_op jit(solution)/shard_map/ppermute | solution.py:311
  56.3 5.9 %collective-permute-start.14 = (bf16[2,144,128]{2,1,0:T(8,128)(2,1)S(1)}, bf16[2,144,128]{2,1,0:T(8,128)(2,1)S(1)}, u32[]{:S(2)}, u32[]{:S(2)}) collective-permute-start(bf16[2,144,128]{2,1,0:T(8,128)(2,1)S(1)} %get-tuple-element.37), channel_id=1, source_target_pairs={{0,128},{1,17},{8,136},{9,25},{16,144},{17,1},{24,152},{25,9},{64,... | collective-permute-start | bytes 221192 | tf_op jit(solution)/shard_map/ppermute | solution.py:311
  58.3 4.6 %collective-permute-start.16 = (bf16[2,144,128]{2,1,0:T(8,128)(2,1)S(1)}, bf16[2,144,128]{2,1,0:T(8,128)(2,1)S(1)}, u32[]{:S(2)}, u32[]{:S(2)}) collective-permute-start(bf16[2,144,128]{2,1,0:T(8,128)(2,1)S(1)} %get-tuple-element.38), channel_id=1, source_target_pairs={{0,192},{1,25},{8,200},{9,1},{16,208},{17,9},{24,216},{25,17},{64,... | collective-permute-start | bytes 221192 | tf_op jit(solution)/shard_map/ppermute | solution.py:311
  59.4 5.6 %collective-permute-start.15 = (bf16[2,144,128]{2,1,0:T(8,128)(2,1)S(1)}, bf16[2,144,128]{2,1,0:T(8,128)(2,1)S(1)}, u32[]{:S(2)}, u32[]{:S(2)}) collective-permute-start(bf16[2,144,128]{2,1,0:T(8,128)(2,1)S(1)} %get-tuple-element.39), channel_id=1, source_target_pairs={{0,64},{1,9},{8,72},{9,17},{16,80},{17,25},{24,88},{25,1},{64,128}... | collective-permute-start | bytes 221192 | tf_op jit(solution)/shard_map/ppermute | solution.py:311

commit v7 on v6

--- a/solution.py
+++ b/solution.py
@@ -22,7 +22,7 @@
 LANES = 128
 OWNED = 32
 PACKED = OWNED * DK // LANES
-MAIN_VMEM = 28 * 1024 * 1024
+MAIN_VMEM = 23 * 1024 * 1024
 FIRST = 3
 WHOLE = 5
 SWAPPED = (3, 4)
@@ -41,17 +41,23 @@
     return lax.dot_general(a, b, (((1,), (1,)), ((), ())), preferred_element_type=F32)
 
 
-def positions(place_ref):
-    core, y, zl = (place_ref[n] for n in range(3))
+def directions(place_ref):
+    core, zl = place_ref[0], place_ref[2]
     turn = 2 * core
     ahead = [(0 - dy) & 3 for dy in (0, 1 + turn, 1 + turn, 3 - turn, 3 - turn, 0, 2, 2)]
     floors = [zl ^ dz for dz in (0, 0, 1, 0, 1, 1, 0, 1)]
-    mine = place_ref[4 + y * 2 + zl]
+    return ahead, floors
+
+
+def positions(place_ref, query_blocks_ref, key_blocks_ref):
+    core, y, zl = (place_ref[n] for n in range(3))
+    ahead, floors = directions(place_ref)
+    mine = query_blocks_ref[y * 2 + zl]
     limits = []
     for up, floor in zip(ahead, floors):
-        lag = (mine - place_ref[4 + NG + ((y + up) & 3) * 2 + floor]) * TILE
+        lag = (mine - key_blocks_ref[((y + up) & 3) * 2 + floor]) * TILE
         limits.append((lag - core * 8, lag - (core ^ 1) * 8))
-    return ahead, floors, limits
+    return limits
 
 
 def halves(refs):
@@ -89,9 +95,9 @@
     return e, dot(keys[:, :DL], got), peak, total
 
 
-def first_kernel(place_ref, qt_ref, go_ref, *refs):
+def first_kernel(place_ref, query_blocks_ref, key_blocks_ref, qt_ref, go_ref, *refs):
     e_ref, gp_ref, stat_ref, gl_ref, gr_ref, got_ref, k_s = refs[FIRST:]
-    limits = positions(place_ref)[2]
+    limits = positions(place_ref, query_blocks_ref, key_blocks_ref)
     for slot, pair in enumerate(halves(refs[:FIRST])):
         for b in range(2):
             at = slot * TILE + b * HALF
@@ -115,7 +121,7 @@
 
 
 def to_keys(place_ref, half, w_ref, gl_ref, gr_ref, ref):
-    ahead, floors, _ = positions(place_ref)
+    ahead, floors = directions(place_ref)
     core, x = place_ref[0], place_ref[3]
     later = core ^ half
     for c in range(NG // 2):
@@ -142,11 +148,11 @@
                 ref[i, j, floors[slot], DL // LANES * OWNED :, :] = both.astype(ref.dtype)
 
 
-def main_kernel(place_ref, qt_ref, *refs):
+def main_kernel(place_ref, query_blocks_ref, key_blocks_ref, qt_ref, *refs):
     k_refs, refs = refs[: 2 * NG - WHOLE], refs[2 * NG - WHOLE :]
     e1_ref, gp1_ref, stat_ref, gl_ref, gr_ref, got_ref = refs[:6]
     dqt_ref, own_w_ref, other_ref, kt_s, k_s, e_s, gp_s, other_w_s = refs[6:]
-    limits = positions(place_ref)[2]
+    limits = positions(place_ref, query_blocks_ref, key_blocks_ref)
     w_refs = (own_w_ref, other_w_s)
     for slot, pair in enumerate(halves(k_refs)):
         for b in range(2):
@@ -228,7 +234,7 @@
 SMEM = pl.BlockSpec(memory_space=pltpu.SMEM)
 
 
-def first_part(place, qt, go, k_blocks):
+def first_part(place, query_blocks, key_blocks, qt, go, k_blocks):
     shapes = [
         ((H_LOC, FIRST * TILE, TILE), F32),
         ((H_LOC, FIRST * TILE, TILE), F32),
@@ -239,22 +245,22 @@
     ]
     return pl.pallas_call(
         first_kernel,
-        in_specs=[SMEM] + [VMEM] * (2 + FIRST),
+        in_specs=[SMEM] * 3 + [VMEM] * (2 + FIRST),
         out_specs=[VMEM] * len(shapes),
         out_shape=[jax.ShapeDtypeStruct(*s) for s in shapes],
         scratch_shapes=[pltpu.VMEM((FIRST * TILE, DK), BF)],
         cost_estimate=pl.CostEstimate(
             flops=2 * 1024 * FIRST * TILE * (DK + DL), bytes_accessed=20_000_000, transcendentals=0
         ),
-        compiler_params=pltpu.CompilerParams(vmem_limit_bytes=24 * 1024 * 1024),
-    )(place, qt, go, *k_blocks)
-
-
-def main_part(place, qt, k_blocks, early):
+        compiler_params=pltpu.CompilerParams(vmem_limit_bytes=16 * 1024 * 1024),
+    )(place, query_blocks, key_blocks, qt, go, *k_blocks)
+
+
+def main_part(place, query_blocks, key_blocks, qt, k_blocks, early):
     rest = (NG - FIRST) * TILE
     return pl.pallas_call(
         main_kernel,
-        in_specs=[SMEM] + [VMEM] * (1 + len(k_blocks) + len(early)),
+        in_specs=[SMEM] * 3 + [VMEM] * (1 + len(k_blocks) + len(early)),
         out_specs=[VMEM] * 3,
         out_shape=[
             jax.ShapeDtypeStruct((H_LOC, DK, TILE), BF),
@@ -269,7 +275,7 @@
             pltpu.VMEM((KEYS // 2, H_LOC * 2 * TILE), BF),
         ],
         compiler_params=pltpu.CompilerParams(vmem_limit_bytes=MAIN_VMEM),
-    )(place, qt, *k_blocks, *early)
+    )(place, query_blocks, key_blocks, qt, *k_blocks, *early)
 
 
 def own_part(place, weights, gl, gr):
@@ -281,7 +287,7 @@
         cost_estimate=pl.CostEstimate(
             flops=KEYS * H_LOC * 2 * TILE * DK, bytes_accessed=9_000_000, transcendentals=0
         ),
-        compiler_params=pltpu.CompilerParams(vmem_limit_bytes=16 * 1024 * 1024),
+        compiler_params=pltpu.CompilerParams(vmem_limit_bytes=12 * 1024 * 1024),
     )(place, weights, gl, gr)
 
 
@@ -309,11 +315,6 @@
         return (y * 4 + x) * 2 + c
 
     return lax.ppermute(x, ("y", "x", "c"), [(n, target(n)) for n in range(32)])
-
-
-def opposite(x, dz):
-    pairs = [(y * 2 + z, (y + 2) % 4 * 2 + (z ^ dz)) for y in range(4) for z in range(2)]
-    return lax.ppermute(x, ("y", "zl"), pairs)
 
 
 def unpack(x):
@@ -336,22 +337,18 @@
 
     near = onward(here, 0)
     slant = onward(here, 1)
-    singles = [
-        lax.ppermute(here[:DK], "zl", [(0, 1), (1, 0)]),
-        opposite(here[:DK], 0),
-        opposite(here[:DK], 1),
-    ]
-
-    place = jnp.concatenate([jnp.stack([core, y, zl, x]), query_blocks, key_blocks])
+    beside = lax.ppermute(here[:DK], "zl", [(0, 1), (1, 0)])
+
+    place = jnp.stack([core, y, zl, x])
     qt = queries.transpose(1, 2, 0)
     go = grad_output.transpose(1, 0, 2)
-    go, place = lax.optimization_barrier((go, place))
-    blocks = [here, near, slant]
-    early = list(first_part(place, qt, go, blocks))
-    blocks += [swap_cores(near), swap_cores(slant)]
+    go, near, slant = lax.optimization_barrier((go, near, slant))
+    singles = [beside, onward(near[:DK], 0), onward(slant[:DK], 0)]
+    swapped = [swap_cores(near), swap_cores(slant)]
+    early = list(first_part(place, query_blocks, key_blocks, qt, go, [here, near, slant]))
     early[2], *singles = lax.optimization_barrier((early[2], *singles))
-    blocks += singles + [swap_cores(k) for k in singles]
-    dqt, weights, other = main_part(place, qt, blocks, early)
+    blocks = [here, near, slant] + swapped + singles + [swap_cores(k) for k in singles]
+    dqt, weights, other = main_part(place, query_blocks, key_blocks, qt, blocks, early)
     other = swap_cores(other)
     own = own_part(place, weights, early[3], early[4])
 

time: 82.8 us -> 79 us (0.954)
  waiting for transfers between devices: 19.1 us -> 22.3 us
  local copies, waits for them, and re-layouts: 5.25 us -> 2.63 us
  starting transfers between devices: 18.4 us -> 15.9 us
  other arithmetic: 1.98 us -> 1.15 us
    ppermute x3 -> x1, starting transfers between devices: 4.99 us -> 1.92 us  [shards(): beside = lax.ppermute(here[:DK], 'zl', [(0, 1), (1, 0)])]
    ppermute x2 -> x4, waiting for transfers between devices: 6.24 us -> 9.2 us  [onward(): return lax.ppermute(x, ('y', 'zl', 'c'), pairs)]
    ppermute x2 -> x4, starting transfers between devices: 2.77 us -> 4.48 us  [onward(): return lax.ppermute(x, ('y', 'zl', 'c'), pairs)]
    concatenate x1 -> x0, local copies, waits for them, and re-layouts: 1.34 us -> none  [shards(): jnp.concatenate([jnp.stack([core, y, zl, x]), query_blocks, key_blocks])]
    ppermute x6, starting transfers between devices: 8.89 us -> 7.8 us  [crossed(): return lax.ppermute(x, ('y', 'x', 'c'), [(n, target(n)) for n in range(32)])]
    concatenate x1, other arithmetic: 0.93 us -> 0.02 us  [shards(): here = jnp.concatenate([here[:, :HALF], here[:, HALF:]], axis=0)]
    unnamed x7 -> x9, local copies, waits for them, and re-layouts: 3.02 us -> 2.38 us
  transfers between devices with their start and end apart: 17 -> 17, of which waited for: 10 -> 12; matrix products, arithmetic and copies ran while one was open for 3% -> 2% of each run, Pallas kernels for 8% -> 8%
where the time goes in v7:
time: 79 us; the launch traced here: 78.8 us
  waiting for transfers between devices  22.3 us (28%)
  Pallas kernels  19.9 us (25%)
  starting transfers between devices  15.9 us (20%)
  blocking collectives  15.9 us (20%)
  local copies, waits for them, and re-layouts  2.63 us (3%)
  other arithmetic  1.15 us (1%)
  between operations  0.82 us (1%)
    all_to_all x1, blocking collectives, shards(): got = lax.all_to_all(part, ('zl', 'zh'), 0, 0, tiled=True)  15.9 us
    pallas_call x1, Pallas kernels, main_part(): pl.pallas_call(main_kernel, in_specs=[SMEM] * 3 + [VMEM] * (1 + len(k_blo...  13.3 us
    ppermute x6, waiting for transfers between devices, crossed(): return lax.ppermute(x, ('y', 'x', 'c'), [(n, target(n)) for n in range(32)])  11.7 us
    ppermute x4, waiting for transfers between devices, onward(): return lax.ppermute(x, ('y', 'zl', 'c'), pairs)  9.2 us
    ppermute x6, starting transfers between devices, crossed(): return lax.ppermute(x, ('y', 'x', 'c'), [(n, target(n)) for n in range(32)])  7.8 us
    ppermute x4, starting transfers between devices, onward(): return lax.ppermute(x, ('y', 'zl', 'c'), pairs)  4.48 us
    pallas_call x1, Pallas kernels, own_part(): pl.pallas_call(own_kernel, in_specs=[SMEM] + [VMEM] * 3, out_specs=VMEM,...  3.52 us
    pallas_call x1, Pallas kernels, first_part(): pl.pallas_call(first_kernel, in_specs=[SMEM] * 3 + [VMEM] * (2 + FIRST),...  3.04 us
  transfers between devices with their start and end apart: 17, of which 12 were waited for; matrix products, arithmetic and copies ran while one was open for 2% of the time, Pallas kernels for 8%

profile of v7, /device:TPU:32, one launch (start us, length us, event | category | flops | bytes accessed | tf_op | source)
XLA Modules:
  0.0 78.8 jit_solution(9161460145381650463)
XLA Ops:
  0.6 0.0 copy-start
  0.7 0.9 %copy-done = bf16[256,576]{0,1:T(8,128)(2,1)S(1)} copy-done((bf16[256,576]{0,1:T(8,128)(2,1)S(1)}, bf16[256,576]{0,1:T(8,128)(2,1)}, u32[]{:S(2)}) %copy-start) | copy-done | bytes 294936
  1.6 0.2 fusion
  1.9 0.0 copy-start.1
  1.9 0.0 copy-start.2
  1.9 0.0 copy-start.3
  2.0 1.2 %collective-permute-start.1 = (bf16[1152,128]{1,0:T(8,128)(2,1)S(1)}, bf16[1152,128]{1,0:T(8,128)(2,1)S(1)}, u32[]{:S(2)}, u32[]{:S(2)}) collective-permute-start(bf16[1152,128]{1,0:T(8,128)(2,1)S(1)} %pad_maximum_fusion.refs_0_), channel_id=1, source_target_pairs={{0,96},{1,225},{32,64},{33,193},{64,160},{65,33},{96,128},{97,1},{... | collective-permute-start | bytes 884744 | tf_op jit(solution)/shard_map/ppermute | solution.py:305
  3.2 1.6 %collective-permute-start = (bf16[1152,128]{1,0:T(8,128)(2,1)S(1)}, bf16[1152,128]{1,0:T(8,128)(2,1)S(1)}, u32[]{:S(2)}, u32[]{:S(2)}) collective-permute-start(bf16[1152,128]{1,0:T(8,128)(2,1)S(1)} %pad_maximum_fusion.refs_0_), channel_id=1, source_target_pairs={{0,64},{1,193},{32,96},{33,225},{64,128},{65,1},{96,160},{97,33},{... | collective-permute-start | bytes 884744 | tf_op jit(solution)/shard_map/ppermute | solution.py:305
  4.7 1.9 %collective-permute-start.4 = (bf16[576,128]{1,0:T(8,128)(2,1)S(1)}, bf16[576,128]{1,0:T(8,128)(2,1)S(1)}, u32[]{:S(2)}, u32[]{:S(2)}) collective-permute-start(bf16[576,128]{1,0:T(8,128)(2,1)S(1)} %get-tuple-element.42), channel_id=1, source_target_pairs={{0,32},{32,0},{1,33},{33,1},{2,34},{34,2},{3,35},{35,3},{4,36},{36... | collective-permute-start | bytes 442376 | tf_op jit(solution)/shard_map/ppermute | solution.py:340
  6.6 1.4 %copy.16 = bf16[256,4,512]{2,0,1:T(8,128)(2,1)S(1)} copy(bf16[256,4,512]{2,1,0:T(4,128)(2,1)} %param.7) | data formatting | bytes 2097152 | tf_op args[2]
  8.1 0.1 pad_add_fusion.place_ref
  8.1 5.8 %collective-permute-done.1.refs_2_ = bf16[1152,128]{1,0:T(8,128)(2,1)S(1)} collective-permute-done((bf16[1152,128]{1,0:T(8,128)(2,1)S(1)}, bf16[1152,128]{1,0:T(8,128)(2,1)S(1)}, u32[]{:S(2)}, u32[]{:S(2)}) %collective-permute-start.1) | collective-permute-done | bytes 294944 | tf_op jit(solution)/shard_map/ppermute | solution.py:305
  14.0 0.2 collective-permute-done.refs_1_
  14.2 0.1 collective-permute-start.2
  14.3 0.6 collective-permute-start.3
  14.9 0.2 collective-permute-start.6
  15.1 1.5 %collective-permute-start.5 = (bf16[576,128]{1,0:T(8,128)(2,1)S(1)}, bf16[576,128]{1,0:T(8,128)(2,1)S(1)}, u32[]{:S(2)}, u32[]{:S(2)}) collective-permute-start(bf16[576,128]{1,0:T(8,128)(2,1)S(1)} %slice.79), channel_id=1, source_target_pairs={{0,64},{1,193},{32,96},{33,225},{64,128},{65,1},{96,160},{97,33},{... | collective-permute-start | bytes 442376 | tf_op jit(solution)/shard_map/ppermute | solution.py:305
  16.6 0.0 copy-done.1
  16.6 0.0 copy-done.2
  16.6 0.0 copy-done.3
  16.6 3.0 %shard_map.68 = (f32[4,768,256]{2,1,0:T(8,128)S(1)}, f32[4,768,256]{2,1,0:T(8,128)S(1)}, f32[2,4,8,256]{3,2,1,0:T(8,128)S(1)}, bf16[2048,512]{1,0:T(8,128)(2,1)S...) custom-call(s32[4]{0:T(128)S(1)} %pad_add_fusion.place_ref, s32[8]{0:T(128)S(1)} %copy-done.2, ...), custom_call_target="tpu_custom_call" | custom-call | flops 1711276032 | bytes 20000000 | tf_op jit(solution)/shard_map/pallas_call | solution.py:246
  19.7 0.0 collective-permute-done.4.refs_5_
  19.7 1.6 %collective-permute-done.6.refs_7_ = bf16[576,128]{1,0:T(8,128)(2,1)S(1)} collective-permute-done((bf16[576,128]{1,0:T(8,128)(2,1)S(1)}, bf16[576,128]{1,0:T(8,128)(2,1)S(1)}, u32[]{:S(2)}, u32[]{:S(2)}) %collective-permute-start.6) | collective-permute-done | bytes 147488 | tf_op jit(solution)/shard_map/ppermute | solution.py:305
  21.3 1.6 %collective-permute-done.5.refs_6_ = bf16[576,128]{1,0:T(8,128)(2,1)S(1)} collective-permute-done((bf16[576,128]{1,0:T(8,128)(2,1)S(1)}, bf16[576,128]{1,0:T(8,128)(2,1)S(1)}, u32[]{:S(2)}, u32[]{:S(2)}) %collective-permute-start.5) | collective-permute-done | bytes 147488 | tf_op jit(solution)/shard_map/ppermute | solution.py:305
  22.8 0.0 collective-permute-start.7
  22.8 0.5 collective-permute-start.8
  23.3 0.0 collective-permute-start.9
  23.3 0.0 collective-permute-done.2.refs_3_
  23.4 0.0 collective-permute-done.3.refs_4_
  23.4 0.8 %collective-permute-done.7.refs_8_ = bf16[576,128]{1,0:T(8,128)(2,1)S(1)} collective-permute-done((bf16[576,128]{1,0:T(8,128)(2,1)S(1)}, bf16[576,128]{1,0:T(8,128)(2,1)S(1)}, u32[]{:S(2)}, u32[]{:S(2)}) %collective-permute-start.7) | collective-permute-done | bytes 147488 | tf_op jit(solution)/shard_map/ppermute | solution.py:295
  24.2 0.2 collective-permute-done.8.refs_9_
  24.4 0.3 collective-permute-done.9.refs_10_
  24.7 13.3 %shard_map.69 = (bf16[4,576,256]{2,1,0:T(8,128)(2,1)}, bf16[1024,2048]{1,0:T(8,128)(2,1)S(1)}, bf16[4,4,2,144,128]{4,3,2,1,0:T(8,128)(2,1)S(1)}) custom-call(s32[4]{0:T(128)S(1)} %pad_add_fusion.place_ref, s32[8]{0:T(128)S(1)} %copy-done.2, s32[8]{0:T(128)S(1)} %copy-done.3, bf16[4,576,256]{2,1,0:T(8,128)(2,1)S(1)} %bitcast.52, ...), custom_call_target="tpu_custom_call" | custom-call | tf_op jit(solution)/shard_map/pallas_call | solution.py:261
  38.0 0.5 collective-permute-start.10
  38.5 3.5 %shard_map.70 = f32[4,4,2,144,128]{4,3,2,1,0:T(8,128)S(1)} custom-call(s32[4]{0:T(128)S(1)} %pad_add_fusion.place_ref, bf16[1024,2048]{1,0:T(8,128)(2,1)S(1)} %get-tuple-element.32.w_ref, bf16[2048,512]{1,0:T(8,128)(2,1)S(1)} %get-tuple-element.28.refs_14_.gl_ref, bf16[1024,64]{1,0:T(8,128)(2,1)S(1)} %get-tuple-element.29.refs_15_.gr_ref), custom_call_target="tpu_custom_call" | custom-call | flops 2415919104 | bytes 9000000 | tf_op jit(solution)/shard_map/pallas_call | solution.py:282
  42.1 0.0 collective-permute-done.10
  42.1 0.2 fusion.6
  42.3 3.0 %collective-permute-start.11 = (bf16[4,2,144,128]{3,2,1,0:T(8,128)(2,1)S(1)}, bf16[4,2,144,128]{3,2,1,0:T(8,128)(2,1)S(1)}, u32[]{:S(2)}, u32[]{:S(2)}) collective-permute-start(bf16[4,2,144,128]{3,2,1,0:T(8,128)(2,1)S(1)} %get-tuple-element.36), channel_id=1, source_target_pairs={{0,16},{1,129},{8,24},{9,137},{16,0},{17,145},{24,8},{25,153},{64,... | collective-permute-start | bytes 884744 | tf_op jit(solution)/shard_map/ppermute | solution.py:317
  45.3 1.1 %collective-permute-start.13 = (bf16[4,2,144,128]{3,2,1,0:T(8,128)(2,1)S(1)}, bf16[4,2,144,128]{3,2,1,0:T(8,128)(2,1)S(1)}, u32[]{:S(2)}, u32[]{:S(2)}) collective-permute-start(bf16[4,2,144,128]{3,2,1,0:T(8,128)(2,1)S(1)} %get-tuple-element.37), channel_id=1, source_target_pairs={{0,24},{1,193},{8,0},{9,201},{16,8},{17,209},{24,16},{25,217},{64,... | collective-permute-start | bytes 884744 | tf_op jit(solution)/shard_map/ppermute | solution.py:317
  46.4 0.9 %collective-permute-start.12 = (bf16[4,2,144,128]{3,2,1,0:T(8,128)(2,1)S(1)}, bf16[4,2,144,128]{3,2,1,0:T(8,128)(2,1)S(1)}, u32[]{:S(2)}, u32[]{:S(2)}) collective-permute-start(bf16[4,2,144,128]{3,2,1,0:T(8,128)(2,1)S(1)} %get-tuple-element.38), channel_id=1, source_target_pairs={{0,8},{1,65},{8,16},{9,73},{16,24},{17,81},{24,0},{25,89},{64,72},... | collective-permute-start | bytes 884744 | tf_op jit(solution)/shard_map/ppermute | solution.py:317
  47.3 3.2 %collective-permute-done.11 = bf16[4,2,144,128]{3,2,1,0:T(8,128)(2,1)S(1)} collective-permute-done((bf16[4,2,144,128]{3,2,1,0:T(8,128)(2,1)S(1)}, bf16[4,2,144,128]{3,2,1,0:T(8,128)(2,1)S(1)}, u32[]{:S(2)}, u32[]{:S(2)}) %collective-permute-start.11) | collective-permute-done | bytes 294944 | tf_op jit(solution)/shard_map/ppermute | solution.py:317
  50.6 3.2 %collective-permute-done.13 = bf16[4,2,144,128]{3,2,1,0:T(8,128)(2,1)S(1)} collective-permute-done((bf16[4,2,144,128]{3,2,1,0:T(8,128)(2,1)S(1)}, bf16[4,2,144,128]{3,2,1,0:T(8,128)(2,1)S(1)}, u32[]{:S(2)}, u32[]{:S(2)}) %collective-permute-start.13) | collective-permute-done | bytes 294944 | tf_op jit(solution)/shard_map/ppermute | solution.py:317
  53.8 0.6 collective-permute-done.12
  54.4 0.2 fusion.12
  54.6 0.7 collective-permute-start.14
  55.3 1.1 %collective-permute-start.16 = (bf16[2,144,128]{2,1,0:T(8,128)(2,1)S(1)}, bf16[2,144,128]{2,1,0:T(8,128)(2,1)S(1)}, u32[]{:S(2)}, u32[]{:S(2)}) collective-permute-start(bf16[2,144,128]{2,1,0:T(8,128)(2,1)S(1)} %get-tuple-element.40), channel_id=1, source_target_pairs={{0,192},{1,25},{8,200},{9,1},{16,208},{17,9},{24,216},{25,17},{64,... | collective-permute-start | bytes 221192 | tf_op jit(solution)/shard_map/ppermute | solution.py:317
  56.4 0.9 %collective-permute-start.15 = (bf16[2,144,128]{2,1,0:T(8,128)(2,1)S(1)}, bf16[2,144,128]{2,1,0:T(8,128)(2,1)S(1)}, u32[]{:S(2)}, u32[]{:S(2)}) collective-permute-start(bf16[2,144,128]{2,1,0:T(8,128)(2,1)S(1)} %get-tuple-element.41), channel_id=1, source_target_pairs={{0,64},{1,9},{8,72},{9,17},{16,80},{17,25},{24,88},{25,1},{64,128}... | collective-permute-start | bytes 221192 | tf_op jit(solution)/shard_map/ppermute | solution.py:317
  57.3 3.2 %collective-permute-done.14 = bf16[2,144,128]{2,1,0:T(8,128)(2,1)S(1)} collective-permute-done((bf16[2,144,128]{2,1,0:T(8,128)(2,1)S(1)}, bf16[2,144,128]{2,1,0:T(8,128)(2,1)S(1)}, u32[]{:S(2)}, u32[]{:S(2)}) %collective-permute-start.14) | collective-permute-done | bytes 73760 | tf_op jit(solution)/shard_map/ppermute | solution.py:317
  60.5 0.0 collective-permute-done.16
  60.5 1.5 %collective-permute-done.15 = bf16[2,144,128]{2,1,0:T(8,128)(2,1)S(1)} collective-permute-done((bf16[2,144,128]{2,1,0:T(8,128)(2,1)S(1)}, bf16[2,144,128]{2,1,0:T(8,128)(2,1)S(1)}, u32[]{:S(2)}, u32[]{:S(2)}) %collective-permute-start.15) | collective-permute-done | bytes 73760 | tf_op jit(solution)/shard_map/ppermute | solution.py:317
  62.1 0.1 reshape.60
  62.2 0.1 reshape.64
  62.3 15.9 %all_to_all.5 = bf16[8,8,576]{2,1,0:T(8,128)(2,1)S(1)} all-to-all(bf16[8,8,576]{2,1,0:T(8,128)(2,1)S(1)} %maximum_maximum_fusion), channel_id=1, replica_groups=mesh['y'=4,'zl'=2,'x'=4,'zh'=4,'c'=2] {'zl','zh'}, dimensions={0} | all-to-all | bytes 147456 | tf_op jit(solution)/shard_map/all_to_all | solution.py:360
  78.2 0.6 convert_reduce_fusion
  (13 shorter events, 0.2 us)
Async XLA Ops:
  0.6 1.0 %copy-start = (bf16[256,576]{0,1:T(8,128)(2,1)S(1)}, bf16[256,576]{0,1:T(8,128)(2,1)}, u32[]{:S(2)}) copy-start(bf16[256,576]{0,1:T(8,128)(2,1)} %param.6) | copy-start | bytes 884740
  1.9 14.8 %copy-start.1 = (bf16[256,4,576]{0,2,1:T(8,128)(2,1)S(1)}, bf16[256,4,576]{0,2,1:T(8,128)(2,1)}, u32[]{:S(2)}) copy-start(bf16[256,4,576]{0,2,1:T(8,128)(2,1)} %param.5) | copy-start | bytes 3538948
  1.9 14.7 %copy-start.2 = (s32[8]{0:T(128)S(1)}, s32[8]{0:T(128)}, u32[]{:S(2)}) copy-start(s32[8]{0:T(128)} %query_blocks_ref.3) | copy-start | bytes 100
  1.9 14.7 %copy-start.3 = (s32[8]{0:T(128)S(1)}, s32[8]{0:T(128)}, u32[]{:S(2)}) copy-start(s32[8]{0:T(128)} %key_blocks_ref.3) | copy-start | bytes 100
  2.0 12.0 %collective-permute-start.1 = (bf16[1152,128]{1,0:T(8,128)(2,1)S(1)}, bf16[1152,128]{1,0:T(8,128)(2,1)S(1)}, u32[]{:S(2)}, u32[]{:S(2)}) collective-permute-start(bf16[1152,128]{1,0:T(8,128)(2,1)S(1)} %pad_maximum_fusion.refs_0_), channel_id=1, source_target_pairs={{0,96},{1,225},{32,64},{33,193},{64,160},{65,33},{96,128},{97,1},{... | collective-permute-start | bytes 884744 | tf_op jit(solution)/shard_map/ppermute | solution.py:305
  3.2 11.0 %collective-permute-start = (bf16[1152,128]{1,0:T(8,128)(2,1)S(1)}, bf16[1152,128]{1,0:T(8,128)(2,1)S(1)}, u32[]{:S(2)}, u32[]{:S(2)}) collective-permute-start(bf16[1152,128]{1,0:T(8,128)(2,1)S(1)} %pad_maximum_fusion.refs_0_), channel_id=1, source_target_pairs={{0,64},{1,193},{32,96},{33,225},{64,128},{65,1},{96,160},{97,33},{... | collective-permute-start | bytes 884744 | tf_op jit(solution)/shard_map/ppermute | solution.py:305
  4.7 14.9 %collective-permute-start.4 = (bf16[576,128]{1,0:T(8,128)(2,1)S(1)}, bf16[576,128]{1,0:T(8,128)(2,1)S(1)}, u32[]{:S(2)}, u32[]{:S(2)}) collective-permute-start(bf16[576,128]{1,0:T(8,128)(2,1)S(1)} %get-tuple-element.42), channel_id=1, source_target_pairs={{0,32},{32,0},{1,33},{33,1},{2,34},{34,2},{3,35},{35,3},{4,36},{36... | collective-permute-start | bytes 442376 | tf_op jit(solution)/shard_map/ppermute | solution.py:340
  14.2 9.2 %collective-permute-start.2 = (bf16[1152,128]{1,0:T(8,128)(2,1)S(1)}, bf16[1152,128]{1,0:T(8,128)(2,1)S(1)}, u32[]{:S(2)}, u32[]{:S(2)}) collective-permute-start(bf16[1152,128]{1,0:T(8,128)(2,1)S(1)} %collective-permute-done.refs_1_), channel_id=1, source_target_pairs={{0,1},{1,0},{2,3},{3,2},{4,5},{5,4},{6,7},{7,6},{8,9},{9,8},{10,11... | collective-permute-start | bytes 884744 | tf_op jit(solution)/shard_map/ppermute | solution.py:295
  14.3 9.0 %collective-permute-start.3 = (bf16[1152,128]{1,0:T(8,128)(2,1)S(1)}, bf16[1152,128]{1,0:T(8,128)(2,1)S(1)}, u32[]{:S(2)}, u32[]{:S(2)}) collective-permute-start(bf16[1152,128]{1,0:T(8,128)(2,1)S(1)} %collective-permute-done.1.refs_2_), channel_id=1, source_target_pairs={{0,1},{1,0},{2,3},{3,2},{4,5},{5,4},{6,7},{7,6},{8,9},{9,8},{10,11... | collective-permute-start | bytes 884744 | tf_op jit(solution)/shard_map/ppermute | solution.py:295
  14.9 6.4 %collective-permute-start.6 = (bf16[576,128]{1,0:T(8,128)(2,1)S(1)}, bf16[576,128]{1,0:T(8,128)(2,1)S(1)}, u32[]{:S(2)}, u32[]{:S(2)}) collective-permute-start(bf16[576,128]{1,0:T(8,128)(2,1)S(1)} %slice.80), channel_id=1, source_target_pairs={{0,64},{1,193},{32,96},{33,225},{64,128},{65,1},{96,160},{97,33},{... | collective-permute-start | bytes 442376 | tf_op jit(solution)/shard_map/ppermute | solution.py:305
  15.1 7.7 %collective-permute-start.5 = (bf16[576,128]{1,0:T(8,128)(2,1)S(1)}, bf16[576,128]{1,0:T(8,128)(2,1)S(1)}, u32[]{:S(2)}, u32[]{:S(2)}) collective-permute-start(bf16[576,128]{1,0:T(8,128)(2,1)S(1)} %slice.79), channel_id=1, source_target_pairs={{0,64},{1,193},{32,96},{33,225},{64,128},{65,1},{96,160},{97,33},{... | collective-permute-start | bytes 442376 | tf_op jit(solution)/shard_map/ppermute | solution.py:305
  22.8 1.4 %collective-permute-start.7 = (bf16[576,128]{1,0:T(8,128)(2,1)S(1)}, bf16[576,128]{1,0:T(8,128)(2,1)S(1)}, u32[]{:S(2)}, u32[]{:S(2)}) collective-permute-start(bf16[576,128]{1,0:T(8,128)(2,1)S(1)} %collective-permute-done.4.refs_5_), channel_id=1, source_target_pairs={{0,1},{1,0},{2,3},{3,2},{4,5},{5,4},{6,7},{7,6},{8,9},{9,8},{10,11... | collective-permute-start | bytes 442376 | tf_op jit(solution)/shard_map/ppermute | solution.py:295
  22.8 1.6 %collective-permute-start.8 = (bf16[576,128]{1,0:T(8,128)(2,1)S(1)}, bf16[576,128]{1,0:T(8,128)(2,1)S(1)}, u32[]{:S(2)}, u32[]{:S(2)}) collective-permute-start(bf16[576,128]{1,0:T(8,128)(2,1)S(1)} %collective-permute-done.5.refs_6_), channel_id=1, source_target_pairs={{0,1},{1,0},{2,3},{3,2},{4,5},{5,4},{6,7},{7,6},{8,9},{9,8},{10,11... | collective-permute-start | bytes 442376 | tf_op jit(solution)/shard_map/ppermute | solution.py:295
  23.3 1.4 %collective-permute-start.9 = (bf16[576,128]{1,0:T(8,128)(2,1)S(1)}, bf16[576,128]{1,0:T(8,128)(2,1)S(1)}, u32[]{:S(2)}, u32[]{:S(2)}) collective-permute-start(bf16[576,128]{1,0:T(8,128)(2,1)S(1)} %collective-permute-done.6.refs_7_), channel_id=1, source_target_pairs={{0,1},{1,0},{2,3},{3,2},{4,5},{5,4},{6,7},{7,6},{8,9},{9,8},{10,11... | collective-permute-start | bytes 442376 | tf_op jit(solution)/shard_map/ppermute | solution.py:295
  38.0 4.0 %collective-permute-start.10 = (bf16[4,4,2,144,128]{4,3,2,1,0:T(8,128)(2,1)S(1)}, bf16[4,4,2,144,128]{4,3,2,1,0:T(8,128)(2,1)S(1)}, u32[]{:S(2)}, u32[]{:S(2)}) collective-permute-start(bf16[4,4,2,144,128]{4,3,2,1,0:T(8,128)(2,1)S(1)} %get-tuple-element.33), channel_id=1, source_target_pairs={{0,1},{1,0},{2,3},{3,2},{4,5},{5,4},{6,7},{7,6},{8,9},{9,8},{10,11... | collective-permute-start | bytes 3538952 | tf_op jit(solution)/shard_map/ppermute | solution.py:295
  42.3 8.3 %collective-permute-start.11 = (bf16[4,2,144,128]{3,2,1,0:T(8,128)(2,1)S(1)}, bf16[4,2,144,128]{3,2,1,0:T(8,128)(2,1)S(1)}, u32[]{:S(2)}, u32[]{:S(2)}) collective-permute-start(bf16[4,2,144,128]{3,2,1,0:T(8,128)(2,1)S(1)} %get-tuple-element.36), channel_id=1, source_target_pairs={{0,16},{1,129},{8,24},{9,137},{16,0},{17,145},{24,8},{25,153},{64,... | collective-permute-start | bytes 884744 | tf_op jit(solution)/shard_map/ppermute | solution.py:317
  45.3 8.5 %collective-permute-start.13 = (bf16[4,2,144,128]{3,2,1,0:T(8,128)(2,1)S(1)}, bf16[4,2,144,128]{3,2,1,0:T(8,128)(2,1)S(1)}, u32[]{:S(2)}, u32[]{:S(2)}) collective-permute-start(bf16[4,2,144,128]{3,2,1,0:T(8,128)(2,1)S(1)} %get-tuple-element.37), channel_id=1, source_target_pairs={{0,24},{1,193},{8,0},{9,201},{16,8},{17,209},{24,16},{25,217},{64,... | collective-permute-start | bytes 884744 | tf_op jit(solution)/shard_map/ppermute | solution.py:317
  46.4 7.9 %collective-permute-start.12 = (bf16[4,2,144,128]{3,2,1,0:T(8,128)(2,1)S(1)}, bf16[4,2,144,128]{3,2,1,0:T(8,128)(2,1)S(1)}, u32[]{:S(2)}, u32[]{:S(2)}) collective-permute-start(bf16[4,2,144,128]{3,2,1,0:T(8,128)(2,1)S(1)} %get-tuple-element.38), channel_id=1, source_target_pairs={{0,8},{1,65},{8,16},{9,73},{16,24},{17,81},{24,0},{25,89},{64,72},... | collective-permute-start | bytes 884744 | tf_op jit(solution)/shard_map/ppermute | solution.py:317
  54.6 5.9 %collective-permute-start.14 = (bf16[2,144,128]{2,1,0:T(8,128)(2,1)S(1)}, bf16[2,144,128]{2,1,0:T(8,128)(2,1)S(1)}, u32[]{:S(2)}, u32[]{:S(2)}) collective-permute-start(bf16[2,144,128]{2,1,0:T(8,128)(2,1)S(1)} %get-tuple-element.39), channel_id=1, source_target_pairs={{0,128},{1,17},{8,136},{9,25},{16,144},{17,1},{24,152},{25,9},{64,... | collective-permute-start | bytes 221192 | tf_op jit(solution)/shard_map/ppermute | solution.py:317
  55.3 5.2 %collective-permute-start.16 = (bf16[2,144,128]{2,1,0:T(8,128)(2,1)S(1)}, bf16[2,144,128]{2,1,0:T(8,128)(2,1)S(1)}, u32[]{:S(2)}, u32[]{:S(2)}) collective-permute-start(bf16[2,144,128]{2,1,0:T(8,128)(2,1)S(1)} %get-tuple-element.40), channel_id=1, source_target_pairs={{0,192},{1,25},{8,200},{9,1},{16,208},{17,9},{24,216},{25,17},{64,... | collective-permute-start | bytes 221192 | tf_op jit(solution)/shard_map/ppermute | solution.py:317
  56.4 5.6 %collective-permute-start.15 = (bf16[2,144,128]{2,1,0:T(8,128)(2,1)S(1)}, bf16[2,144,128]{2,1,0:T(8,128)(2,1)S(1)}, u32[]{:S(2)}, u32[]{:S(2)}) collective-permute-start(bf16[2,144,128]{2,1,0:T(8,128)(2,1)S(1)} %get-tuple-element.41), channel_id=1, source_target_pairs={{0,64},{1,9},{8,72},{9,17},{16,80},{17,25},{24,88},{25,1},{64,128}... | collective-permute-start | bytes 221192 | tf_op jit(solution)/shard_map/ppermute | solution.py:317

commit v8 on v7

--- a/solution.py
+++ b/solution.py
@@ -22,8 +22,8 @@
 LANES = 128
 OWNED = 32
 PACKED = OWNED * DK // LANES
-MAIN_VMEM = 23 * 1024 * 1024
-FIRST = 3
+MAIN_VMEM = 20 * 1024 * 1024
+FIRST = 5
 WHOLE = 5
 SWAPPED = (3, 4)
 
@@ -252,7 +252,7 @@
         cost_estimate=pl.CostEstimate(
             flops=2 * 1024 * FIRST * TILE * (DK + DL), bytes_accessed=20_000_000, transcendentals=0
         ),
-        compiler_params=pltpu.CompilerParams(vmem_limit_bytes=16 * 1024 * 1024),
+        compiler_params=pltpu.CompilerParams(vmem_limit_bytes=20 * 1024 * 1024),
     )(place, query_blocks, key_blocks, qt, go, *k_blocks)
 
 
@@ -342,10 +342,10 @@
     place = jnp.stack([core, y, zl, x])
     qt = queries.transpose(1, 2, 0)
     go = grad_output.transpose(1, 0, 2)
-    go, near, slant = lax.optimization_barrier((go, near, slant))
+    go, beside, near, slant = lax.optimization_barrier((go, beside, near, slant))
     singles = [beside, onward(near[:DK], 0), onward(slant[:DK], 0)]
     swapped = [swap_cores(near), swap_cores(slant)]
-    early = list(first_part(place, query_blocks, key_blocks, qt, go, [here, near, slant]))
+    early = list(first_part(place, query_blocks, key_blocks, qt, go, [here, near, slant] + swapped))
     early[2], *singles = lax.optimization_barrier((early[2], *singles))
     blocks = [here, near, slant] + swapped + singles + [swap_cores(k) for k in singles]
     dqt, weights, other = main_part(place, query_blocks, key_blocks, qt, blocks, early)

time: 79 us -> 81.3 us (1.029)
  starting transfers between devices: 15.9 us -> 17.8 us
  Pallas kernels: 19.9 us -> 21 us
    ppermute x4, waiting for transfers between devices: 9.2 us -> 0.13 us  [onward(): return lax.ppermute(x, ('y', 'zl', 'c'), pairs)]
    ppermute x1, waiting for transfers between devices: 0.01 us -> 8.93 us  [shards(): beside = lax.ppermute(here[:DK], 'zl', [(0, 1), (1, 0)])]
    ppermute x6, starting transfers between devices: 7.8 us -> 10.5 us  [crossed(): return lax.ppermute(x, ('y', 'x', 'c'), [(n, target(n)) for n in range(32)])]
    pallas_call x1, Pallas kernels: 3.04 us -> 5.04 us  [first_part(): pl.pallas_call(first_kernel, in_specs=[SMEM] * 3 + [VMEM] * (2 + FIRST),...]
    pallas_call x1, Pallas kernels: 13.3 us -> 12.4 us  [main_part(): pl.pallas_call(main_kernel, in_specs=[SMEM] * 3 + [VMEM] * (1 + len(k_blo...]
    unnamed x9 -> x13, local copies, waits for them, and re-layouts: 2.38 us -> 2.45 us
  transfers between devices with their start and end apart: 17 -> 17, of which waited for: 12 -> 12; matrix products, arithmetic and copies ran while one was open for 2% -> 0% of each run, Pallas kernels for 8% -> 11%
where the time goes in v8:
time: 81.3 us; the launch traced here: 81.1 us
  waiting for transfers between devices  21.8 us (27%)
  Pallas kernels  21 us (26%)
  starting transfers between devices  17.8 us (22%)
  blocking collectives  15.5 us (19%)
  local copies, waits for them, and re-layouts  2.7 us (3%)
  other arithmetic  1.18 us (1%)
    all_to_all x1, blocking collectives, shards(): got = lax.all_to_all(part, ('zl', 'zh'), 0, 0, tiled=True)  15.5 us
    pallas_call x1, Pallas kernels, main_part(): pl.pallas_call(main_kernel, in_specs=[SMEM] * 3 + [VMEM] * (1 + len(k_blo...  12.4 us
    ppermute x6, waiting for transfers between devices, crossed(): return lax.ppermute(x, ('y', 'x', 'c'), [(n, target(n)) for n in range(32)])  11.3 us
    ppermute x6, starting transfers between devices, crossed(): return lax.ppermute(x, ('y', 'x', 'c'), [(n, target(n)) for n in range(32)])  10.5 us
    ppermute x1, waiting for transfers between devices, shards(): beside = lax.ppermute(here[:DK], 'zl', [(0, 1), (1, 0)])  8.93 us
    pallas_call x1, Pallas kernels, first_part(): pl.pallas_call(first_kernel, in_specs=[SMEM] * 3 + [VMEM] * (2 + FIRST),...  5.04 us
    ppermute x4, starting transfers between devices, onward(): return lax.ppermute(x, ('y', 'zl', 'c'), pairs)  4.09 us
    pallas_call x1, Pallas kernels, own_part(): pl.pallas_call(own_kernel, in_specs=[SMEM] + [VMEM] * 3, out_specs=VMEM,...  3.53 us
  transfers between devices with their start and end apart: 17, of which 12 were waited for; matrix products, arithmetic and copies ran while one was open for 0% of the time, Pallas kernels for 11%

profile of v8, /device:TPU:32, one launch (start us, length us, event | category | flops | bytes accessed | tf_op | source)
XLA Modules:
  0.0 81.1 jit_solution(1285894992372930449)
XLA Ops:
  0.6 0.0 copy-start
  0.6 0.0 copy-start.5
  0.7 0.9 %copy-done = bf16[256,576]{0,1:T(8,128)(2,1)S(1)} copy-done((bf16[256,576]{0,1:T(8,128)(2,1)S(1)}, bf16[256,576]{0,1:T(8,128)(2,1)}, u32[]{:S(2)}) %copy-start) | copy-done | bytes 294936
  1.6 0.2 fusion
  1.9 0.0 copy-start.1
  1.9 1.2 %collective-permute-start.2 = (bf16[1152,128]{1,0:T(8,128)(2,1)S(1)}, bf16[1152,128]{1,0:T(8,128)(2,1)S(1)}, u32[]{:S(2)}, u32[]{:S(2)}) collective-permute-start(bf16[1152,128]{1,0:T(8,128)(2,1)S(1)} %pad_maximum_fusion.refs_0_), channel_id=1, source_target_pairs={{0,96},{1,225},{32,64},{33,193},{64,160},{65,33},{96,128},{97,1},{... | collective-permute-start | bytes 884744 | tf_op jit(solution)/shard_map/ppermute | solution.py:305
  3.1 1.6 %collective-permute-start.1 = (bf16[1152,128]{1,0:T(8,128)(2,1)S(1)}, bf16[1152,128]{1,0:T(8,128)(2,1)S(1)}, u32[]{:S(2)}, u32[]{:S(2)}) collective-permute-start(bf16[1152,128]{1,0:T(8,128)(2,1)S(1)} %pad_maximum_fusion.refs_0_), channel_id=1, source_target_pairs={{0,64},{1,193},{32,96},{33,225},{64,128},{65,1},{96,160},{97,33},{... | collective-permute-start | bytes 884744 | tf_op jit(solution)/shard_map/ppermute | solution.py:305
  4.7 1.9 %collective-permute-start = (bf16[576,128]{1,0:T(8,128)(2,1)S(1)}, bf16[576,128]{1,0:T(8,128)(2,1)S(1)}, u32[]{:S(2)}, u32[]{:S(2)}) collective-permute-start(bf16[576,128]{1,0:T(8,128)(2,1)S(1)} %get-tuple-element.44), channel_id=1, source_target_pairs={{0,32},{32,0},{1,33},{33,1},{2,34},{34,2},{3,35},{35,3},{4,36},{36... | collective-permute-start | bytes 442376 | tf_op jit(solution)/shard_map/ppermute | solution.py:340
  6.6 0.0 copy-done.5
  6.6 0.2 copy.16
  6.8 8.9 %collective-permute-done.refs_5_ = bf16[576,128]{1,0:T(8,128)(2,1)S(1)} collective-permute-done((bf16[576,128]{1,0:T(8,128)(2,1)S(1)}, bf16[576,128]{1,0:T(8,128)(2,1)S(1)}, u32[]{:S(2)}, u32[]{:S(2)}) %collective-permute-start) | collective-permute-done | bytes 147488 | tf_op jit(solution)/shard_map/ppermute | solution.py:340
  15.8 0.0 collective-permute-done.2.refs_2_
  15.8 0.0 collective-permute-done.1.refs_1_
  15.8 0.1 collective-permute-start.3
  15.9 0.4 collective-permute-start.4
  16.3 0.1 pad_add_fusion.place_ref
  16.4 0.1 collective-permute-start.6
  16.5 1.2 %collective-permute-start.5 = (bf16[576,128]{1,0:T(8,128)(2,1)S(1)}, bf16[576,128]{1,0:T(8,128)(2,1)S(1)}, u32[]{:S(2)}, u32[]{:S(2)}) collective-permute-start(bf16[576,128]{1,0:T(8,128)(2,1)S(1)} %slice.79), channel_id=1, source_target_pairs={{0,64},{1,193},{32,96},{33,225},{64,128},{65,1},{96,160},{97,33},{... | collective-permute-start | bytes 442376 | tf_op jit(solution)/shard_map/ppermute | solution.py:305
  17.7 0.0 collective-permute-done.3.refs_3_
  17.7 0.2 collective-permute-done.4.refs_4_
  17.9 0.0 copy-done.1
  17.9 0.0 copy-start.2
  17.9 0.7 copy-done.2
  18.6 0.0 copy-start.3
  18.6 0.7 copy-done.3
  19.2 0.0 copy-start.4
  19.2 5.0 %shard_map.68 = (f32[4,1280,256]{2,1,0:T(8,128)S(1)}, f32[4,1280,256]{2,1,0:T(8,128)S(1)}, f32[2,4,8,256]{3,2,1,0:T(8,128)S(1)}, bf16[2048,512]{1,0:T(8,128)(2,1...) custom-call(s32[4]{0:T(128)S(1)} %pad_add_fusion.place_ref, s32[8]{0:T(128)S(1)} %copy-done.2, ...), custom_call_target="tpu_custom_call" | custom-call | flops 2852126720 | bytes 20000000 | tf_op jit(solution)/shard_map/pallas_call | solution.py:246
  24.3 0.0 collective-permute-done.6.refs_7_
  24.3 0.1 collective-permute-done.5.refs_6_
  24.4 0.1 collective-permute-start.7
  24.5 0.4 collective-permute-start.8
  24.9 0.1 collective-permute-start.9
  25.0 0.8 collective-permute-done.7.refs_8_
  25.8 0.2 collective-permute-done.8.refs_9_
  26.0 0.3 collective-permute-done.9.refs_10_
  26.3 0.0 copy-done.4
  26.3 12.4 %shard_map.69 = (bf16[4,576,256]{2,1,0:T(8,128)(2,1)}, bf16[1024,2048]{1,0:T(8,128)(2,1)S(1)}, bf16[4,4,2,144,128]{4,3,2,1,0:T(8,128)(2,1)S(1)}) custom-call(s32[4]{0:T(128)S(1)} %pad_add_fusion.place_ref, s32[8]{0:T(128)S(1)} %copy-done.2, s32[8]{0:T(128)S(1)} %copy-done.4, bf16[4,576,256]{2,1,0:T(8,128)(2,1)S(1)} %bitcast.52, ...), custom_call_target="tpu_custom_call" | custom-call | tf_op jit(solution)/shard_map/pallas_call | solution.py:261
  38.7 0.2 collective-permute-start.10
  38.9 3.5 %shard_map.70 = f32[4,4,2,144,128]{4,3,2,1,0:T(8,128)S(1)} custom-call(s32[4]{0:T(128)S(1)} %pad_add_fusion.place_ref, bf16[1024,2048]{1,0:T(8,128)(2,1)S(1)} %get-tuple-element.34.w_ref, bf16[2048,512]{1,0:T(8,128)(2,1)S(1)} %get-tuple-element.30.refs_14_.gl_ref, bf16[1024,64]{1,0:T(8,128)(2,1)S(1)} %get-tuple-element.31.refs_15_.gr_ref), custom_call_target="tpu_custom_call" | custom-call | flops 2415919104 | bytes 9000000 | tf_op jit(solution)/shard_map/pallas_call | solution.py:282
  42.5 0.0 collective-permute-done.10
  42.5 0.2 fusion.6
  42.7 3.1 %collective-permute-start.11 = (bf16[4,2,144,128]{3,2,1,0:T(8,128)(2,1)S(1)}, bf16[4,2,144,128]{3,2,1,0:T(8,128)(2,1)S(1)}, u32[]{:S(2)}, u32[]{:S(2)}) collective-permute-start(bf16[4,2,144,128]{3,2,1,0:T(8,128)(2,1)S(1)} %get-tuple-element.38), channel_id=1, source_target_pairs={{0,16},{1,129},{8,24},{9,137},{16,0},{17,145},{24,8},{25,153},{64,... | collective-permute-start | bytes 884744 | tf_op jit(solution)/shard_map/ppermute | solution.py:317
  45.8 1.1 %collective-permute-start.13 = (bf16[4,2,144,128]{3,2,1,0:T(8,128)(2,1)S(1)}, bf16[4,2,144,128]{3,2,1,0:T(8,128)(2,1)S(1)}, u32[]{:S(2)}, u32[]{:S(2)}) collective-permute-start(bf16[4,2,144,128]{3,2,1,0:T(8,128)(2,1)S(1)} %get-tuple-element.39), channel_id=1, source_target_pairs={{0,24},{1,193},{8,0},{9,201},{16,8},{17,209},{24,16},{25,217},{64,... | collective-permute-start | bytes 884744 | tf_op jit(solution)/shard_map/ppermute | solution.py:317
  46.9 0.9 %collective-permute-start.12 = (bf16[4,2,144,128]{3,2,1,0:T(8,128)(2,1)S(1)}, bf16[4,2,144,128]{3,2,1,0:T(8,128)(2,1)S(1)}, u32[]{:S(2)}, u32[]{:S(2)}) collective-permute-start(bf16[4,2,144,128]{3,2,1,0:T(8,128)(2,1)S(1)} %get-tuple-element.40), channel_id=1, source_target_pairs={{0,8},{1,65},{8,16},{9,73},{16,24},{17,81},{24,0},{25,89},{64,72},... | collective-permute-start | bytes 884744 | tf_op jit(solution)/shard_map/ppermute | solution.py:317
  47.8 3.2 %collective-permute-done.11 = bf16[4,2,144,128]{3,2,1,0:T(8,128)(2,1)S(1)} collective-permute-done((bf16[4,2,144,128]{3,2,1,0:T(8,128)(2,1)S(1)}, bf16[4,2,144,128]{3,2,1,0:T(8,128)(2,1)S(1)}, u32[]{:S(2)}, u32[]{:S(2)}) %collective-permute-start.11) | collective-permute-done | bytes 294944 | tf_op jit(solution)/shard_map/ppermute | solution.py:317
  51.0 3.3 %collective-permute-done.13 = bf16[4,2,144,128]{3,2,1,0:T(8,128)(2,1)S(1)} collective-permute-done((bf16[4,2,144,128]{3,2,1,0:T(8,128)(2,1)S(1)}, bf16[4,2,144,128]{3,2,1,0:T(8,128)(2,1)S(1)}, u32[]{:S(2)}, u32[]{:S(2)}) %collective-permute-start.13) | collective-permute-done | bytes 294944 | tf_op jit(solution)/shard_map/ppermute | solution.py:317
  54.3 0.6 collective-permute-done.12
  54.9 0.2 fusion.12
  55.1 3.3 %collective-permute-start.14 = (bf16[2,144,128]{2,1,0:T(8,128)(2,1)S(1)}, bf16[2,144,128]{2,1,0:T(8,128)(2,1)S(1)}, u32[]{:S(2)}, u32[]{:S(2)}) collective-permute-start(bf16[2,144,128]{2,1,0:T(8,128)(2,1)S(1)} %get-tuple-element.41), channel_id=1, source_target_pairs={{0,128},{1,17},{8,136},{9,25},{16,144},{17,1},{24,152},{25,9},{64,... | collective-permute-start | bytes 221192 | tf_op jit(solution)/shard_map/ppermute | solution.py:317
  58.4 0.7 collective-permute-start.16
  59.2 1.3 %collective-permute-start.15 = (bf16[2,144,128]{2,1,0:T(8,128)(2,1)S(1)}, bf16[2,144,128]{2,1,0:T(8,128)(2,1)S(1)}, u32[]{:S(2)}, u32[]{:S(2)}) collective-permute-start(bf16[2,144,128]{2,1,0:T(8,128)(2,1)S(1)} %get-tuple-element.43), channel_id=1, source_target_pairs={{0,64},{1,9},{8,72},{9,17},{16,80},{17,25},{24,88},{25,1},{64,128}... | collective-permute-start | bytes 221192 | tf_op jit(solution)/shard_map/ppermute | solution.py:317
  60.4 0.6 collective-permute-done.14
  61.0 1.7 %collective-permute-done.16 = bf16[2,144,128]{2,1,0:T(8,128)(2,1)S(1)} collective-permute-done((bf16[2,144,128]{2,1,0:T(8,128)(2,1)S(1)}, bf16[2,144,128]{2,1,0:T(8,128)(2,1)S(1)}, u32[]{:S(2)}, u32[]{:S(2)}) %collective-permute-start.16) | collective-permute-done | bytes 73760 | tf_op jit(solution)/shard_map/ppermute | solution.py:317
  62.8 1.9 %collective-permute-done.15 = bf16[2,144,128]{2,1,0:T(8,128)(2,1)S(1)} collective-permute-done((bf16[2,144,128]{2,1,0:T(8,128)(2,1)S(1)}, bf16[2,144,128]{2,1,0:T(8,128)(2,1)S(1)}, u32[]{:S(2)}, u32[]{:S(2)}) %collective-permute-start.15) | collective-permute-done | bytes 73760 | tf_op jit(solution)/shard_map/ppermute | solution.py:317
  64.8 0.1 reshape.60
  64.9 0.1 reshape.64
  65.0 15.5 %all_to_all.5 = bf16[8,8,576]{2,1,0:T(8,128)(2,1)S(1)} all-to-all(bf16[8,8,576]{2,1,0:T(8,128)(2,1)S(1)} %maximum_maximum_fusion), channel_id=1, replica_groups=mesh['y'=4,'zl'=2,'x'=4,'zh'=4,'c'=2] {'zl','zh'}, dimensions={0} | all-to-all | bytes 147456 | tf_op jit(solution)/shard_map/all_to_all | solution.py:360
  80.5 0.6 convert_reduce_fusion
  (13 shorter events, 0.2 us)
Async XLA Ops:
  0.6 1.0 %copy-start = (bf16[256,576]{0,1:T(8,128)(2,1)S(1)}, bf16[256,576]{0,1:T(8,128)(2,1)}, u32[]{:S(2)}) copy-start(bf16[256,576]{0,1:T(8,128)(2,1)} %param.6) | copy-start | bytes 884740
  0.6 6.0 %copy-start.5 = (bf16[256,4,512]{2,1,0:T(4,128)(2,1)S(1)}, bf16[256,4,512]{2,1,0:T(4,128)(2,1)}, u32[]{:S(2)}) copy-start(bf16[256,4,512]{2,1,0:T(4,128)(2,1)} %param.7) | copy-start | bytes 3145732
  1.9 16.0 %copy-start.1 = (bf16[256,4,576]{0,2,1:T(8,128)(2,1)S(1)}, bf16[256,4,576]{0,2,1:T(8,128)(2,1)}, u32[]{:S(2)}) copy-start(bf16[256,4,576]{0,2,1:T(8,128)(2,1)} %param.5) | copy-start | bytes 3538948
  1.9 13.8 %collective-permute-start.2 = (bf16[1152,128]{1,0:T(8,128)(2,1)S(1)}, bf16[1152,128]{1,0:T(8,128)(2,1)S(1)}, u32[]{:S(2)}, u32[]{:S(2)}) collective-permute-start(bf16[1152,128]{1,0:T(8,128)(2,1)S(1)} %pad_maximum_fusion.refs_0_), channel_id=1, source_target_pairs={{0,96},{1,225},{32,64},{33,193},{64,160},{65,33},{96,128},{97,1},{... | collective-permute-start | bytes 884744 | tf_op jit(solution)/shard_map/ppermute | solution.py:305
  3.1 12.6 %collective-permute-start.1 = (bf16[1152,128]{1,0:T(8,128)(2,1)S(1)}, bf16[1152,128]{1,0:T(8,128)(2,1)S(1)}, u32[]{:S(2)}, u32[]{:S(2)}) collective-permute-start(bf16[1152,128]{1,0:T(8,128)(2,1)S(1)} %pad_maximum_fusion.refs_0_), channel_id=1, source_target_pairs={{0,64},{1,193},{32,96},{33,225},{64,128},{65,1},{96,160},{97,33},{... | collective-permute-start | bytes 884744 | tf_op jit(solution)/shard_map/ppermute | solution.py:305
  4.7 11.1 %collective-permute-start = (bf16[576,128]{1,0:T(8,128)(2,1)S(1)}, bf16[576,128]{1,0:T(8,128)(2,1)S(1)}, u32[]{:S(2)}, u32[]{:S(2)}) collective-permute-start(bf16[576,128]{1,0:T(8,128)(2,1)S(1)} %get-tuple-element.44), channel_id=1, source_target_pairs={{0,32},{32,0},{1,33},{33,1},{2,34},{34,2},{3,35},{35,3},{4,36},{36... | collective-permute-start | bytes 442376 | tf_op jit(solution)/shard_map/ppermute | solution.py:340
  15.8 2.0 %collective-permute-start.3 = (bf16[1152,128]{1,0:T(8,128)(2,1)S(1)}, bf16[1152,128]{1,0:T(8,128)(2,1)}, u32[]{:S(2)}, u32[]{:S(2)}) collective-permute-start(bf16[1152,128]{1,0:T(8,128)(2,1)S(1)} %collective-permute-done.1.refs_1_), channel_id=1, source_target_pairs={{0,1},{1,0},{2,3},{3,2},{4,5},{5,4},{6,7},{7,6},{8,9},{9,8},{10,11... | collective-permute-start | bytes 884744 | tf_op jit(solution)/shard_map/ppermute | solution.py:295
  15.9 2.0 %collective-permute-start.4 = (bf16[1152,128]{1,0:T(8,128)(2,1)S(1)}, bf16[1152,128]{1,0:T(8,128)(2,1)}, u32[]{:S(2)}, u32[]{:S(2)}) collective-permute-start(bf16[1152,128]{1,0:T(8,128)(2,1)S(1)} %collective-permute-done.2.refs_2_), channel_id=1, source_target_pairs={{0,1},{1,0},{2,3},{3,2},{4,5},{5,4},{6,7},{7,6},{8,9},{9,8},{10,11... | collective-permute-start | bytes 884744 | tf_op jit(solution)/shard_map/ppermute | solution.py:295
  16.4 7.9 %collective-permute-start.6 = (bf16[576,128]{1,0:T(8,128)(2,1)S(1)}, bf16[576,128]{1,0:T(8,128)(2,1)S(1)}, u32[]{:S(2)}, u32[]{:S(2)}) collective-permute-start(bf16[576,128]{1,0:T(8,128)(2,1)S(1)} %slice.80), channel_id=1, source_target_pairs={{0,64},{1,193},{32,96},{33,225},{64,128},{65,1},{96,160},{97,33},{... | collective-permute-start | bytes 442376 | tf_op jit(solution)/shard_map/ppermute | solution.py:305
  16.5 7.9 %collective-permute-start.5 = (bf16[576,128]{1,0:T(8,128)(2,1)S(1)}, bf16[576,128]{1,0:T(8,128)(2,1)S(1)}, u32[]{:S(2)}, u32[]{:S(2)}) collective-permute-start(bf16[576,128]{1,0:T(8,128)(2,1)S(1)} %slice.79), channel_id=1, source_target_pairs={{0,64},{1,193},{32,96},{33,225},{64,128},{65,1},{96,160},{97,33},{... | collective-permute-start | bytes 442376 | tf_op jit(solution)/shard_map/ppermute | solution.py:305
  17.9 0.7 copy-start.2
  18.6 0.7 copy-start.3
  19.2 7.1 %copy-start.4 = (s32[8]{0:T(128)S(1)}, s32[8]{0:T(128)}, u32[]{:S(2)}) copy-start(s32[8]{0:T(128)} %key_blocks_ref.3) | copy-start | bytes 100
  24.4 1.4 %collective-permute-start.7 = (bf16[576,128]{1,0:T(8,128)(2,1)S(1)}, bf16[576,128]{1,0:T(8,128)(2,1)S(1)}, u32[]{:S(2)}, u32[]{:S(2)}) collective-permute-start(bf16[576,128]{1,0:T(8,128)(2,1)S(1)} %collective-permute-done.refs_5_), channel_id=1, source_target_pairs={{0,1},{1,0},{2,3},{3,2},{4,5},{5,4},{6,7},{7,6},{8,9},{9,8},{10,11... | collective-permute-start | bytes 442376 | tf_op jit(solution)/shard_map/ppermute | solution.py:295
  24.5 1.5 %collective-permute-start.8 = (bf16[576,128]{1,0:T(8,128)(2,1)S(1)}, bf16[576,128]{1,0:T(8,128)(2,1)S(1)}, u32[]{:S(2)}, u32[]{:S(2)}) collective-permute-start(bf16[576,128]{1,0:T(8,128)(2,1)S(1)} %collective-permute-done.5.refs_6_), channel_id=1, source_target_pairs={{0,1},{1,0},{2,3},{3,2},{4,5},{5,4},{6,7},{7,6},{8,9},{9,8},{10,11... | collective-permute-start | bytes 442376 | tf_op jit(solution)/shard_map/ppermute | solution.py:295
  24.9 1.4 %collective-permute-start.9 = (bf16[576,128]{1,0:T(8,128)(2,1)S(1)}, bf16[576,128]{1,0:T(8,128)(2,1)S(1)}, u32[]{:S(2)}, u32[]{:S(2)}) collective-permute-start(bf16[576,128]{1,0:T(8,128)(2,1)S(1)} %collective-permute-done.6.refs_7_), channel_id=1, source_target_pairs={{0,1},{1,0},{2,3},{3,2},{4,5},{5,4},{6,7},{7,6},{8,9},{9,8},{10,11... | collective-permute-start | bytes 442376 | tf_op jit(solution)/shard_map/ppermute | solution.py:295
  38.7 3.8 %collective-permute-start.10 = (bf16[4,4,2,144,128]{4,3,2,1,0:T(8,128)(2,1)S(1)}, bf16[4,4,2,144,128]{4,3,2,1,0:T(8,128)(2,1)S(1)}, u32[]{:S(2)}, u32[]{:S(2)}) collective-permute-start(bf16[4,4,2,144,128]{4,3,2,1,0:T(8,128)(2,1)S(1)} %get-tuple-element.35), channel_id=1, source_target_pairs={{0,1},{1,0},{2,3},{3,2},{4,5},{5,4},{6,7},{7,6},{8,9},{9,8},{10,11... | collective-permute-start | bytes 3538952 | tf_op jit(solution)/shard_map/ppermute | solution.py:295
  42.7 8.3 %collective-permute-start.11 = (bf16[4,2,144,128]{3,2,1,0:T(8,128)(2,1)S(1)}, bf16[4,2,144,128]{3,2,1,0:T(8,128)(2,1)S(1)}, u32[]{:S(2)}, u32[]{:S(2)}) collective-permute-start(bf16[4,2,144,128]{3,2,1,0:T(8,128)(2,1)S(1)} %get-tuple-element.38), channel_id=1, source_target_pairs={{0,16},{1,129},{8,24},{9,137},{16,0},{17,145},{24,8},{25,153},{64,... | collective-permute-start | bytes 884744 | tf_op jit(solution)/shard_map/ppermute | solution.py:317
  45.8 8.5 %collective-permute-start.13 = (bf16[4,2,144,128]{3,2,1,0:T(8,128)(2,1)S(1)}, bf16[4,2,144,128]{3,2,1,0:T(8,128)(2,1)S(1)}, u32[]{:S(2)}, u32[]{:S(2)}) collective-permute-start(bf16[4,2,144,128]{3,2,1,0:T(8,128)(2,1)S(1)} %get-tuple-element.39), channel_id=1, source_target_pairs={{0,24},{1,193},{8,0},{9,201},{16,8},{17,209},{24,16},{25,217},{64,... | collective-permute-start | bytes 884744 | tf_op jit(solution)/shard_map/ppermute | solution.py:317
  46.9 7.9 %collective-permute-start.12 = (bf16[4,2,144,128]{3,2,1,0:T(8,128)(2,1)S(1)}, bf16[4,2,144,128]{3,2,1,0:T(8,128)(2,1)S(1)}, u32[]{:S(2)}, u32[]{:S(2)}) collective-permute-start(bf16[4,2,144,128]{3,2,1,0:T(8,128)(2,1)S(1)} %get-tuple-element.40), channel_id=1, source_target_pairs={{0,8},{1,65},{8,16},{9,73},{16,24},{17,81},{24,0},{25,89},{64,72},... | collective-permute-start | bytes 884744 | tf_op jit(solution)/shard_map/ppermute | solution.py:317
  55.1 5.9 %collective-permute-start.14 = (bf16[2,144,128]{2,1,0:T(8,128)(2,1)S(1)}, bf16[2,144,128]{2,1,0:T(8,128)(2,1)S(1)}, u32[]{:S(2)}, u32[]{:S(2)}) collective-permute-start(bf16[2,144,128]{2,1,0:T(8,128)(2,1)S(1)} %get-tuple-element.41), channel_id=1, source_target_pairs={{0,128},{1,17},{8,136},{9,25},{16,144},{17,1},{24,152},{25,9},{64,... | collective-permute-start | bytes 221192 | tf_op jit(solution)/shard_map/ppermute | solution.py:317
  58.4 4.4 %collective-permute-start.16 = (bf16[2,144,128]{2,1,0:T(8,128)(2,1)S(1)}, bf16[2,144,128]{2,1,0:T(8,128)(2,1)S(1)}, u32[]{:S(2)}, u32[]{:S(2)}) collective-permute-start(bf16[2,144,128]{2,1,0:T(8,128)(2,1)S(1)} %get-tuple-element.42), channel_id=1, source_target_pairs={{0,192},{1,25},{8,200},{9,1},{16,208},{17,9},{24,216},{25,17},{64,... | collective-permute-start | bytes 221192 | tf_op jit(solution)/shard_map/ppermute | solution.py:317
  59.2 5.6 %collective-permute-start.15 = (bf16[2,144,128]{2,1,0:T(8,128)(2,1)S(1)}, bf16[2,144,128]{2,1,0:T(8,128)(2,1)S(1)}, u32[]{:S(2)}, u32[]{:S(2)}) collective-permute-start(bf16[2,144,128]{2,1,0:T(8,128)(2,1)S(1)} %get-tuple-element.43), channel_id=1, source_target_pairs={{0,64},{1,9},{8,72},{9,17},{16,80},{17,25},{24,88},{25,1},{64,128}... | collective-permute-start | bytes 221192 | tf_op jit(solution)/shard_map/ppermute | solution.py:317

commit v9 on v7

--- a/solution.py
+++ b/solution.py
@@ -24,8 +24,6 @@
 PACKED = OWNED * DK // LANES
 MAIN_VMEM = 23 * 1024 * 1024
 FIRST = 3
-WHOLE = 5
-SWAPPED = (3, 4)
 
 softmax_scale = 0.07216878364870322
 
@@ -61,15 +59,7 @@
 
 
 def halves(refs):
-    out = []
-    for slot in range(min(WHOLE, len(refs))):
-        flip = slot in SWAPPED
-        blocks = [refs[slot][n * DK : (n + 1) * DK, :] for n in range(2)]
-        out.append(blocks[::-1] if flip else blocks)
-    rest = refs[WHOLE:]
-    for slot in range(len(rest) // 2):
-        out.append([rest[slot][...], rest[slot + len(rest) // 2][...]])
-    return out
+    return [[ref[...] for ref in refs[2 * n : 2 * n + 2]] for n in range(len(refs) // 2)]
 
 
 def offsets():
@@ -96,9 +86,9 @@
 
 
 def first_kernel(place_ref, query_blocks_ref, key_blocks_ref, qt_ref, go_ref, *refs):
-    e_ref, gp_ref, stat_ref, gl_ref, gr_ref, got_ref, k_s = refs[FIRST:]
+    e_ref, gp_ref, stat_ref, gl_ref, gr_ref, got_ref, k_s = refs[2 * FIRST :]
     limits = positions(place_ref, query_blocks_ref, key_blocks_ref)
-    for slot, pair in enumerate(halves(refs[:FIRST])):
+    for slot, pair in enumerate(halves(refs[: 2 * FIRST])):
         for b in range(2):
             at = slot * TILE + b * HALF
             k_s[at : at + HALF, :] = pair[b].T
@@ -149,7 +139,7 @@
 
 
 def main_kernel(place_ref, query_blocks_ref, key_blocks_ref, qt_ref, *refs):
-    k_refs, refs = refs[: 2 * NG - WHOLE], refs[2 * NG - WHOLE :]
+    k_refs, refs = refs[: 2 * NG], refs[2 * NG :]
     e1_ref, gp1_ref, stat_ref, gl_ref, gr_ref, got_ref = refs[:6]
     dqt_ref, own_w_ref, other_ref, kt_s, k_s, e_s, gp_s, other_w_s = refs[6:]
     limits = positions(place_ref, query_blocks_ref, key_blocks_ref)
@@ -245,7 +235,7 @@
     ]
     return pl.pallas_call(
         first_kernel,
-        in_specs=[SMEM] * 3 + [VMEM] * (2 + FIRST),
+        in_specs=[SMEM] * 3 + [VMEM] * (2 + 2 * FIRST),
         out_specs=[VMEM] * len(shapes),
         out_shape=[jax.ShapeDtypeStruct(*s) for s in shapes],
         scratch_shapes=[pltpu.VMEM((FIRST * TILE, DK), BF)],
@@ -333,21 +323,26 @@
     here = lax.dot_general(
         latent_cache, pick, (((0,), (0,)), ((), ())), preferred_element_type=F32
     ).astype(BF)
-    here = jnp.concatenate([here[:, :HALF], here[:, HALF:]], axis=0)
-
-    near = onward(here, 0)
-    slant = onward(here, 1)
-    beside = lax.ppermute(here[:DK], "zl", [(0, 1), (1, 0)])
-
+    mine, rest = here[:, :HALF], here[:, HALF:]
+
+    slant = [onward(mine, 1)]
+    near = [onward(mine, 0)]
+    beside = lax.ppermute(mine, "zl", [(0, 1), (1, 0)])
+    slant.append(onward(rest, 1))
+    near.append(onward(rest, 0))
     place = jnp.stack([core, y, zl, x])
+
     qt = queries.transpose(1, 2, 0)
     go = grad_output.transpose(1, 0, 2)
-    go, near, slant = lax.optimization_barrier((go, near, slant))
-    singles = [beside, onward(near[:DK], 0), onward(slant[:DK], 0)]
-    swapped = [swap_cores(near), swap_cores(slant)]
-    early = list(first_part(place, query_blocks, key_blocks, qt, go, [here, near, slant]))
-    early[2], *singles = lax.optimization_barrier((early[2], *singles))
-    blocks = [here, near, slant] + swapped + singles + [swap_cores(k) for k in singles]
+    far = [onward(near[0], 0), onward(slant[0], 0)]
+    blocks = [mine, rest] + near + slant
+    early = list(first_part(place, query_blocks, key_blocks, qt, go, blocks))
+    early[2], beside, *whole = lax.optimization_barrier((early[2], beside, *near, *slant))
+    for pair in (whole[:2], whole[2:]):
+        blocks += [swap_cores(pair[1]), swap_cores(pair[0])]
+    early[2], *far = lax.optimization_barrier((early[2], *far))
+    for k in [beside] + far:
+        blocks += [k, swap_cores(k)]
     dqt, weights, other = main_part(place, query_blocks, key_blocks, qt, blocks, early)
     other = swap_cores(other)
     own = own_part(place, weights, early[3], early[4])

time: 79 us -> 76.1 us (0.963)
  waiting for transfers between devices: 22.3 us -> 15.6 us
  starting transfers between devices: 15.9 us -> 19.5 us
    ppermute x4 -> x6, waiting for transfers between devices: 9.2 us -> 2.52 us  [onward(): return lax.ppermute(x, ('y', 'zl', 'c'), pairs)]
    ppermute x4 -> x6, starting transfers between devices: 4.48 us -> 6.8 us  [onward(): return lax.ppermute(x, ('y', 'zl', 'c'), pairs)]
    ppermute x6 -> x8, starting transfers between devices: 1.7 us -> 2.28 us  [swap_cores(): return lax.ppermute(x, 'c', [(0, 1), (1, 0)])]
  transfers between devices with their start and end apart: 17 -> 21, of which waited for: 12 -> 13; matrix products, arithmetic and copies ran while one was open for 2% -> 2% of each run, Pallas kernels for 8% -> 9%
where the time goes in v9:
time: 76.1 us; the launch traced here: 76 us
  Pallas kernels  20.2 us (27%)
  starting transfers between devices  19.5 us (26%)
  blocking collectives  15.9 us (21%)
  waiting for transfers between devices  15.6 us (20%)
  local copies, waits for them, and re-layouts  2.57 us (3%)
  other arithmetic  1.17 us (2%)
  between operations  0.81 us (1%)
    all_to_all x1, blocking collectives, shards(): got = lax.all_to_all(part, ('zl', 'zh'), 0, 0, tiled=True)  15.9 us
    pallas_call x1, Pallas kernels, main_part(): pl.pallas_call(main_kernel, in_specs=[SMEM] * 3 + [VMEM] * (1 + len(k_blo...  13.5 us
    ppermute x6, waiting for transfers between devices, crossed(): return lax.ppermute(x, ('y', 'x', 'c'), [(n, target(n)) for n in range(32)])  11.7 us
    ppermute x6, starting transfers between devices, crossed(): return lax.ppermute(x, ('y', 'x', 'c'), [(n, target(n)) for n in range(32)])  8.58 us
    ppermute x6, starting transfers between devices, onward(): return lax.ppermute(x, ('y', 'zl', 'c'), pairs)  6.8 us
    pallas_call x1, Pallas kernels, own_part(): pl.pallas_call(own_kernel, in_specs=[SMEM] + [VMEM] * 3, out_specs=VMEM,...  3.52 us
    pallas_call x1, Pallas kernels, first_part(): pl.pallas_call(first_kernel, in_specs=[SMEM] * 3 + [VMEM] * (2 + 2 * FIRS...  3.19 us
    ppermute x6, waiting for transfers between devices, onward(): return lax.ppermute(x, ('y', 'zl', 'c'), pairs)  2.52 us
  transfers between devices with their start and end apart: 21, of which 13 were waited for; matrix products, arithmetic and copies ran while one was open for 2% of the time, Pallas kernels for 9%

profile of v9, /device:TPU:32, one launch (start us, length us, event | category | flops | bytes accessed | tf_op | source)
XLA Modules:
  0.0 76.0 jit_solution(11562746462680562412)
XLA Ops:
  0.6 0.0 copy-start
  0.6 0.0 copy-start.3
  0.7 0.0 copy-start.2
  0.7 0.0 copy-start.1
  0.7 0.9 %copy-done = bf16[256,576]{0,1:T(8,128)(2,1)S(1)} copy-done((bf16[256,576]{0,1:T(8,128)(2,1)S(1)}, bf16[256,576]{0,1:T(8,128)(2,1)}, u32[]{:S(2)}) %copy-start) | copy-done | bytes 294936
  1.6 0.2 fusion
  1.9 1.2 %collective-permute-start.2 = (bf16[576,128]{1,0:T(8,128)(2,1)S(1)}, bf16[576,128]{1,0:T(8,128)(2,1)S(1)}, u32[]{:S(2)}, u32[]{:S(2)}) collective-permute-start(bf16[576,128]{1,0:T(8,128)(2,1)S(1)} %get-tuple-element.47.refs_0_), channel_id=1, source_target_pairs={{0,96},{1,225},{32,64},{33,193},{64,160},{65,33},{96,128},{97,1},{... | collective-permute-start | bytes 442376 | tf_op jit(solution)/shard_map/ppermute | solution.py:295
  3.1 1.6 %collective-permute-start = (bf16[576,128]{1,0:T(8,128)(2,1)S(1)}, bf16[576,128]{1,0:T(8,128)(2,1)S(1)}, u32[]{:S(2)}, u32[]{:S(2)}) collective-permute-start(bf16[576,128]{1,0:T(8,128)(2,1)S(1)} %get-tuple-element.47.refs_0_), channel_id=1, source_target_pairs={{0,64},{1,193},{32,96},{33,225},{64,128},{65,1},{96,160},{97,33},{... | collective-permute-start | bytes 442376 | tf_op jit(solution)/shard_map/ppermute | solution.py:295
  4.7 2.6 %collective-permute-start.3 = (bf16[576,128]{1,0:T(8,128)(2,1)S(1)}, bf16[576,128]{1,0:T(8,128)(2,1)S(1)}, u32[]{:S(2)}, u32[]{:S(2)}) collective-permute-start(bf16[576,128]{1,0:T(8,128)(2,1)S(1)} %get-tuple-element.46.refs_1_), channel_id=1, source_target_pairs={{0,96},{1,225},{32,64},{33,193},{64,160},{65,33},{96,128},{97,1},{... | collective-permute-start | bytes 442376 | tf_op jit(solution)/shard_map/ppermute | solution.py:295
  7.3 0.2 collective-permute-start.1
  7.5 1.8 %collective-permute-start.4 = (bf16[576,128]{1,0:T(8,128)(2,1)S(1)}, bf16[576,128]{1,0:T(8,128)(2,1)S(1)}, u32[]{:S(2)}, u32[]{:S(2)}) collective-permute-start(bf16[576,128]{1,0:T(8,128)(2,1)S(1)} %get-tuple-element.47.refs_0_), channel_id=1, source_target_pairs={{0,32},{32,0},{1,33},{33,1},{2,34},{34,2},{3,35},{35,3},{4,36},{36... | collective-permute-start | bytes 442376 | tf_op jit(solution)/shard_map/ppermute | solution.py:330
  9.4 1.4 %copy.16 = bf16[256,4,512]{2,0,1:T(8,128)(2,1)S(1)} copy(bf16[256,4,512]{2,1,0:T(4,128)(2,1)} %param.7) | data formatting | bytes 2097152 | tf_op args[2]
  10.8 0.1 pad_add_fusion.place_ref
  10.9 0.0 collective-permute-done.2.refs_4_
  10.9 0.0 collective-permute-start.11
  10.9 0.3 collective-permute-done.refs_2_
  11.2 1.1 %collective-permute-start.10 = (bf16[576,128]{1,0:T(8,128)(2,1)S(1)}, bf16[576,128]{1,0:T(8,128)(2,1)S(1)}, u32[]{:S(2)}, u32[]{:S(2)}) collective-permute-start(bf16[576,128]{1,0:T(8,128)(2,1)S(1)} %collective-permute-done.refs_2_), channel_id=1, source_target_pairs={{0,64},{1,193},{32,96},{33,225},{64,128},{65,1},{96,160},{97,33},{... | collective-permute-start | bytes 442376 | tf_op jit(solution)/shard_map/ppermute | solution.py:295
  12.3 1.6 %collective-permute-done.3.refs_5_ = bf16[576,128]{1,0:T(8,128)(2,1)S(1)} collective-permute-done((bf16[576,128]{1,0:T(8,128)(2,1)S(1)}, bf16[576,128]{1,0:T(8,128)(2,1)S(1)}, u32[]{:S(2)}, u32[]{:S(2)}) %collective-permute-start.3) | collective-permute-done | bytes 147488 | tf_op jit(solution)/shard_map/ppermute | solution.py:295
  13.9 0.7 collective-permute-done.1.refs_3_
  14.6 0.0 copy-done.3
  14.6 0.0 copy-done.2
  14.6 0.0 copy-done.1
  14.6 3.2 %shard_map.68 = (f32[4,768,256]{2,1,0:T(8,128)S(1)}, f32[4,768,256]{2,1,0:T(8,128)S(1)}, f32[2,4,8,256]{3,2,1,0:T(8,128)S(1)}, bf16[2048,512]{1,0:T(8,128)(2,1)S...) custom-call(s32[4]{0:T(128)S(1)} %pad_add_fusion.place_ref, s32[8]{0:T(128)S(1)} %copy-done.2, ...), custom_call_target="tpu_custom_call" | custom-call | flops 1711276032 | bytes 20000000 | tf_op jit(solution)/shard_map/pallas_call | solution.py:236
  17.8 0.0 collective-permute-done.4.refs_10_
  17.8 0.1 collective-permute-start.5
  17.9 0.5 collective-permute-start.6
  18.4 0.1 collective-permute-start.7
  18.5 0.0 collective-permute-done.11.refs_14_
  18.5 0.4 collective-permute-start.8
  18.9 0.0 collective-permute-done.10.refs_12_
  18.9 0.1 collective-permute-start.9
  19.0 0.2 collective-permute-done.5.refs_6_
  19.2 0.2 collective-permute-start.12
  19.4 0.0 collective-permute-done.6.refs_7_
  19.5 0.3 collective-permute-start.13
  19.8 0.0 collective-permute-done.7.refs_8_
  19.8 0.2 collective-permute-done.8.refs_9_
  20.0 0.3 collective-permute-done.9.refs_11_
  20.3 0.3 collective-permute-done.12.refs_13_
  20.6 0.2 collective-permute-done.13.refs_15_
  20.8 13.5 %shard_map.69 = (bf16[4,576,256]{2,1,0:T(8,128)(2,1)}, bf16[1024,2048]{1,0:T(8,128)(2,1)S(1)}, bf16[4,4,2,144,128]{4,3,2,1,0:T(8,128)(2,1)S(1)}) custom-call(s32[4]{0:T(128)S(1)} %pad_add_fusion.place_ref, s32[8]{0:T(128)S(1)} %copy-done.2, s32[8]{0:T(128)S(1)} %copy-done.3, bf16[4,576,256]{2,1,0:T(8,128)(2,1)S(1)} %bitcast.52, ...), custom_call_target="tpu_custom_call" | custom-call | tf_op jit(solution)/shard_map/pallas_call | solution.py:251
  34.3 0.6 collective-permute-start.14
  34.9 3.5 %shard_map.70 = f32[4,4,2,144,128]{4,3,2,1,0:T(8,128)S(1)} custom-call(s32[4]{0:T(128)S(1)} %pad_add_fusion.place_ref, bf16[1024,2048]{1,0:T(8,128)(2,1)S(1)} %get-tuple-element.36.w_ref, bf16[2048,512]{1,0:T(8,128)(2,1)S(1)} %get-tuple-element.32.refs_19_.gl_ref, bf16[1024,64]{1,0:T(8,128)(2,1)S(1)} %get-tuple-element.33.refs_20_.gr_ref), custom_call_target="tpu_custom_call" | custom-call | flops 2415919104 | bytes 9000000 | tf_op jit(solution)/shard_map/pallas_call | solution.py:272
  38.5 0.0 collective-permute-done.14
  38.5 0.2 fusion.6
  38.7 3.1 %collective-permute-start.15 = (bf16[4,2,144,128]{3,2,1,0:T(8,128)(2,1)S(1)}, bf16[4,2,144,128]{3,2,1,0:T(8,128)(2,1)S(1)}, u32[]{:S(2)}, u32[]{:S(2)}) collective-permute-start(bf16[4,2,144,128]{3,2,1,0:T(8,128)(2,1)S(1)} %get-tuple-element.40), channel_id=1, source_target_pairs={{0,16},{1,129},{8,24},{9,137},{16,0},{17,145},{24,8},{25,153},{64,... | collective-permute-start | bytes 884744 | tf_op jit(solution)/shard_map/ppermute | solution.py:307
  41.8 1.1 %collective-permute-start.17 = (bf16[4,2,144,128]{3,2,1,0:T(8,128)(2,1)S(1)}, bf16[4,2,144,128]{3,2,1,0:T(8,128)(2,1)S(1)}, u32[]{:S(2)}, u32[]{:S(2)}) collective-permute-start(bf16[4,2,144,128]{3,2,1,0:T(8,128)(2,1)S(1)} %get-tuple-element.41), channel_id=1, source_target_pairs={{0,24},{1,193},{8,0},{9,201},{16,8},{17,209},{24,16},{25,217},{64,... | collective-permute-start | bytes 884744 | tf_op jit(solution)/shard_map/ppermute | solution.py:307
  42.9 0.9 %collective-permute-start.16 = (bf16[4,2,144,128]{3,2,1,0:T(8,128)(2,1)S(1)}, bf16[4,2,144,128]{3,2,1,0:T(8,128)(2,1)S(1)}, u32[]{:S(2)}, u32[]{:S(2)}) collective-permute-start(bf16[4,2,144,128]{3,2,1,0:T(8,128)(2,1)S(1)} %get-tuple-element.42), channel_id=1, source_target_pairs={{0,8},{1,65},{8,16},{9,73},{16,24},{17,81},{24,0},{25,89},{64,72},... | collective-permute-start | bytes 884744 | tf_op jit(solution)/shard_map/ppermute | solution.py:307
  43.8 3.2 %collective-permute-done.15 = bf16[4,2,144,128]{3,2,1,0:T(8,128)(2,1)S(1)} collective-permute-done((bf16[4,2,144,128]{3,2,1,0:T(8,128)(2,1)S(1)}, bf16[4,2,144,128]{3,2,1,0:T(8,128)(2,1)S(1)}, u32[]{:S(2)}, u32[]{:S(2)}) %collective-permute-start.15) | collective-permute-done | bytes 294944 | tf_op jit(solution)/shard_map/ppermute | solution.py:307
  47.0 3.3 %collective-permute-done.17 = bf16[4,2,144,128]{3,2,1,0:T(8,128)(2,1)S(1)} collective-permute-done((bf16[4,2,144,128]{3,2,1,0:T(8,128)(2,1)S(1)}, bf16[4,2,144,128]{3,2,1,0:T(8,128)(2,1)S(1)}, u32[]{:S(2)}, u32[]{:S(2)}) %collective-permute-start.17) | collective-permute-done | bytes 294944 | tf_op jit(solution)/shard_map/ppermute | solution.py:307
  50.3 0.6 collective-permute-done.16
  50.9 0.2 fusion.12
  51.1 1.4 %collective-permute-start.18 = (bf16[2,144,128]{2,1,0:T(8,128)(2,1)S(1)}, bf16[2,144,128]{2,1,0:T(8,128)(2,1)S(1)}, u32[]{:S(2)}, u32[]{:S(2)}) collective-permute-start(bf16[2,144,128]{2,1,0:T(8,128)(2,1)S(1)} %get-tuple-element.43), channel_id=1, source_target_pairs={{0,128},{1,17},{8,136},{9,25},{16,144},{17,1},{24,152},{25,9},{64,... | collective-permute-start | bytes 221192 | tf_op jit(solution)/shard_map/ppermute | solution.py:307
  52.5 1.1 %collective-permute-start.20 = (bf16[2,144,128]{2,1,0:T(8,128)(2,1)S(1)}, bf16[2,144,128]{2,1,0:T(8,128)(2,1)S(1)}, u32[]{:S(2)}, u32[]{:S(2)}) collective-permute-start(bf16[2,144,128]{2,1,0:T(8,128)(2,1)S(1)} %get-tuple-element.44), channel_id=1, source_target_pairs={{0,192},{1,25},{8,200},{9,1},{16,208},{17,9},{24,216},{25,17},{64,... | collective-permute-start | bytes 221192 | tf_op jit(solution)/shard_map/ppermute | solution.py:307
  53.6 0.9 %collective-permute-start.19 = (bf16[2,144,128]{2,1,0:T(8,128)(2,1)S(1)}, bf16[2,144,128]{2,1,0:T(8,128)(2,1)S(1)}, u32[]{:S(2)}, u32[]{:S(2)}) collective-permute-start(bf16[2,144,128]{2,1,0:T(8,128)(2,1)S(1)} %get-tuple-element.45), channel_id=1, source_target_pairs={{0,64},{1,9},{8,72},{9,17},{16,80},{17,25},{24,88},{25,1},{64,128}... | collective-permute-start | bytes 221192 | tf_op jit(solution)/shard_map/ppermute | solution.py:307
  54.5 2.5 %collective-permute-done.18 = bf16[2,144,128]{2,1,0:T(8,128)(2,1)S(1)} collective-permute-done((bf16[2,144,128]{2,1,0:T(8,128)(2,1)S(1)}, bf16[2,144,128]{2,1,0:T(8,128)(2,1)S(1)}, u32[]{:S(2)}, u32[]{:S(2)}) %collective-permute-start.18) | collective-permute-done | bytes 73760 | tf_op jit(solution)/shard_map/ppermute | solution.py:307
  57.0 0.0 collective-permute-done.20
  57.0 2.1 %collective-permute-done.19 = bf16[2,144,128]{2,1,0:T(8,128)(2,1)S(1)} collective-permute-done((bf16[2,144,128]{2,1,0:T(8,128)(2,1)S(1)}, bf16[2,144,128]{2,1,0:T(8,128)(2,1)S(1)}, u32[]{:S(2)}, u32[]{:S(2)}) %collective-permute-start.19) | collective-permute-done | bytes 73760 | tf_op jit(solution)/shard_map/ppermute | solution.py:307
  59.3 0.1 reshape.60
  59.3 0.1 reshape.64
  59.5 15.9 %all_to_all.5 = bf16[8,8,576]{2,1,0:T(8,128)(2,1)S(1)} all-to-all(bf16[8,8,576]{2,1,0:T(8,128)(2,1)S(1)} %maximum_maximum_fusion), channel_id=1, replica_groups=mesh['y'=4,'zl'=2,'x'=4,'zh'=4,'c'=2] {'zl','zh'}, dimensions={0} | all-to-all | bytes 147456 | tf_op jit(solution)/shard_map/all_to_all | solution.py:355
  75.3 0.6 convert_reduce_fusion
  (10 shorter events, 0.1 us)
Async XLA Ops:
  0.6 1.0 %copy-start = (bf16[256,576]{0,1:T(8,128)(2,1)S(1)}, bf16[256,576]{0,1:T(8,128)(2,1)}, u32[]{:S(2)}) copy-start(bf16[256,576]{0,1:T(8,128)(2,1)} %param.6) | copy-start | bytes 884740
  0.6 13.9 %copy-start.3 = (s32[8]{0:T(128)S(1)}, s32[8]{0:T(128)}, u32[]{:S(2)}) copy-start(s32[8]{0:T(128)} %key_blocks_ref.3) | copy-start | bytes 100
  0.7 13.9 %copy-start.2 = (s32[8]{0:T(128)S(1)}, s32[8]{0:T(128)}, u32[]{:S(2)}) copy-start(s32[8]{0:T(128)} %query_blocks_ref.3) | copy-start | bytes 100
  0.7 13.9 %copy-start.1 = (bf16[256,4,576]{0,2,1:T(8,128)(2,1)S(1)}, bf16[256,4,576]{0,2,1:T(8,128)(2,1)}, u32[]{:S(2)}) copy-start(bf16[256,4,576]{0,2,1:T(8,128)(2,1)} %param.5) | copy-start | bytes 3538948
  1.9 9.0 %collective-permute-start.2 = (bf16[576,128]{1,0:T(8,128)(2,1)S(1)}, bf16[576,128]{1,0:T(8,128)(2,1)S(1)}, u32[]{:S(2)}, u32[]{:S(2)}) collective-permute-start(bf16[576,128]{1,0:T(8,128)(2,1)S(1)} %get-tuple-element.47.refs_0_), channel_id=1, source_target_pairs={{0,96},{1,225},{32,64},{33,193},{64,160},{65,33},{96,128},{97,1},{... | collective-permute-start | bytes 442376 | tf_op jit(solution)/shard_map/ppermute | solution.py:295
  3.1 8.1 %collective-permute-start = (bf16[576,128]{1,0:T(8,128)(2,1)S(1)}, bf16[576,128]{1,0:T(8,128)(2,1)S(1)}, u32[]{:S(2)}, u32[]{:S(2)}) collective-permute-start(bf16[576,128]{1,0:T(8,128)(2,1)S(1)} %get-tuple-element.47.refs_0_), channel_id=1, source_target_pairs={{0,64},{1,193},{32,96},{33,225},{64,128},{65,1},{96,160},{97,33},{... | collective-permute-start | bytes 442376 | tf_op jit(solution)/shard_map/ppermute | solution.py:295
  4.7 9.2 %collective-permute-start.3 = (bf16[576,128]{1,0:T(8,128)(2,1)S(1)}, bf16[576,128]{1,0:T(8,128)(2,1)S(1)}, u32[]{:S(2)}, u32[]{:S(2)}) collective-permute-start(bf16[576,128]{1,0:T(8,128)(2,1)S(1)} %get-tuple-element.46.refs_1_), channel_id=1, source_target_pairs={{0,96},{1,225},{32,64},{33,193},{64,160},{65,33},{96,128},{97,1},{... | collective-permute-start | bytes 442376 | tf_op jit(solution)/shard_map/ppermute | solution.py:295
  7.3 7.3 %collective-permute-start.1 = (bf16[576,128]{1,0:T(8,128)(2,1)S(1)}, bf16[576,128]{1,0:T(8,128)(2,1)S(1)}, u32[]{:S(2)}, u32[]{:S(2)}) collective-permute-start(bf16[576,128]{1,0:T(8,128)(2,1)S(1)} %get-tuple-element.46.refs_1_), channel_id=1, source_target_pairs={{0,64},{1,193},{32,96},{33,225},{64,128},{65,1},{96,160},{97,33},{... | collective-permute-start | bytes 442376 | tf_op jit(solution)/shard_map/ppermute | solution.py:295
  7.5 10.3 %collective-permute-start.4 = (bf16[576,128]{1,0:T(8,128)(2,1)S(1)}, bf16[576,128]{1,0:T(8,128)(2,1)S(1)}, u32[]{:S(2)}, u32[]{:S(2)}) collective-permute-start(bf16[576,128]{1,0:T(8,128)(2,1)S(1)} %get-tuple-element.47.refs_0_), channel_id=1, source_target_pairs={{0,32},{32,0},{1,33},{33,1},{2,34},{34,2},{3,35},{35,3},{4,36},{36... | collective-permute-start | bytes 442376 | tf_op jit(solution)/shard_map/ppermute | solution.py:330
  10.9 7.6 %collective-permute-start.11 = (bf16[576,128]{1,0:T(8,128)(2,1)S(1)}, bf16[576,128]{1,0:T(8,128)(2,1)S(1)}, u32[]{:S(2)}, u32[]{:S(2)}) collective-permute-start(bf16[576,128]{1,0:T(8,128)(2,1)S(1)} %collective-permute-done.2.refs_4_), channel_id=1, source_target_pairs={{0,64},{1,193},{32,96},{33,225},{64,128},{65,1},{96,160},{97,33},{... | collective-permute-start | bytes 442376 | tf_op jit(solution)/shard_map/ppermute | solution.py:295
  11.2 7.7 %collective-permute-start.10 = (bf16[576,128]{1,0:T(8,128)(2,1)S(1)}, bf16[576,128]{1,0:T(8,128)(2,1)S(1)}, u32[]{:S(2)}, u32[]{:S(2)}) collective-permute-start(bf16[576,128]{1,0:T(8,128)(2,1)S(1)} %collective-permute-done.refs_2_), channel_id=1, source_target_pairs={{0,64},{1,193},{32,96},{33,225},{64,128},{65,1},{96,160},{97,33},{... | collective-permute-start | bytes 442376 | tf_op jit(solution)/shard_map/ppermute | solution.py:295
  17.8 1.5 %collective-permute-start.5 = (bf16[576,128]{1,0:T(8,128)(2,1)S(1)}, bf16[576,128]{1,0:T(8,128)(2,1)S(1)}, u32[]{:S(2)}, u32[]{:S(2)}) collective-permute-start(bf16[576,128]{1,0:T(8,128)(2,1)S(1)} %collective-permute-done.1.refs_3_), channel_id=1, source_target_pairs={{0,1},{1,0},{2,3},{3,2},{4,5},{5,4},{6,7},{7,6},{8,9},{9,8},{10,11... | collective-permute-start | bytes 442376 | tf_op jit(solution)/shard_map/ppermute | solution.py:285
  17.9 1.6 %collective-permute-start.6 = (bf16[576,128]{1,0:T(8,128)(2,1)S(1)}, bf16[576,128]{1,0:T(8,128)(2,1)S(1)}, u32[]{:S(2)}, u32[]{:S(2)}) collective-permute-start(bf16[576,128]{1,0:T(8,128)(2,1)S(1)} %collective-permute-done.refs_2_), channel_id=1, source_target_pairs={{0,1},{1,0},{2,3},{3,2},{4,5},{5,4},{6,7},{7,6},{8,9},{9,8},{10,11... | collective-permute-start | bytes 442376 | tf_op jit(solution)/shard_map/ppermute | solution.py:285
  18.4 1.4 %collective-permute-start.7 = (bf16[576,128]{1,0:T(8,128)(2,1)S(1)}, bf16[576,128]{1,0:T(8,128)(2,1)S(1)}, u32[]{:S(2)}, u32[]{:S(2)}) collective-permute-start(bf16[576,128]{1,0:T(8,128)(2,1)S(1)} %collective-permute-done.3.refs_5_), channel_id=1, source_target_pairs={{0,1},{1,0},{2,3},{3,2},{4,5},{5,4},{6,7},{7,6},{8,9},{9,8},{10,11... | collective-permute-start | bytes 442376 | tf_op jit(solution)/shard_map/ppermute | solution.py:285
  18.5 1.5 %collective-permute-start.8 = (bf16[576,128]{1,0:T(8,128)(2,1)S(1)}, bf16[576,128]{1,0:T(8,128)(2,1)S(1)}, u32[]{:S(2)}, u32[]{:S(2)}) collective-permute-start(bf16[576,128]{1,0:T(8,128)(2,1)S(1)} %collective-permute-done.2.refs_4_), channel_id=1, source_target_pairs={{0,1},{1,0},{2,3},{3,2},{4,5},{5,4},{6,7},{7,6},{8,9},{9,8},{10,11... | collective-permute-start | bytes 442376 | tf_op jit(solution)/shard_map/ppermute | solution.py:285
  18.9 1.4 %collective-permute-start.9 = (bf16[576,128]{1,0:T(8,128)(2,1)S(1)}, bf16[576,128]{1,0:T(8,128)(2,1)S(1)}, u32[]{:S(2)}, u32[]{:S(2)}) collective-permute-start(bf16[576,128]{1,0:T(8,128)(2,1)S(1)} %collective-permute-done.4.refs_10_), channel_id=1, source_target_pairs={{0,1},{1,0},{2,3},{3,2},{4,5},{5,4},{6,7},{7,6},{8,9},{9,8},{10,11... | collective-permute-start | bytes 442376 | tf_op jit(solution)/shard_map/ppermute | solution.py:285
  19.2 1.4 %collective-permute-start.12 = (bf16[576,128]{1,0:T(8,128)(2,1)S(1)}, bf16[576,128]{1,0:T(8,128)(2,1)S(1)}, u32[]{:S(2)}, u32[]{:S(2)}) collective-permute-start(bf16[576,128]{1,0:T(8,128)(2,1)S(1)} %collective-permute-done.10.refs_12_), channel_id=1, source_target_pairs={{0,1},{1,0},{2,3},{3,2},{4,5},{5,4},{6,7},{7,6},{8,9},{9,8},{10,11... | collective-permute-start | bytes 442376 | tf_op jit(solution)/shard_map/ppermute | solution.py:285
  19.5 1.4 %collective-permute-start.13 = (bf16[576,128]{1,0:T(8,128)(2,1)S(1)}, bf16[576,128]{1,0:T(8,128)(2,1)S(1)}, u32[]{:S(2)}, u32[]{:S(2)}) collective-permute-start(bf16[576,128]{1,0:T(8,128)(2,1)S(1)} %collective-permute-done.11.refs_14_), channel_id=1, source_target_pairs={{0,1},{1,0},{2,3},{3,2},{4,5},{5,4},{6,7},{7,6},{8,9},{9,8},{10,11... | collective-permute-start | bytes 442376 | tf_op jit(solution)/shard_map/ppermute | solution.py:285
  34.3 4.1 %collective-permute-start.14 = (bf16[4,4,2,144,128]{4,3,2,1,0:T(8,128)(2,1)S(1)}, bf16[4,4,2,144,128]{4,3,2,1,0:T(8,128)(2,1)S(1)}, u32[]{:S(2)}, u32[]{:S(2)}) collective-permute-start(bf16[4,4,2,144,128]{4,3,2,1,0:T(8,128)(2,1)S(1)} %get-tuple-element.37), channel_id=1, source_target_pairs={{0,1},{1,0},{2,3},{3,2},{4,5},{5,4},{6,7},{7,6},{8,9},{9,8},{10,11... | collective-permute-start | bytes 3538952 | tf_op jit(solution)/shard_map/ppermute | solution.py:285
  38.7 8.3 %collective-permute-start.15 = (bf16[4,2,144,128]{3,2,1,0:T(8,128)(2,1)S(1)}, bf16[4,2,144,128]{3,2,1,0:T(8,128)(2,1)S(1)}, u32[]{:S(2)}, u32[]{:S(2)}) collective-permute-start(bf16[4,2,144,128]{3,2,1,0:T(8,128)(2,1)S(1)} %get-tuple-element.40), channel_id=1, source_target_pairs={{0,16},{1,129},{8,24},{9,137},{16,0},{17,145},{24,8},{25,153},{64,... | collective-permute-start | bytes 884744 | tf_op jit(solution)/shard_map/ppermute | solution.py:307
  41.8 8.5 %collective-permute-start.17 = (bf16[4,2,144,128]{3,2,1,0:T(8,128)(2,1)S(1)}, bf16[4,2,144,128]{3,2,1,0:T(8,128)(2,1)S(1)}, u32[]{:S(2)}, u32[]{:S(2)}) collective-permute-start(bf16[4,2,144,128]{3,2,1,0:T(8,128)(2,1)S(1)} %get-tuple-element.41), channel_id=1, source_target_pairs={{0,24},{1,193},{8,0},{9,201},{16,8},{17,209},{24,16},{25,217},{64,... | collective-permute-start | bytes 884744 | tf_op jit(solution)/shard_map/ppermute | solution.py:307
  42.9 7.9 %collective-permute-start.16 = (bf16[4,2,144,128]{3,2,1,0:T(8,128)(2,1)S(1)}, bf16[4,2,144,128]{3,2,1,0:T(8,128)(2,1)S(1)}, u32[]{:S(2)}, u32[]{:S(2)}) collective-permute-start(bf16[4,2,144,128]{3,2,1,0:T(8,128)(2,1)S(1)} %get-tuple-element.42), channel_id=1, source_target_pairs={{0,8},{1,65},{8,16},{9,73},{16,24},{17,81},{24,0},{25,89},{64,72},... | collective-permute-start | bytes 884744 | tf_op jit(solution)/shard_map/ppermute | solution.py:307
  51.1 5.9 %collective-permute-start.18 = (bf16[2,144,128]{2,1,0:T(8,128)(2,1)S(1)}, bf16[2,144,128]{2,1,0:T(8,128)(2,1)S(1)}, u32[]{:S(2)}, u32[]{:S(2)}) collective-permute-start(bf16[2,144,128]{2,1,0:T(8,128)(2,1)S(1)} %get-tuple-element.43), channel_id=1, source_target_pairs={{0,128},{1,17},{8,136},{9,25},{16,144},{17,1},{24,152},{25,9},{64,... | collective-permute-start | bytes 221192 | tf_op jit(solution)/shard_map/ppermute | solution.py:307
  52.5 4.5 %collective-permute-start.20 = (bf16[2,144,128]{2,1,0:T(8,128)(2,1)S(1)}, bf16[2,144,128]{2,1,0:T(8,128)(2,1)S(1)}, u32[]{:S(2)}, u32[]{:S(2)}) collective-permute-start(bf16[2,144,128]{2,1,0:T(8,128)(2,1)S(1)} %get-tuple-element.44), channel_id=1, source_target_pairs={{0,192},{1,25},{8,200},{9,1},{16,208},{17,9},{24,216},{25,17},{64,... | collective-permute-start | bytes 221192 | tf_op jit(solution)/shard_map/ppermute | solution.py:307
  53.6 5.6 %collective-permute-start.19 = (bf16[2,144,128]{2,1,0:T(8,128)(2,1)S(1)}, bf16[2,144,128]{2,1,0:T(8,128)(2,1)S(1)}, u32[]{:S(2)}, u32[]{:S(2)}) collective-permute-start(bf16[2,144,128]{2,1,0:T(8,128)(2,1)S(1)} %get-tuple-element.45), channel_id=1, source_target_pairs={{0,64},{1,9},{8,72},{9,17},{16,80},{17,25},{24,88},{25,1},{64,128}... | collective-permute-start | bytes 221192 | tf_op jit(solution)/shard_map/ppermute | solution.py:307

commit v10 on v9

--- a/solution.py
+++ b/solution.py
@@ -141,7 +141,7 @@
 def main_kernel(place_ref, query_blocks_ref, key_blocks_ref, qt_ref, *refs):
     k_refs, refs = refs[: 2 * NG], refs[2 * NG :]
     e1_ref, gp1_ref, stat_ref, gl_ref, gr_ref, got_ref = refs[:6]
-    dqt_ref, own_w_ref, other_ref, kt_s, k_s, e_s, gp_s, other_w_s = refs[6:]
+    own_w_ref, other_w_s, other_ref, kt_s, k_s, e_s, gp_s = refs[6:]
     limits = positions(place_ref, query_blocks_ref, key_blocks_ref)
     w_refs = (own_w_ref, other_w_s)
     for slot, pair in enumerate(halves(k_refs)):
@@ -184,14 +184,6 @@
         e, gp = load(h, c)
         ds = (e * (factors[h][c] * softmax_scale) * (gp - corrs[h])).astype(BF)
         keep(h, c, 1, ds)
-
-    def to_queries(h):
-        for r in range(2):
-            rows = slice(r * DK // 2, (r + 1) * DK // 2)
-            at = (2 * h + 1) * TILE
-            out = dot(kt_s[rows, : KEYS // 2], own_w_ref[:, at : at + TILE])
-            out = out + dot(kt_s[rows, KEYS // 2 :], other_w_s[:, at : at + TILE])
-            dqt_ref[h, rows, :] = out.astype(BF)
 
     for step in range(H_LOC + 2):
         if 1 <= step <= H_LOC:
@@ -211,9 +203,17 @@
                 correct(step - 1, c)
             if step >= 2:
                 differ(step - 2, c)
-        if step >= 2:
-            to_queries(step - 2)
     to_keys(place_ref, 1, other_w_s, gl_ref, gr_ref, other_ref)
+
+
+def query_kernel(own_w_ref, other_w_ref, kt_ref, dqt_ref):
+    for h in range(H_LOC):
+        at = (2 * h + 1) * TILE
+        for r in range(2):
+            rows = slice(r * DK // 2, (r + 1) * DK // 2)
+            out = dot(kt_ref[rows, : KEYS // 2], own_w_ref[:, at : at + TILE])
+            out = out + dot(kt_ref[rows, KEYS // 2 :], other_w_ref[:, at : at + TILE])
+            dqt_ref[h, rows, :] = out.astype(BF)
 
 
 def own_kernel(place_ref, w_ref, gl_ref, gr_ref, own_ref):
@@ -251,21 +251,33 @@
     return pl.pallas_call(
         main_kernel,
         in_specs=[SMEM] * 3 + [VMEM] * (1 + len(k_blocks) + len(early)),
-        out_specs=[VMEM] * 3,
+        out_specs=[VMEM] * 4,
         out_shape=[
-            jax.ShapeDtypeStruct((H_LOC, DK, TILE), BF),
+            jax.ShapeDtypeStruct((KEYS // 2, H_LOC * 2 * TILE), BF),
             jax.ShapeDtypeStruct((KEYS // 2, H_LOC * 2 * TILE), BF),
             jax.ShapeDtypeStruct((4, 4, 2, PACKED, LANES), BF),
+            jax.ShapeDtypeStruct((DK, KEYS), BF),
         ],
         scratch_shapes=[
-            pltpu.VMEM((DK, KEYS), BF),
             pltpu.VMEM((rest, DK), BF),
             pltpu.VMEM((H_LOC, rest, TILE), F32),
             pltpu.VMEM((H_LOC, rest, TILE), F32),
-            pltpu.VMEM((KEYS // 2, H_LOC * 2 * TILE), BF),
         ],
         compiler_params=pltpu.CompilerParams(vmem_limit_bytes=MAIN_VMEM),
     )(place, query_blocks, key_blocks, qt, *k_blocks, *early)
+
+
+def query_part(own_weights, other_weights, kt):
+    return pl.pallas_call(
+        query_kernel,
+        in_specs=[VMEM] * 3,
+        out_specs=VMEM,
+        out_shape=jax.ShapeDtypeStruct((H_LOC, DK, TILE), BF),
+        cost_estimate=pl.CostEstimate(
+            flops=2 * KEYS * H_LOC * TILE * DK, bytes_accessed=12_000_000, transcendentals=0
+        ),
+        compiler_params=pltpu.CompilerParams(vmem_limit_bytes=16 * 1024 * 1024),
+    )(own_weights, other_weights, kt)
 
 
 def own_part(place, weights, gl, gr):
@@ -343,7 +355,8 @@
     early[2], *far = lax.optimization_barrier((early[2], *far))
     for k in [beside] + far:
         blocks += [k, swap_cores(k)]
-    dqt, weights, other = main_part(place, query_blocks, key_blocks, qt, blocks, early)
+    weights, other_weights, other, kt = main_part(place, query_blocks, key_blocks, qt, blocks, early)
+    dqt = query_part(weights, other_weights, kt)
     other = swap_cores(other)
     own = own_part(place, weights, early[3], early[4])
 

time: 76.1 us -> 76.6 us (level)
  blocking collectives: 15.9 us -> 0 us
  starting transfers between devices: 19.5 us -> 28.6 us
  local copies, waits for them, and re-layouts: 2.57 us -> 8.53 us
    all_to_all x1 -> x0, blocking collectives: 15.9 us -> none  [shards(): got = lax.all_to_all(part, ('zl', 'zh'), 0, 0, tiled=True)]
    all_to_all x0 -> x1, starting transfers between devices: none -> 8.98 us  [shards(): got = lax.all_to_all(part, ('zl', 'zh'), 0, 0, tiled=True)]
    unnamed x9 -> x23, local copies, waits for them, and re-layouts: 2.34 us -> 8.3 us
    pallas_call x0 -> x1, Pallas kernels: none -> 3.64 us  [query_part(): pl.pallas_call(query_kernel, in_specs=[VMEM] * 3, out_specs=VMEM, out_sha...]
    pallas_call x1, Pallas kernels: 13.5 us -> 10.6 us  [main_part(): pl.pallas_call(main_kernel, in_specs=[SMEM] * 3 + [VMEM] * (1 + len(k_blo...]
  transfers between devices with their start and end apart: 21 -> 22, of which waited for: 13 -> 10; matrix products, arithmetic and copies ran while one was open for 2% -> 2% of each run, Pallas kernels for 9% -> 14%
where the time goes in v10:
time: 76.6 us; the launch traced here: 76.3 us
  starting transfers between devices  28.6 us (37%)
  Pallas kernels  20.9 us (27%)
  waiting for transfers between devices  15.3 us (20%)
  local copies, waits for them, and re-layouts  8.53 us (11%)
  other arithmetic  1.76 us (2%)
  between operations  0.85 us (1%)
    ppermute x6, waiting for transfers between devices, crossed(): return lax.ppermute(x, ('y', 'x', 'c'), [(n, target(n)) for n in range(32)])  11.7 us
    pallas_call x1, Pallas kernels, main_part(): pl.pallas_call(main_kernel, in_specs=[SMEM] * 3 + [VMEM] * (1 + len(k_blo...  10.6 us
    all_to_all x1, starting transfers between devices, shards(): got = lax.all_to_all(part, ('zl', 'zh'), 0, 0, tiled=True)  8.98 us
    ppermute x6, starting transfers between devices, crossed(): return lax.ppermute(x, ('y', 'x', 'c'), [(n, target(n)) for n in range(32)])  8.77 us
    unnamed x23, local copies, waits for them, and re-layouts  8.3 us
    ppermute x6, starting transfers between devices, onward(): return lax.ppermute(x, ('y', 'zl', 'c'), pairs)  6.8 us
    pallas_call x1, Pallas kernels, query_part(): pl.pallas_call(query_kernel, in_specs=[VMEM] * 3, out_specs=VMEM, out_sha...  3.64 us
    pallas_call x1, Pallas kernels, own_part(): pl.pallas_call(own_kernel, in_specs=[SMEM] + [VMEM] * 3, out_specs=VMEM,...  3.49 us
  transfers between devices with their start and end apart: 22, of which 10 were waited for; matrix products, arithmetic and copies ran while one was open for 2% of the time, Pallas kernels for 14%

profile of v10, /device:TPU:32, one launch (start us, length us, event | category | flops | bytes accessed | tf_op | source)
XLA Modules:
  0.0 76.3 jit_solution(5400144632325056881)
XLA Ops:
  0.6 0.0 copy-start
  0.7 0.0 copy-start.5
  0.7 0.9 %copy-done = bf16[256,576]{0,1:T(8,128)(2,1)S(1)} copy-done((bf16[256,576]{0,1:T(8,128)(2,1)S(1)}, bf16[256,576]{0,1:T(8,128)(2,1)}, u32[]{:S(2)}) %copy-start) | copy-done | bytes 294936
  1.6 0.2 fusion
  1.9 1.2 %collective-permute-start.2 = (bf16[576,128]{1,0:T(8,128)(2,1)S(1)}, bf16[576,128]{1,0:T(8,128)(2,1)S(1)}, u32[]{:S(2)}, u32[]{:S(2)}) collective-permute-start(bf16[576,128]{1,0:T(8,128)(2,1)S(1)} %get-tuple-element.49.refs_0_), channel_id=1, source_target_pairs={{0,96},{1,225},{32,64},{33,193},{64,160},{65,33},{96,128},{97,1},{... | collective-permute-start | bytes 442376 | tf_op jit(solution)/shard_map/ppermute | solution.py:307
  3.1 1.6 %collective-permute-start = (bf16[576,128]{1,0:T(8,128)(2,1)S(1)}, bf16[576,128]{1,0:T(8,128)(2,1)S(1)}, u32[]{:S(2)}, u32[]{:S(2)}) collective-permute-start(bf16[576,128]{1,0:T(8,128)(2,1)S(1)} %get-tuple-element.49.refs_0_), channel_id=1, source_target_pairs={{0,64},{1,193},{32,96},{33,225},{64,128},{65,1},{96,160},{97,33},{... | collective-permute-start | bytes 442376 | tf_op jit(solution)/shard_map/ppermute | solution.py:307
  4.7 2.6 %collective-permute-start.3 = (bf16[576,128]{1,0:T(8,128)(2,1)S(1)}, bf16[576,128]{1,0:T(8,128)(2,1)S(1)}, u32[]{:S(2)}, u32[]{:S(2)}) collective-permute-start(bf16[576,128]{1,0:T(8,128)(2,1)S(1)} %get-tuple-element.48.refs_1_), channel_id=1, source_target_pairs={{0,96},{1,225},{32,64},{33,193},{64,160},{65,33},{96,128},{97,1},{... | collective-permute-start | bytes 442376 | tf_op jit(solution)/shard_map/ppermute | solution.py:307
  7.3 0.2 collective-permute-start.1
  7.5 1.8 %collective-permute-start.4 = (bf16[576,128]{1,0:T(8,128)(2,1)S(1)}, bf16[576,128]{1,0:T(8,128)(2,1)S(1)}, u32[]{:S(2)}, u32[]{:S(2)}) collective-permute-start(bf16[576,128]{1,0:T(8,128)(2,1)S(1)} %get-tuple-element.49.refs_0_), channel_id=1, source_target_pairs={{0,32},{32,0},{1,33},{33,1},{2,34},{34,2},{3,35},{35,3},{4,36},{36... | collective-permute-start | bytes 442376 | tf_op jit(solution)/shard_map/ppermute | solution.py:342
  9.4 1.4 %copy.16 = bf16[256,4,512]{2,0,1:T(8,128)(2,1)S(1)} copy(bf16[256,4,512]{2,1,0:T(4,128)(2,1)} %param.7) | data formatting | bytes 2097152 | tf_op args[2]
  10.8 0.1 pad_add_fusion.place_ref
  10.9 0.0 collective-permute-done.2.refs_4_
  10.9 0.0 collective-permute-start.11
  10.9 0.3 collective-permute-done.refs_2_
  11.2 1.1 %collective-permute-start.10 = (bf16[576,128]{1,0:T(8,128)(2,1)S(1)}, bf16[576,128]{1,0:T(8,128)(2,1)S(1)}, u32[]{:S(2)}, u32[]{:S(2)}) collective-permute-start(bf16[576,128]{1,0:T(8,128)(2,1)S(1)} %collective-permute-done.refs_2_), channel_id=1, source_target_pairs={{0,64},{1,193},{32,96},{33,225},{64,128},{65,1},{96,160},{97,33},{... | collective-permute-start | bytes 442376 | tf_op jit(solution)/shard_map/ppermute | solution.py:307
  12.3 1.6 %collective-permute-done.3.refs_5_ = bf16[576,128]{1,0:T(8,128)(2,1)S(1)} collective-permute-done((bf16[576,128]{1,0:T(8,128)(2,1)S(1)}, bf16[576,128]{1,0:T(8,128)(2,1)S(1)}, u32[]{:S(2)}, u32[]{:S(2)}) %collective-permute-start.3) | collective-permute-done | bytes 147488 | tf_op jit(solution)/shard_map/ppermute | solution.py:307
  13.9 0.7 collective-permute-done.1.refs_3_
  14.6 0.0 copy-start.6
  14.6 3.2 %shard_map.68 = (f32[4,768,256]{2,1,0:T(8,128)S(1)}, f32[4,768,256]{2,1,0:T(8,128)S(1)}, f32[2,4,8,256]{3,2,1,0:T(8,128)S(1)}, bf16[2048,512]{1,0:T(8,128)(2,1)S...) custom-call(s32[4]{0:T(128)S(1)} %pad_add_fusion.place_ref, s32[8]{0:T(128)S(1)} %copy-done.9, ...), custom_call_target="tpu_custom_call" | custom-call | flops 1711276032 | bytes 20000000 | tf_op jit(solution)/shard_map/pallas_call | solution.py:236
  17.8 0.0 collective-permute-done.4.refs_10_
  17.8 0.1 collective-permute-start.5
  17.9 0.5 collective-permute-start.6
  18.4 0.1 collective-permute-start.7
  18.5 0.0 collective-permute-done.11.refs_14_
  18.5 0.4 collective-permute-start.8
  18.9 0.0 collective-permute-done.10.refs_12_
  18.9 0.1 collective-permute-start.9
  19.0 0.7 copy-done.7
  19.7 0.0 collective-permute-done.5.refs_6_
  19.7 0.4 collective-permute-start.12
  20.1 0.0 collective-permute-done.6.refs_7_
  20.1 0.3 collective-permute-start.13
  20.4 0.0 collective-permute-done.7.refs_8_
  20.4 0.0 collective-permute-done.8.refs_9_
  20.4 0.0 collective-permute-done.9.refs_11_
  20.4 0.7 collective-permute-done.12.refs_13_
  21.1 0.4 collective-permute-done.13.refs_15_
  21.5 0.9 %copy-done.8 = bf16[576,128]{1,0:T(8,128)(2,1)S(1)} copy-done((bf16[576,128]{1,0:T(8,128)(2,1)S(1)}, bf16[576,128]{1,0:T(8,128)(2,1)}, u32[]{:S(2)}) %copy-start.8) | copy-done | bytes 147480
  22.4 10.6 %shard_map.69 = (bf16[1024,2048]{1,0:T(8,128)(2,1)S(1)}, bf16[1024,2048]{1,0:T(8,128)(2,1)S(1)}, bf16[4,4,2,144,128]{4,3,2,1,0:T(8,128)(2,1)S(1)}, bf16[576,2048]{1,0:T(8,128)(2,1)S(1)}) custom-call(s32[4]{0:T(128)S(1)} %pad_add_fusion.place_ref, s32[8]{0:T(128)S(1)} %copy-done.9, s32[8]{0:T(128)S(1)} %copy-done.10, bf16[4,576,256]{2,1,0:T(8,128)(2,1)S(1)} %bitcast.52, ...), custom_call_target="tpu_custom_call" | custom-call | tf_op jit(solution)/shard_map/pallas_call | solution.py:251
  33.0 0.4 collective-permute-start.14
  33.4 3.5 %shard_map.71 = f32[4,4,2,144,128]{4,3,2,1,0:T(8,128)S(1)} custom-call(s32[4]{0:T(128)S(1)} %pad_add_fusion.place_ref, bf16[1024,2048]{1,0:T(8,128)(2,1)S(1)} %get-tuple-element.36.own_w_ref.w_ref, bf16[2048,512]{1,0:T(8,128)(2,1)S(1)} %get-tuple-element.33.refs_19_.gl_ref, bf16[1024,64]{1,0:T(8,128)(2,1)S(1)} %get-tuple-element.34.refs_20_.gr_ref), custom_call_target="tpu_custom_call" | custom-call | flops 2415919104 | bytes 9000000 | tf_op jit(solution)/shard_map/pallas_call | solution.py:284
  36.9 0.0 collective-permute-done.14
  36.9 0.2 fusion.6
  37.1 3.3 %collective-permute-start.15 = (bf16[4,2,144,128]{3,2,1,0:T(8,128)(2,1)S(1)}, bf16[4,2,144,128]{3,2,1,0:T(8,128)(2,1)S(1)}, u32[]{:S(2)}, u32[]{:S(2)}) collective-permute-start(bf16[4,2,144,128]{3,2,1,0:T(8,128)(2,1)S(1)} %get-tuple-element.42), channel_id=1, source_target_pairs={{0,16},{1,129},{8,24},{9,137},{16,0},{17,145},{24,8},{25,153},{64,... | collective-permute-start | bytes 884744 | tf_op jit(solution)/shard_map/ppermute | solution.py:319
  40.4 1.1 %collective-permute-start.17 = (bf16[4,2,144,128]{3,2,1,0:T(8,128)(2,1)S(1)}, bf16[4,2,144,128]{3,2,1,0:T(8,128)(2,1)S(1)}, u32[]{:S(2)}, u32[]{:S(2)}) collective-permute-start(bf16[4,2,144,128]{3,2,1,0:T(8,128)(2,1)S(1)} %get-tuple-element.43), channel_id=1, source_target_pairs={{0,24},{1,193},{8,0},{9,201},{16,8},{17,209},{24,16},{25,217},{64,... | collective-permute-start | bytes 884744 | tf_op jit(solution)/shard_map/ppermute | solution.py:319
  41.5 0.9 %collective-permute-start.16 = (bf16[4,2,144,128]{3,2,1,0:T(8,128)(2,1)S(1)}, bf16[4,2,144,128]{3,2,1,0:T(8,128)(2,1)S(1)}, u32[]{:S(2)}, u32[]{:S(2)}) collective-permute-start(bf16[4,2,144,128]{3,2,1,0:T(8,128)(2,1)S(1)} %get-tuple-element.44), channel_id=1, source_target_pairs={{0,8},{1,65},{8,16},{9,73},{16,24},{17,81},{24,0},{25,89},{64,72},... | collective-permute-start | bytes 884744 | tf_op jit(solution)/shard_map/ppermute | solution.py:319
  42.4 3.2 %collective-permute-done.15 = bf16[4,2,144,128]{3,2,1,0:T(8,128)(2,1)S(1)} collective-permute-done((bf16[4,2,144,128]{3,2,1,0:T(8,128)(2,1)S(1)}, bf16[4,2,144,128]{3,2,1,0:T(8,128)(2,1)S(1)}, u32[]{:S(2)}, u32[]{:S(2)}) %collective-permute-start.15) | collective-permute-done | bytes 294944 | tf_op jit(solution)/shard_map/ppermute | solution.py:319
  45.6 3.3 %collective-permute-done.17 = bf16[4,2,144,128]{3,2,1,0:T(8,128)(2,1)S(1)} collective-permute-done((bf16[4,2,144,128]{3,2,1,0:T(8,128)(2,1)S(1)}, bf16[4,2,144,128]{3,2,1,0:T(8,128)(2,1)S(1)}, u32[]{:S(2)}, u32[]{:S(2)}) %collective-permute-start.17) | collective-permute-done | bytes 294944 | tf_op jit(solution)/shard_map/ppermute | solution.py:319
  48.9 0.6 collective-permute-done.16
  49.5 0.2 fusion.12
  49.7 1.4 %collective-permute-start.18 = (bf16[2,144,128]{2,1,0:T(8,128)(2,1)S(1)}, bf16[2,144,128]{2,1,0:T(8,128)(2,1)S(1)}, u32[]{:S(2)}, u32[]{:S(2)}) collective-permute-start(bf16[2,144,128]{2,1,0:T(8,128)(2,1)S(1)} %get-tuple-element.45), channel_id=1, source_target_pairs={{0,128},{1,17},{8,136},{9,25},{16,144},{17,1},{24,152},{25,9},{64,... | collective-permute-start | bytes 221192 | tf_op jit(solution)/shard_map/ppermute | solution.py:319
  51.1 1.1 %collective-permute-start.20 = (bf16[2,144,128]{2,1,0:T(8,128)(2,1)S(1)}, bf16[2,144,128]{2,1,0:T(8,128)(2,1)S(1)}, u32[]{:S(2)}, u32[]{:S(2)}) collective-permute-start(bf16[2,144,128]{2,1,0:T(8,128)(2,1)S(1)} %get-tuple-element.46), channel_id=1, source_target_pairs={{0,192},{1,25},{8,200},{9,1},{16,208},{17,9},{24,216},{25,17},{64,... | collective-permute-start | bytes 221192 | tf_op jit(solution)/shard_map/ppermute | solution.py:319
  52.2 0.9 %collective-permute-start.19 = (bf16[2,144,128]{2,1,0:T(8,128)(2,1)S(1)}, bf16[2,144,128]{2,1,0:T(8,128)(2,1)S(1)}, u32[]{:S(2)}, u32[]{:S(2)}) collective-permute-start(bf16[2,144,128]{2,1,0:T(8,128)(2,1)S(1)} %get-tuple-element.47), channel_id=1, source_target_pairs={{0,64},{1,9},{8,72},{9,17},{16,80},{17,25},{24,88},{25,1},{64,128}... | collective-permute-start | bytes 221192 | tf_op jit(solution)/shard_map/ppermute | solution.py:319
  53.1 2.5 %collective-permute-done.18 = bf16[2,144,128]{2,1,0:T(8,128)(2,1)S(1)} collective-permute-done((bf16[2,144,128]{2,1,0:T(8,128)(2,1)S(1)}, bf16[2,144,128]{2,1,0:T(8,128)(2,1)S(1)}, u32[]{:S(2)}, u32[]{:S(2)}) %collective-permute-start.18) | collective-permute-done | bytes 73760 | tf_op jit(solution)/shard_map/ppermute | solution.py:319
  55.6 0.0 collective-permute-done.20
  55.6 2.1 %collective-permute-done.19 = bf16[2,144,128]{2,1,0:T(8,128)(2,1)S(1)} collective-permute-done((bf16[2,144,128]{2,1,0:T(8,128)(2,1)S(1)}, bf16[2,144,128]{2,1,0:T(8,128)(2,1)S(1)}, u32[]{:S(2)}, u32[]{:S(2)}) %collective-permute-start.19) | collective-permute-done | bytes 73760 | tf_op jit(solution)/shard_map/ppermute | solution.py:319
  57.9 0.1 reshape.60
  57.9 0.1 reshape.64
  58.0 0.6 maximum_maximum_fusion
  58.7 9.0 %all-to-all-start = ((bf16[8,8,576]{2,1,0:T(8,128)(2,1)}), bf16[8,8,576]{2,1,0:T(8,128)(2,1)S(1)}, u32[]{:S(2)}, u32[]{:S(2)}) async-start(bf16[8,8,576]{2,1,0:T(8,128)(2,1)} %maximum_maximum_fusion), calls=%async_computation | async-start | bytes 163840 | tf_op jit(solution)/shard_map/all_to_all | solution.py:368
  67.7 2.2 %copy-done.2 = bf16[1024,2048]{1,0:T(8,128)(2,1)S(1)} copy-done((bf16[1024,2048]{1,0:T(8,128)(2,1)S(1)}, bf16[1024,2048]{1,0:T(8,128)(2,1)}, u32[]{:S(2)}) %copy-start.2) | copy-done | bytes 4194328
  69.8 2.2 %copy-done.4 = bf16[1024,2048]{1,0:T(8,128)(2,1)S(1)} copy-done((bf16[1024,2048]{1,0:T(8,128)(2,1)S(1)}, bf16[1024,2048]{1,0:T(8,128)(2,1)}, u32[]{:S(2)}) %copy-start.4) | copy-done | bytes 4194328
  72.0 3.6 %shard_map.70 = bf16[4,576,256]{2,1,0:T(8,128)(2,1)} custom-call(bf16[1024,2048]{1,0:T(8,128)(2,1)S(1)} %copy-done.2, bf16[1024,2048]{1,0:T(8,128)(2,1)S(1)} %copy-done.4, bf16[576,2048]{1,0:T(8,128)(2,1)S(1)} %get-tuple-element.38.kt_ref), custom_call_target="tpu_custom_call" | custom-call | flops 2415919104 | bytes 12000000 | tf_op jit(solution)/shard_map/pallas_call | solution.py:271
  75.7 0.6 convert_reduce_fusion
  (24 shorter events, 0.1 us)
Async XLA Ops:
  0.6 1.0 %copy-start = (bf16[256,576]{0,1:T(8,128)(2,1)S(1)}, bf16[256,576]{0,1:T(8,128)(2,1)}, u32[]{:S(2)}) copy-start(bf16[256,576]{0,1:T(8,128)(2,1)} %param.6) | copy-start | bytes 884740
  0.6 13.9 %copy-start.10 = (s32[8]{0:T(128)S(1)}, s32[8]{0:T(128)}, u32[]{:S(2)}) copy-start(s32[8]{0:T(128)} %key_blocks_ref.3) | copy-start | bytes 100
  0.7 13.9 %copy-start.9 = (s32[8]{0:T(128)S(1)}, s32[8]{0:T(128)}, u32[]{:S(2)}) copy-start(s32[8]{0:T(128)} %query_blocks_ref.3) | copy-start | bytes 100
  0.7 13.9 %copy-start.5 = (bf16[256,4,576]{0,2,1:T(8,128)(2,1)S(1)}, bf16[256,4,576]{0,2,1:T(8,128)(2,1)}, u32[]{:S(2)}) copy-start(bf16[256,4,576]{0,2,1:T(8,128)(2,1)} %param.5) | copy-start | bytes 3538948
  1.9 9.0 %collective-permute-start.2 = (bf16[576,128]{1,0:T(8,128)(2,1)S(1)}, bf16[576,128]{1,0:T(8,128)(2,1)S(1)}, u32[]{:S(2)}, u32[]{:S(2)}) collective-permute-start(bf16[576,128]{1,0:T(8,128)(2,1)S(1)} %get-tuple-element.49.refs_0_), channel_id=1, source_target_pairs={{0,96},{1,225},{32,64},{33,193},{64,160},{65,33},{96,128},{97,1},{... | collective-permute-start | bytes 442376 | tf_op jit(solution)/shard_map/ppermute | solution.py:307
  3.1 8.1 %collective-permute-start = (bf16[576,128]{1,0:T(8,128)(2,1)S(1)}, bf16[576,128]{1,0:T(8,128)(2,1)S(1)}, u32[]{:S(2)}, u32[]{:S(2)}) collective-permute-start(bf16[576,128]{1,0:T(8,128)(2,1)S(1)} %get-tuple-element.49.refs_0_), channel_id=1, source_target_pairs={{0,64},{1,193},{32,96},{33,225},{64,128},{65,1},{96,160},{97,33},{... | collective-permute-start | bytes 442376 | tf_op jit(solution)/shard_map/ppermute | solution.py:307
  4.7 9.2 %collective-permute-start.3 = (bf16[576,128]{1,0:T(8,128)(2,1)S(1)}, bf16[576,128]{1,0:T(8,128)(2,1)S(1)}, u32[]{:S(2)}, u32[]{:S(2)}) collective-permute-start(bf16[576,128]{1,0:T(8,128)(2,1)S(1)} %get-tuple-element.48.refs_1_), channel_id=1, source_target_pairs={{0,96},{1,225},{32,64},{33,193},{64,160},{65,33},{96,128},{97,1},{... | collective-permute-start | bytes 442376 | tf_op jit(solution)/shard_map/ppermute | solution.py:307
  7.3 7.3 %collective-permute-start.1 = (bf16[576,128]{1,0:T(8,128)(2,1)S(1)}, bf16[576,128]{1,0:T(8,128)(2,1)S(1)}, u32[]{:S(2)}, u32[]{:S(2)}) collective-permute-start(bf16[576,128]{1,0:T(8,128)(2,1)S(1)} %get-tuple-element.48.refs_1_), channel_id=1, source_target_pairs={{0,64},{1,193},{32,96},{33,225},{64,128},{65,1},{96,160},{97,33},{... | collective-permute-start | bytes 442376 | tf_op jit(solution)/shard_map/ppermute | solution.py:307
  7.5 10.3 %collective-permute-start.4 = (bf16[576,128]{1,0:T(8,128)(2,1)S(1)}, bf16[576,128]{1,0:T(8,128)(2,1)S(1)}, u32[]{:S(2)}, u32[]{:S(2)}) collective-permute-start(bf16[576,128]{1,0:T(8,128)(2,1)S(1)} %get-tuple-element.49.refs_0_), channel_id=1, source_target_pairs={{0,32},{32,0},{1,33},{33,1},{2,34},{34,2},{3,35},{35,3},{4,36},{36... | collective-permute-start | bytes 442376 | tf_op jit(solution)/shard_map/ppermute | solution.py:342
  10.9 7.6 %collective-permute-start.11 = (bf16[576,128]{1,0:T(8,128)(2,1)S(1)}, bf16[576,128]{1,0:T(8,128)(2,1)S(1)}, u32[]{:S(2)}, u32[]{:S(2)}) collective-permute-start(bf16[576,128]{1,0:T(8,128)(2,1)S(1)} %collective-permute-done.2.refs_4_), channel_id=1, source_target_pairs={{0,64},{1,193},{32,96},{33,225},{64,128},{65,1},{96,160},{97,33},{... | collective-permute-start | bytes 442376 | tf_op jit(solution)/shard_map/ppermute | solution.py:307
  11.2 7.7 %collective-permute-start.10 = (bf16[576,128]{1,0:T(8,128)(2,1)S(1)}, bf16[576,128]{1,0:T(8,128)(2,1)S(1)}, u32[]{:S(2)}, u32[]{:S(2)}) collective-permute-start(bf16[576,128]{1,0:T(8,128)(2,1)S(1)} %collective-permute-done.refs_2_), channel_id=1, source_target_pairs={{0,64},{1,193},{32,96},{33,225},{64,128},{65,1},{96,160},{97,33},{... | collective-permute-start | bytes 442376 | tf_op jit(solution)/shard_map/ppermute | solution.py:307
  14.6 6.9 %copy-start.6 = (bf16[256,4,576]{0,2,1:T(8,128)(2,1)S(1)}, bf16[256,4,576]{0,2,1:T(8,128)(2,1)}, u32[]{:S(2)}) copy-start(bf16[256,4,576]{0,2,1:T(8,128)(2,1)} %param.5) | copy-start | bytes 3538948
  17.8 1.9 %collective-permute-start.5 = (bf16[576,128]{1,0:T(8,128)(2,1)S(1)}, bf16[576,128]{1,0:T(8,128)(2,1)S(1)}, u32[]{:S(2)}, u32[]{:S(2)}) collective-permute-start(bf16[576,128]{1,0:T(8,128)(2,1)S(1)} %collective-permute-done.1.refs_3_), channel_id=1, source_target_pairs={{0,1},{1,0},{2,3},{3,2},{4,5},{5,4},{6,7},{7,6},{8,9},{9,8},{10,11... | collective-permute-start | bytes 442376 | tf_op jit(solution)/shard_map/ppermute | solution.py:297
  17.9 2.2 %collective-permute-start.6 = (bf16[576,128]{1,0:T(8,128)(2,1)S(1)}, bf16[576,128]{1,0:T(8,128)(2,1)S(1)}, u32[]{:S(2)}, u32[]{:S(2)}) collective-permute-start(bf16[576,128]{1,0:T(8,128)(2,1)S(1)} %collective-permute-done.refs_2_), channel_id=1, source_target_pairs={{0,1},{1,0},{2,3},{3,2},{4,5},{5,4},{6,7},{7,6},{8,9},{9,8},{10,11... | collective-permute-start | bytes 442376 | tf_op jit(solution)/shard_map/ppermute | solution.py:297
  18.4 2.0 %collective-permute-start.7 = (bf16[576,128]{1,0:T(8,128)(2,1)S(1)}, bf16[576,128]{1,0:T(8,128)(2,1)S(1)}, u32[]{:S(2)}, u32[]{:S(2)}) collective-permute-start(bf16[576,128]{1,0:T(8,128)(2,1)S(1)} %collective-permute-done.3.refs_5_), channel_id=1, source_target_pairs={{0,1},{1,0},{2,3},{3,2},{4,5},{5,4},{6,7},{7,6},{8,9},{9,8},{10,11... | collective-permute-start | bytes 442376 | tf_op jit(solution)/shard_map/ppermute | solution.py:297
  18.5 1.9 %collective-permute-start.8 = (bf16[576,128]{1,0:T(8,128)(2,1)S(1)}, bf16[576,128]{1,0:T(8,128)(2,1)S(1)}, u32[]{:S(2)}, u32[]{:S(2)}) collective-permute-start(bf16[576,128]{1,0:T(8,128)(2,1)S(1)} %collective-permute-done.2.refs_4_), channel_id=1, source_target_pairs={{0,1},{1,0},{2,3},{3,2},{4,5},{5,4},{6,7},{7,6},{8,9},{9,8},{10,11... | collective-permute-start | bytes 442376 | tf_op jit(solution)/shard_map/ppermute | solution.py:297
  18.9 1.5 %collective-permute-start.9 = (bf16[576,128]{1,0:T(8,128)(2,1)S(1)}, bf16[576,128]{1,0:T(8,128)(2,1)S(1)}, u32[]{:S(2)}, u32[]{:S(2)}) collective-permute-start(bf16[576,128]{1,0:T(8,128)(2,1)S(1)} %collective-permute-done.4.refs_10_), channel_id=1, source_target_pairs={{0,1},{1,0},{2,3},{3,2},{4,5},{5,4},{6,7},{7,6},{8,9},{9,8},{10,11... | collective-permute-start | bytes 442376 | tf_op jit(solution)/shard_map/ppermute | solution.py:297
  19.0 0.7 copy-start.7
  19.7 1.4 %collective-permute-start.12 = (bf16[576,128]{1,0:T(8,128)(2,1)S(1)}, bf16[576,128]{1,0:T(8,128)(2,1)S(1)}, u32[]{:S(2)}, u32[]{:S(2)}) collective-permute-start(bf16[576,128]{1,0:T(8,128)(2,1)S(1)} %collective-permute-done.10.refs_12_), channel_id=1, source_target_pairs={{0,1},{1,0},{2,3},{3,2},{4,5},{5,4},{6,7},{7,6},{8,9},{9,8},{10,11... | collective-permute-start | bytes 442376 | tf_op jit(solution)/shard_map/ppermute | solution.py:297
  20.1 1.4 %collective-permute-start.13 = (bf16[576,128]{1,0:T(8,128)(2,1)S(1)}, bf16[576,128]{1,0:T(8,128)(2,1)S(1)}, u32[]{:S(2)}, u32[]{:S(2)}) collective-permute-start(bf16[576,128]{1,0:T(8,128)(2,1)S(1)} %collective-permute-done.11.refs_14_), channel_id=1, source_target_pairs={{0,1},{1,0},{2,3},{3,2},{4,5},{5,4},{6,7},{7,6},{8,9},{9,8},{10,11... | collective-permute-start | bytes 442376 | tf_op jit(solution)/shard_map/ppermute | solution.py:297
  21.5 0.9 %copy-start.8 = (bf16[576,128]{1,0:T(8,128)(2,1)S(1)}, bf16[576,128]{1,0:T(8,128)(2,1)}, u32[]{:S(2)}) copy-start(bf16[576,128]{1,0:T(8,128)(2,1)} %copy-done.7) | copy-start | bytes 442372
  33.0 3.9 %copy-start.1 = (bf16[1024,2048]{1,0:T(8,128)(2,1)}, bf16[1024,2048]{1,0:T(8,128)(2,1)S(1)}, u32[]{:S(2)}) copy-start(bf16[1024,2048]{1,0:T(8,128)(2,1)S(1)} %get-tuple-element.36.own_w_ref.w_ref) | copy-start | bytes 12582916
  33.0 3.9 %copy-start.3 = (bf16[1024,2048]{1,0:T(8,128)(2,1)}, bf16[1024,2048]{1,0:T(8,128)(2,1)S(1)}, u32[]{:S(2)}) copy-start(bf16[1024,2048]{1,0:T(8,128)(2,1)S(1)} %get-tuple-element.37.other_w_ref) | copy-start | bytes 12582916
  33.0 3.9 %collective-permute-start.14 = (bf16[4,4,2,144,128]{4,3,2,1,0:T(8,128)(2,1)S(1)}, bf16[4,4,2,144,128]{4,3,2,1,0:T(8,128)(2,1)S(1)}, u32[]{:S(2)}, u32[]{:S(2)}) collective-permute-start(bf16[4,4,2,144,128]{4,3,2,1,0:T(8,128)(2,1)S(1)} %get-tuple-element.39), channel_id=1, source_target_pairs={{0,1},{1,0},{2,3},{3,2},{4,5},{5,4},{6,7},{7,6},{8,9},{9,8},{10,11... | collective-permute-start | bytes 3538952 | tf_op jit(solution)/shard_map/ppermute | solution.py:297
  37.1 8.5 %collective-permute-start.15 = (bf16[4,2,144,128]{3,2,1,0:T(8,128)(2,1)S(1)}, bf16[4,2,144,128]{3,2,1,0:T(8,128)(2,1)S(1)}, u32[]{:S(2)}, u32[]{:S(2)}) collective-permute-start(bf16[4,2,144,128]{3,2,1,0:T(8,128)(2,1)S(1)} %get-tuple-element.42), channel_id=1, source_target_pairs={{0,16},{1,129},{8,24},{9,137},{16,0},{17,145},{24,8},{25,153},{64,... | collective-permute-start | bytes 884744 | tf_op jit(solution)/shard_map/ppermute | solution.py:319
  40.4 8.5 %collective-permute-start.17 = (bf16[4,2,144,128]{3,2,1,0:T(8,128)(2,1)S(1)}, bf16[4,2,144,128]{3,2,1,0:T(8,128)(2,1)S(1)}, u32[]{:S(2)}, u32[]{:S(2)}) collective-permute-start(bf16[4,2,144,128]{3,2,1,0:T(8,128)(2,1)S(1)} %get-tuple-element.43), channel_id=1, source_target_pairs={{0,24},{1,193},{8,0},{9,201},{16,8},{17,209},{24,16},{25,217},{64,... | collective-permute-start | bytes 884744 | tf_op jit(solution)/shard_map/ppermute | solution.py:319
  41.5 7.9 %collective-permute-start.16 = (bf16[4,2,144,128]{3,2,1,0:T(8,128)(2,1)S(1)}, bf16[4,2,144,128]{3,2,1,0:T(8,128)(2,1)S(1)}, u32[]{:S(2)}, u32[]{:S(2)}) collective-permute-start(bf16[4,2,144,128]{3,2,1,0:T(8,128)(2,1)S(1)} %get-tuple-element.44), channel_id=1, source_target_pairs={{0,8},{1,65},{8,16},{9,73},{16,24},{17,81},{24,0},{25,89},{64,72},... | collective-permute-start | bytes 884744 | tf_op jit(solution)/shard_map/ppermute | solution.py:319
  49.7 5.9 %collective-permute-start.18 = (bf16[2,144,128]{2,1,0:T(8,128)(2,1)S(1)}, bf16[2,144,128]{2,1,0:T(8,128)(2,1)S(1)}, u32[]{:S(2)}, u32[]{:S(2)}) collective-permute-start(bf16[2,144,128]{2,1,0:T(8,128)(2,1)S(1)} %get-tuple-element.45), channel_id=1, source_target_pairs={{0,128},{1,17},{8,136},{9,25},{16,144},{17,1},{24,152},{25,9},{64,... | collective-permute-start | bytes 221192 | tf_op jit(solution)/shard_map/ppermute | solution.py:319
  51.1 4.6 %collective-permute-start.20 = (bf16[2,144,128]{2,1,0:T(8,128)(2,1)S(1)}, bf16[2,144,128]{2,1,0:T(8,128)(2,1)S(1)}, u32[]{:S(2)}, u32[]{:S(2)}) collective-permute-start(bf16[2,144,128]{2,1,0:T(8,128)(2,1)S(1)} %get-tuple-element.46), channel_id=1, source_target_pairs={{0,192},{1,25},{8,200},{9,1},{16,208},{17,9},{24,216},{25,17},{64,... | collective-permute-start | bytes 221192 | tf_op jit(solution)/shard_map/ppermute | solution.py:319
  52.2 5.6 %collective-permute-start.19 = (bf16[2,144,128]{2,1,0:T(8,128)(2,1)S(1)}, bf16[2,144,128]{2,1,0:T(8,128)(2,1)S(1)}, u32[]{:S(2)}, u32[]{:S(2)}) collective-permute-start(bf16[2,144,128]{2,1,0:T(8,128)(2,1)S(1)} %get-tuple-element.47), channel_id=1, source_target_pairs={{0,64},{1,9},{8,72},{9,17},{16,80},{17,25},{24,88},{25,1},{64,128}... | collective-permute-start | bytes 221192 | tf_op jit(solution)/shard_map/ppermute | solution.py:319
  58.7 17.0 %all-to-all-start = ((bf16[8,8,576]{2,1,0:T(8,128)(2,1)}), bf16[8,8,576]{2,1,0:T(8,128)(2,1)S(1)}, u32[]{:S(2)}, u32[]{:S(2)}) async-start(bf16[8,8,576]{2,1,0:T(8,128)(2,1)} %maximum_maximum_fusion), calls=%async_computation | async-start | bytes 163840 | tf_op jit(solution)/shard_map/all_to_all | solution.py:368
  67.7 2.2 %copy-start.2 = (bf16[1024,2048]{1,0:T(8,128)(2,1)S(1)}, bf16[1024,2048]{1,0:T(8,128)(2,1)}, u32[]{:S(2)}) copy-start(bf16[1024,2048]{1,0:T(8,128)(2,1)} %copy-done.1) | copy-start | bytes 12582916
  69.8 2.2 %copy-start.4 = (bf16[1024,2048]{1,0:T(8,128)(2,1)S(1)}, bf16[1024,2048]{1,0:T(8,128)(2,1)}, u32[]{:S(2)}) copy-start(bf16[1024,2048]{1,0:T(8,128)(2,1)} %copy-done.3) | copy-start | bytes 12582916

commit v11 on v10

--- a/solution.py
+++ b/solution.py
@@ -22,7 +22,7 @@
 LANES = 128
 OWNED = 32
 PACKED = OWNED * DK // LANES
-MAIN_VMEM = 23 * 1024 * 1024
+MAIN_VMEM = 19 * 1024 * 1024
 FIRST = 3
 
 softmax_scale = 0.07216878364870322
@@ -356,13 +356,16 @@
     for k in [beside] + far:
         blocks += [k, swap_cores(k)]
     weights, other_weights, other, kt = main_part(place, query_blocks, key_blocks, qt, blocks, early)
-    dqt = query_part(weights, other_weights, kt)
     other = swap_cores(other)
     own = own_part(place, weights, early[3], early[4])
 
     sums = [own[d] + other[d].astype(F32) for d in range(4)]
+    kt, *sums = lax.optimization_barrier((kt, *sums))
+    dqt = query_part(weights, other_weights, kt)
     for first in (True, False):
         got = [crossed(sums[d].astype(BF), first, d) for d in (2, 1, 3)]
+        if first:
+            dqt, *got = lax.optimization_barrier((dqt, *got))
         sums = sums[0] + sum(g.astype(F32) for g in got)
     part = jnp.concatenate([unpack(sums[z]).astype(BF) for z in range(2)], axis=0)
     got = lax.all_to_all(part, ("zl", "zh"), 0, 0, tiled=True)

time: 76.6 us -> 73.5 us (0.960)
  blocking collectives: 0 us -> 15.9 us
  starting transfers between devices: 28.6 us -> 20.7 us
  local copies, waits for them, and re-layouts: 8.53 us -> 2.57 us
  waiting for transfers between devices: 15.3 us -> 10.1 us
    all_to_all x0 -> x1, blocking collectives: none -> 15.9 us  [shards(): got = lax.all_to_all(part, ('zl', 'zh'), 0, 0, tiled=True)]
    all_to_all x1 -> x0, starting transfers between devices: 8.98 us -> none  [shards(): got = lax.all_to_all(part, ('zl', 'zh'), 0, 0, tiled=True)]
    unnamed x23 -> x9, local copies, waits for them, and re-layouts: 8.3 us -> 2.34 us
    ppermute x6, waiting for transfers between devices: 11.7 us -> 6.25 us  [crossed(): return lax.ppermute(x, ('y', 'x', 'c'), [(n, target(n)) for n in range(32)])]
    ppermute x6, starting transfers between devices: 8.77 us -> 9.99 us  [crossed(): return lax.ppermute(x, ('y', 'x', 'c'), [(n, target(n)) for n in range(32)])]
  transfers between devices with their start and end apart: 22 -> 21, of which waited for: 10 -> 12; matrix products, arithmetic and copies ran while one was open for 2% -> 2% of each run, Pallas kernels for 14% -> 14%
where the time goes in v11:
time: 73.5 us; the launch traced here: 72.7 us
  Pallas kernels  21.2 us (29%)
  starting transfers between devices  20.7 us (28%)
  blocking collectives  15.9 us (22%)
  waiting for transfers between devices  10.1 us (14%)
  local copies, waits for them, and re-layouts  2.57 us (3%)
  other arithmetic  1.18 us (2%)
  between operations  0.81 us (1%)
    all_to_all x1, blocking collectives, shards(): got = lax.all_to_all(part, ('zl', 'zh'), 0, 0, tiled=True)  15.9 us
    pallas_call x1, Pallas kernels, main_part(): pl.pallas_call(main_kernel, in_specs=[SMEM] * 3 + [VMEM] * (1 + len(k_blo...  10.9 us
    ppermute x6, starting transfers between devices, crossed(): return lax.ppermute(x, ('y', 'x', 'c'), [(n, target(n)) for n in range(32)])  9.99 us
    ppermute x6, starting transfers between devices, onward(): return lax.ppermute(x, ('y', 'zl', 'c'), pairs)  6.8 us
    ppermute x6, waiting for transfers between devices, crossed(): return lax.ppermute(x, ('y', 'x', 'c'), [(n, target(n)) for n in range(32)])  6.25 us
    pallas_call x1, Pallas kernels, query_part(): pl.pallas_call(query_kernel, in_specs=[VMEM] * 3, out_specs=VMEM, out_sha...  3.62 us
    pallas_call x1, Pallas kernels, own_part(): pl.pallas_call(own_kernel, in_specs=[SMEM] + [VMEM] * 3, out_specs=VMEM,...  3.52 us
    pallas_call x1, Pallas kernels, first_part(): pl.pallas_call(first_kernel, in_specs=[SMEM] * 3 + [VMEM] * (2 + 2 * FIRS...  3.19 us
  transfers between devices with their start and end apart: 21, of which 12 were waited for; matrix products, arithmetic and copies ran while one was open for 2% of the time, Pallas kernels for 14%

profile of v11, /device:TPU:32, one launch (start us, length us, event | category | flops | bytes accessed | tf_op | source)
XLA Modules:
  0.0 72.7 jit_solution(18062968552715874438)
XLA Ops:
  0.6 0.0 copy-start
  0.6 0.0 copy-start.3
  0.7 0.0 copy-start.2
  0.7 0.0 copy-start.1
  0.7 0.9 %copy-done = bf16[256,576]{0,1:T(8,128)(2,1)S(1)} copy-done((bf16[256,576]{0,1:T(8,128)(2,1)S(1)}, bf16[256,576]{0,1:T(8,128)(2,1)}, u32[]{:S(2)}) %copy-start) | copy-done | bytes 294936
  1.6 0.2 fusion
  1.9 1.2 %collective-permute-start.2 = (bf16[576,128]{1,0:T(8,128)(2,1)S(1)}, bf16[576,128]{1,0:T(8,128)(2,1)S(1)}, u32[]{:S(2)}, u32[]{:S(2)}) collective-permute-start(bf16[576,128]{1,0:T(8,128)(2,1)S(1)} %get-tuple-element.67.refs_0_), channel_id=1, source_target_pairs={{0,96},{1,225},{32,64},{33,193},{64,160},{65,33},{96,128},{97,1},{... | collective-permute-start | bytes 442376 | tf_op jit(solution)/shard_map/ppermute | solution.py:307
  3.1 1.6 %collective-permute-start = (bf16[576,128]{1,0:T(8,128)(2,1)S(1)}, bf16[576,128]{1,0:T(8,128)(2,1)S(1)}, u32[]{:S(2)}, u32[]{:S(2)}) collective-permute-start(bf16[576,128]{1,0:T(8,128)(2,1)S(1)} %get-tuple-element.67.refs_0_), channel_id=1, source_target_pairs={{0,64},{1,193},{32,96},{33,225},{64,128},{65,1},{96,160},{97,33},{... | collective-permute-start | bytes 442376 | tf_op jit(solution)/shard_map/ppermute | solution.py:307
  4.7 2.6 %collective-permute-start.3 = (bf16[576,128]{1,0:T(8,128)(2,1)S(1)}, bf16[576,128]{1,0:T(8,128)(2,1)S(1)}, u32[]{:S(2)}, u32[]{:S(2)}) collective-permute-start(bf16[576,128]{1,0:T(8,128)(2,1)S(1)} %get-tuple-element.66.refs_1_), channel_id=1, source_target_pairs={{0,96},{1,225},{32,64},{33,193},{64,160},{65,33},{96,128},{97,1},{... | collective-permute-start | bytes 442376 | tf_op jit(solution)/shard_map/ppermute | solution.py:307
  7.3 0.2 collective-permute-start.1
  7.5 1.8 %collective-permute-start.4 = (bf16[576,128]{1,0:T(8,128)(2,1)S(1)}, bf16[576,128]{1,0:T(8,128)(2,1)S(1)}, u32[]{:S(2)}, u32[]{:S(2)}) collective-permute-start(bf16[576,128]{1,0:T(8,128)(2,1)S(1)} %get-tuple-element.67.refs_0_), channel_id=1, source_target_pairs={{0,32},{32,0},{1,33},{33,1},{2,34},{34,2},{3,35},{35,3},{4,36},{36... | collective-permute-start | bytes 442376 | tf_op jit(solution)/shard_map/ppermute | solution.py:342
  9.4 1.4 %copy.16 = bf16[256,4,512]{2,0,1:T(8,128)(2,1)S(1)} copy(bf16[256,4,512]{2,1,0:T(4,128)(2,1)} %param.7) | data formatting | bytes 2097152 | tf_op args[2]
  10.8 0.1 pad_add_fusion.place_ref
  10.9 0.0 collective-permute-done.2.refs_4_
  10.9 0.0 collective-permute-start.11
  10.9 0.3 collective-permute-done.refs_2_
  11.2 1.1 %collective-permute-start.10 = (bf16[576,128]{1,0:T(8,128)(2,1)S(1)}, bf16[576,128]{1,0:T(8,128)(2,1)S(1)}, u32[]{:S(2)}, u32[]{:S(2)}) collective-permute-start(bf16[576,128]{1,0:T(8,128)(2,1)S(1)} %collective-permute-done.refs_2_), channel_id=1, source_target_pairs={{0,64},{1,193},{32,96},{33,225},{64,128},{65,1},{96,160},{97,33},{... | collective-permute-start | bytes 442376 | tf_op jit(solution)/shard_map/ppermute | solution.py:307
  12.3 1.6 %collective-permute-done.3.refs_5_ = bf16[576,128]{1,0:T(8,128)(2,1)S(1)} collective-permute-done((bf16[576,128]{1,0:T(8,128)(2,1)S(1)}, bf16[576,128]{1,0:T(8,128)(2,1)S(1)}, u32[]{:S(2)}, u32[]{:S(2)}) %collective-permute-start.3) | collective-permute-done | bytes 147488 | tf_op jit(solution)/shard_map/ppermute | solution.py:307
  13.9 0.7 collective-permute-done.1.refs_3_
  14.6 0.0 copy-done.3
  14.6 0.0 copy-done.2
  14.6 0.0 copy-done.1
  14.6 3.2 %shard_map.68 = (f32[4,768,256]{2,1,0:T(8,128)S(1)}, f32[4,768,256]{2,1,0:T(8,128)S(1)}, f32[2,4,8,256]{3,2,1,0:T(8,128)S(1)}, bf16[2048,512]{1,0:T(8,128)(2,1)S...) custom-call(s32[4]{0:T(128)S(1)} %pad_add_fusion.place_ref, s32[8]{0:T(128)S(1)} %copy-done.2, ...), custom_call_target="tpu_custom_call" | custom-call | flops 1711276032 | bytes 20000000 | tf_op jit(solution)/shard_map/pallas_call | solution.py:236
  17.8 0.0 collective-permute-done.4.refs_10_
  17.8 0.1 collective-permute-start.5
  17.9 0.5 collective-permute-start.6
  18.4 0.1 collective-permute-start.7
  18.5 0.0 collective-permute-done.11.refs_14_
  18.5 0.4 collective-permute-start.8
  18.9 0.0 collective-permute-done.10.refs_12_
  18.9 0.1 collective-permute-start.9
  19.0 0.2 collective-permute-done.5.refs_6_
  19.2 0.2 collective-permute-start.12
  19.4 0.0 collective-permute-done.6.refs_7_
  19.5 0.3 collective-permute-start.13
  19.8 0.0 collective-permute-done.7.refs_8_
  19.8 0.2 collective-permute-done.8.refs_9_
  20.0 0.3 collective-permute-done.9.refs_11_
  20.3 0.3 collective-permute-done.12.refs_13_
  20.6 0.2 collective-permute-done.13.refs_15_
  20.8 10.9 %shard_map.69 = (bf16[1024,2048]{1,0:T(8,128)(2,1)S(1)}, bf16[1024,2048]{1,0:T(8,128)(2,1)S(1)}, bf16[4,4,2,144,128]{4,3,2,1,0:T(8,128)(2,1)S(1)}, bf16[576,2048]{1,0:T(8,128)(2,1)S(1)}) custom-call(s32[4]{0:T(128)S(1)} %pad_add_fusion.place_ref, s32[8]{0:T(128)S(1)} %copy-done.2, s32[8]{0:T(128)S(1)} %copy-done.3, bf16[4,576,256]{2,1,0:T(8,128)(2,1)S(1)} %bitcast.49, ...), custom_call_target="tpu_custom_call" | custom-call | tf_op jit(solution)/shard_map/pallas_call | solution.py:251
  31.7 0.4 collective-permute-start.14
  32.1 3.5 %shard_map.70 = f32[4,4,2,144,128]{4,3,2,1,0:T(8,128)S(1)} custom-call(s32[4]{0:T(128)S(1)} %pad_add_fusion.place_ref, bf16[1024,2048]{1,0:T(8,128)(2,1)S(1)} %get-tuple-element.45.w_ref.own_w_ref, bf16[2048,512]{1,0:T(8,128)(2,1)S(1)} %get-tuple-element.42.refs_19_.gl_ref, bf16[1024,64]{1,0:T(8,128)(2,1)S(1)} %get-tuple-element.43.refs_20_.gr_ref), custom_call_target="tpu_custom_call" | custom-call | flops 2415919104 | bytes 9000000 | tf_op jit(solution)/shard_map/pallas_call | solution.py:284
  35.6 0.0 collective-permute-done.14
  35.6 0.1 fusion.4
  35.7 0.2 fusion.1
  35.9 3.3 %collective-permute-start.15 = (bf16[4,2,144,128]{3,2,1,0:T(8,128)(2,1)S(1)}, bf16[4,2,144,128]{3,2,1,0:T(8,128)(2,1)S(1)}, u32[]{:S(2)}, u32[]{:S(2)}) collective-permute-start(bf16[4,2,144,128]{3,2,1,0:T(8,128)(2,1)S(1)} %get-tuple-element.50), channel_id=1, source_target_pairs={{0,16},{1,129},{8,24},{9,137},{16,0},{17,145},{24,8},{25,153},{64,... | collective-permute-start | bytes 884744 | tf_op jit(solution)/shard_map/ppermute | solution.py:319
  39.2 0.6 collective-permute-start.16
  39.8 2.6 %collective-permute-start.17 = (bf16[4,2,144,128]{3,2,1,0:T(8,128)(2,1)S(1)}, bf16[4,2,144,128]{3,2,1,0:T(8,128)(2,1)S(1)}, u32[]{:S(2)}, u32[]{:S(2)}) collective-permute-start(bf16[4,2,144,128]{3,2,1,0:T(8,128)(2,1)S(1)} %get-tuple-element.52), channel_id=1, source_target_pairs={{0,24},{1,193},{8,0},{9,201},{16,8},{17,209},{24,16},{25,217},{64,... | collective-permute-start | bytes 884744 | tf_op jit(solution)/shard_map/ppermute | solution.py:319
  42.5 3.6 %shard_map.71 = bf16[4,576,256]{2,1,0:T(8,128)(2,1)} custom-call(bf16[1024,2048]{1,0:T(8,128)(2,1)S(1)} %get-tuple-element.45.w_ref.own_w_ref, bf16[1024,2048]{1,0:T(8,128)(2,1)S(1)} %get-tuple-element.46.other_w_ref, bf16[576,2048]{1,0:T(8,128)(2,1)S(1)} %get-tuple-element.49.kt_ref), custom_call_target="tpu_custom_call" | custom-call | flops 2415919104 | bytes 12000000 | tf_op jit(solution)/shard_map/pallas_call | solution.py:271
  46.1 0.0 collective-permute-done.15
  46.1 1.5 %collective-permute-done.16 = bf16[4,2,144,128]{3,2,1,0:T(8,128)(2,1)S(1)} collective-permute-done((bf16[4,2,144,128]{3,2,1,0:T(8,128)(2,1)S(1)}, bf16[4,2,144,128]{3,2,1,0:T(8,128)(2,1)S(1)}, u32[]{:S(2)}, u32[]{:S(2)}) %collective-permute-start.16) | collective-permute-done | bytes 294944 | tf_op jit(solution)/shard_map/ppermute | solution.py:319
  47.6 0.1 collective-permute-done.17
  47.7 0.2 fusion.8
  47.8 1.4 %collective-permute-start.18 = (bf16[2,144,128]{2,1,0:T(8,128)(2,1)S(1)}, bf16[2,144,128]{2,1,0:T(8,128)(2,1)S(1)}, u32[]{:S(2)}, u32[]{:S(2)}) collective-permute-start(bf16[2,144,128]{2,1,0:T(8,128)(2,1)S(1)} %get-tuple-element.63), channel_id=1, source_target_pairs={{0,128},{1,17},{8,136},{9,25},{16,144},{17,1},{24,152},{25,9},{64,... | collective-permute-start | bytes 221192 | tf_op jit(solution)/shard_map/ppermute | solution.py:319
  49.2 1.1 %collective-permute-start.20 = (bf16[2,144,128]{2,1,0:T(8,128)(2,1)S(1)}, bf16[2,144,128]{2,1,0:T(8,128)(2,1)S(1)}, u32[]{:S(2)}, u32[]{:S(2)}) collective-permute-start(bf16[2,144,128]{2,1,0:T(8,128)(2,1)S(1)} %get-tuple-element.64), channel_id=1, source_target_pairs={{0,192},{1,25},{8,200},{9,1},{16,208},{17,9},{24,216},{25,17},{64,... | collective-permute-start | bytes 221192 | tf_op jit(solution)/shard_map/ppermute | solution.py:319
  50.4 0.9 %collective-permute-start.19 = (bf16[2,144,128]{2,1,0:T(8,128)(2,1)S(1)}, bf16[2,144,128]{2,1,0:T(8,128)(2,1)S(1)}, u32[]{:S(2)}, u32[]{:S(2)}) collective-permute-start(bf16[2,144,128]{2,1,0:T(8,128)(2,1)S(1)} %get-tuple-element.65), channel_id=1, source_target_pairs={{0,64},{1,9},{8,72},{9,17},{16,80},{17,25},{24,88},{25,1},{64,128}... | collective-permute-start | bytes 221192 | tf_op jit(solution)/shard_map/ppermute | solution.py:319
  51.3 2.5 %collective-permute-done.18 = bf16[2,144,128]{2,1,0:T(8,128)(2,1)S(1)} collective-permute-done((bf16[2,144,128]{2,1,0:T(8,128)(2,1)S(1)}, bf16[2,144,128]{2,1,0:T(8,128)(2,1)S(1)}, u32[]{:S(2)}, u32[]{:S(2)}) %collective-permute-start.18) | collective-permute-done | bytes 73760 | tf_op jit(solution)/shard_map/ppermute | solution.py:319
  53.8 0.0 collective-permute-done.20
  53.8 2.1 %collective-permute-done.19 = bf16[2,144,128]{2,1,0:T(8,128)(2,1)S(1)} collective-permute-done((bf16[2,144,128]{2,1,0:T(8,128)(2,1)S(1)}, bf16[2,144,128]{2,1,0:T(8,128)(2,1)S(1)}, u32[]{:S(2)}, u32[]{:S(2)}) %collective-permute-start.19) | collective-permute-done | bytes 73760 | tf_op jit(solution)/shard_map/ppermute | solution.py:319
  56.0 0.1 reshape.57
  56.1 0.1 reshape.61
  56.2 15.9 %all_to_all.5 = bf16[8,8,576]{2,1,0:T(8,128)(2,1)S(1)} all-to-all(bf16[8,8,576]{2,1,0:T(8,128)(2,1)S(1)} %maximum_maximum_fusion), channel_id=1, replica_groups=mesh['y'=4,'zl'=2,'x'=4,'zh'=4,'c'=2] {'zl','zh'}, dimensions={0} | all-to-all | bytes 147456 | tf_op jit(solution)/shard_map/all_to_all | solution.py:371
  72.1 0.6 convert_reduce_fusion
  (10 shorter events, 0.1 us)
Async XLA Ops:
  0.6 1.0 %copy-start = (bf16[256,576]{0,1:T(8,128)(2,1)S(1)}, bf16[256,576]{0,1:T(8,128)(2,1)}, u32[]{:S(2)}) copy-start(bf16[256,576]{0,1:T(8,128)(2,1)} %param.6) | copy-start | bytes 884740
  0.6 13.9 %copy-start.3 = (s32[8]{0:T(128)S(1)}, s32[8]{0:T(128)}, u32[]{:S(2)}) copy-start(s32[8]{0:T(128)} %key_blocks_ref.3) | copy-start | bytes 100
  0.7 13.9 %copy-start.2 = (s32[8]{0:T(128)S(1)}, s32[8]{0:T(128)}, u32[]{:S(2)}) copy-start(s32[8]{0:T(128)} %query_blocks_ref.3) | copy-start | bytes 100
  0.7 13.9 %copy-start.1 = (bf16[256,4,576]{0,2,1:T(8,128)(2,1)S(1)}, bf16[256,4,576]{0,2,1:T(8,128)(2,1)}, u32[]{:S(2)}) copy-start(bf16[256,4,576]{0,2,1:T(8,128)(2,1)} %param.5) | copy-start | bytes 3538948
  1.9 9.0 %collective-permute-start.2 = (bf16[576,128]{1,0:T(8,128)(2,1)S(1)}, bf16[576,128]{1,0:T(8,128)(2,1)S(1)}, u32[]{:S(2)}, u32[]{:S(2)}) collective-permute-start(bf16[576,128]{1,0:T(8,128)(2,1)S(1)} %get-tuple-element.67.refs_0_), channel_id=1, source_target_pairs={{0,96},{1,225},{32,64},{33,193},{64,160},{65,33},{96,128},{97,1},{... | collective-permute-start | bytes 442376 | tf_op jit(solution)/shard_map/ppermute | solution.py:307
  3.1 8.1 %collective-permute-start = (bf16[576,128]{1,0:T(8,128)(2,1)S(1)}, bf16[576,128]{1,0:T(8,128)(2,1)S(1)}, u32[]{:S(2)}, u32[]{:S(2)}) collective-permute-start(bf16[576,128]{1,0:T(8,128)(2,1)S(1)} %get-tuple-element.67.refs_0_), channel_id=1, source_target_pairs={{0,64},{1,193},{32,96},{33,225},{64,128},{65,1},{96,160},{97,33},{... | collective-permute-start | bytes 442376 | tf_op jit(solution)/shard_map/ppermute | solution.py:307
  4.7 9.2 %collective-permute-start.3 = (bf16[576,128]{1,0:T(8,128)(2,1)S(1)}, bf16[576,128]{1,0:T(8,128)(2,1)S(1)}, u32[]{:S(2)}, u32[]{:S(2)}) collective-permute-start(bf16[576,128]{1,0:T(8,128)(2,1)S(1)} %get-tuple-element.66.refs_1_), channel_id=1, source_target_pairs={{0,96},{1,225},{32,64},{33,193},{64,160},{65,33},{96,128},{97,1},{... | collective-permute-start | bytes 442376 | tf_op jit(solution)/shard_map/ppermute | solution.py:307
  7.3 7.3 %collective-permute-start.1 = (bf16[576,128]{1,0:T(8,128)(2,1)S(1)}, bf16[576,128]{1,0:T(8,128)(2,1)S(1)}, u32[]{:S(2)}, u32[]{:S(2)}) collective-permute-start(bf16[576,128]{1,0:T(8,128)(2,1)S(1)} %get-tuple-element.66.refs_1_), channel_id=1, source_target_pairs={{0,64},{1,193},{32,96},{33,225},{64,128},{65,1},{96,160},{97,33},{... | collective-permute-start | bytes 442376 | tf_op jit(solution)/shard_map/ppermute | solution.py:307
  7.5 10.3 %collective-permute-start.4 = (bf16[576,128]{1,0:T(8,128)(2,1)S(1)}, bf16[576,128]{1,0:T(8,128)(2,1)S(1)}, u32[]{:S(2)}, u32[]{:S(2)}) collective-permute-start(bf16[576,128]{1,0:T(8,128)(2,1)S(1)} %get-tuple-element.67.refs_0_), channel_id=1, source_target_pairs={{0,32},{32,0},{1,33},{33,1},{2,34},{34,2},{3,35},{35,3},{4,36},{36... | collective-permute-start | bytes 442376 | tf_op jit(solution)/shard_map/ppermute | solution.py:342
  10.9 7.6 %collective-permute-start.11 = (bf16[576,128]{1,0:T(8,128)(2,1)S(1)}, bf16[576,128]{1,0:T(8,128)(2,1)S(1)}, u32[]{:S(2)}, u32[]{:S(2)}) collective-permute-start(bf16[576,128]{1,0:T(8,128)(2,1)S(1)} %collective-permute-done.2.refs_4_), channel_id=1, source_target_pairs={{0,64},{1,193},{32,96},{33,225},{64,128},{65,1},{96,160},{97,33},{... | collective-permute-start | bytes 442376 | tf_op jit(solution)/shard_map/ppermute | solution.py:307
  11.2 7.7 %collective-permute-start.10 = (bf16[576,128]{1,0:T(8,128)(2,1)S(1)}, bf16[576,128]{1,0:T(8,128)(2,1)S(1)}, u32[]{:S(2)}, u32[]{:S(2)}) collective-permute-start(bf16[576,128]{1,0:T(8,128)(2,1)S(1)} %collective-permute-done.refs_2_), channel_id=1, source_target_pairs={{0,64},{1,193},{32,96},{33,225},{64,128},{65,1},{96,160},{97,33},{... | collective-permute-start | bytes 442376 | tf_op jit(solution)/shard_map/ppermute | solution.py:307
  17.8 1.5 %collective-permute-start.5 = (bf16[576,128]{1,0:T(8,128)(2,1)S(1)}, bf16[576,128]{1,0:T(8,128)(2,1)S(1)}, u32[]{:S(2)}, u32[]{:S(2)}) collective-permute-start(bf16[576,128]{1,0:T(8,128)(2,1)S(1)} %collective-permute-done.1.refs_3_), channel_id=1, source_target_pairs={{0,1},{1,0},{2,3},{3,2},{4,5},{5,4},{6,7},{7,6},{8,9},{9,8},{10,11... | collective-permute-start | bytes 442376 | tf_op jit(solution)/shard_map/ppermute | solution.py:297
  17.9 1.6 %collective-permute-start.6 = (bf16[576,128]{1,0:T(8,128)(2,1)S(1)}, bf16[576,128]{1,0:T(8,128)(2,1)S(1)}, u32[]{:S(2)}, u32[]{:S(2)}) collective-permute-start(bf16[576,128]{1,0:T(8,128)(2,1)S(1)} %collective-permute-done.refs_2_), channel_id=1, source_target_pairs={{0,1},{1,0},{2,3},{3,2},{4,5},{5,4},{6,7},{7,6},{8,9},{9,8},{10,11... | collective-permute-start | bytes 442376 | tf_op jit(solution)/shard_map/ppermute | solution.py:297
  18.4 1.4 %collective-permute-start.7 = (bf16[576,128]{1,0:T(8,128)(2,1)S(1)}, bf16[576,128]{1,0:T(8,128)(2,1)S(1)}, u32[]{:S(2)}, u32[]{:S(2)}) collective-permute-start(bf16[576,128]{1,0:T(8,128)(2,1)S(1)} %collective-permute-done.3.refs_5_), channel_id=1, source_target_pairs={{0,1},{1,0},{2,3},{3,2},{4,5},{5,4},{6,7},{7,6},{8,9},{9,8},{10,11... | collective-permute-start | bytes 442376 | tf_op jit(solution)/shard_map/ppermute | solution.py:297
  18.5 1.5 %collective-permute-start.8 = (bf16[576,128]{1,0:T(8,128)(2,1)S(1)}, bf16[576,128]{1,0:T(8,128)(2,1)S(1)}, u32[]{:S(2)}, u32[]{:S(2)}) collective-permute-start(bf16[576,128]{1,0:T(8,128)(2,1)S(1)} %collective-permute-done.2.refs_4_), channel_id=1, source_target_pairs={{0,1},{1,0},{2,3},{3,2},{4,5},{5,4},{6,7},{7,6},{8,9},{9,8},{10,11... | collective-permute-start | bytes 442376 | tf_op jit(solution)/shard_map/ppermute | solution.py:297
  18.9 1.4 %collective-permute-start.9 = (bf16[576,128]{1,0:T(8,128)(2,1)S(1)}, bf16[576,128]{1,0:T(8,128)(2,1)S(1)}, u32[]{:S(2)}, u32[]{:S(2)}) collective-permute-start(bf16[576,128]{1,0:T(8,128)(2,1)S(1)} %collective-permute-done.4.refs_10_), channel_id=1, source_target_pairs={{0,1},{1,0},{2,3},{3,2},{4,5},{5,4},{6,7},{7,6},{8,9},{9,8},{10,11... | collective-permute-start | bytes 442376 | tf_op jit(solution)/shard_map/ppermute | solution.py:297
  19.2 1.4 %collective-permute-start.12 = (bf16[576,128]{1,0:T(8,128)(2,1)S(1)}, bf16[576,128]{1,0:T(8,128)(2,1)S(1)}, u32[]{:S(2)}, u32[]{:S(2)}) collective-permute-start(bf16[576,128]{1,0:T(8,128)(2,1)S(1)} %collective-permute-done.10.refs_12_), channel_id=1, source_target_pairs={{0,1},{1,0},{2,3},{3,2},{4,5},{5,4},{6,7},{7,6},{8,9},{9,8},{10,11... | collective-permute-start | bytes 442376 | tf_op jit(solution)/shard_map/ppermute | solution.py:297
  19.5 1.4 %collective-permute-start.13 = (bf16[576,128]{1,0:T(8,128)(2,1)S(1)}, bf16[576,128]{1,0:T(8,128)(2,1)S(1)}, u32[]{:S(2)}, u32[]{:S(2)}) collective-permute-start(bf16[576,128]{1,0:T(8,128)(2,1)S(1)} %collective-permute-done.11.refs_14_), channel_id=1, source_target_pairs={{0,1},{1,0},{2,3},{3,2},{4,5},{5,4},{6,7},{7,6},{8,9},{9,8},{10,11... | collective-permute-start | bytes 442376 | tf_op jit(solution)/shard_map/ppermute | solution.py:297
  31.7 3.9 %collective-permute-start.14 = (bf16[4,4,2,144,128]{4,3,2,1,0:T(8,128)(2,1)S(1)}, bf16[4,4,2,144,128]{4,3,2,1,0:T(8,128)(2,1)S(1)}, u32[]{:S(2)}, u32[]{:S(2)}) collective-permute-start(bf16[4,4,2,144,128]{4,3,2,1,0:T(8,128)(2,1)S(1)} %get-tuple-element.48), channel_id=1, source_target_pairs={{0,1},{1,0},{2,3},{3,2},{4,5},{5,4},{6,7},{7,6},{8,9},{9,8},{10,11... | collective-permute-start | bytes 3538952 | tf_op jit(solution)/shard_map/ppermute | solution.py:297
  35.9 10.2 %collective-permute-start.15 = (bf16[4,2,144,128]{3,2,1,0:T(8,128)(2,1)S(1)}, bf16[4,2,144,128]{3,2,1,0:T(8,128)(2,1)S(1)}, u32[]{:S(2)}, u32[]{:S(2)}) collective-permute-start(bf16[4,2,144,128]{3,2,1,0:T(8,128)(2,1)S(1)} %get-tuple-element.50), channel_id=1, source_target_pairs={{0,16},{1,129},{8,24},{9,137},{16,0},{17,145},{24,8},{25,153},{64,... | collective-permute-start | bytes 884744 | tf_op jit(solution)/shard_map/ppermute | solution.py:319
  39.2 8.4 %collective-permute-start.16 = (bf16[4,2,144,128]{3,2,1,0:T(8,128)(2,1)S(1)}, bf16[4,2,144,128]{3,2,1,0:T(8,128)(2,1)S(1)}, u32[]{:S(2)}, u32[]{:S(2)}) collective-permute-start(bf16[4,2,144,128]{3,2,1,0:T(8,128)(2,1)S(1)} %get-tuple-element.51), channel_id=1, source_target_pairs={{0,8},{1,65},{8,16},{9,73},{16,24},{17,81},{24,0},{25,89},{64,72},... | collective-permute-start | bytes 884744 | tf_op jit(solution)/shard_map/ppermute | solution.py:319
  39.8 7.9 %collective-permute-start.17 = (bf16[4,2,144,128]{3,2,1,0:T(8,128)(2,1)S(1)}, bf16[4,2,144,128]{3,2,1,0:T(8,128)(2,1)S(1)}, u32[]{:S(2)}, u32[]{:S(2)}) collective-permute-start(bf16[4,2,144,128]{3,2,1,0:T(8,128)(2,1)S(1)} %get-tuple-element.52), channel_id=1, source_target_pairs={{0,24},{1,193},{8,0},{9,201},{16,8},{17,209},{24,16},{25,217},{64,... | collective-permute-start | bytes 884744 | tf_op jit(solution)/shard_map/ppermute | solution.py:319
  47.8 5.9 %collective-permute-start.18 = (bf16[2,144,128]{2,1,0:T(8,128)(2,1)S(1)}, bf16[2,144,128]{2,1,0:T(8,128)(2,1)S(1)}, u32[]{:S(2)}, u32[]{:S(2)}) collective-permute-start(bf16[2,144,128]{2,1,0:T(8,128)(2,1)S(1)} %get-tuple-element.63), channel_id=1, source_target_pairs={{0,128},{1,17},{8,136},{9,25},{16,144},{17,1},{24,152},{25,9},{64,... | collective-permute-start | bytes 221192 | tf_op jit(solution)/shard_map/ppermute | solution.py:319
  49.2 4.6 %collective-permute-start.20 = (bf16[2,144,128]{2,1,0:T(8,128)(2,1)S(1)}, bf16[2,144,128]{2,1,0:T(8,128)(2,1)S(1)}, u32[]{:S(2)}, u32[]{:S(2)}) collective-permute-start(bf16[2,144,128]{2,1,0:T(8,128)(2,1)S(1)} %get-tuple-element.64), channel_id=1, source_target_pairs={{0,192},{1,25},{8,200},{9,1},{16,208},{17,9},{24,216},{25,17},{64,... | collective-permute-start | bytes 221192 | tf_op jit(solution)/shard_map/ppermute | solution.py:319
  50.4 5.6 %collective-permute-start.19 = (bf16[2,144,128]{2,1,0:T(8,128)(2,1)S(1)}, bf16[2,144,128]{2,1,0:T(8,128)(2,1)S(1)}, u32[]{:S(2)}, u32[]{:S(2)}) collective-permute-start(bf16[2,144,128]{2,1,0:T(8,128)(2,1)S(1)} %get-tuple-element.65), channel_id=1, source_target_pairs={{0,64},{1,9},{8,72},{9,17},{16,80},{17,25},{24,88},{25,1},{64,128}... | collective-permute-start | bytes 221192 | tf_op jit(solution)/shard_map/ppermute | solution.py:319
